TPU v7x, 32 devices: a whole 2x2x4 slice. The times are simulated.
32 devices in a mesh: seq: 32 (over z, y, x, core).
Axes of the slice: x: 2, y: 2, z: 4, core: 2. Of those that a mesh axis runs over, the one named last changes fastest.
Arguments:
- tokens: float32 [4096, 256], P('seq'), may hold values from -6 to 6
- resets: int32 [4096], P('seq'), may hold values from 0 to 1, as said below
- pad_mask: int32 [4096], P('seq'), may hold values 0 or 1
- norm_gain: float32 [1, 256], replicated, may hold values from 0.5 to 1.5
- w_in: float32 [1, 256, 1024], replicated, may hold values from -0.375 to 0.375
- conv_w: float32 [1, 4, 512], replicated, may hold values from -3 to 3
- conv_b: float32 [1, 512], replicated, may hold values from -3 to 3
- w_x: float32 [1, 512, 48], replicated, may hold values from -0.25 to 0.25
- w_dt: float32 [1, 16, 512], replicated, may hold values from -1.5 to 1.5
- dt_bias: float32 [1, 512], replicated, may hold values from -7 to -2.5
- a_log: float32 [1, 512, 16], replicated, may hold values from -10 to 1
- d_skip: float32 [1, 512], replicated, may hold values from 0.5 to 1.5
- w_out: float32 [1, 512, 256], replicated, may hold values from -0.25 to 0.25
- grad_out: float32 [4096, 256], P('seq'), may hold values from -6 to 6
Outputs:
- mixed: float32 [4096, 256], P('seq')
- grad_tokens: float32 [4096, 256], P('seq')
- grad_norm_gain: float32 [1, 256], replicated
- grad_w_in: float32 [1, 256, 1024], replicated
- grad_conv_w: float32 [1, 4, 512], replicated
- grad_conv_b: float32 [1, 512], replicated
- grad_w_x: float32 [1, 512, 48], replicated
- grad_w_dt: float32 [1, 16, 512], replicated
- grad_dt_bias: float32 [1, 512], replicated
- grad_a_log: float32 [1, 512, 16], replicated
- grad_d_skip: float32 [1, 512], replicated
- grad_w_out: float32 [1, 512, 256], replicated
Inputs may be any that keep to these rules, and one draw needn't show every extreme that they name: `resets`: 1 marks the first token of a contig. One contig begins within the first 65 tokens and ends within the last 64 tokens, with no 1 inside it.
All inputs are finite; a program needn't handle non-finite values. No bound on the sum of `pad_mask` on one device may be relied on, other than what follows from the above.
Results may differ from a plain program's by a relative error of at most 0.0003.
Values sent between devices are 32-bit elements; how exact they have to be, the bound alone decides.
No kernel may reach another device: no remote copies, remote signals or barrier semaphores. Data moves between devices by JAX's collectives and lax.ppermute only.
A program may use at most 192 MiB of HBM per device.

v0:
```python
from functools import partial

import jax
import jax.numpy as jnp
from jax import lax
from jax.sharding import PartitionSpec as P

epsilon = 1e-05
precise = lax.Precision.HIGHEST


def padded_2(block, sides, width):
    for axis, dim in sides:
        count = lax.axis_size(axis)
        forward = [(i, i + 1) for i in range(count - 1)]
        backward = [(target, source) for source, target in forward]
        low = lax.ppermute(
            lax.slice_in_dim(block, block.shape[dim] - width, None, axis=dim), axis, forward
        )
        high = lax.ppermute(lax.slice_in_dim(block, 0, width, axis=dim), axis, backward)
        block = jnp.concatenate([low, block, high], axis=dim)
    return block


def entering(value, axis, join, neutral, backward):
    count, mine = (lax.axis_size(axis), lax.axis_index(axis))
    pieces = jax.tree.map(lambda part: lax.all_gather(part, axis), value)
    if backward:
        pieces = jax.tree.map(lambda part: part[::-1], pieces)
        mine = count - 1 - mine
    so_far = jax.tree.map(
        lambda part, zero: jnp.full_like(part, 0) + jnp.asarray(zero, part.dtype), value, neutral
    )

    def step(position, so_far):
        longer = join(so_far, jax.tree.map(lambda part: part[position], pieces))
        return jax.tree.map(lambda new, old: jnp.where(position < mine, new, old), longer, so_far)

    return lax.fori_loop(0, count - 1, step, so_far)


def matmul(left, right):
    return jnp.dot(left, right, precision=precise, preferred_element_type=jnp.float32)


def section_one(inputs, norm_gain, w_in, pad_rows):
    inner_dim = w_in.shape[1] // 2
    factor = lax.rsqrt(jnp.mean(inputs * inputs, axis=1, keepdims=True) + epsilon)
    normed = inputs * factor * norm_gain
    fwd_proj = matmul(normed, w_in)
    rev_proj = matmul(normed[:, ::-1], w_in)
    return (
        fwd_proj[:, :inner_dim] * pad_rows[:, None],
        fwd_proj[:, inner_dim:],
        rev_proj[:, :inner_dim] * pad_rows[:, None],
        rev_proj[:, inner_dim:],
    )


def prepare(extended, cut_rows, conv_w, conv_b, w_x, w_dt, dt_bias):
    padded = jnp.concatenate([jnp.ones((3,), jnp.float32), cut_rows])
    valid_one = padded[3:]
    valid_two = valid_one * padded[2:-1]
    valid_three = valid_two * padded[1:-2]
    summed = conv_b + conv_w[0] * extended[3:]
    summed = summed + conv_w[1] * (valid_one[:, None] * extended[2:-1])
    summed = summed + conv_w[2] * (valid_two[:, None] * extended[1:-2])
    summed = summed + conv_w[3] * (valid_three[:, None] * extended[:-3])
    conv_out = jax.nn.silu(summed)
    doubled = matmul(conv_out, w_x)
    rank_width = w_dt.shape[0]
    state_width = (w_x.shape[1] - rank_width) // 2
    delta = jax.nn.softplus(matmul(doubled[:, :rank_width], w_dt) + dt_bias)
    return (
        conv_out,
        delta,
        doubled[:, rank_width : rank_width + state_width],
        doubled[:, rank_width + state_width :],
    )


def section_two(bordered, xb_fwd, xb_rev, conv_w, conv_b, w_x, w_dt, dt_bias, cut_fwd, cut_rev):
    ext_fwd = jnp.concatenate([bordered[:3], xb_fwd], axis=0)
    ext_rev = jnp.concatenate([xb_rev, bordered[-3:]], axis=0)[::-1]
    return prepare(ext_fwd, cut_fwd, conv_w, conv_b, w_x, w_dt, dt_bias) + prepare(
        ext_rev, cut_rev, conv_w, conv_b, w_x, w_dt, dt_bias
    )


def block_size():
    return 32


def recur(conv_out, delta, b_rows, c_rows, cut_rows, a_neg, start_state):
    length, inner_dim = conv_out.shape
    block_len = block_size()
    block_count = length // block_len

    def one_block(carried, pieces):
        x_block, d_block, b_block, c_block, k_block = pieces
        outputs = []
        for position in range(block_len):
            decay = jnp.exp(d_block[position][:, None] * a_neg) * k_block[position]
            carried = (
                decay * carried
                + (d_block[position] * x_block[position])[:, None] * b_block[position][None, :]
            )
            outputs.append(jnp.sum(carried * c_block[position][None, :], axis=1))
        return (carried, jnp.stack(outputs))

    pieces = (
        conv_out.reshape(block_count, block_len, inner_dim),
        delta.reshape(block_count, block_len, inner_dim),
        b_rows.reshape(block_count, block_len, -1),
        c_rows.reshape(block_count, block_len, -1),
        cut_rows.reshape(block_count, block_len),
    )
    final, outputs = lax.scan(jax.checkpoint(one_block), start_state, pieces)
    return (final, outputs.reshape(length, inner_dim))


def run_scan(conv_out, delta, b_rows, c_rows, a_log, d_skip, cut_rows, carry):
    final, outputs = recur(conv_out, delta, b_rows, c_rows, cut_rows, -jnp.exp(a_log), carry)
    return (outputs + d_skip * conv_out, final)


def summarize(conv_out, delta, b_rows, c_rows, a_log, cut_rows):
    a_neg = -jnp.exp(a_log)
    total = jnp.sum(delta, axis=0)
    running = jnp.cumsum(delta, axis=0)
    kept_from = jnp.cumprod(cut_rows[::-1])[::-1]
    kept_after = jnp.concatenate([kept_from[1:], jnp.ones((1,), jnp.float32)])
    weight = (
        jnp.exp((total[None, :] - running)[:, :, None] * a_neg[None]) * kept_after[:, None, None]
    )
    final = jnp.einsum("ti,tn,tin->in", delta * conv_out, b_rows, weight, precision=precise)
    product = jnp.exp(a_neg * total[:, None]) * jnp.prod(cut_rows)
    return (product, final)


def adjoint_sum(delta, c_rows, cut_rows, a_neg, grad_y):
    running = jnp.cumsum(delta, axis=0)
    kept_upto = jnp.cumprod(cut_rows)
    weight = jnp.exp(running[:, :, None] * a_neg[None]) * kept_upto[:, None, None]
    return jnp.einsum("ti,tn,tin->in", grad_y, c_rows, weight, precision=precise)


def compose(earlier, later):
    return (earlier[0] * later[0], earlier[1] * later[0] + later[1])


def tail(y_fwd, y_rev, z_fwd, z_rev, w_out):
    out_fwd = y_fwd * jax.nn.silu(z_fwd)
    out_rev = y_rev[::-1] * jax.nn.silu(z_rev)
    return matmul(out_fwd, w_out) + matmul(out_rev, w_out)[:, ::-1]


def layer_forward(inputs, weights, masks):
    norm_gain, w_in, conv_w, conv_b, w_x, w_dt, dt_bias, a_log, d_skip, w_out = weights
    cut_fwd, cut_rev, pad_rows, edge_last, edge_first, first_keep = masks
    first_out, first_back = jax.vjp(
        partial(section_one, pad_rows=pad_rows), inputs, norm_gain, w_in
    )
    xb_fwd, z_fwd, xb_rev, z_rev = first_out
    border = jnp.concatenate(
        [xb_rev[:3] * edge_first[:, None], xb_fwd[-3:] * edge_last[:, None]], axis=0
    )
    bordered = padded_2(border, (("seq", 0),), 3)
    second_out, second_back = jax.vjp(
        partial(section_two, cut_fwd=cut_fwd, cut_rev=cut_rev),
        bordered,
        xb_fwd,
        xb_rev,
        conv_w,
        conv_b,
        w_x,
        w_dt,
        dt_bias,
    )
    parts_fwd = second_out[:4]
    parts_rev = second_out[4:]
    decay_fwd, local_fwd = summarize(*parts_fwd, a_log, cut_fwd)
    decay_rev, local_rev = summarize(*parts_rev, a_log, cut_rev)
    identity = (jnp.ones_like(decay_fwd), jnp.zeros_like(decay_fwd))
    carry_fwd = entering((decay_fwd, local_fwd), "seq", compose, identity, False)[1]
    carry_rev = entering(
        (first_keep * decay_rev, first_keep * local_rev), "seq", compose, identity, True
    )[1]
    y_fwd = run_scan(*parts_fwd, a_log, d_skip, cut_fwd, carry_fwd)[0]
    y_rev = run_scan(*parts_rev, a_log, d_skip, cut_rev, carry_rev)[0]
    tail_out, tail_back = jax.vjp(tail, y_fwd, y_rev, z_fwd, z_rev, w_out)
    result = inputs + tail_out
    record = (
        first_back,
        second_back,
        tail_back,
        parts_fwd,
        parts_rev,
        carry_fwd,
        carry_rev,
        decay_fwd,
        decay_rev,
    )
    return (result, record)


def layer_backward(upstream, record, weights, masks):
    norm_gain, w_in, conv_w, conv_b, w_x, w_dt, dt_bias, a_log, d_skip, w_out = weights
    cut_fwd, cut_rev, pad_rows, edge_last, edge_first, first_keep = masks
    (
        first_back,
        second_back,
        tail_back,
        parts_fwd,
        parts_rev,
        carry_fwd,
        carry_rev,
        decay_fwd,
        decay_rev,
    ) = record
    gy_fwd, gy_rev, gz_fwd, gz_rev, grad_wout = tail_back(upstream)
    grad_wout = lax.psum(grad_wout, "seq")
    a_neg = -jnp.exp(a_log)
    mu_fwd = adjoint_sum(parts_fwd[1], parts_fwd[3], cut_fwd, a_neg, gy_fwd)
    mu_rev = adjoint_sum(parts_rev[1], parts_rev[3], cut_rev, a_neg, gy_rev)
    identity = (jnp.ones_like(decay_fwd), jnp.zeros_like(decay_fwd))
    end_fwd = entering((decay_fwd, mu_fwd), "seq", compose, identity, True)[1]
    end_rev = (
        first_keep * entering((first_keep * decay_rev, mu_rev), "seq", compose, identity, False)[1]
    )
    unused_fwd, back_fwd = jax.vjp(
        partial(run_scan, cut_rows=cut_fwd, carry=carry_fwd), *parts_fwd, a_log, d_skip
    )
    unused_rev, back_rev = jax.vjp(
        partial(run_scan, cut_rows=cut_rev, carry=carry_rev), *parts_rev, a_log, d_skip
    )
    grads_fwd = back_fwd((gy_fwd, end_fwd))
    grads_rev = back_rev((gy_rev, end_rev))
    grads_two = second_back(tuple(grads_fwd[:4]) + tuple(grads_rev[:4]))
    g_bordered, g_xb_fwd, g_xb_rev = (grads_two[0], grads_two[1], grads_two[2])
    outgoing = jnp.concatenate([g_bordered[:3], g_bordered[-3:]], axis=0)
    returned = padded_2(outgoing, (("seq", 0),), 3)
    filler = jnp.zeros((g_xb_fwd.shape[0] - 3, g_xb_fwd.shape[1]), jnp.float32)
    g_xb_fwd = g_xb_fwd + jnp.concatenate([filler, returned[-3:] * edge_last[:, None]], axis=0)
    g_xb_rev = g_xb_rev + jnp.concatenate([returned[:3] * edge_first[:, None], filler], axis=0)
    g_inputs, grad_gain, grad_win = first_back((g_xb_fwd, gz_fwd, g_xb_rev, gz_rev))
    grads = (
        grad_gain,
        grad_win,
        grads_two[3],
        grads_two[4],
        grads_two[5],
        grads_two[6],
        grads_two[7],
        grads_fwd[4] + grads_rev[4],
        grads_fwd[5] + grads_rev[5],
        grad_wout,
    )
    return (upstream + g_inputs, grads)


def body(
    tokens,
    resets,
    pad_mask,
    norm_gain,
    w_in,
    conv_w,
    conv_b,
    w_x,
    w_dt,
    dt_bias,
    a_log,
    d_skip,
    w_out,
    grad_out,
):
    keep_fwd = 1.0 - resets.astype(jnp.float32)
    cut_rev = jnp.concatenate([keep_fwd[1:], jnp.ones((1,), jnp.float32)])[::-1]
    pad_rows = pad_mask.astype(jnp.float32)
    edge_last = jnp.stack([keep_fwd[-1] * keep_fwd[-2], keep_fwd[-1], jnp.ones((), jnp.float32)])
    edge_first = jnp.stack(
        [keep_fwd[0], keep_fwd[0] * keep_fwd[1], keep_fwd[0] * keep_fwd[1] * keep_fwd[2]]
    )
    masks = (keep_fwd, cut_rev, pad_rows, edge_last, edge_first, keep_fwd[0])
    stacked = (norm_gain, w_in, conv_w, conv_b, w_x, w_dt, dt_bias, a_log, d_skip, w_out)
    layers = norm_gain.shape[0]
    current = tokens
    layer_no = 0
    weights = tuple((weight_arr[layer_no] for weight_arr in stacked))
    current, record = layer_forward(current, weights, masks)
    records = [record]
    upstream = grad_out
    per_layer = [None] * layers
    for layer_no in reversed(range(layers)):
        weights = tuple((weight_arr[layer_no] for weight_arr in stacked))
        upstream, grads = layer_backward(upstream, records[layer_no], weights, masks)
        per_layer[layer_no] = grads
    summed = tuple((jnp.stack([per_layer[0][member]]) for member in range(10)))
    others = lax.psum(summed[:9], "seq")
    summed = tuple(others) + (summed[9],)
    return (current, upstream) + tuple(summed)


def solution(mesh):
    placed = (
        P("seq", None),
        P("seq"),
        P("seq"),
        P(),
        P(),
        P(),
        P(),
        P(),
        P(),
        P(),
        P(),
        P(),
        P(),
        P("seq", None),
    )
    return jax.shard_map(
        body,
        mesh=mesh,
        in_specs=placed,
        out_specs=(
            P("seq", None),
            P("seq", None),
            P(),
            P(),
            P(),
            P(),
            P(),
            P(),
            P(),
            P(),
            P(),
            P(),
        ),
        check_vma=False,
    )
```

profile of v0, /device:TPU:0, one launch (start us, length us, event | category | flops | bytes accessed | tf_op | source)
XLA Modules:
  0.0 2292.4 jit_solution(4390522898391773759)
XLA Ops:
  54.1 53.1 %all-gather.17.cloned.1.call-done = f32[16384,16]{0,1:T(8,128)} async-done(((f32[512,16]{0,1:T(8,128)}), f32[16384,16]{0,1:T(8,128)}) %all-gather.17.cloned.1.call-update) | async-done | bytes 1048592 | tf_op jit(solution)/shard_map/all_gather | solution.py:27
  109.5 53.1 %all-gather.13.cloned.1.call-done = f32[32,512,16]{1,2,0:T(8,128)} async-done(((f32[1,512,16]{1,2,0:T(8,128)}), f32[32,512,16]{1,2,0:T(8,128)}) %all-gather.13.cloned.1.call-update) | async-done | bytes 1048592 | tf_op jit(solution)/shard_map/all_gather | solution.py:27
  164.0 24.7 %while.159 = (s32[]{:T(128)}, f32[512,16]{0,1:T(8,128)S(1)}, s32[]{:T(128)}, f32[32,512,16]{1,2,0:T(8,128)S(1)}, f32[32,512,16]{1,2,0:T(8,128)}, /*index=5*/s32[]{:T(128)}, s32[]{:T(128)}) while((s32[]{:T(128)}, f32[512,16]{0,1:T(8,128)S(1)}, s32[]{:T(128)}, f32[32,512,16]{1,2,0:T(8,128)S(1)}, f32[32,512,16]{1,2,0:T(8,128)}, ...), condition=%wide.region_46.48_spmd.clone, body=%wide.region_45.47_spmd.clone.sunk | while | flops 32772 | bytes 131173 | solution.py:39
  188.7 29.5 %all-gather.15.cloned.1.call-done = f32[16384,16]{0,1:T(8,128)} async-done(((f32[512,16]{0,1:T(8,128)}), f32[16384,16]{0,1:T(8,128)}) %all-gather.15.cloned.1.call-update) | async-done | bytes 1048592 | tf_op jit(solution)/shard_map/all_gather | solution.py:27
  221.0 53.1 %all-gather.11.cloned.1.call-done = f32[32,512,16]{1,2,0:T(8,128)} async-done(((f32[1,512,16]{1,2,0:T(8,128)}), f32[32,512,16]{1,2,0:T(8,128)}) %all-gather.11.cloned.1.call-update) | async-done | bytes 1048592 | tf_op jit(solution)/shard_map/all_gather | solution.py:27
  274.1 54.5 %while.158 = (s32[]{:T(128)}, f32[512,16]{0,1:T(8,128)S(1)}, s32[]{:T(128)}, f32[32,512,16]{1,2,0:T(8,128)}, f32[32,512,16]{1,0,2:T(8,128)}, /*index=5*/s32[]{:T(128)}, s32[]{:T(128)}) while((s32[]{:T(128)}, f32[512,16]{0,1:T(8,128)S(1)}, s32[]{:T(128)}, f32[32,512,16]{1,2,0:T(8,128)}, f32[32,512,16]{1,0,2:T(8,128)}, ...), condition=%wide.region_6.8_spmd.clone, body=%wide.region_5.7_spmd.clone.sunk | while | flops 32772 | bytes 196713 | solution.py:39
  328.7 147.1 %while.154 = (s32[]{:T(128)}, f32[512,16]{0,1:T(8,128)S(1)}, f32[4,32,512]{2,1,0:T(8,128)S(1)}, f32[4,32,512]{2,1,0:T(8,128)S(1)}, f32[512,16]{0,1:T(8,128)S(1)}...) while((s32[]{:T(128)}, f32[512,16]{0,1:T(8,128)S(1)}, ...), condition=%wide.region_40.42_spmd, body=%wide.region_7.41_spmd.sunk | while | flops 2490401 | bytes 2505589 | solution.py:118
  332.9 20.4 multiply_reduce_fusion.415
  369.6 20.4 multiply_reduce_fusion.415
  406.4 20.4 multiply_reduce_fusion.415
  443.2 20.4 multiply_reduce_fusion.415
  476.5 96.4 %while.156 = (s32[]{:T(128)}, f32[512,16]{0,1:T(8,128)S(1)}, f32[4,512,16]{1,2,0:T(8,128)}, f32[4,32,512]{2,1,0:T(8,128)S(1)}, f32[512,16]{0,1:T(8,128)S(1)}, /*...) while((s32[]{:T(128)}, f32[512,16]{0,1:T(8,128)S(1)}, ...), condition=%wide.region_85.87_spmd, body=%wide.region_84.86_spmd.sunk | while | flops 1327137 | bytes 762081 | solution.py:118
  480.2 20.4 multiply_add_fusion.277
  504.3 20.4 multiply_add_fusion.277
  528.5 20.4 multiply_add_fusion.277
  552.6 20.4 multiply_add_fusion.277
  575.8 54.5 %while.160 = (s32[]{:T(128)}, f32[512,16]{0,1:T(8,128)S(1)}, s32[]{:T(128)}, f32[32,512,16]{1,2,0:T(8,128)}, f32[32,512,16]{1,0,2:T(8,128)}, /*index=5*/s32[]{:T(128)}, s32[]{:T(128)}) while((s32[]{:T(128)}, f32[512,16]{0,1:T(8,128)S(1)}, s32[]{:T(128)}, f32[32,512,16]{1,2,0:T(8,128)}, f32[32,512,16]{1,0,2:T(8,128)}, ...), condition=%wide.region_83.85_spmd.clone, body=%wide.region_82.84_spmd.clone.sunk | while | flops 32772 | bytes 196713 | solution.py:39
  633.8 572.4 %while.161 = (s32[]{:T(128)}, f32[512,16]{0,1:T(8,128)}, f32[512,16]{0,1:T(8,128)S(1)}, f32[4,32,512]{2,1,0:T(8,128)}, f32[4,32,512]{2,1,0:T(8,128)}, /*index=5*...) while((s32[]{:T(128)}, f32[512,16]{0,1:T(8,128)}, ...), condition=%wide.region_215.217_spmd.clone, body=%wide.region_86.216_spmd.clone.sunk | while | flops 12687364 | bytes 7370059 | solution.py:118
  640.5 21.3 multiply_reduce_fusion.437
  754.0 22.5 select_add_fusion.4
  783.5 21.3 multiply_reduce_fusion.437
  897.0 22.5 select_add_fusion.4
  926.5 21.3 multiply_reduce_fusion.437
  1040.0 22.5 select_add_fusion.4
  1069.5 21.3 multiply_reduce_fusion.437
  1183.0 22.5 select_add_fusion.4
  1206.2 146.9 %while.155 = (s32[]{:T(128)}, f32[512,16]{0,1:T(8,128)S(1)}, f32[4,32,512]{2,1,0:T(8,128)S(1)}, f32[4,32,512]{2,1,0:T(8,128)S(1)}, f32[512,16]{0,1:T(8,128)S(1)}...) while((s32[]{:T(128)}, f32[512,16]{0,1:T(8,128)S(1)}, ...), condition=%wide.region_80.82_spmd, body=%wide.region_47.81_spmd.sunk | while | flops 2490401 | bytes 2505589 | solution.py:118
  1210.4 20.4 multiply_reduce_fusion.426
  1247.1 20.4 multiply_reduce_fusion.426
  1283.8 20.4 multiply_reduce_fusion.426
  1320.5 20.4 multiply_reduce_fusion.426
  1353.9 97.2 %while.157 = (s32[]{:T(128)}, f32[512,16]{0,1:T(8,128)S(1)}, f32[4,512,16]{1,2,0:T(8,128)}, f32[4,32,512]{2,1,0:T(8,128)S(1)}, f32[512,16]{0,1:T(8,128)S(1)}, /*...) while((s32[]{:T(128)}, f32[512,16]{0,1:T(8,128)S(1)}, ...), condition=%wide.region_220.222_spmd, body=%wide.region_219.221_spmd.sunk | while | flops 1327137 | bytes 762081 | solution.py:118
  1357.8 20.5 multiply_add_fusion.278
  1382.1 20.5 multiply_add_fusion.278
  1406.4 20.5 multiply_add_fusion.278
  1430.7 20.5 multiply_add_fusion.278
  1456.6 31.8 %while.162 = (s32[]{:T(128)}, f32[512,16]{0,1:T(8,128)S(1)}, s32[]{:T(128)}, f32[32,512,16]{1,2,0:T(8,128)S(1)}, f32[32,512,16]{1,0,2:T(8,128)}, /*index=5*/s32[]{:T(128)}, s32[]{:T(128)}) while((s32[]{:T(128)}, f32[512,16]{0,1:T(8,128)S(1)}, s32[]{:T(128)}, f32[32,512,16]{1,2,0:T(8,128)S(1)}, f32[32,512,16]{1,0,2:T(8,128)}, ...), condition=%wide.region_218.220_spmd.clone, body=%wide.region_217.219_spmd.clone.sunk | while | flops 32772 | bytes 196713 | solution.py:39
  1491.1 476.8 %while.163 = (s32[]{:T(128)}, f32[512,16]{0,1:T(8,128)}, f32[512,16]{0,1:T(8,128)S(1)}, f32[4,32,512]{2,1,0:T(8,128)}, f32[4,32,512]{2,1,0:T(8,128)}, /*index=5*...) while((s32[]{:T(128)}, f32[512,16]{0,1:T(8,128)}, ...), condition=%wide.region_350.352_spmd.clone, body=%wide.region_221.351_spmd.clone.sunk | while | flops 12687364 | bytes 7295523 | solution.py:118
  1496.2 20.4 multiply_reduce_fusion.465
  1588.2 21.4 select_add_fusion.5
  1615.4 20.4 multiply_reduce_fusion.465
  1707.4 21.4 select_add_fusion.5
  1734.6 20.4 multiply_reduce_fusion.465
  1826.6 21.4 select_add_fusion.5
  1853.8 20.4 multiply_reduce_fusion.465
  1945.8 21.4 select_add_fusion.5
  2014.6 119.6 %all-reduce.356.cloned.1.call-done = (f32[1,256]{1,0:T(1,128)}, f32[1,4,512]{2,1,0:T(4,128)}, f32[1,512]{1,0:T(1,128)}, f32[1,16,512]{2,1,0:T(8,128)}, f32[1,512...) async-done(((f32[1,256]{1,0:T(1,128)}, f32[1,4,512]{2,1,0:T(4,128)}, f32[1,512]{1,0:T(1,128)}, f32[1,16,512]{2,1,0:T(8,128)}, f32[1,512]{1,0:T(1,128)}, ...) | async-done | bytes 80912 | tf_op jit(solution)/shard_map/psum | solution.py:300
  2134.2 142.5 %all-reduce.358.cloned.1.call-done = (f32[1,256,1024]{2,1,0:T(8,128)}, f32[1,512,48]{1,2,0:T(8,128)}, f32[1,512,256]{2,1,0:T(8,128)}) async-done(((f32[1,256,1024]{2,1,0:T(8,128)}, f32[1,512,48]{1,2,0:T(8,128)}, f32[1,512,256]{2,1,0:T(8,128)}), (f32[1,256,1024]{2,1,0:T(8,128)}, f32[1,512,48]{1,2,0:T(8,128)}, f32[1,512,256]{2,1,0:T(8,128)})) %all-reduce.358.cloned.1.call-update) | async-done | bytes 1671184 | tf_op jit(solution)/shard_map/psum | solution.py:300
  (2523 shorter events, 1139.6 us)
Async XLA Ops:
  7.2 100.0 %all-gather.17.cloned.1.call-start = ((), (), s32[]{:S(2)}) async-start(), calls=%async_computation.3 | async-start | bytes 1081344 | tf_op jit(solution)/shard_map/all_gather | solution.py:27
  19.3 9.7 collective-permute-start.1
  22.6 8.5 collective-permute-start
  49.2 113.5 %all-gather.13.cloned.1.call-start = ((), (), s32[]{:S(2)}) async-start(), calls=%async_computation.1 | async-start | bytes 1081344 | tf_op jit(solution)/shard_map/all_gather | solution.py:27
  50.0 168.2 %all-gather.15.cloned.1.call-start = ((), (), s32[]{:S(2)}) async-start(), calls=%async_computation.2 | async-start | bytes 1081344 | tf_op jit(solution)/shard_map/all_gather | solution.py:27
  50.7 223.4 %all-gather.11.cloned.1.call-start = ((), (), s32[]{:S(2)}) async-start(), calls=%async_computation | async-start | bytes 1081344 | tf_op jit(solution)/shard_map/all_gather | solution.py:27
  51.3 521.7 %all-gather.19.cloned.1.call-start = ((), (), s32[]{:S(2)}) async-start(), calls=%async_computation.4 | async-start | bytes 1081344 | tf_op jit(solution)/shard_map/all_gather | solution.py:27
  51.9 1399.3 %all-gather.21.cloned.1.call-start = ((), (), s32[]{:S(2)}) async-start(), calls=%async_computation.5 | async-start | bytes 1081344 | tf_op jit(solution)/shard_map/all_gather | solution.py:27
  53.3 2080.9 %all-reduce.356.cloned.1.call-start = ((), (), s32[]{:S(2)}) async-start(), calls=%async_computation.6 | async-start | bytes 161792 | tf_op jit(solution)/shard_map/psum | solution.py:300
  221.0 107.7 %copy-start.24 = (f32[128,16]{1,0:T(8,128)S(1)}, f32[128,16]{1,0:T(8,128)}, u32[]{:S(2)}) copy-start(f32[128,16]{1,0:T(8,128)} %copy-done.23) | copy-start | bytes 24580
  328.7 147.8 %copy-start.27 = (f32[128,16]{1,0:T(8,128)S(1)}, f32[128,16]{1,0:T(8,128)}, u32[]{:S(2)}) copy-start(f32[128,16]{1,0:T(8,128)} %copy-done.26) | copy-start | bytes 24580
  636.4 97.8 %copy-start.40 = (f32[1,512]{1,0:T(1,128)}, f32[1,512]{1,0:T(1,128)S(1)}, u32[]{:S(2)}) copy-start(f32[1,512]{1,0:T(1,128)S(1)} %get-tuple-element.6152) | copy-start | bytes 6148 | tf_op jit(solution)/shard_map/transpose(jvp())/while
  636.4 112.3 %copy-start.39 = (f32[1,512]{1,0:T(1,128)}, f32[1,512]{1,0:T(1,128)S(1)}, u32[]{:S(2)}) copy-start(f32[1,512]{1,0:T(1,128)S(1)} %get-tuple-element.6180) | copy-start | bytes 6148 | tf_op jit(solution)/shard_map/transpose(jvp())/while
  636.5 92.7 %copy-start.80 = (f32[512]{0:T(512)}, f32[512]{0:T(512)S(1)}, u32[]{:S(2)}) copy-start(f32[512]{0:T(512)S(1)} %mul.43644) | copy-start | bytes 6148 | tf_op jit(solution)/shard_map/transpose(jvp())/while
  636.7 112.0 %copy-start.30 = (f32[512]{0:T(512)}, f32[512]{0:T(512)S(1)}, u32[]{:S(2)}) copy-start(f32[512]{0:T(512)S(1)} %mul.43633) | copy-start | bytes 6148 | tf_op jit(solution)/shard_map/transpose(jvp())/while
  636.8 97.5 %copy-start.82 = (f32[512]{0:T(512)}, f32[512]{0:T(512)S(1)}, u32[]{:S(2)}) copy-start(f32[512]{0:T(512)S(1)} %mul.43657) | copy-start | bytes 6148 | tf_op jit(solution)/shard_map/transpose(jvp())/while
  636.8 97.5 %copy-start.83 = (f32[512]{0:T(512)}, f32[512]{0:T(512)S(1)}, u32[]{:S(2)}) copy-start(f32[512]{0:T(512)S(1)} %mul.43656) | copy-start | bytes 6148 | tf_op jit(solution)/shard_map/transpose(jvp())/while
  637.0 111.7 %copy-start.92 = (f32[512]{0:T(512)}, f32[512]{0:T(512)S(1)}, u32[]{:S(2)}) copy-start(f32[512]{0:T(512)S(1)} %mul.43632) | copy-start | bytes 6148 | tf_op jit(solution)/shard_map/transpose(jvp())/while
  637.0 111.7 %copy-start.93 = (f32[512]{0:T(512)}, f32[512]{0:T(512)S(1)}, u32[]{:S(2)}) copy-start(f32[512]{0:T(512)S(1)} %mul.43631) | copy-start | bytes 6148 | tf_op jit(solution)/shard_map/transpose(jvp())/while
  639.8 108.9 %copy-start.47 = (f32[1,512]{1,0:T(1,128)}, f32[1,512]{1,0:T(1,128)S(1)}, u32[]{:S(2)}) copy-start(f32[1,512]{1,0:T(1,128)S(1)} %get-tuple-element.6202) | copy-start | bytes 6148 | tf_op jit(solution)/shard_map/transpose(jvp())/while
  779.4 97.8 %copy-start.40 = (f32[1,512]{1,0:T(1,128)}, f32[1,512]{1,0:T(1,128)S(1)}, u32[]{:S(2)}) copy-start(f32[1,512]{1,0:T(1,128)S(1)} %get-tuple-element.6152) | copy-start | bytes 6148 | tf_op jit(solution)/shard_map/transpose(jvp())/while
  779.4 112.3 %copy-start.39 = (f32[1,512]{1,0:T(1,128)}, f32[1,512]{1,0:T(1,128)S(1)}, u32[]{:S(2)}) copy-start(f32[1,512]{1,0:T(1,128)S(1)} %get-tuple-element.6180) | copy-start | bytes 6148 | tf_op jit(solution)/shard_map/transpose(jvp())/while
  779.5 92.7 %copy-start.80 = (f32[512]{0:T(512)}, f32[512]{0:T(512)S(1)}, u32[]{:S(2)}) copy-start(f32[512]{0:T(512)S(1)} %mul.43644) | copy-start | bytes 6148 | tf_op jit(solution)/shard_map/transpose(jvp())/while
  779.7 112.0 %copy-start.30 = (f32[512]{0:T(512)}, f32[512]{0:T(512)S(1)}, u32[]{:S(2)}) copy-start(f32[512]{0:T(512)S(1)} %mul.43633) | copy-start | bytes 6148 | tf_op jit(solution)/shard_map/transpose(jvp())/while
  779.8 97.5 %copy-start.82 = (f32[512]{0:T(512)}, f32[512]{0:T(512)S(1)}, u32[]{:S(2)}) copy-start(f32[512]{0:T(512)S(1)} %mul.43657) | copy-start | bytes 6148 | tf_op jit(solution)/shard_map/transpose(jvp())/while
  779.8 97.5 %copy-start.83 = (f32[512]{0:T(512)}, f32[512]{0:T(512)S(1)}, u32[]{:S(2)}) copy-start(f32[512]{0:T(512)S(1)} %mul.43656) | copy-start | bytes 6148 | tf_op jit(solution)/shard_map/transpose(jvp())/while
  780.0 111.7 %copy-start.92 = (f32[512]{0:T(512)}, f32[512]{0:T(512)S(1)}, u32[]{:S(2)}) copy-start(f32[512]{0:T(512)S(1)} %mul.43632) | copy-start | bytes 6148 | tf_op jit(solution)/shard_map/transpose(jvp())/while
  780.0 111.7 %copy-start.93 = (f32[512]{0:T(512)}, f32[512]{0:T(512)S(1)}, u32[]{:S(2)}) copy-start(f32[512]{0:T(512)S(1)} %mul.43631) | copy-start | bytes 6148 | tf_op jit(solution)/shard_map/transpose(jvp())/while
  782.8 108.9 %copy-start.47 = (f32[1,512]{1,0:T(1,128)}, f32[1,512]{1,0:T(1,128)S(1)}, u32[]{:S(2)}) copy-start(f32[1,512]{1,0:T(1,128)S(1)} %get-tuple-element.6202) | copy-start | bytes 6148 | tf_op jit(solution)/shard_map/transpose(jvp())/while
  922.5 97.8 %copy-start.40 = (f32[1,512]{1,0:T(1,128)}, f32[1,512]{1,0:T(1,128)S(1)}, u32[]{:S(2)}) copy-start(f32[1,512]{1,0:T(1,128)S(1)} %get-tuple-element.6152) | copy-start | bytes 6148 | tf_op jit(solution)/shard_map/transpose(jvp())/while
  922.5 112.3 %copy-start.39 = (f32[1,512]{1,0:T(1,128)}, f32[1,512]{1,0:T(1,128)S(1)}, u32[]{:S(2)}) copy-start(f32[1,512]{1,0:T(1,128)S(1)} %get-tuple-element.6180) | copy-start | bytes 6148 | tf_op jit(solution)/shard_map/transpose(jvp())/while
  922.8 112.0 %copy-start.30 = (f32[512]{0:T(512)}, f32[512]{0:T(512)S(1)}, u32[]{:S(2)}) copy-start(f32[512]{0:T(512)S(1)} %mul.43633) | copy-start | bytes 6148 | tf_op jit(solution)/shard_map/transpose(jvp())/while
  922.8 97.5 %copy-start.82 = (f32[512]{0:T(512)}, f32[512]{0:T(512)S(1)}, u32[]{:S(2)}) copy-start(f32[512]{0:T(512)S(1)} %mul.43657) | copy-start | bytes 6148 | tf_op jit(solution)/shard_map/transpose(jvp())/while
  922.8 97.5 %copy-start.83 = (f32[512]{0:T(512)}, f32[512]{0:T(512)S(1)}, u32[]{:S(2)}) copy-start(f32[512]{0:T(512)S(1)} %mul.43656) | copy-start | bytes 6148 | tf_op jit(solution)/shard_map/transpose(jvp())/while
  923.0 111.7 %copy-start.92 = (f32[512]{0:T(512)}, f32[512]{0:T(512)S(1)}, u32[]{:S(2)}) copy-start(f32[512]{0:T(512)S(1)} %mul.43632) | copy-start | bytes 6148 | tf_op jit(solution)/shard_map/transpose(jvp())/while
  923.1 111.7 %copy-start.93 = (f32[512]{0:T(512)}, f32[512]{0:T(512)S(1)}, u32[]{:S(2)}) copy-start(f32[512]{0:T(512)S(1)} %mul.43631) | copy-start | bytes 6148 | tf_op jit(solution)/shard_map/transpose(jvp())/while
  925.9 108.9 %copy-start.47 = (f32[1,512]{1,0:T(1,128)}, f32[1,512]{1,0:T(1,128)S(1)}, u32[]{:S(2)}) copy-start(f32[1,512]{1,0:T(1,128)S(1)} %get-tuple-element.6202) | copy-start | bytes 6148 | tf_op jit(solution)/shard_map/transpose(jvp())/while
  1065.5 97.8 %copy-start.40 = (f32[1,512]{1,0:T(1,128)}, f32[1,512]{1,0:T(1,128)S(1)}, u32[]{:S(2)}) copy-start(f32[1,512]{1,0:T(1,128)S(1)} %get-tuple-element.6152) | copy-start | bytes 6148 | tf_op jit(solution)/shard_map/transpose(jvp())/while
  1065.5 112.3 %copy-start.39 = (f32[1,512]{1,0:T(1,128)}, f32[1,512]{1,0:T(1,128)S(1)}, u32[]{:S(2)}) copy-start(f32[1,512]{1,0:T(1,128)S(1)} %get-tuple-element.6180) | copy-start | bytes 6148 | tf_op jit(solution)/shard_map/transpose(jvp())/while
  1065.8 112.0 %copy-start.30 = (f32[512]{0:T(512)}, f32[512]{0:T(512)S(1)}, u32[]{:S(2)}) copy-start(f32[512]{0:T(512)S(1)} %mul.43633) | copy-start | bytes 6148 | tf_op jit(solution)/shard_map/transpose(jvp())/while
  1065.8 97.5 %copy-start.82 = (f32[512]{0:T(512)}, f32[512]{0:T(512)S(1)}, u32[]{:S(2)}) copy-start(f32[512]{0:T(512)S(1)} %mul.43657) | copy-start | bytes 6148 | tf_op jit(solution)/shard_map/transpose(jvp())/while
  1065.9 97.5 %copy-start.83 = (f32[512]{0:T(512)}, f32[512]{0:T(512)S(1)}, u32[]{:S(2)}) copy-start(f32[512]{0:T(512)S(1)} %mul.43656) | copy-start | bytes 6148 | tf_op jit(solution)/shard_map/transpose(jvp())/while
  1066.1 111.7 %copy-start.92 = (f32[512]{0:T(512)}, f32[512]{0:T(512)S(1)}, u32[]{:S(2)}) copy-start(f32[512]{0:T(512)S(1)} %mul.43632) | copy-start | bytes 6148 | tf_op jit(solution)/shard_map/transpose(jvp())/while
  1066.1 111.7 %copy-start.93 = (f32[512]{0:T(512)}, f32[512]{0:T(512)S(1)}, u32[]{:S(2)}) copy-start(f32[512]{0:T(512)S(1)} %mul.43631) | copy-start | bytes 6148 | tf_op jit(solution)/shard_map/transpose(jvp())/while
  1068.9 108.9 %copy-start.47 = (f32[1,512]{1,0:T(1,128)}, f32[1,512]{1,0:T(1,128)S(1)}, u32[]{:S(2)}) copy-start(f32[1,512]{1,0:T(1,128)S(1)} %get-tuple-element.6202) | copy-start | bytes 6148 | tf_op jit(solution)/shard_map/transpose(jvp())/while
  1991.1 9.7 collective-permute-start.2
  1993.4 7.4 collective-permute-start.3
  2008.5 268.3 %all-reduce.358.cloned.1.call-start = ((), (), s32[]{:S(2)}) async-start(), calls=%async_computation.7 | async-start | bytes 3342336 | tf_op jit(solution)/shard_map/psum | solution.py:300
  (285 other events, 9992.8 us)
Sparse Core Ops, SparseCore 0:
  49.3 57.7 all-gather.16
  110.0 52.6 all-gather.12
  165.6 52.5 all-gather.14
  221.5 52.6 all-gather.10
  276.9 52.5 all-gather.18
  332.2 52.6 all-gather.20
  2008.6 125.6 all-reduce.355
  2142.1 134.6 all-reduce.357
where the time goes:
time: 2330 us; the launch traced here: 2290 us
  other arithmetic  1510 us (65%)
  waiting for transfers between devices  453 us (19%)
  local copies, waits for them, and re-layouts  250 us (11%)
  matrix products  32.6 us (1%)
    reduce_sum x128, other arithmetic, one_block(): decay = jnp.exp(d_block[position][:, None] * a_neg) * k_block[position]  529 us
    reduce_sum x96, other arithmetic, one_block(): outputs.append(jnp.sum(carried * c_block[position][None, :], axis=1))  417 us
    psum x2, waiting for transfers between devices, body(): others = lax.psum(summed[:9], 'seq')  262 us
    all_gather x6, waiting for transfers between devices, entering(): pieces = jax.tree.map(lambda part: lax.all_gather(part, axis), value)  189 us
    add_any x8, other arithmetic, recur(): final, outputs = lax.scan(jax.checkpoint(one_block), start_state, pieces)  176 us
    add x8, other arithmetic, one_block(): decay * carried  163 us
    reduce_sum x88, other arithmetic, one_block(): (d_block[position] * x_block[position])[:, None]  91.8 us
    dynamic_slice x93, local copies, waits for them, and re-layouts, step(): longer = join(so_far, jax.tree.map(lambda part: part[position], pieces))  91 us
  transfers between devices with their start and end apart: 12, of which 6 were waited for; matrix products, arithmetic and copies ran while one was open for 53% of the time, Pallas kernels for 0%

commit v1 on v0

v1 whole, which is shorter than its diff:
```python
import jax
import jax.numpy as jnp
from jax import lax
from jax.experimental import pallas as pl
from jax.experimental.pallas import tpu as pltpu
from jax.sharding import PartitionSpec as P

F32 = jnp.float32
BF16 = jnp.bfloat16
EPS = 1e-05
LOG2E = 1.4426950408889634
LN2 = 0.6931471805599453
BIG = 1e9
CH = 8
LANE = 128
VMEM_LIMIT = 56 * 1024 * 1024


def nn(a, b):
    return lax.dot_general(a, b, (((1,), (0,)), ((), ())), preferred_element_type=F32)


def nt(a, b):
    return lax.dot_general(a, b, (((1,), (1,)), ((), ())), preferred_element_type=F32)


def tn(a, b):
    return lax.dot_general(a, b, (((0,), (0,)), ((), ())), preferred_element_type=F32)


def split(x):
    high = x.astype(BF16)
    return high, (x - high.astype(F32)).astype(BF16)


def split3(x):
    high = x.astype(BF16)
    rest = x - high.astype(F32)
    mid = rest.astype(BF16)
    return high, mid, (rest - mid.astype(F32)).astype(BF16)


def mm(dot, a, b):
    ah, al = a if isinstance(a, tuple) else split(a)
    bh, bl = b if isinstance(b, tuple) else split(b)
    return dot(ah, bh) + (dot(ah, bl) + dot(al, bh))


def flip_matrix(size):
    rows = lax.broadcasted_iota(jnp.int32, (size, size), 0)
    cols = lax.broadcasted_iota(jnp.int32, (size, size), 1)
    return jnp.where(rows + cols == size - 1, 1.0, 0.0).astype(BF16)


def flipped(x):
    flip = flip_matrix(x.shape[1])
    high, mid, low = split3(x)
    return nn(high, flip) + (nn(mid, flip) + nn(low, flip))


def order_matrix(length):
    steps = length // CH
    rows = lax.broadcasted_iota(jnp.int32, (length, length), 0)
    cols = lax.broadcasted_iota(jnp.int32, (length, length), 1)
    token = (rows & (CH - 1)) * steps + (rows >> 3)
    return jnp.where(cols == token, 1.0, 0.0)


def exact(dot, order, x):
    high, mid, low = split3(x)
    order = order.astype(BF16)
    return dot(order, high) + (dot(order, mid) + dot(order, low))


def ordered(ref):
    return exact(nn, order_matrix(ref.shape[0]), ref[...])


def store_ordered(ref, value):
    ref[...] = exact(tn, order_matrix(ref.shape[0]), value)


def spread(row):
    length = row.shape[1]
    picked = (order_matrix(length) * row).astype(BF16)
    return nn(picked, jnp.ones((length, LANE), BF16))


def sigmoid(x):
    return 1.0 / (1.0 + jnp.exp(-x))


def normalize(x, gain):
    factor = lax.rsqrt(jnp.mean(x * x, axis=1, keepdims=True) + EPS)
    return factor, x * factor * gain


def both_orders(normed):
    flip = flip_matrix(normed.shape[1])
    high, low = split(normed)
    return (
        jnp.concatenate([high, nn(high, flip).astype(BF16)], axis=0),
        jnp.concatenate([low, nn(low, flip).astype(BF16)], axis=0),
    )


def params():
    return pltpu.CompilerParams(vmem_limit_bytes=VMEM_LIMIT)


def project_kernel(tok, pad, gain, w_in, gout, w_out, xb_o, z_o, go_o, gy_o):
    inner = w_out.shape[0]
    x = ordered(tok)
    normed = normalize(x, gain[...])[1]
    proj = mm(nn, both_orders(normed), split(w_in[...]))
    pad_col = spread(pad[...].astype(F32))
    pad_all = jnp.concatenate([pad_col, pad_col], axis=0)
    g = ordered(gout)
    gh, gl = both_orders(g)
    go = mm(nt, (gh, gl), split(w_out[...]))
    for lt in range(inner // LANE):
        cols = slice(lt * LANE, (lt + 1) * LANE)
        z = proj[:, inner + lt * LANE : inner + (lt + 1) * LANE]
        xb_o[:, cols] = proj[:, cols] * pad_all
        z_o[:, cols] = z
        go_o[:, cols] = go[:, cols]
        gy_o[:, cols] = go[:, cols] * (z * sigmoid(z))


def project(tok, pad, gain, w_in, gout, w_out):
    length, inner = tok.shape[0], w_out.shape[0]
    big = jax.ShapeDtypeStruct((2 * length, inner), F32)
    return pl.pallas_call(
        project_kernel,
        out_shape=(big, big, big, big),
        compiler_params=params(),
        name="project",
    )(tok, pad, gain, w_in, gout, w_out)


def pick_sides(from_sibling, from_other):
    odd = (lax.axis_index("seq") & 1) == 1
    left = jnp.where(odd, from_sibling, from_other)
    right = jnp.where(odd, from_other, from_sibling)
    return left, right


def rows_of(ref, first, count, cols):
    block = ref[pl.ds(pl.multiple_of(first, CH), count), cols]
    return [jnp.broadcast_to(block[n : n + 1], (CH, LANE)) for n in range(count)]


def sub_iota():
    return lax.broadcasted_iota(jnp.int32, (CH, LANE), 0)


def shifted(value, up):
    return pltpu.roll(value, 1 if up else CH - 1, 0)


def chunk_weights(total, up):
    sub = sub_iota()
    found = []
    width = total
    for reach in (1, 2, 4):
        inside = (sub >= reach) if up else (sub < CH - reach)
        found.append(jnp.where(inside, width, BIG))
        width = width + pltpu.roll(width, reach if up else CH - reach, 0)
    return found


def outside_sum(total, up):
    sub = sub_iota()
    value = jnp.where((sub >= 1) if up else (sub < CH - 1), shifted(total, up), 0.0)
    for reach in (1, 2, 4):
        inside = (sub >= reach) if up else (sub < CH - reach)
        value = value + jnp.where(inside, pltpu.roll(value, reach if up else CH - reach, 0), 0.0)
    return value


def chunk_scan(value, weights, a2, up):
    for reach, weight in zip((1, 2, 4), weights):
        value = value + jnp.exp2(weight * a2) * pltpu.roll(value, reach if up else CH - reach, 0)
    sub = sub_iota()
    enter = jnp.where((sub >= 1) if up else (sub < CH - 1), shifted(value, up), 0.0)
    leave = value[CH - 1 : CH] if up else value[0:1]
    return enter, leave


def prepare_kernel(
    sib, oth, keep, gain, w_in, conv_w, conv_b, w_x, w_dt, dt_bias, a_log, xb, gy,
    xc_o, dt_o, sig_o, conv_o, mask_o, dbl_o, xbh_o, sx_o, mx_o, sum_o,
    ext, de_s, dx_s, bc_s, a2_s,
):
    inner, rank = w_x.shape[0], w_dt.shape[0]
    state = a_log.shape[0]
    length = xb.shape[0] // 2
    steps = length // CH
    tiles = inner // LANE
    left, right = pick_sides(sib[...], oth[...])
    hn_l = normalize(left, gain[...])[1]
    hn_r = normalize(right, gain[...])[1]
    flip = flip_matrix(hn_r.shape[1])
    lh, ll = split(hn_l)
    rh, rl = split(hn_r)
    halo = (
        jnp.concatenate([lh, nn(rh, flip).astype(BF16)], axis=0),
        jnp.concatenate([ll, nn(rl, flip).astype(BF16)], axis=0),
    )
    xbh = mm(nn, halo, split(w_in[:, :inner]))
    xbh_o[...] = xbh
    lane = lax.broadcasted_iota(jnp.int32, (1, length), 1)
    here = 1.0 - keep[...].astype(F32)
    before, after = left[3:4, :length], right[3:4, :length]

    def back(k):
        return jnp.where(lane < k, pltpu.roll(before, k, 1), pltpu.roll(here, k, 1))

    def ahead(k):
        return jnp.where(
            lane >= length - k,
            pltpu.roll(after, length - k, 1),
            pltpu.roll(here, length - k, 1),
        )

    f1 = here
    f2 = f1 * back(1)
    f3 = f2 * back(2)
    r1 = ahead(1)
    r2 = r1 * ahead(2)
    r3 = r2 * ahead(3)
    for i, row in enumerate((f1, f2, f3, r1, r2, r3)):
        mask_o[i * length : (i + 1) * length, :] = spread(row)

    sub = sub_iota()

    def conv_tile(lt, carry):
        cols = pl.ds(pl.multiple_of(lt * LANE, LANE), LANE)
        xbh_t = xbh_o[:, cols]
        taps = [conv_w[k : k + 1, cols] for k in range(4)]
        bias = conv_b[:, cols]
        xf = [xb[j * CH : (j + 1) * CH, cols] for j in range(steps)]
        edge = [
            jnp.where(sub == 0, xbh_t[b : b + 1], pltpu.roll(xf[steps - 3 + b], 1, 0))
            for b in range(3)
        ]
        xf = edge + xf
        for j in range(steps):
            rows = slice(j * CH, (j + 1) * CH)
            v = bias + taps[0] * xf[j + 3]
            for k in range(1, 4):
                v = v + taps[k] * (mask_o[(k - 1) * length + j * CH : (k - 1) * length + (j + 1) * CH, :] * xf[j + 3 - k])
            conv_o[rows, cols] = v
            xc_o[rows, cols] = v * sigmoid(v)
        xr = [xb[length + j * CH : length + (j + 1) * CH, cols] for j in range(steps)]
        xr = xr + [
            jnp.where(sub == CH - 1, xbh_t[8 + b : 9 + b], pltpu.roll(xr[b], CH - 1, 0))
            for b in range(3)
        ]
        for j in range(steps):
            rows = slice(length + j * CH, length + (j + 1) * CH)
            v = bias + taps[0] * xr[j]
            for k in range(1, 4):
                v = v + taps[k] * (mask_o[(k + 2) * length + j * CH : (k + 2) * length + (j + 1) * CH, :] * xr[j + k])
            conv_o[rows, cols] = v
            xc_o[rows, cols] = v * sigmoid(v)
        return carry

    lax.fori_loop(0, tiles, conv_tile, 0)
    dbl = mm(nn, xc_o[...], w_x[...])
    dbl_o[...] = dbl
    pre_all = mm(nn, dbl[:, :rank], w_dt[...])
    expand_bc(dbl, rank, state, bc_s)
    a2_s[...] = jnp.exp(a_log[...]) * (-LOG2E)
    for lt in range(tiles):
        cols = slice(lt * LANE, (lt + 1) * LANE)
        pre = pre_all[:, cols] + dt_bias[:, cols]
        e = jnp.exp(-jnp.abs(pre))
        u = 1.0 + e
        log1p = jnp.where(u == 1.0, e, jnp.log(u) * (e / (u - 1.0)))
        dt = jnp.maximum(pre, 0.0) + log1p
        dt_o[:, cols] = dt
        sig_o[:, cols] = jnp.where(pre >= 0.0, 1.0, e) / u
        dx_s[:, cols] = dt * xc_o[:, cols]
        cut = jnp.concatenate([mask_o[:length], mask_o[3 * length : 4 * length]], axis=0)
        de_s[:, cols] = dt + BIG * (1.0 - cut)

    half = state // 2
    for dirn in range(2):
        order = range(steps) if dirn == 0 else range(steps - 1, -1, -1)
        base = dirn * length

        def tile(lt, carry, dirn=dirn, order=order, base=base):
            cols = pl.ds(pl.multiple_of(lt * LANE, LANE), LANE)
            total = jnp.zeros((CH, LANE), F32)
            for j in range(steps):
                total = total + de_s[base + j * CH : base + (j + 1) * CH, cols]
            up = dirn == 0
            w_s = chunk_weights(total, up)
            w_m = chunk_weights(total, not up)
            whole = jnp.sum(total, axis=0, keepdims=True)
            sum_o[4 * state + dirn : 4 * state + dirn + 1, cols] = whole

            def some(part, carry):
                n0 = part * half
                a2 = rows_of(a2_s, n0, half, cols)
                h = [jnp.zeros((CH, LANE), F32) for _ in range(half)]
                run = [jnp.ones((CH, LANE), F32) for _ in range(half)]
                m = [jnp.zeros((CH, LANE), F32) for _ in range(half)]
                for j in order:
                    rows = slice(base + j * CH, base + (j + 1) * CH)
                    de, dx, gyj = de_s[rows, cols], dx_s[rows, cols], gy[rows, cols]
                    for n in range(half):
                        at_b = pl.ds(pl.multiple_of((n0 + n) * LANE, LANE), LANE)
                        at_c = pl.ds(pl.multiple_of((state + n0 + n) * LANE, LANE), LANE)
                        d = jnp.exp2(de * a2[n])
                        h[n] = d * h[n] + dx * bc_s[rows, at_b]
                        run[n] = run[n] * d
                        m[n] = m[n] + run[n] * (gyj * bc_s[rows, at_c])
                s_row, m_row = (0, 3) if dirn == 0 else (2, 1)
                s_leave, m_leave = [], []
                for n in range(half):
                    enter, leave = chunk_scan(h[n], w_s, a2[n], up)
                    sx_o[dirn, n0 + n, :, cols] = enter
                    s_leave.append(leave)
                    enter, leave = chunk_scan(m[n], w_m, a2[n], not up)
                    mx_o[dirn, n0 + n, :, cols] = enter
                    m_leave.append(leave)
                for row, leave in ((s_row, s_leave), (m_row, m_leave)):
                    at = pl.multiple_of(row * state + n0, CH)
                    sum_o[pl.ds(at, half), cols] = jnp.concatenate(leave, axis=0)
                return carry

            return lax.fori_loop(0, 2, some, carry)

        lax.fori_loop(0, tiles, tile, 0)
    sum_o[4 * state + 2 :, :] = jnp.zeros((sum_o.shape[0] - 4 * state - 2, inner), F32)


def expand_bc(dbl, rank, state, bc_s):
    pieces = split3(dbl[:, rank:])
    width = dbl.shape[1] - rank
    lhs = jnp.concatenate(pieces, axis=1)
    rows = lax.broadcasted_iota(jnp.int32, (3 * width, width * LANE), 0)
    cols = lax.broadcasted_iota(jnp.int32, (3 * width, width * LANE), 1)
    entry = cols >> 7
    hit = (rows == entry) | (rows == entry + width) | (rows == entry + 2 * width)
    bc_s[...] = nn(lhs, jnp.where(hit, 1.0, 0.0).astype(BF16))


def prepare(sib, oth, keep, gain, w_in, conv_w, conv_b, w_x, w_dt, dt_bias, a_log, xb, gy):
    rows, inner = xb.shape
    state, width = a_log.shape[0], w_x.shape[1]
    big = jax.ShapeDtypeStruct((rows, inner), F32)
    edge = jax.ShapeDtypeStruct((2, state, CH, inner), F32)
    return pl.pallas_call(
        prepare_kernel,
        out_shape=(
            big, big, big, big,
            jax.ShapeDtypeStruct((3 * rows, LANE), F32),
            jax.ShapeDtypeStruct((rows, width), F32),
            jax.ShapeDtypeStruct((2 * CH, inner), F32),
            edge, edge,
            jax.ShapeDtypeStruct((4 * state + 8, inner), F32),
        ),
        scratch_shapes=[
            pltpu.VMEM((8, LANE), F32),
            pltpu.VMEM((rows, inner), F32),
            pltpu.VMEM((rows, inner), F32),
            pltpu.VMEM((rows, 2 * state * LANE), F32),
            pltpu.VMEM((state, inner), F32),
        ],
        compiler_params=params(),
        name="prepare",
    )(sib, oth, keep, gain, w_in, conv_w, conv_b, w_x, w_dt, dt_bias, a_log, xb, gy)


def join_kernel(bit, a_log, mine, theirs, total):
    state = a_log.shape[0]
    a2 = jnp.exp(a_log[...]) * (-LOG2E)
    upper_me = ((lax.axis_index("seq") >> bit) & 1) == 1
    low = jnp.where(upper_me, theirs[...], mine[...])
    high = jnp.where(upper_me, mine[...], theirs[...])
    f_row, r_row = 4 * state, 4 * state + 1

    def part(value, i):
        return value[i * state : (i + 1) * state]

    p_f = jnp.exp2(high[f_row : f_row + 1] * a2)
    p_r = jnp.exp2(high[r_row : r_row + 1] * a2)
    total[:state] = part(low, 0) * p_f + part(high, 0)
    total[state : 2 * state] = part(low, 1) * p_r + part(high, 1)
    p_f = jnp.exp2(low[f_row : f_row + 1] * a2)
    p_r = jnp.exp2(low[r_row : r_row + 1] * a2)
    total[2 * state : 3 * state] = part(high, 2) * p_r + part(low, 2)
    total[3 * state : 4 * state] = part(high, 3) * p_f + part(low, 3)
    total[4 * state :] = mine[4 * state :] + theirs[4 * state :]


def join(bit, a_log, mine, theirs):
    return pl.pallas_call(
        lambda *refs: join_kernel(bit, *refs),
        out_shape=jax.ShapeDtypeStruct(mine.shape, F32),
        compiler_params=params(),
        name="join",
    )(a_log, mine, theirs)


def enter_kernel(bits, a_log, *refs):
    theirs, out = refs[:-1], refs[-1]
    state, inner = a_log.shape
    a2 = jnp.exp(a_log[...]) * (-LOG2E)
    me = lax.axis_index("seq")
    f_row, r_row = 4 * state, 4 * state + 1
    out[...] = jnp.zeros(out.shape, F32)
    early = [jnp.zeros((1, inner), F32)] * 2
    late = [jnp.zeros((1, inner), F32)] * 2
    for bit, ref in zip(bits, theirs):
        upper = ((me >> bit) & 1) == 1
        use_low = jnp.where(upper, 1.0, 0.0)
        use_high = 1.0 - use_low
        df, dr = ref[f_row : f_row + 1], ref[r_row : r_row + 1]
        out[:state] += use_low * (ref[:state] * jnp.exp2(early[0] * a2))
        out[state : 2 * state] += use_low * (ref[state : 2 * state] * jnp.exp2(early[1] * a2))
        out[2 * state : 3 * state] += use_high * (ref[2 * state : 3 * state] * jnp.exp2(late[1] * a2))
        out[3 * state :] += use_high * (ref[3 * state : 4 * state] * jnp.exp2(late[0] * a2))
        early = [early[0] + use_low * df, early[1] + use_low * dr]
        late = [late[0] + use_high * df, late[1] + use_high * dr]


def enter(bits, a_log, theirs):
    state, inner = a_log.shape
    return pl.pallas_call(
        lambda *refs: enter_kernel(bits, *refs),
        out_shape=jax.ShapeDtypeStruct((4 * state, inner), F32),
        compiler_params=params(),
        name="enter",
    )(a_log, *theirs)


def main_kernel(
    rs_bits,
    tok, gout, pad, sib, oth, gain, w_in, conv_w, w_x, w_dt, a_log, d_skip, w_out,
    xb, z, go, gy, xc, dt, sig, conv, mask, dbl, xbh, sx, mx, car,
    mixed_o, gtok_o, to_sib, to_oth, *rest,
):
    outs, (de_s, dx_s, bc_s, a2_s, h_s, y_s, sb_s, sa_s, accb, accc, ga_s, gp_s, gpre_s, xcg_s, gscr) = rest[: rs_bits + 1], rest[rs_bits + 1 :]
    inner, rank = w_x.shape[0], w_dt.shape[0]
    feat = w_in.shape[0]
    state = a_log.shape[0]
    rows2 = xb.shape[0]
    length = rows2 // 2
    steps = length // CH
    tiles = inner // LANE
    half = state // 2
    sub = sub_iota()

    expand_bc(dbl[...], rank, state, bc_s)
    a2_s[...] = jnp.exp(a_log[...]) * (-LOG2E)
    accb[...] = jnp.zeros(accb.shape, F32)
    accc[...] = jnp.zeros(accc.shape, F32)
    ga_s[...] = jnp.zeros(ga_s.shape, F32)
    for lt in range(tiles):
        cols = slice(lt * LANE, (lt + 1) * LANE)
        cut = jnp.concatenate([mask[:length], mask[3 * length : 4 * length]], axis=0)
        de_s[:, cols] = dt[:, cols] + BIG * (1.0 - cut)
        dx_s[:, cols] = dt[:, cols] * xc[:, cols]

    for dirn in range(2):
        order = list(range(steps)) if dirn == 0 else list(range(steps - 1, -1, -1))
        base = dirn * length
        s_row, m_row = (0, 3) if dirn == 0 else (2, 1)

        def tile(lt, carry, dirn=dirn, order=order, base=base, s_row=s_row, m_row=m_row):
            cols = pl.ds(pl.multiple_of(lt * LANE, LANE), LANE)
            total = jnp.zeros((CH, LANE), F32)
            for j in range(steps):
                total = total + de_s[base + j * CH : base + (j + 1) * CH, cols]
            up = dirn == 0
            w_s = outside_sum(total, up)
            w_m = outside_sum(total, not up)

            def block(j):
                return slice(base + j * CH, base + (j + 1) * CH)

            def some(part, carry):
                n0 = part * half
                a2 = rows_of(a2_s, n0, half, cols)
                at_b = [pl.ds(pl.multiple_of((n0 + n) * LANE, LANE), LANE) for n in range(half)]
                at_c = [
                    pl.ds(pl.multiple_of((state + n0 + n) * LANE, LANE), LANE)
                    for n in range(half)
                ]
                h = []
                enter_h = rows_of(car, s_row * state + n0, half, cols)
                for n in range(half):
                    h.append(sx[dirn, n0 + n, :, cols] + jnp.exp2(w_s * a2[n]) * enter_h[n])
                    h_s[0, n] = h[n]
                for at, j in enumerate(order):
                    rows = block(j)
                    de, dx = de_s[rows, cols], dx_s[rows, cols]
                    y = None
                    for n in range(half):
                        h[n] = jnp.exp2(de * a2[n]) * h[n] + dx * bc_s[rows, at_b[n]]
                        h_s[at + 1, n] = h[n]
                        term = h[n] * bc_s[rows, at_c[n]]
                        y = term if y is None else y + term
                    y_s[rows, cols] = y + y_s[rows, cols]
                q = []
                ga = []
                enter_q = rows_of(car, m_row * state + n0, half, cols)
                for n in range(half):
                    q.append(mx[dirn, n0 + n, :, cols] + jnp.exp2(w_m * a2[n]) * enter_q[n])
                    ga.append(jnp.zeros((CH, LANE), F32))
                for at in range(steps - 1, -1, -1):
                    rows = block(order[at])
                    de, dx, gyj = de_s[rows, cols], dx_s[rows, cols], gy[rows, cols]
                    sb = sa = None
                    for n in range(half):
                        gh = gyj * bc_s[rows, at_c[n]] + q[n]
                        accc[rows, at_b[n]] += gyj * h_s[at + 1, n]
                        accb[rows, at_b[n]] += gh * dx
                        term_b = gh * bc_s[rows, at_b[n]]
                        q[n] = jnp.exp2(de * a2[n]) * gh
                        r = q[n] * h_s[at, n]
                        term_a = a2[n] * r
                        ga[n] = ga[n] + de * r
                        sb = term_b if sb is None else sb + term_b
                        sa = term_a if sa is None else sa + term_a
                    sb_s[rows, cols] = sb + sb_s[rows, cols]
                    sa_s[rows, cols] = sa + sa_s[rows, cols]
                for n in range(half):
                    ga_s[n0 + n, :, cols] += ga[n]
                return carry

            zero = jnp.zeros((CH, LANE), F32)
            for j in range(steps):
                y_s[block(j), cols] = zero
                sb_s[block(j), cols] = zero
                sa_s[block(j), cols] = zero
            return lax.fori_loop(0, 2, some, carry)

        lax.fori_loop(0, tiles, tile, 0)

    small = {}
    skip_rows, bias_rows = [], []
    for lt in range(tiles):
        cols = slice(lt * LANE, (lt + 1) * LANE)
        zt, xct, gyt = z[:, cols], xc[:, cols], gy[:, cols]
        s = sigmoid(zt)
        gate = zt * s
        y = y_s[:, cols] + d_skip[:, cols] * xct
        y_s[:, cols] = y * gate
        gp_s[:, inner + lt * LANE : inner + (lt + 1) * LANE] = go[:, cols] * y * (s * (1.0 + zt * (1.0 - s)))
        g_dt = xct * sb_s[:, cols] + LN2 * sa_s[:, cols]
        g_pre = g_dt * sig[:, cols]
        gpre_s[:, cols] = g_pre
        xcg_s[:, cols] = d_skip[:, cols] * gyt + dt[:, cols] * sb_s[:, cols]
        skip_rows.append(jnp.sum(gyt * xct, axis=0, keepdims=True))
        bias_rows.append(jnp.sum(g_pre, axis=0, keepdims=True))
    small["skip"] = jnp.concatenate(skip_rows, axis=1)
    small["dtb"] = jnp.concatenate(bias_rows, axis=1)

    x = ordered(tok)
    g_all = both_orders(ordered(gout))
    out_parts = split(y_s[...])
    w_out_parts = split(w_out[...])
    sb_s[:, :feat] = mm(nn, out_parts, w_out_parts)
    sa_s[:length, :feat] = flipped(sb_s[length:, :feat])
    store_ordered(mixed_o, x + (sb_s[:length, :feat] + sa_s[:length, :feat]))
    gw_out = mm(tn, out_parts, g_all)

    lanes = state * LANE
    e_row = lax.broadcasted_iota(jnp.int32, (lanes, LANE), 0) >> 7
    e_col = lax.broadcasted_iota(jnp.int32, (lanes, LANE), 1)
    pick_b = jnp.where(e_col == e_row + rank, 1.0, 0.0).astype(BF16)
    pick_c = jnp.where(e_col == e_row + rank + state, 1.0, 0.0).astype(BF16)
    bh, bl = split(accb[...])
    ch, cl = split(accc[...])
    g_bc = nn(bh, pick_b) + nn(bl, pick_b) + nn(ch, pick_c) + nn(cl, pick_c)
    gpre_parts = split(gpre_s[...])
    w_dt_parts = split(w_dt[...])
    g_rank = mm(nt, gpre_parts, w_dt_parts)
    width = rank + 2 * state
    g_dbl = jnp.concatenate([g_rank, g_bc[:, rank:width]], axis=1)
    g_dbl_parts = split(g_dbl)
    gw_dt = mm(tn, split(dbl[:, :rank]), gpre_parts)
    gw_x = mm(tn, g_dbl_parts, split(xc[...]))
    xcg_s[...] += mm(nt, g_dbl_parts, split(w_x[...]))

    cw_rows = [[] for _ in range(4)]
    cb_rows = []
    halo_f, halo_r = [], []
    for lt in range(tiles):
        cols = slice(lt * LANE, (lt + 1) * LANE)
        taps = [conv_w[k : k + 1, cols] for k in range(4)]
        xbh_t = xbh[:, cols]
        xf = [xb[j * CH : (j + 1) * CH, cols] for j in range(steps)]
        xf = [
            jnp.where(sub == 0, xbh_t[b : b + 1], pltpu.roll(xf[steps - 3 + b], 1, 0))
            for b in range(3)
        ] + xf
        gcw = [jnp.zeros((CH, LANE), F32) for _ in range(4)]
        gcb = jnp.zeros((CH, LANE), F32)
        grads = [None] * (steps + 3)
        for j in range(steps):
            rows = slice(j * CH, (j + 1) * CH)
            v = conv[rows, cols]
            s = sigmoid(v)
            u = xcg_s[rows, cols] * (s * (1.0 + v * (1.0 - s)))
            gcb = gcb + u
            for k in range(4):
                uk = u if k == 0 else u * mask[(k - 1) * length + j * CH : (k - 1) * length + (j + 1) * CH, :]
                gcw[k] = gcw[k] + uk * xf[j + 3 - k]
                add = taps[k] * uk
                at = j + 3 - k
                grads[at] = add if grads[at] is None else grads[at] + add
        for b in range(3):
            halo_f.append(grads[b][0:1])
            at = steps + b
            grads[at] = grads[at] + jnp.where(sub == CH - 1, 0.0, pltpu.roll(grads[b], CH - 1, 0))
        for j in range(steps):
            gp_s[j * CH : (j + 1) * CH, cols] = grads[j + 3]
        xr = [xb[length + j * CH : length + (j + 1) * CH, cols] for j in range(steps)]
        xr = xr + [
            jnp.where(sub == CH - 1, xbh_t[8 + b : 9 + b], pltpu.roll(xr[b], CH - 1, 0))
            for b in range(3)
        ]
        grads = [None] * (steps + 3)
        for j in range(steps):
            rows = slice(length + j * CH, length + (j + 1) * CH)
            v = conv[rows, cols]
            s = sigmoid(v)
            u = xcg_s[rows, cols] * (s * (1.0 + v * (1.0 - s)))
            gcb = gcb + u
            for k in range(4):
                uk = u if k == 0 else u * mask[(k + 2) * length + j * CH : (k + 2) * length + (j + 1) * CH, :]
                gcw[k] = gcw[k] + uk * xr[j + k]
                add = taps[k] * uk
                grads[j + k] = add if grads[j + k] is None else grads[j + k] + add
        for b in range(3):
            halo_r.append(grads[steps + b][CH - 1 : CH])
            grads[b] = grads[b] + jnp.where(sub == 0, 0.0, pltpu.roll(grads[steps + b], 1, 0))
        for j in range(steps):
            gp_s[length + j * CH : length + (j + 1) * CH, cols] = grads[j]
        for k in range(4):
            cw_rows[k].append(jnp.sum(gcw[k], axis=0, keepdims=True))
        cb_rows.append(jnp.sum(gcb, axis=0, keepdims=True))
    pad_col = spread(pad[...].astype(F32))
    pad_all = jnp.concatenate([pad_col, pad_col], axis=0)
    for lt in range(tiles):
        cols = slice(lt * LANE, (lt + 1) * LANE)
        gp_s[:, cols] *= pad_all

    blank = jnp.zeros((5, inner), F32)

    def gather(found):
        return jnp.concatenate(
            [jnp.concatenate([found[lt * 3 + b] for lt in range(tiles)], axis=1) for b in range(3)]
            + [blank],
            axis=0,
        )

    gh = jnp.concatenate([gather(halo_f), gather(halo_r)], axis=0)
    gh_parts = split(gh)
    left, right = pick_sides(sib[...], oth[...])
    factor_l, hn_l = normalize(left, gain[...])
    factor_r, hn_r = normalize(right, gain[...])
    flip = flip_matrix(feat)
    lh, ll = split(hn_l)
    rh, rl = split(hn_r)
    halo = (
        jnp.concatenate([lh, nn(rh, flip).astype(BF16)], axis=0),
        jnp.concatenate([ll, nn(rl, flip).astype(BF16)], axis=0),
    )

    factor, normed = normalize(x, gain[...])
    n_parts = both_orders(normed)
    w_in_parts = split(w_in[...])
    gp_parts = split(gp_s[...])
    gw_in = mm(tn, n_parts, gp_parts)
    gw_in_halo = mm(tn, halo, gh_parts)
    back = mm(nt, gp_parts, w_in_parts)
    g_normed = back[:length] + flipped(back[length:])
    back_h = mm(nt, gh_parts, (w_in_parts[0][:, :inner], w_in_parts[1][:, :inner]))
    gn_l = back_h[:CH]
    gn_r = flipped(back_h[CH:])

    def norm_back(x, factor, gn):
        scaled = gn * gain[...]
        return factor * scaled - x * (factor * factor * factor * jnp.mean(scaled * x, axis=1, keepdims=True))

    store_ordered(gtok_o, ordered(gout) + norm_back(x, factor, g_normed))
    to_left = norm_back(left, factor_l, gn_l)
    to_right = norm_back(right, factor_r, gn_r)
    odd = (lax.axis_index("seq") & 1) == 1
    to_sib[...] = jnp.where(odd, to_left, to_right)
    to_oth[...] = jnp.where(odd, to_right, to_left)
    three = lax.broadcasted_iota(jnp.int32, (CH, feat), 0) < 3
    g_gain = (
        jnp.sum(g_normed * (x * factor), axis=0, keepdims=True)
        + jnp.sum(jnp.where(three, gn_l * (left * factor_l) + gn_r * (right * factor_r), 0.0), axis=0, keepdims=True)
    )

    ga = jnp.concatenate([jnp.sum(ga_s[n], axis=0, keepdims=True) for n in range(state)], axis=0)
    few = jnp.concatenate(
        [gw_x, ga * (a2_s[...] * LN2), gw_dt]
        + [jnp.concatenate(cw_rows[k], axis=1) for k in range(4)]
        + [
            jnp.concatenate(cb_rows, axis=1),
            small["dtb"],
            small["skip"],
            jnp.concatenate([g_gain, jnp.zeros((1, inner - feat), F32)], axis=1),
        ],
        axis=0,
    )
    pieces = 1 << rs_bits
    mine = reverse_bits(lax.axis_index("seq"), rs_bits)
    in_rows, out_rows = feat // pieces, inner // pieces
    for p in range(pieces):
        slot = mine ^ reverse_bits(p, rs_bits)
        at = 0
        for lt in range(2 * tiles):
            value = gw_in[p * in_rows : (p + 1) * in_rows, lt * LANE : (lt + 1) * LANE]
            if lt < tiles:
                value = value + gw_in_halo[p * in_rows : (p + 1) * in_rows, lt * LANE : (lt + 1) * LANE]
            gscr[slot, at : at + in_rows, :] = value
            at += in_rows
        for lt in range(feat // LANE):
            gscr[slot, at : at + out_rows, :] = gw_out[p * out_rows : (p + 1) * out_rows, lt * LANE : (lt + 1) * LANE]
            at += out_rows
        for t in range(2 * p, 2 * p + 2):
            rb, lt = t // tiles, t % tiles
            if rb * CH < few.shape[0]:
                gscr[slot, at : at + CH, :] = few[rb * CH : (rb + 1) * CH, lt * LANE : (lt + 1) * LANE]
            else:
                gscr[slot, at : at + CH, :] = jnp.zeros((CH, LANE), F32)
            at += CH
    top = pieces
    for i in range(rs_bits):
        outs[i][...] = gscr[top // 2 : top]
        top //= 2
    outs[rs_bits][...] = gscr[0:1]


def reverse_bits(value, bits):
    found = 0
    for i in range(bits):
        found = found | (((value >> i) & 1) << (bits - 1 - i))
    return found


def piece_rows(rs_bits, feat, inner):
    pieces = 1 << rs_bits
    return (feat * 2 * inner + inner * feat) // LANE // pieces + 16 * 32 // pieces


def main(rs_bits, *arrays):
    tok, w_in, a_log, xb, dbl = arrays[0], arrays[6], arrays[10], arrays[13], arrays[22]
    length, feat = tok.shape
    rows2, inner = xb.shape
    state, rank = a_log.shape[0], arrays[9].shape[0]
    width = dbl.shape[1]
    tall = piece_rows(rs_bits, feat, inner)
    sizes = [1 << (rs_bits - 1 - i) for i in range(rs_bits)] + [1]
    big = pltpu.VMEM((rows2, inner), F32)
    return pl.pallas_call(
        lambda *refs: main_kernel(rs_bits, *refs),
        out_shape=(
            jax.ShapeDtypeStruct((length, feat), F32),
            jax.ShapeDtypeStruct((length, feat), F32),
            jax.ShapeDtypeStruct((CH, feat), F32),
            jax.ShapeDtypeStruct((CH, feat), F32),
        )
        + tuple(jax.ShapeDtypeStruct((size, tall, LANE), F32) for size in sizes),
        scratch_shapes=[
            big, big,
            pltpu.VMEM((rows2, 2 * state * LANE), F32),
            pltpu.VMEM((state, inner), F32),
            pltpu.VMEM((length // CH + 1, state // 2, CH, LANE), F32),
            big, big, big,
            pltpu.VMEM((rows2, state * LANE), F32),
            pltpu.VMEM((rows2, state * LANE), F32),
            pltpu.VMEM((state, CH, inner), F32),
            pltpu.VMEM((rows2, 2 * inner), F32),
            big, big,
            pltpu.VMEM((1 << rs_bits, tall, LANE), F32),
        ],
        compiler_params=params(),
        name="main",
    )(*arrays)


def unpack_kernel(
    rs_bits, near, far, gtok, from_sib, from_oth, pad,
    gtok_o, gain_o, w_in_o, conv_w_o, conv_b_o, w_x_o, w_dt_o, dt_bias_o, a_log_o, d_skip_o, w_out_o, few_s,
):
    feat = w_in_o.shape[0]
    inner = w_out_o.shape[0]
    tiles = inner // LANE
    pieces = 1 << rs_bits
    mine = reverse_bits(lax.axis_index("seq"), rs_bits)
    in_rows, out_rows = feat // pieces, inner // pieces
    for slot in range(pieces):
        source = near if slot < pieces // 2 else far
        i = slot % (pieces // 2)
        p = reverse_bits(mine ^ slot, rs_bits)
        at = 0
        rows = pl.ds(pl.multiple_of(p * in_rows, in_rows), in_rows)
        for lt in range(2 * tiles):
            w_in_o[rows, lt * LANE : (lt + 1) * LANE] = source[i, at : at + in_rows, :]
            at += in_rows
        rows = pl.ds(pl.multiple_of(p * out_rows, out_rows), out_rows)
        for lt in range(feat // LANE):
            w_out_o[rows, lt * LANE : (lt + 1) * LANE] = source[i, at : at + out_rows, :]
            at += out_rows
        few_s[p] = source[i, at : at + 2 * CH, :]

    def few_rows(first, count):
        found = []
        for lt in range(tiles):
            t = first // CH * tiles + lt
            found.append(few_s[t // 2, (t % 2) * CH + first % CH : (t % 2) * CH + first % CH + count, :])
        return jnp.concatenate(found, axis=1)

    width, state = w_x_o.shape[1], a_log_o.shape[1]
    rank = w_dt_o.shape[0]
    w_x_o[...] = jnp.concatenate([few_rows(r, CH) for r in range(0, width, CH)], axis=0).T
    at = width
    a_log_o[...] = jnp.concatenate([few_rows(r, CH) for r in range(at, at + state, CH)], axis=0).T
    at += state
    w_dt_o[...] = jnp.concatenate([few_rows(r, CH) for r in range(at, at + rank, CH)], axis=0)
    at += rank
    conv_w_o[...] = few_rows(at, 4)
    conv_b_o[...] = few_rows(at + 4, 1)
    dt_bias_o[...] = few_rows(at + 5, 1)
    d_skip_o[...] = few_rows(at + 6, 1)
    gain_o[...] = few_rows(at + 7, 1)[:, :feat]

    left, right = pick_sides(from_sib[...], from_oth[...])
    length = gtok.shape[0]
    row = lax.broadcasted_iota(jnp.int32, (length, feat), 0)
    sub = lax.broadcasted_iota(jnp.int32, (CH, feat), 0)
    padded = spread_plain(pad[...].astype(F32), feat)
    first = jnp.where(sub < 3, left, 0.0)
    last = jnp.where(sub >= CH - 3, pltpu.roll(right, CH - 3, 0), 0.0)
    gtok_o[...] = gtok[...]
    gtok_o[:CH] = gtok[:CH] + padded[:CH] * first
    gtok_o[length - CH :] = gtok[length - CH :] + padded[length - CH :] * last


def spread_plain(row, width):
    length = row.shape[1]
    rows = lax.broadcasted_iota(jnp.int32, (length, length), 0)
    cols = lax.broadcasted_iota(jnp.int32, (length, length), 1)
    picked = (jnp.where(rows == cols, 1.0, 0.0) * row).astype(BF16)
    return nn(picked, jnp.ones((length, width), BF16))


def unpack(rs_bits, near, far, gtok, from_sib, from_oth, pad, state, rank):
    length, feat = gtok.shape
    pieces = 1 << rs_bits
    inner = 4 * LANE if state is None else state[1]
    width = rank + 2 * state[0]
    shape = lambda *dims: jax.ShapeDtypeStruct(dims, F32)
    return pl.pallas_call(
        lambda *refs: unpack_kernel(rs_bits, *refs),
        out_shape=(
            shape(length, feat),
            shape(1, feat),
            shape(feat, 2 * inner),
            shape(4, inner),
            shape(1, inner),
            shape(inner, width),
            shape(rank, inner),
            shape(1, inner),
            shape(inner, state[0]),
            shape(1, inner),
            shape(inner, feat),
        ),
        scratch_shapes=[pltpu.VMEM((pieces, 2 * CH, LANE), F32)],
        compiler_params=params(),
        name="unpack",
    )(near, far, gtok, from_sib, from_oth, pad)


def body(tokens, resets, pad_mask, norm_gain, w_in, conv_w, conv_b, w_x, w_dt, dt_bias, a_log, d_skip, w_out, grad_out):
    count = lax.axis_size("seq")
    bits = count.bit_length() - 1
    rs_bits = min(5, bits)
    odd = (lax.axis_index("seq") & 1) == 1
    length, feat = tokens.shape
    keep_row, pad_row = resets.reshape(1, length), pad_mask.reshape(1, length)
    gain, a_log_t = norm_gain, a_log[0].T

    def swap(value, bit):
        return lax.ppermute(value, "seq", [(i, i ^ (1 << bit)) for i in range(count)])

    across = [(i, i + 1) for i in range(1, count - 1, 2)] + [(i + 1, i) for i in range(1, count - 1, 2)]

    def swap_across(value):
        return lax.ppermute(value, "seq", across)

    kept = jnp.pad(1.0 - resets.astype(F32), (0, feat - length))[None]
    real = pad_mask.astype(F32)[:, None]
    fill = jnp.zeros((4, feat), F32)
    first = jnp.concatenate([tokens[:3] * real[:3], kept, fill], axis=0)
    last = jnp.concatenate([tokens[-3:] * real[-3:], kept, fill], axis=0)
    oth = swap_across(jnp.where(odd, last, first))
    sib = swap(jnp.where(odd, first, last), 0)

    xb, z, go, gy = project(tokens, pad_row, gain, w_in[0], grad_out, w_out[0])
    xc, dt, sig, conv, mask, dbl, xbh, sx, mx, total = prepare(
        sib, oth, keep_row, gain, w_in[0], conv_w[0], conv_b, w_x[0], w_dt[0], dt_bias, a_log_t, xb, gy
    )
    theirs = []
    for bit in range(bits):
        theirs.append(swap(total, bit))
        if bit < bits - 1:
            total = join(bit, a_log_t, total, theirs[-1])
    car = enter(tuple(range(bits)), a_log_t, theirs)
    found = main(
        rs_bits,
        tokens, grad_out, pad_row, sib, oth, gain, w_in[0], conv_w[0], w_x[0], w_dt[0], a_log_t, d_skip, w_out[0],
        xb, z, go, gy, xc, dt, sig, conv, mask, dbl, xbh, sx, mx, car,
    )
    mixed, gtok, to_sib, to_oth = found[:4]
    parts = list(found[4:])

    for bit in range(rs_bits):
        got = swap(parts[bit], bit)
        for later in range(bit + 1, rs_bits + 1):
            size = parts[later].shape[0]
            start = size if later < rs_bits else 0
            parts[later] = parts[later] + got[start : start + size]
    own = parts[rs_bits]
    for bit in range(rs_bits, bits):
        own = own + swap(own, bit)
    from_sib, from_oth = swap(to_sib, 0), swap_across(to_oth)
    for bit in range(rs_bits - 1, 0, -1):
        own = jnp.concatenate([own, swap(own, bit)], axis=0)
    far = swap(own, 0)
    outs = unpack(rs_bits, own, far, gtok, from_sib, from_oth, pad_row, a_log_t.shape, w_dt.shape[1])
    gtok, g_gain, g_w_in, g_conv_w, g_conv_b, g_w_x, g_w_dt, g_dt_bias, g_a_log, g_d_skip, g_w_out = outs
    return (
        mixed, gtok, g_gain, g_w_in[None], g_conv_w[None], g_conv_b, g_w_x[None], g_w_dt[None],
        g_dt_bias, g_a_log[None], g_d_skip, g_w_out[None],
    )


def solution(mesh):
    rows, whole = P("seq", None), P()
    return jax.shard_map(
        body,
        mesh=mesh,
        in_specs=(rows, P("seq"), P("seq")) + (whole,) * 10 + (rows,),
        out_specs=(rows, rows) + (whole,) * 10,
        check_vma=False,
    )
```

time: 2330 us -> 162 us (0.07)
  the two profiles are of different devices: /device:TPU:0 before, /device:TPU:8 now
where the time goes in v1:
time: 162 us
  waiting for transfers between devices  71.5 us (44%)
  Pallas kernels  52.5 us (32%)
  starting transfers between devices  24.5 us (15%)
  local copies, waits for them, and re-layouts  10.6 us (7%)
  other arithmetic  2.2 us (1%)
    ppermute x17, waiting for transfers between devices, swap(): return lax.ppermute(value, 'seq', [(i, i ^ 1 << bit) for i in range(count)])  68.2 us
    pallas_call x1, Pallas kernels, main(): pl.pallas_call(lambda *refs: main_kernel(rs_bits, *refs), out_shape=(jax....  26.1 us
    ppermute x17, starting transfers between devices, swap(): return lax.ppermute(value, 'seq', [(i, i ^ 1 << bit) for i in range(count)])  17.3 us
    unnamed x46, local copies, waits for them, and re-layouts  10.4 us
    pallas_call x1, Pallas kernels, prepare(): pl.pallas_call(prepare_kernel, out_shape=(big, big, big, big, jax.ShapeDt...  10.2 us
    ppermute x2, starting transfers between devices, swap_across(): return lax.ppermute(value, 'seq', across)  7.17 us
    pallas_call x4, Pallas kernels, join(): pl.pallas_call(lambda *refs: join_kernel(bit, *refs), out_shape=jax.Shape...  6.8 us
    pallas_call x1, Pallas kernels, project(): pl.pallas_call(project_kernel, out_shape=(big, big, big, big), compiler_p...  3.96 us
  transfers between devices with their start and end apart: 19, of which 15 were waited for; matrix products, arithmetic and copies ran while one was open for 1% of the time, Pallas kernels for 2%

profile of v1, /device:TPU:8, one launch (start us, length us, event | category | flops | bytes accessed | tf_op | source)
XLA Modules:
  0.0 162.0 jit_solution(983820714627956914)
XLA Ops:
  0.7 0.6 copy-done.17
  1.3 0.6 copy-done.16
  2.1 0.8 slice_multiply_fusion.1
  3.0 3.7 %collective-permute-start.1 = (f32[8,256]{1,0:T(8,128)S(1)}, f32[8,256]{1,0:T(8,128)S(1)}, u32[]{:S(2)}, u32[]{:S(2)}) collective-permute-start(f32[8,256]{1,0:T(8,128)S(1)} %get-tuple-element.98), channel_id=1, source_target_pairs={{1,2},{3,4},{5,6},{7,8},{9,10},{11,12},{13,14},{15,16},{17,18},{19... | collective-permute-start | bytes 24584 | tf_op jit(solution)/shard_map/ppermute | solution.py:902
  6.7 1.7 %copy.26 = f32[1,512,48]{2,1,0:T(8,128)} copy(f32[1,512,48]{1,2,0:T(8,128)} %param.21) | data formatting | bytes 196608 | tf_op args[7]
  8.5 4.0 %project.1 = (f32[256,512]{1,0:T(8,128)}, f32[256,512]{1,0:T(8,128)}, f32[256,512]{1,0:T(8,128)}, f32[256,512]{1,0:T(8,128)}) custom-call(f32[128,256]{1,0:T(8,128)} %refs_0_.1, s32[1,128]{1,0:T(1,128)} %bitcast.37, f32[1,256]{1,0:T(1,128)} %refs_5_.1, f32[256,1024]{1,0:T(8,128)} %bitcast.17, f32[128,256]{1,0:T(8,128)} %refs_1_.1, f32[512,256]{1,0:T(8,128)} %bitcast.22), custom_call_target="tpu_custom_call" | custom-call | tf_op jit(solution)/shard_map/project/pallas_call | solution.py:133
  13.1 10.2 %prepare.1 = (f32[256,512]{1,0:T(8,128)}, f32[256,512]{1,0:T(8,128)}, f32[256,512]{1,0:T(8,128)}, f32[256,512]{1,0:T(8,128)}, f32[768,128]{1,0:T(8,128)}, /*inde...) custom-call(f32[8,256]{1,0:T(8,128)} %copy-done.13, ...), custom_call_target="tpu_custom_call" | custom-call | tf_op jit(solution)/shard_map/prepare/pallas_call | solution.py:356
  23.8 1.2 collective-permute-done.2.refs_2_.refs_1_
  25.0 0.7 copy-done.2
  25.7 1.7 %join.4.refs_1_ = f32[72,512]{1,0:T(8,128)} custom-call(f32[16,512]{1,0:T(8,128)} %bitcast.25, f32[72,512]{1,0:T(8,128)} %get-tuple-element.60.refs_1_, f32[72,512]{1,0:T(8,128)} %copy-done.2), custom_call_target="tpu_custom_call" | custom-call | tf_op jit(solution)/shard_map/join/pallas_call | solution.py:401
  27.4 1.2 collective-permute-start.3
  28.5 5.2 %collective-permute-done.3.refs_2_ = f32[72,512]{1,0:T(8,128)S(1)} collective-permute-done((f32[72,512]{1,0:T(8,128)}, f32[72,512]{1,0:T(8,128)S(1)}, u32[]{:S(2)}, u32[]{:S(2)}) %collective-permute-start.3) | collective-permute-done | bytes 147488 | tf_op jit(solution)/shard_map/ppermute | solution.py:897
  33.7 0.7 copy-done.3
  34.4 1.7 %join.5.refs_1_ = f32[72,512]{1,0:T(8,128)} custom-call(f32[16,512]{1,0:T(8,128)} %bitcast.26, f32[72,512]{1,0:T(8,128)} %join.4.refs_1_, f32[72,512]{1,0:T(8,128)} %copy-done.3), custom_call_target="tpu_custom_call" | custom-call | tf_op jit(solution)/shard_map/join/pallas_call | solution.py:401
  36.1 1.0 collective-permute-start.4
  37.0 4.5 %collective-permute-done.4.refs_2_.refs_3_ = f32[72,512]{1,0:T(8,128)S(1)} collective-permute-done((f32[72,512]{1,0:T(8,128)}, f32[72,512]{1,0:T(8,128)S(1)}, u32[]{:S(2)}, u32[]{:S(2)}) %collective-permute-start.4) | collective-permute-done | bytes 147488 | tf_op jit(solution)/shard_map/ppermute | solution.py:897
  41.6 0.6 copy-done.4
  42.2 1.7 %join.6.refs_1_ = f32[72,512]{1,0:T(8,128)} custom-call(f32[16,512]{1,0:T(8,128)} %bitcast.27, f32[72,512]{1,0:T(8,128)} %join.5.refs_1_, f32[72,512]{1,0:T(8,128)} %copy-done.4), custom_call_target="tpu_custom_call" | custom-call | tf_op jit(solution)/shard_map/join/pallas_call | solution.py:401
  43.9 5.4 %collective-permute-done.5.refs_2_.refs_4_ = f32[72,512]{1,0:T(8,128)S(1)} collective-permute-done((f32[72,512]{1,0:T(8,128)}, f32[72,512]{1,0:T(8,128)S(1)}, u32[]{:S(2)}, u32[]{:S(2)}) %collective-permute-start.5) | collective-permute-done | bytes 147488 | tf_op jit(solution)/shard_map/ppermute | solution.py:897
  49.3 0.7 copy-done.5
  49.9 1.7 %join.7 = f32[72,512]{1,0:T(8,128)} custom-call(f32[16,512]{1,0:T(8,128)} %bitcast.28, f32[72,512]{1,0:T(8,128)} %join.6.refs_1_, f32[72,512]{1,0:T(8,128)} %copy-done.5), custom_call_target="tpu_custom_call" | custom-call | tf_op jit(solution)/shard_map/join/pallas_call | solution.py:401
  51.6 2.6 %collective-permute-start.6 = (f32[72,512]{1,0:T(8,128)}, f32[72,512]{1,0:T(8,128)S(1)}, u32[]{:S(2)}, u32[]{:S(2)}) collective-permute-start(f32[72,512]{1,0:T(8,128)} %join.7), channel_id=1, source_target_pairs={{0,16},{1,17},{2,18},{3,19},{4,20},{5,21},{6,22},{7,23},{8,24},{9,... | collective-permute-start | bytes 442376 | tf_op jit(solution)/shard_map/ppermute | solution.py:897
  54.2 4.4 %collective-permute-done.6.refs_5_ = f32[72,512]{1,0:T(8,128)S(1)} collective-permute-done((f32[72,512]{1,0:T(8,128)}, f32[72,512]{1,0:T(8,128)S(1)}, u32[]{:S(2)}, u32[]{:S(2)}) %collective-permute-start.6) | collective-permute-done | bytes 147488 | tf_op jit(solution)/shard_map/ppermute | solution.py:897
  58.7 0.7 copy-done.8
  59.3 2.0 %enter.1.refs_26_ = f32[64,512]{1,0:T(8,128)} custom-call(f32[16,512]{1,0:T(8,128)} %bitcast.29, f32[72,512]{1,0:T(8,128)} %copy-done.2, f32[72,512]{1,0:T(8,128)} %copy-done.3, f32[72,512]{1,0:T(8,128)} %copy-done.4, f32[72,512]{1,0:T(8,128)} %copy-done.5, f32[72,512]{1,0:T(8,128)} %copy-done.8), custom_call_target="tpu_custom_call" | custom-call | tf_op jit(solution)/shard_map/enter/pallas_call | solution.py:433
  61.3 26.1 %main.1 = (f32[128,256]{1,0:T(8,128)}, f32[128,256]{1,0:T(8,128)}, f32[8,256]{1,0:T(8,128)}, f32[8,256]{1,0:T(8,128)}, f32[16,112,128]{2,1,0:T(8,128)}, /*index=...) custom-call(f32[128,256]{1,0:T(8,128)} %refs_0_.1, ...), custom_call_target="tpu_custom_call" | custom-call | tf_op jit(solution)/shard_map/main/pallas_call | solution.py:767
  87.5 2.7 %collective-permute-done.7 = f32[16,112,128]{2,1,0:T(8,128)S(1)} collective-permute-done((f32[16,112,128]{2,1,0:T(8,128)}, f32[16,112,128]{2,1,0:T(8,128)S(1)}, u32[]{:S(2)}, u32[]{:S(2)}) %collective-permute-start.7) | collective-permute-done | bytes 917536 | tf_op jit(solution)/shard_map/ppermute | solution.py:897
  90.2 1.1 slice_add_fusion
  91.3 0.9 collective-permute-start.8
  92.2 11.8 %collective-permute-done.8 = f32[8,112,128]{2,1,0:T(8,128)S(1)} collective-permute-done((f32[8,112,128]{2,1,0:T(8,128)S(1)}, f32[8,112,128]{2,1,0:T(8,128)S(1)}, u32[]{:S(2)}, u32[]{:S(2)}) %collective-permute-start.8) | collective-permute-done | bytes 458784 | tf_op jit(solution)/shard_map/ppermute | solution.py:897
  104.0 0.9 collective-permute-start.9
  104.9 6.0 %collective-permute-done.9 = f32[4,112,128]{2,1,0:T(8,128)S(1)} collective-permute-done((f32[4,112,128]{2,1,0:T(8,128)S(1)}, f32[4,112,128]{2,1,0:T(8,128)S(1)}, u32[]{:S(2)}, u32[]{:S(2)}) %collective-permute-start.9) | collective-permute-done | bytes 229408 | tf_op jit(solution)/shard_map/ppermute | solution.py:897
  110.9 1.0 collective-permute-start.10
  111.9 3.9 %collective-permute-done.10 = f32[2,112,128]{2,1,0:T(8,128)S(1)} collective-permute-done((f32[2,112,128]{2,1,0:T(8,128)S(1)}, f32[2,112,128]{2,1,0:T(8,128)S(1)}, u32[]{:S(2)}, u32[]{:S(2)}) %collective-permute-start.10) | collective-permute-done | bytes 114720 | tf_op jit(solution)/shard_map/ppermute | solution.py:897
  115.8 3.4 %collective-permute-start.11 = (f32[1,112,128]{2,1,0:T(8,128)S(1)}, f32[1,112,128]{2,1,0:T(8,128)S(1)}, u32[]{:S(2)}, u32[]{:S(2)}) collective-permute-start(f32[1,112,128]{2,1,0:T(8,128)S(1)} %slice_add_fusion.6), channel_id=1, source_target_pairs={{0,16},{1,17},{2,18},{3,19},{4,20},{5,21},{6,22},{7,23},{8,24},{9,... | collective-permute-start | bytes 172040 | tf_op jit(solution)/shard_map/ppermute | solution.py:897
  119.2 2.9 %collective-permute-done.11 = f32[1,112,128]{2,1,0:T(8,128)S(1)} collective-permute-done((f32[1,112,128]{2,1,0:T(8,128)S(1)}, f32[1,112,128]{2,1,0:T(8,128)S(1)}, u32[]{:S(2)}, u32[]{:S(2)}) %collective-permute-start.11) | collective-permute-done | bytes 57376 | tf_op jit(solution)/shard_map/ppermute | solution.py:897
  122.1 3.4 %collective-permute-start.12 = (f32[1,112,128]{2,1,0:T(8,128)S(1)}, f32[1,112,128]{2,1,0:T(8,128)S(1)}, u32[]{:S(2)}, u32[]{:S(2)}) collective-permute-start(f32[1,112,128]{2,1,0:T(8,128)S(1)} %get-tuple-element.95), channel_id=1, source_target_pairs={{0,16},{1,17},{2,18},{3,19},{4,20},{5,21},{6,22},{7,23},{8,24},{9,... | collective-permute-start | bytes 172040 | tf_op jit(solution)/shard_map/ppermute | solution.py:897
  125.6 2.7 %collective-permute-done.12 = f32[1,112,128]{2,1,0:T(8,128)S(1)} collective-permute-done((f32[1,112,128]{2,1,0:T(8,128)S(1)}, f32[1,112,128]{2,1,0:T(8,128)S(1)}, u32[]{:S(2)}, u32[]{:S(2)}) %collective-permute-start.12) | collective-permute-done | bytes 57376 | tf_op jit(solution)/shard_map/ppermute | solution.py:897
  128.4 4.8 %collective-permute-done.13 = f32[2,112,128]{2,1,0:T(8,128)S(1)} collective-permute-done((f32[2,112,128]{2,1,0:T(8,128)S(1)}, f32[2,112,128]{2,1,0:T(8,128)S(1)}, u32[]{:S(2)}, u32[]{:S(2)}) %collective-permute-start.13) | collective-permute-done | bytes 114720 | tf_op jit(solution)/shard_map/ppermute | solution.py:897
  133.2 0.9 collective-permute-start.14
  134.1 5.2 %collective-permute-done.14 = f32[4,112,128]{2,1,0:T(8,128)S(1)} collective-permute-done((f32[4,112,128]{2,1,0:T(8,128)S(1)}, f32[4,112,128]{2,1,0:T(8,128)S(1)}, u32[]{:S(2)}, u32[]{:S(2)}) %collective-permute-start.14) | collective-permute-done | bytes 229408 | tf_op jit(solution)/shard_map/ppermute | solution.py:897
  139.3 0.8 collective-permute-start.15
  140.2 7.6 %collective-permute-done.15 = f32[8,112,128]{2,1,0:T(8,128)S(1)} collective-permute-done((f32[8,112,128]{2,1,0:T(8,128)S(1)}, f32[8,112,128]{2,1,0:T(8,128)S(1)}, u32[]{:S(2)}, u32[]{:S(2)}) %collective-permute-start.15) | collective-permute-done | bytes 458784 | tf_op jit(solution)/shard_map/ppermute | solution.py:897
  148.5 3.5 %collective-permute-start.18 = (f32[8,256]{1,0:T(8,128)S(1)}, f32[8,256]{1,0:T(8,128)S(1)}, u32[]{:S(2)}, u32[]{:S(2)}) collective-permute-start(f32[8,256]{1,0:T(8,128)S(1)} %copy-done.18), channel_id=1, source_target_pairs={{1,2},{3,4},{5,6},{7,8},{9,10},{11,12},{13,14},{15,16},{17,18},{19... | collective-permute-start | bytes 24584 | tf_op jit(solution)/shard_map/ppermute | solution.py:902
  152.0 3.2 %collective-permute-done.18.refs_4_ = f32[8,256]{1,0:T(8,128)S(1)} collective-permute-done((f32[8,256]{1,0:T(8,128)S(1)}, f32[8,256]{1,0:T(8,128)S(1)}, u32[]{:S(2)}, u32[]{:S(2)}) %collective-permute-start.18) | collective-permute-done | bytes 8224 | tf_op jit(solution)/shard_map/ppermute | solution.py:902
  156.2 3.4 %unpack.1 = (f32[128,256]{1,0:T(8,128)}, f32[1,256]{1,0:T(1,128)}, f32[256,1024]{1,0:T(8,128)}, f32[4,512]{1,0:T(4,128)}, f32[1,512]{1,0:T(1,128)}, /*index=5*/f...) custom-call(f32[16,112,128]{2,1,0:T(8,128)} %copy-done, ...), custom_call_target="tpu_custom_call" | custom-call | tf_op jit(solution)/shard_map/unpack/pallas_call | solution.py:866
  159.5 1.7 %copy.28 = f32[1,512,16]{1,2,0:T(8,128)} copy(f32[1,512,16]{2,1,0:T(8,128)} %bitcast.31) | data formatting | bytes 65536
  161.2 0.8 copy.27
  (62 shorter events, 3.3 us)
Async XLA Ops:
  0.6 0.7 copy-start.17
  1.3 0.7 copy-start.16
  3.0 9.5 %collective-permute-start.1 = (f32[8,256]{1,0:T(8,128)S(1)}, f32[8,256]{1,0:T(8,128)S(1)}, u32[]{:S(2)}, u32[]{:S(2)}) collective-permute-start(f32[8,256]{1,0:T(8,128)S(1)} %get-tuple-element.98), channel_id=1, source_target_pairs={{1,2},{3,4},{5,6},{7,8},{9,10},{11,12},{13,14},{15,16},{17,18},{19... | collective-permute-start | bytes 24584 | tf_op jit(solution)/shard_map/ppermute | solution.py:902
  6.7 5.8 %collective-permute-start = (f32[8,256]{1,0:T(8,128)S(1)}, f32[8,256]{1,0:T(8,128)S(1)}, u32[]{:S(2)}, u32[]{:S(2)}) collective-permute-start(f32[8,256]{1,0:T(8,128)S(1)} %get-tuple-element.99), channel_id=1, source_target_pairs={{0,1},{1,0},{2,3},{3,2},{4,5},{5,4},{6,7},{7,6},{8,9},{9,8},{10,11... | collective-permute-start | bytes 24584 | tf_op jit(solution)/shard_map/ppermute | solution.py:897
  12.4 0.6 copy-start.12
  12.5 0.6 copy-start.13
  23.3 1.7 %collective-permute-start.2 = (f32[72,512]{1,0:T(8,128)}, f32[72,512]{1,0:T(8,128)S(1)}, u32[]{:S(2)}, u32[]{:S(2)}) collective-permute-start(f32[72,512]{1,0:T(8,128)} %get-tuple-element.60.refs_1_), channel_id=1, source_target_pairs={{0,1},{1,0},{2,3},{3,2},{4,5},{5,4},{6,7},{7,6},{8,9},{9,8},{10,11... | collective-permute-start | bytes 442376 | tf_op jit(solution)/shard_map/ppermute | solution.py:897
  25.0 0.7 copy-start.2
  27.4 6.3 %collective-permute-start.3 = (f32[72,512]{1,0:T(8,128)}, f32[72,512]{1,0:T(8,128)S(1)}, u32[]{:S(2)}, u32[]{:S(2)}) collective-permute-start(f32[72,512]{1,0:T(8,128)} %join.4.refs_1_), channel_id=1, source_target_pairs={{0,2},{1,3},{2,0},{3,1},{4,6},{5,7},{6,4},{7,5},{8,10},{9,11},{10,... | collective-permute-start | bytes 442376 | tf_op jit(solution)/shard_map/ppermute | solution.py:897
  33.7 0.7 copy-start.3
  36.1 5.5 %collective-permute-start.4 = (f32[72,512]{1,0:T(8,128)}, f32[72,512]{1,0:T(8,128)S(1)}, u32[]{:S(2)}, u32[]{:S(2)}) collective-permute-start(f32[72,512]{1,0:T(8,128)} %join.5.refs_1_), channel_id=1, source_target_pairs={{0,4},{1,5},{2,6},{3,7},{4,0},{5,1},{6,2},{7,3},{8,12},{9,13},{10,... | collective-permute-start | bytes 442376 | tf_op jit(solution)/shard_map/ppermute | solution.py:897
  41.6 0.7 copy-start.4
  43.9 5.4 %collective-permute-start.5 = (f32[72,512]{1,0:T(8,128)}, f32[72,512]{1,0:T(8,128)S(1)}, u32[]{:S(2)}, u32[]{:S(2)}) collective-permute-start(f32[72,512]{1,0:T(8,128)} %join.6.refs_1_), channel_id=1, source_target_pairs={{0,8},{1,9},{2,10},{3,11},{4,12},{5,13},{6,14},{7,15},{8,0},{9,1},... | collective-permute-start | bytes 442376 | tf_op jit(solution)/shard_map/ppermute | solution.py:897
  49.3 0.7 copy-start.5
  51.6 7.0 %collective-permute-start.6 = (f32[72,512]{1,0:T(8,128)}, f32[72,512]{1,0:T(8,128)S(1)}, u32[]{:S(2)}, u32[]{:S(2)}) collective-permute-start(f32[72,512]{1,0:T(8,128)} %join.7), channel_id=1, source_target_pairs={{0,16},{1,17},{2,18},{3,19},{4,20},{5,21},{6,22},{7,23},{8,24},{9,... | collective-permute-start | bytes 442376 | tf_op jit(solution)/shard_map/ppermute | solution.py:897
  58.7 0.7 copy-start.8
  87.5 2.7 %collective-permute-start.7 = (f32[16,112,128]{2,1,0:T(8,128)}, f32[16,112,128]{2,1,0:T(8,128)S(1)}, u32[]{:S(2)}, u32[]{:S(2)}) collective-permute-start(f32[16,112,128]{2,1,0:T(8,128)} %get-tuple-element.63), channel_id=1, source_target_pairs={{0,1},{1,0},{2,3},{3,2},{4,5},{5,4},{6,7},{7,6},{8,9},{9,8},{10,11... | collective-permute-start | bytes 2752520 | tf_op jit(solution)/shard_map/ppermute | solution.py:897
  90.2 13.8 %copy-start.7 = (f32[4,112,128]{2,1,0:T(8,128)S(1)}, f32[4,112,128]{2,1,0:T(8,128)}, u32[]{:S(2)}) copy-start(f32[4,112,128]{2,1,0:T(8,128)} %get-tuple-element.65) | copy-start | bytes 688132
  91.3 12.6 %collective-permute-start.8 = (f32[8,112,128]{2,1,0:T(8,128)S(1)}, f32[8,112,128]{2,1,0:T(8,128)S(1)}, u32[]{:S(2)}, u32[]{:S(2)}) collective-permute-start(f32[8,112,128]{2,1,0:T(8,128)S(1)} %slice_add_fusion), channel_id=1, source_target_pairs={{0,2},{1,3},{2,0},{3,1},{4,6},{5,7},{6,4},{7,5},{8,10},{9,11},{10,... | collective-permute-start | bytes 1376264 | tf_op jit(solution)/shard_map/ppermute | solution.py:897
  104.0 6.9 %copy-start.9 = (f32[2,112,128]{2,1,0:T(8,128)S(1)}, f32[2,112,128]{2,1,0:T(8,128)}, u32[]{:S(2)}) copy-start(f32[2,112,128]{2,1,0:T(8,128)} %get-tuple-element.66) | copy-start | bytes 344068
  104.0 6.9 %collective-permute-start.9 = (f32[4,112,128]{2,1,0:T(8,128)S(1)}, f32[4,112,128]{2,1,0:T(8,128)S(1)}, u32[]{:S(2)}, u32[]{:S(2)}) collective-permute-start(f32[4,112,128]{2,1,0:T(8,128)S(1)} %slice_add_fusion.1), channel_id=1, source_target_pairs={{0,4},{1,5},{2,6},{3,7},{4,0},{5,1},{6,2},{7,3},{8,12},{9,13},{10,... | collective-permute-start | bytes 688136 | tf_op jit(solution)/shard_map/ppermute | solution.py:897
  110.9 4.9 %copy-start.11 = (f32[1,112,128]{2,1,0:T(8,128)S(1)}, f32[1,112,128]{2,1,0:T(8,128)}, u32[]{:S(2)}) copy-start(f32[1,112,128]{2,1,0:T(8,128)} %get-tuple-element.67) | copy-start | bytes 172036
  110.9 4.9 %collective-permute-start.10 = (f32[2,112,128]{2,1,0:T(8,128)S(1)}, f32[2,112,128]{2,1,0:T(8,128)S(1)}, u32[]{:S(2)}, u32[]{:S(2)}) collective-permute-start(f32[2,112,128]{2,1,0:T(8,128)S(1)} %slice_add_fusion.3), channel_id=1, source_target_pairs={{0,8},{1,9},{2,10},{3,11},{4,12},{5,13},{6,14},{7,15},{8,0},{9,1},... | collective-permute-start | bytes 344072 | tf_op jit(solution)/shard_map/ppermute | solution.py:897
  115.8 6.3 %copy-start.10 = (f32[1,112,128]{2,1,0:T(8,128)S(1)}, f32[1,112,128]{2,1,0:T(8,128)}, u32[]{:S(2)}) copy-start(f32[1,112,128]{2,1,0:T(8,128)} %get-tuple-element.62) | copy-start | bytes 172036
  115.8 6.3 %collective-permute-start.11 = (f32[1,112,128]{2,1,0:T(8,128)S(1)}, f32[1,112,128]{2,1,0:T(8,128)S(1)}, u32[]{:S(2)}, u32[]{:S(2)}) collective-permute-start(f32[1,112,128]{2,1,0:T(8,128)S(1)} %slice_add_fusion.6), channel_id=1, source_target_pairs={{0,16},{1,17},{2,18},{3,19},{4,20},{5,21},{6,22},{7,23},{8,24},{9,... | collective-permute-start | bytes 172040 | tf_op jit(solution)/shard_map/ppermute | solution.py:897
  122.1 6.2 %collective-permute-start.12 = (f32[1,112,128]{2,1,0:T(8,128)S(1)}, f32[1,112,128]{2,1,0:T(8,128)S(1)}, u32[]{:S(2)}, u32[]{:S(2)}) collective-permute-start(f32[1,112,128]{2,1,0:T(8,128)S(1)} %get-tuple-element.95), channel_id=1, source_target_pairs={{0,16},{1,17},{2,18},{3,19},{4,20},{5,21},{6,22},{7,23},{8,24},{9,... | collective-permute-start | bytes 172040 | tf_op jit(solution)/shard_map/ppermute | solution.py:897
  128.3 4.9 %collective-permute-start.13 = (f32[2,112,128]{2,1,0:T(8,128)S(1)}, f32[2,112,128]{2,1,0:T(8,128)S(1)}, u32[]{:S(2)}, u32[]{:S(2)}) collective-permute-start(f32[2,112,128]{2,1,0:T(8,128)S(1)} %pad_maximum_fusion.2), channel_id=1, source_target_pairs={{0,8},{1,9},{2,10},{3,11},{4,12},{5,13},{6,14},{7,15},{8,0},{9,1},... | collective-permute-start | bytes 344072 | tf_op jit(solution)/shard_map/ppermute | solution.py:897
  133.2 6.1 %collective-permute-start.14 = (f32[4,112,128]{2,1,0:T(8,128)S(1)}, f32[4,112,128]{2,1,0:T(8,128)S(1)}, u32[]{:S(2)}, u32[]{:S(2)}) collective-permute-start(f32[4,112,128]{2,1,0:T(8,128)S(1)} %pad_maximum_fusion.1), channel_id=1, source_target_pairs={{0,4},{1,5},{2,6},{3,7},{4,0},{5,1},{6,2},{7,3},{8,12},{9,13},{10,... | collective-permute-start | bytes 688136 | tf_op jit(solution)/shard_map/ppermute | solution.py:897
  139.3 8.5 %collective-permute-start.15 = (f32[8,112,128]{2,1,0:T(8,128)S(1)}, f32[8,112,128]{2,1,0:T(8,128)S(1)}, u32[]{:S(2)}, u32[]{:S(2)}) collective-permute-start(f32[8,112,128]{2,1,0:T(8,128)S(1)} %pad_maximum_fusion), channel_id=1, source_target_pairs={{0,2},{1,3},{2,0},{3,1},{4,6},{5,7},{6,4},{7,5},{8,10},{9,11},{10,... | collective-permute-start | bytes 1376264 | tf_op jit(solution)/shard_map/ppermute | solution.py:897
  140.2 7.8 %copy-start.19 = (f32[8,256]{1,0:T(8,128)S(1)}, f32[8,256]{1,0:T(8,128)}, u32[]{:S(2)}) copy-start(f32[8,256]{1,0:T(8,128)} %get-tuple-element.69) | copy-start | bytes 24580
  140.2 8.3 %copy-start.18 = (f32[8,256]{1,0:T(8,128)S(1)}, f32[8,256]{1,0:T(8,128)}, u32[]{:S(2)}) copy-start(f32[8,256]{1,0:T(8,128)} %get-tuple-element.70) | copy-start | bytes 24580
  147.9 7.4 %copy-start = (f32[16,112,128]{2,1,0:T(8,128)}, f32[16,112,128]{2,1,0:T(8,128)S(1)}, u32[]{:S(2)}) copy-start(f32[16,112,128]{2,1,0:T(8,128)S(1)} %constant_dynamic-update-slice_fusion.refs_0_) | copy-start | bytes 2752516
  147.9 7.3 %collective-permute-start.16 = (f32[16,112,128]{2,1,0:T(8,128)S(1)}, f32[16,112,128]{2,1,0:T(8,128)S(1)}, u32[]{:S(2)}, u32[]{:S(2)}) collective-permute-start(f32[16,112,128]{2,1,0:T(8,128)S(1)} %constant_dynamic-update-slice_fusion.refs_0_), channel_id=1, source_target_pairs={{0,1},{1,0},{2,3},{3,2},{4,5},{5,4},{6,7},{7,6},{8,9},{9,8},{10,11... | collective-permute-start | bytes 2752520 | tf_op jit(solution)/shard_map/ppermute | solution.py:897
  148.0 4.0 %collective-permute-start.17 = (f32[8,256]{1,0:T(8,128)S(1)}, f32[8,256]{1,0:T(8,128)S(1)}, u32[]{:S(2)}, u32[]{:S(2)}) collective-permute-start(f32[8,256]{1,0:T(8,128)S(1)} %copy-done.19), channel_id=1, source_target_pairs={{0,1},{1,0},{2,3},{3,2},{4,5},{5,4},{6,7},{7,6},{8,9},{9,8},{10,11... | collective-permute-start | bytes 24584 | tf_op jit(solution)/shard_map/ppermute | solution.py:897
  148.5 6.8 %collective-permute-start.18 = (f32[8,256]{1,0:T(8,128)S(1)}, f32[8,256]{1,0:T(8,128)S(1)}, u32[]{:S(2)}, u32[]{:S(2)}) collective-permute-start(f32[8,256]{1,0:T(8,128)S(1)} %copy-done.18), channel_id=1, source_target_pairs={{1,2},{3,4},{5,6},{7,8},{9,10},{11,12},{13,14},{15,16},{17,18},{19... | collective-permute-start | bytes 24584 | tf_op jit(solution)/shard_map/ppermute | solution.py:902
  152.0 3.2 %copy-start.14 = (f32[8,256]{1,0:T(8,128)}, f32[8,256]{1,0:T(8,128)S(1)}, u32[]{:S(2)}) copy-start(f32[8,256]{1,0:T(8,128)S(1)} %collective-permute-done.17.refs_3_) | copy-start | bytes 24580
  155.2 0.6 copy-start.15
  155.2 0.9 copy-start.1
  159.5 1.7 %copy-start.6 = (f32[512,48]{1,0:T(8,128)S(1)}, f32[512,48]{1,0:T(8,128)}, u32[]{:S(2)}) copy-start(f32[512,48]{1,0:T(8,128)} %get-tuple-element.76) | copy-start | bytes 294916

commit v2 on v1

v2 whole, which is shorter than its diff:
```python
import jax
import jax.numpy as jnp
from jax import lax
from jax.experimental import pallas as pl
from jax.experimental.pallas import tpu as pltpu
from jax.sharding import PartitionSpec as P

F32 = jnp.float32
BF16 = jnp.bfloat16
EPS = 1e-05
LOG2E = 1.4426950408889634
LN2 = 0.6931471805599453
BIG = 1e9
CH = 8
LANE = 128
MIB = 1024 * 1024


def nn(a, b):
    return lax.dot_general(a, b, (((1,), (0,)), ((), ())), preferred_element_type=F32)


def nt(a, b):
    return lax.dot_general(a, b, (((1,), (1,)), ((), ())), preferred_element_type=F32)


def tn(a, b):
    return lax.dot_general(a, b, (((0,), (0,)), ((), ())), preferred_element_type=F32)


def split(x):
    high = x.astype(BF16)
    return high, (x - high.astype(F32)).astype(BF16)


def split3(x):
    high = x.astype(BF16)
    rest = x - high.astype(F32)
    mid = rest.astype(BF16)
    return high, mid, (rest - mid.astype(F32)).astype(BF16)


def mm(dot, a, b):
    ah, al = a if isinstance(a, tuple) else split(a)
    bh, bl = b if isinstance(b, tuple) else split(b)
    return dot(ah, bh) + (dot(ah, bl) + dot(al, bh))


def flip_matrix(size):
    rows = lax.broadcasted_iota(jnp.int32, (size, size), 0)
    cols = lax.broadcasted_iota(jnp.int32, (size, size), 1)
    return jnp.where(rows + cols == size - 1, 1.0, 0.0).astype(BF16)


def flipped(x):
    flip = flip_matrix(x.shape[1])
    high, mid, low = split3(x)
    return nn(high, flip) + (nn(mid, flip) + nn(low, flip))


def order_matrix(length):
    steps = length // CH
    rows = lax.broadcasted_iota(jnp.int32, (length, length), 0)
    cols = lax.broadcasted_iota(jnp.int32, (length, length), 1)
    token = (rows & (CH - 1)) * steps + (rows >> 3)
    return jnp.where(cols == token, 1.0, 0.0)


def exact(dot, order, x):
    high, mid, low = split3(x)
    order = order.astype(BF16)
    return dot(order, high) + (dot(order, mid) + dot(order, low))


def ordered(ref):
    return exact(nn, order_matrix(ref.shape[0]), ref[...])


def store_ordered(ref, value):
    ref[...] = exact(tn, order_matrix(ref.shape[0]), value)


def spread(row):
    length = row.shape[1]
    picked = (order_matrix(length) * row).astype(BF16)
    return nn(picked, jnp.ones((length, LANE), BF16))


def sigmoid(x):
    return 1.0 / (1.0 + jnp.exp(-x))


def normalize(x, gain):
    factor = lax.rsqrt(jnp.mean(x * x, axis=1, keepdims=True) + EPS)
    return factor, x * factor * gain


def both_orders(normed):
    flip = flip_matrix(normed.shape[1])
    high, low = split(normed)
    return (
        jnp.concatenate([high, nn(high, flip).astype(BF16)], axis=0),
        jnp.concatenate([low, nn(low, flip).astype(BF16)], axis=0),
    )


def params(mib):
    return pltpu.CompilerParams(vmem_limit_bytes=mib * MIB)


def in_hbm(*arrays):
    return tuple(pltpu.with_memory_space_constraint(x, pltpu.HBM) for x in arrays)


def edges_kernel(first_rows, last_rows, resets, pad, to_sib, to_oth):
    length = resets.shape[1]
    sub = lax.broadcasted_iota(jnp.int32, (CH, length), 0)
    lane = lax.broadcasted_iota(jnp.int32, (CH, length), 1)
    real = pad[...].astype(F32)
    row = lax.broadcasted_iota(jnp.int32, first_rows.shape, 0)
    kept = 1.0 - resets[...].astype(F32)
    kept = jnp.concatenate([kept, jnp.zeros((1, first_rows.shape[1] - length), F32)], axis=1)

    def message(rows, start):
        col = jnp.sum(jnp.where(lane == sub + start, real, 0.0), axis=1, keepdims=True)
        return jnp.where(row < 3, rows * col, jnp.where(row == 3, kept, 0.0))

    first = message(first_rows[...], 0)
    last = message(pltpu.roll(last_rows[...], 3, 0), length - 3)
    odd = (lax.axis_index("seq") & 1) == 1
    to_sib[...] = jnp.where(odd, first, last)
    to_oth[...] = jnp.where(odd, last, first)


def edges(tok, resets, pad):
    length, feat = tok.shape
    shape = jax.ShapeDtypeStruct((CH, feat), F32)
    whole = lambda *dims: pl.BlockSpec(dims, lambda i: (0, 0))
    return pl.pallas_call(
        edges_kernel,
        grid=(1,),
        in_specs=[
            whole(CH, feat),
            pl.BlockSpec((CH, feat), lambda i: (length // CH - 1, 0)),
            whole(1, length),
            whole(1, length),
        ],
        out_specs=(whole(CH, feat), whole(CH, feat)),
        out_shape=(shape, shape),
        compiler_params=params(2),
        name="edges",
    )(*in_hbm(tok, tok, resets, pad))


def project_kernel(tok, pad, gain, w_in, gout, w_out, *refs):
    more = (len(refs) - 10) // 2
    xb_o, z_o, go_o, gy_o, *kept = refs[more:]
    for ref, kept_o in zip((tok, pad, gain, w_in, gout, w_out) + refs[:more], kept):
        kept_o[...] = ref[...]
    inner = w_out.shape[0]
    x = ordered(tok)
    normed = normalize(x, gain[...])[1]
    proj = mm(nn, both_orders(normed), split(w_in[...]))
    pad_col = spread(pad[...].astype(F32))
    pad_all = jnp.concatenate([pad_col, pad_col], axis=0)
    g = ordered(gout)
    gh, gl = both_orders(g)
    go = mm(nt, (gh, gl), split(w_out[...]))
    for lt in range(inner // LANE):
        cols = slice(lt * LANE, (lt + 1) * LANE)
        z = proj[:, inner + lt * LANE : inner + (lt + 1) * LANE]
        xb_o[:, cols] = proj[:, cols] * pad_all
        z_o[:, cols] = z
        go_o[:, cols] = go[:, cols]
        gy_o[:, cols] = go[:, cols] * (z * sigmoid(z))


def project(*arrays):
    tok, w_out = arrays[0], arrays[5]
    length, inner = tok.shape[0], w_out.shape[0]
    big = jax.ShapeDtypeStruct((2 * length, inner), F32)
    found = pl.pallas_call(
        project_kernel,
        out_shape=(big, big, big, big) + tuple(jax.ShapeDtypeStruct(x.shape, x.dtype) for x in arrays),
        compiler_params=params(8),
        name="project",
    )(*in_hbm(*arrays))
    return found[:4], found[4:]


def pick_sides(from_sibling, from_other):
    odd = (lax.axis_index("seq") & 1) == 1
    left = jnp.where(odd, from_sibling, from_other)
    right = jnp.where(odd, from_other, from_sibling)
    return left, right


def rows_of(ref, first, count, cols):
    block = ref[pl.ds(pl.multiple_of(first, CH), count), cols]
    return [jnp.broadcast_to(block[n : n + 1], (CH, LANE)) for n in range(count)]


def sub_iota():
    return lax.broadcasted_iota(jnp.int32, (CH, LANE), 0)


def shifted(value, up):
    return pltpu.roll(value, 1 if up else CH - 1, 0)


def chunk_weights(total, up):
    sub = sub_iota()
    found = []
    width = total
    for reach in (1, 2, 4):
        inside = (sub >= reach) if up else (sub < CH - reach)
        found.append(jnp.where(inside, width, BIG))
        width = width + pltpu.roll(width, reach if up else CH - reach, 0)
    return found


def outside_sum(total, up):
    sub = sub_iota()
    value = jnp.where((sub >= 1) if up else (sub < CH - 1), shifted(total, up), 0.0)
    for reach in (1, 2, 4):
        inside = (sub >= reach) if up else (sub < CH - reach)
        value = value + jnp.where(inside, pltpu.roll(value, reach if up else CH - reach, 0), 0.0)
    return value


def chunk_scan(value, weights, a2, up):
    for reach, weight in zip((1, 2, 4), weights):
        value = value + jnp.exp2(weight * a2) * pltpu.roll(value, reach if up else CH - reach, 0)
    sub = sub_iota()
    enter = jnp.where((sub >= 1) if up else (sub < CH - 1), shifted(value, up), 0.0)
    leave = value[CH - 1 : CH] if up else value[0:1]
    return enter, leave


def prepare_kernel(
    sib, oth, keep, gain, w_in, conv_w, conv_b, w_x, w_dt, dt_bias, a_log, xb, gy,
    xc_o, dt_o, sig_o, conv_o, mask_o, dbl_o, xbh_o, sx_o, mx_o, sum_o, de_s, dx_s, bc_s, a2_s, decay_o,
    leave_s,
):
    inner, rank = w_x.shape[1], w_dt.shape[0]
    state = a_log.shape[0]
    length = xb.shape[0] // 2
    steps = length // CH
    tiles = inner // LANE
    left, right = pick_sides(sib[...], oth[...])
    hn_l = normalize(left, gain[...])[1]
    hn_r = normalize(right, gain[...])[1]
    flip = flip_matrix(hn_r.shape[1])
    lh, ll = split(hn_l)
    rh, rl = split(hn_r)
    halo = (
        jnp.concatenate([lh, nn(rh, flip).astype(BF16)], axis=0),
        jnp.concatenate([ll, nn(rl, flip).astype(BF16)], axis=0),
    )
    xbh = mm(nn, halo, split(w_in[:, :inner]))
    xbh_o[...] = xbh
    lane = lax.broadcasted_iota(jnp.int32, (1, length), 1)
    here = 1.0 - keep[...].astype(F32)
    before, after = left[3:4, :length], right[3:4, :length]

    def back(k):
        return jnp.where(lane < k, pltpu.roll(before, k, 1), pltpu.roll(here, k, 1))

    def ahead(k):
        return jnp.where(
            lane >= length - k,
            pltpu.roll(after, length - k, 1),
            pltpu.roll(here, length - k, 1),
        )

    f1 = here
    f2 = f1 * back(1)
    f3 = f2 * back(2)
    r1 = ahead(1)
    r2 = r1 * ahead(2)
    r3 = r2 * ahead(3)
    for i, row in enumerate((f1, f2, f3, r1, r2, r3)):
        mask_o[i * length : (i + 1) * length, :] = spread(row)

    sub = sub_iota()

    def conv_tile(lt, carry):
        cols = pl.ds(pl.multiple_of(lt * LANE, LANE), LANE)
        xbh_t = xbh_o[:, cols]
        taps = [conv_w[k : k + 1, cols] for k in range(4)]
        bias = conv_b[:, cols]
        xf = [xb[j * CH : (j + 1) * CH, cols] for j in range(steps)]
        edge = [
            jnp.where(sub == 0, xbh_t[b : b + 1], pltpu.roll(xf[steps - 3 + b], 1, 0))
            for b in range(3)
        ]
        xf = edge + xf
        for j in range(steps):
            rows = slice(j * CH, (j + 1) * CH)
            v = bias + taps[0] * xf[j + 3]
            for k in range(1, 4):
                v = v + taps[k] * (mask_o[(k - 1) * length + j * CH : (k - 1) * length + (j + 1) * CH, :] * xf[j + 3 - k])
            conv_o[rows, cols] = v
            xc_o[rows, cols] = v * sigmoid(v)
        xr = [xb[length + j * CH : length + (j + 1) * CH, cols] for j in range(steps)]
        xr = xr + [
            jnp.where(sub == CH - 1, xbh_t[8 + b : 9 + b], pltpu.roll(xr[b], CH - 1, 0))
            for b in range(3)
        ]
        for j in range(steps):
            rows = slice(length + j * CH, length + (j + 1) * CH)
            v = bias + taps[0] * xr[j]
            for k in range(1, 4):
                v = v + taps[k] * (mask_o[(k + 2) * length + j * CH : (k + 2) * length + (j + 1) * CH, :] * xr[j + k])
            conv_o[rows, cols] = v
            xc_o[rows, cols] = v * sigmoid(v)
        return carry

    lax.fori_loop(0, tiles, conv_tile, 0)
    dbl = mm(nt, xc_o[...], w_x[...])
    dbl_o[...] = dbl
    pre_all = mm(nn, dbl[:, :rank], w_dt[...])
    expand_bc(dbl, rank, state, bc_s)
    a2 = jnp.exp(a_log[...]) * (-LOG2E)
    for n in range(state):
        a2_s[n] = jnp.broadcast_to(a2[n : n + 1], (CH, inner))
    for lt in range(tiles):
        cols = slice(lt * LANE, (lt + 1) * LANE)
        pre = pre_all[:, cols] + dt_bias[:, cols]
        e = jnp.exp(-jnp.abs(pre))
        u = 1.0 + e
        log1p = jnp.where(u == 1.0, e, jnp.log(u) * (e / (u - 1.0)))
        dt = jnp.maximum(pre, 0.0) + log1p
        dt_o[:, cols] = dt
        sig_o[:, cols] = jnp.where(pre >= 0.0, 1.0, e) / u
        dx_s[:, cols] = dt * xc_o[:, cols]
        cut = jnp.concatenate([mask_o[:length], mask_o[3 * length : 4 * length]], axis=0)
        de_s[:, cols] = dt + BIG * (1.0 - cut)

    group = 4
    cols_of = [slice(t * LANE, (t + 1) * LANE) for t in range(tiles)]
    for dirn in range(2):
        order = list(range(steps)) if dirn == 0 else list(range(steps - 1, -1, -1))
        base = dirn * length
        up = dirn == 0
        s_row, m_row = (0, 3) if dirn == 0 else (2, 1)
        totals = []
        for cols in cols_of:
            total = jnp.zeros((CH, LANE), F32)
            for j in range(steps):
                total = total + de_s[base + j * CH : base + (j + 1) * CH, cols]
            sum_o[4 * state + dirn : 4 * state + dirn + 1, cols] = jnp.sum(total, axis=0, keepdims=True)
            totals.append(total)

        def some(g, carry, order=order, base=base, up=up, dirn=dirn, s_row=s_row, m_row=m_row, totals=totals):
            n0 = g * group
            at_b, at_c = lanes_of(n0, group), lanes_of(state + n0, group)
            keys = [(n, t) for n in range(group) for t in range(tiles)]
            a2 = {(n, t): a2_s[n0 + n, :, cols_of[t]] for n, t in keys}
            h, m = {}, {}
            for at, j in enumerate(order):
                rows = slice(base + j * CH, base + (j + 1) * CH)
                de = [de_s[rows, c] for c in cols_of]
                dx = [dx_s[rows, c] for c in cols_of]
                for n in range(group):
                    b_n = bc_s[rows, at_b[n]]
                    for t, cols in enumerate(cols_of):
                        d = jnp.exp2(de[t] * a2[n, t])
                        decay_o[dirn, at, n0 + n, :, cols] = d
                        h[n, t] = dx[t] * b_n if at == 0 else d * h[n, t] + dx[t] * b_n
            for at in range(steps - 1, -1, -1):
                rows = slice(base + order[at] * CH, base + (order[at] + 1) * CH)
                gyj = [gy[rows, c] for c in cols_of]
                for n in range(group):
                    c_n = bc_s[rows, at_c[n]]
                    for t, cols in enumerate(cols_of):
                        own = gyj[t] * c_n
                        d = decay_o[dirn, at, n0 + n, :, cols]
                        m[n, t] = d * (own if at == steps - 1 else own + m[n, t])
            for t in range(tiles):
                w_s, w_m = chunk_weights(totals[t], up), chunk_weights(totals[t], not up)
                for n in range(group):
                    enter, leave = chunk_scan(h[n, t], w_s, a2[n, t], up)
                    sx_o[dirn, n0 + n, :, cols_of[t]] = enter
                    leave_s[s_row * state + n0 + n, :, cols_of[t]] = jnp.broadcast_to(leave, (CH, LANE))
                    enter, leave = chunk_scan(m[n, t], w_m, a2[n, t], not up)
                    mx_o[dirn, n0 + n, :, cols_of[t]] = enter
                    leave_s[m_row * state + n0 + n, :, cols_of[t]] = jnp.broadcast_to(leave, (CH, LANE))
            return carry

        lax.fori_loop(0, state // group, some, 0)
    for row in range(0, 4 * state, CH):
        for cols in cols_of:
            sum_o[row : row + CH, cols] = jnp.concatenate([leave_s[row + i, 0:1, cols] for i in range(CH)], axis=0)
    sum_o[4 * state + 2 :, :] = jnp.zeros((sum_o.shape[0] - 4 * state - 2, inner), F32)


def lanes_of(first, count):
    return [pl.ds(pl.multiple_of((first + n) * LANE, LANE), LANE) for n in range(count)]


def expand_bc(dbl, rank, state, bc_s):
    pieces = split3(dbl[:, rank:])
    width = dbl.shape[1] - rank
    lhs = jnp.concatenate(pieces, axis=1)
    rows = lax.broadcasted_iota(jnp.int32, (3 * width, width * LANE), 0)
    cols = lax.broadcasted_iota(jnp.int32, (3 * width, width * LANE), 1)
    entry = cols >> 7
    hit = (rows == entry) | (rows == entry + width) | (rows == entry + 2 * width)
    bc_s[...] = nn(lhs, jnp.where(hit, 1.0, 0.0).astype(BF16))


def prepare(sib, oth, keep, gain, w_in, conv_w, conv_b, w_x, w_dt, dt_bias, a_log, xb, gy):
    rows, inner = xb.shape
    state, width = a_log.shape[0], w_x.shape[0]
    big = pltpu.VMEM((rows, inner), F32)
    edge = pltpu.VMEM((2, state, CH, inner), F32)
    return pl.pallas_call(
        prepare_kernel,
        out_shape=(
            big, big, big, big,
            pltpu.VMEM((3 * rows, LANE), F32),
            pltpu.VMEM((rows, width), F32),
            pltpu.VMEM((2 * CH, inner), F32),
            edge, edge,
            pltpu.VMEM((4 * state + 8, inner), F32),
            big, big,
            pltpu.VMEM((rows, 2 * state * LANE), F32),
            pltpu.VMEM((state, CH, inner), F32),
            pltpu.VMEM((2, rows // 2 // CH, state, CH, inner), F32),
        ),
        scratch_shapes=[pltpu.VMEM((4 * state, CH, inner), F32)],
        compiler_params=params(8),
        name="prepare",
    )(sib, oth, keep, gain, w_in, conv_w, conv_b, w_x, w_dt, dt_bias, a_log, xb, gy)


def summary_parts(ref_value, state):
    return [ref_value[i * state : (i + 1) * state] for i in range(4)]


def pair_kernel(a2_s, mine, theirs, out):
    state, half = a2_s.shape[0], out.shape[1]
    core = lax.axis_index("seq") & 1
    cols = pl.ds(pl.multiple_of(core * half, half), half)
    a2 = half_a2(a2_s, half)
    me, it = mine[:, cols], theirs[:, cols]
    low, high = jnp.where(core == 1, it, me), jnp.where(core == 1, me, it)
    put_total(out, joined(low, high, a2, state), state)


def joined(low, high, a2, state):
    low_f, low_r = low[4 * state : 4 * state + 1], low[4 * state + 1 : 4 * state + 2]
    high_f, high_r = high[4 * state : 4 * state + 1], high[4 * state + 1 : 4 * state + 2]
    lows, highs = summary_parts(low, state), summary_parts(high, state)
    return [
        lows[0] * jnp.exp2(high_f * a2) + highs[0],
        lows[1] * jnp.exp2(high_r * a2) + highs[1],
        highs[2] * jnp.exp2(low_r * a2) + lows[2],
        highs[3] * jnp.exp2(low_f * a2) + lows[3],
        low_f + high_f,
        low_r + high_r,
    ]


def put_total(out, parts, state):
    for i in range(4):
        out[i * state : (i + 1) * state] = parts[i]
    rest = jnp.zeros((out.shape[0] - 4 * state - 2, out.shape[1]), F32)
    out[4 * state :] = jnp.concatenate([parts[4], parts[5], rest], axis=0)


def half_a2(a2_s, half):
    core = lax.axis_index("seq") & 1
    cols = pl.ds(pl.multiple_of(core * half, half), half)
    return jnp.concatenate([a2_s[n, 0:1, cols] for n in range(a2_s.shape[0])], axis=0)


def stage_kernel(first, halves, a2_s, *refs):
    outs = 1 + len(halves) if halves else 2
    members, out, held = refs[: -outs - 1], refs[-outs - 1 : -1], refs[-1]
    count = len(members)
    state, half = a2_s.shape[0], out[0].shape[1]
    a2 = half_a2(a2_s, half)
    at = (lax.axis_index("seq") >> first) & (count - 1)
    for i, ref in enumerate(members):
        held[at ^ i] = ref[...]
    zero, none = jnp.zeros((state, half), F32), jnp.zeros((1, half), F32)

    def run_through(order, rows, reach):
        run = [zero, zero, none, none]
        seen = list(run)
        for i in order:
            seen = [jnp.where(at == i, now, old) for now, old in zip(run, seen)]
            df, dr = held[i, 4 * state : 4 * state + 1], held[i, 4 * state + 1 : 4 * state + 2]
            decays = [jnp.exp2((df, dr)[w] * a2) for w in reach]
            run = [run[k] * decays[k] + held[i, rows[k] * state : (rows[k] + 1) * state] for k in range(2)] + [
                run[2] + df,
                run[3] + dr,
            ]
        return run, seen

    right, seen = run_through(range(count), (0, 1), (0, 1))
    left, seen_left = run_through(range(count - 1, -1, -1), (2, 3), (1, 0))
    enter = out[0]
    enter[:state], enter[state : 2 * state] = seen[0], seen[1]
    enter[2 * state : 3 * state], enter[3 * state : 4 * state] = seen_left[0], seen_left[1]
    blank = jnp.zeros((CH, half), F32)
    enter[4 * state :] = jnp.concatenate([seen[2], seen[3], seen_left[2], seen_left[3], blank[:4]], axis=0)
    sums = jnp.concatenate([right[2], right[3], blank[:6]], axis=0)
    if halves:
        me = lax.axis_index("seq")
        for ref, apart in zip(out[1:], halves):
            later = (me ^ apart) > me
            ref[:state] = jnp.where(later, right[0], left[0])
            ref[state : 2 * state] = jnp.where(later, right[1], left[1])
            ref[2 * state :] = sums
    else:
        for i, value in enumerate((right[0], right[1], left[0], left[1])):
            out[1][i * state : (i + 1) * state] = value
        out[1][4 * state :] = sums


def last_kernel(first, a2_s, *refs):
    theirs, out, held = refs[:-2], refs[-2], refs[-1]
    count = len(theirs) + 1
    state, half = a2_s.shape[0], out.shape[1]
    a2 = half_a2(a2_s, half)
    at = (lax.axis_index("seq") >> first) & (count - 1)
    held[at] = jnp.zeros(held.shape[1:], F32)
    for i, ref in enumerate(theirs):
        held[at ^ (i + 1)] = ref[...]

    def run_through(order, reach, inside):
        run = [jnp.zeros((state, half), F32)] * 2
        for i in order:
            sums = held[i, 2 * state : 2 * state + 1], held[i, 2 * state + 1 : 2 * state + 2]
            for k in range(2):
                longer = run[k] * jnp.exp2(sums[reach[k]] * a2) + held[i, k * state : (k + 1) * state]
                run[k] = jnp.where(inside(i), longer, run[k])
        return run

    found = run_through(range(count - 1), (0, 1), lambda i: i < at)
    found = found + run_through(range(count - 1, 0, -1), (1, 0), lambda i: i > at)
    for i in range(4):
        out[i * state : (i + 1) * state] = found[i]


def pair(a2_s, mine, theirs):
    rows, inner = mine.shape
    return pl.pallas_call(
        pair_kernel,
        out_shape=jax.ShapeDtypeStruct((rows, inner // 2), F32),
        compiler_params=params(2),
        name="pair",
    )(a2_s, mine, theirs)


def stage(first, halves, a2_s, members):
    shape = jax.ShapeDtypeStruct(members[0].shape, F32)
    part = jax.ShapeDtypeStruct((2 * a2_s.shape[0] + CH, members[0].shape[1]), F32)
    return pl.pallas_call(
        lambda *refs: stage_kernel(first, halves, *refs),
        out_shape=(shape,) + (part,) * len(halves) if halves else (shape, shape),
        scratch_shapes=[pltpu.VMEM((len(members),) + members[0].shape, F32)],
        compiler_params=params(4),
        name="stage",
    )(a2_s, *members)


def last_stage(first, a2_s, theirs):
    return pl.pallas_call(
        lambda *refs: last_kernel(first, *refs),
        out_shape=jax.ShapeDtypeStruct((4 * a2_s.shape[0], theirs[0].shape[1]), F32),
        scratch_shapes=[pltpu.VMEM((len(theirs) + 1,) + theirs[0].shape, F32)],
        compiler_params=params(4),
        name="stage",
    )(a2_s, *theirs)


def enter_kernel(a2_s, *refs):
    stages, out = refs[:-1], refs[-1]
    state, half = a2_s.shape[0], out.shape[1]
    a2 = half_a2(a2_s, half)
    value = [stages[-1][i * state : (i + 1) * state] for i in range(4)]
    for ref in reversed(stages[:-1]):
        reach = [ref[4 * state + i : 4 * state + i + 1] for i in range(4)]
        value = [
            ref[i * state : (i + 1) * state] + value[i] * jnp.exp2(reach[w] * a2)
            for i, w in ((0, 0), (1, 1), (2, 3), (3, 2))
        ]
    for i in range(4):
        out[i * state : (i + 1) * state] = value[i]


def enter(a2_s, stages):
    half = stages[0].shape[1]
    return pl.pallas_call(
        enter_kernel,
        out_shape=jax.ShapeDtypeStruct((4 * a2_s.shape[0], half), F32),
        compiler_params=params(2),
        name="enter",
    )(a2_s, *stages)


def carry_in(car_s, a2_s, mine_half, other_half, sibling):
    state, inner = a2_s.shape[0], a2_s.shape[2]
    half = inner // 2
    odd = (lax.axis_index("seq") & 1) == 1
    a2 = jnp.concatenate([a2_s[n, 0:1, :] for n in range(state)], axis=0)
    left, right = jnp.where(odd, other_half[...], mine_half[...]), jnp.where(odd, mine_half[...], other_half[...])
    into = jnp.concatenate([left, right], axis=1)
    df, dr = sibling[4 * state : 4 * state + 1], sibling[4 * state + 1 : 4 * state + 2]
    for i, reach, through in ((0, df, odd), (1, dr, odd), (2, dr, ~odd), (3, df, ~odd)):
        rows = slice(i * state, (i + 1) * state)
        value = jnp.where(through, into[rows] * jnp.exp2(reach * a2) + sibling[rows], into[rows])
        for n in range(state):
            car_s[i * state + n] = jnp.broadcast_to(value[n : n + 1], (CH, inner))


def forward_kernel(
    mine_half, other_half, sibling, sx, de_s, dx_s, bc_s, a2_s, decay,
    y_s, h_s, car_o,
    before_s,
):
    rows2, inner = de_s.shape
    length = rows2 // 2
    steps = length // CH
    tiles = inner // LANE
    state = a2_s.shape[0]
    carry_in(car_o, a2_s, mine_half, other_half, sibling)
    y_s[...] = jnp.zeros(y_s.shape, F32)
    group = 4
    cols_of = [slice(t * LANE, (t + 1) * LANE) for t in range(tiles)]
    for dirn in range(2):
        order = list(range(steps)) if dirn == 0 else list(range(steps - 1, -1, -1))
        base = dirn * length
        s_row = 0 if dirn == 0 else 2
        for cols in cols_of:
            total = jnp.zeros((CH, LANE), F32)
            for j in range(steps):
                total = total + de_s[base + j * CH : base + (j + 1) * CH, cols]
            before_s[:, cols] = outside_sum(total, dirn == 0)

        def some(g, carry, dirn=dirn, order=order, base=base, s_row=s_row):
            n0 = g * group
            at_b, at_c = lanes_of(n0, group), lanes_of(state + n0, group)
            h = {}
            for n in range(group):
                for t, cols in enumerate(cols_of):
                    into = jnp.exp2(before_s[:, cols] * a2_s[n0 + n, :, cols]) * car_o[s_row * state + n0 + n, :, cols]
                    h[n, t] = sx[dirn, n0 + n, :, cols] + into
                    h_s[dirn, 0, n0 + n, :, cols] = h[n, t]
            for at, j in enumerate(order):
                rows = slice(base + j * CH, base + (j + 1) * CH)
                dx = [dx_s[rows, c] for c in cols_of]
                y = [None] * tiles
                for n in range(group):
                    b_n, c_n = bc_s[rows, at_b[n]], bc_s[rows, at_c[n]]
                    for t, cols in enumerate(cols_of):
                        h[n, t] = decay[dirn, at, n0 + n, :, cols] * h[n, t] + dx[t] * b_n
                        h_s[dirn, at + 1, n0 + n, :, cols] = h[n, t]
                        term = h[n, t] * c_n
                        y[t] = term if n == 0 else y[t] + term
                for t, cols in enumerate(cols_of):
                    y_s[rows, cols] += y[t]
            return carry

        lax.fori_loop(0, state // group, some, 0)


def forward(mine_half, other_half, sibling, sx, de, dx, bc, a2, decay):
    rows2, inner = de.shape
    state = a2.shape[0]
    steps = rows2 // 2 // CH
    return pl.pallas_call(
        forward_kernel,
        out_shape=(
            jax.ShapeDtypeStruct((rows2, inner), F32),
            jax.ShapeDtypeStruct((2, steps + 1, state, CH, inner), F32),
            jax.ShapeDtypeStruct((4 * state, CH, inner), F32),
        ),
        scratch_shapes=[pltpu.VMEM((CH, inner), F32)],
        compiler_params=params(4),
        name="forward",
    )(mine_half, other_half, sibling, sx, de, dx, bc, a2, decay)


def ready_kernel(
    rank, tok, gout, gain, w_in, w_out, d_skip, z, go, conv, xc, gy,
    x_o, g_o, nth_o, ntl_o, gh_o, gl_o, wih_o, wil_o, wfh_o, wfl_o, woh_o, wol_o, vfh_o, vfl_o,
    gate_o, zgrad_o, cgrad_o, xch_o, xcl_o, skip_o, pickb_o, pickc_o,
):
    feat, inner = gain.shape[1], w_out.shape[0]
    x = ordered(tok)
    x_o[...] = x
    g = ordered(gout)
    g_o[...] = g
    high, low = both_orders(normalize(x, gain[...])[1])
    nth_o[...] = high.astype(F32).T.astype(BF16)
    ntl_o[...] = low.astype(F32).T.astype(BF16)
    gh_o[...], gl_o[...] = both_orders(g)
    flip = flip_matrix(feat)
    high, low = split(w_in[...])
    wih_o[...], wil_o[...] = high, low
    wfh_o[...], wfl_o[...] = nn(flip, high).astype(BF16), nn(flip, low).astype(BF16)
    high, low = split(w_out[...])
    woh_o[...], wol_o[...] = high, low
    vfh_o[...], vfl_o[...] = nn(high, flip).astype(BF16), nn(low, flip).astype(BF16)
    xch_o[...], xcl_o[...] = split(xc[...])
    for lt in range(inner // LANE):
        cols = slice(lt * LANE, (lt + 1) * LANE)
        zt, v = z[:, cols], conv[:, cols]
        s = sigmoid(zt)
        gate_o[:, cols] = zt * s
        zgrad_o[:, cols] = go[:, cols] * (s * (1.0 + zt * (1.0 - s)))
        s = sigmoid(v)
        cgrad_o[:, cols] = s * (1.0 + v * (1.0 - s))
        skip_o[:, cols] = jnp.sum(gy[:, cols] * xc[:, cols], axis=0, keepdims=True)
    row = lax.broadcasted_iota(jnp.int32, pickb_o.shape, 0) >> 7
    col = lax.broadcasted_iota(jnp.int32, pickb_o.shape, 1)
    pickb_o[...] = jnp.where(col == row + rank, 1.0, 0.0).astype(BF16)
    pickc_o[...] = jnp.where(col == row + (rank + pickb_o.shape[0] // LANE), 1.0, 0.0).astype(BF16)


def ready(rank, state, tok, gout, gain, w_in, w_out, d_skip, z, go, conv, xc, gy):
    length, feat = tok.shape
    rows2, inner = z.shape
    f32 = lambda *dims: jax.ShapeDtypeStruct(dims, F32)
    b16 = lambda *dims: jax.ShapeDtypeStruct(dims, BF16)
    both = lambda *dims: (b16(*dims), b16(*dims))
    return pl.pallas_call(
        lambda *refs: ready_kernel(rank, *refs),
        out_shape=(f32(length, feat), f32(length, feat))
        + both(feat, rows2) + both(rows2, feat) + both(feat, 2 * inner) + both(feat, 2 * inner)
        + both(inner, feat) + both(inner, feat)
        + (f32(rows2, inner), f32(rows2, inner), f32(rows2, inner))
        + both(rows2, inner) + (f32(1, inner),) + both(state * LANE, LANE),
        compiler_params=params(8),
        name="ready",
    )(tok, gout, gain, w_in, w_out, d_skip, z, go, conv, xc, gy)


def early_kernel(
    rs_bits, x, nth, ntl, gh, gl, woh, wol, vfh, vfl, gate, zgrad, d_skip, xc, y_s,
    mixed_o, gzh_o, gzl_o, pieces_o,
):
    rows2, inner = xc.shape
    length = rows2 // 2
    y = y_s[...] + d_skip[...] * xc[...]
    gz = split(zgrad[...] * y)
    gzh_o[...], gzl_o[...] = gz
    out = split(y * gate[...])
    gw_out = mm(tn, out, (gh[...], gl[...]))
    gw_in = mm(nn, (nth[...], ntl[...]), gz)
    put_pieces(rs_bits, pieces_o, [(gw_in, None), (gw_out, None)])
    fwd = mm(nn, (out[0][:length], out[1][:length]), (woh[...], wol[...]))
    rev = mm(nn, (out[0][length:], out[1][length:]), (vfh[...], vfl[...]))
    store_ordered(mixed_o, x[...] + (fwd + rev))


def early(rs_bits, x, nth, ntl, gh, gl, woh, wol, vfh, vfl, gate, zgrad, d_skip, xc, y):
    length, feat = x.shape
    rows2, inner = xc.shape
    pieces = 1 << rs_bits
    tall = 2 * feat * inner // LANE // pieces
    gz = jax.ShapeDtypeStruct((rows2, inner), BF16)
    return pl.pallas_call(
        lambda *refs: early_kernel(rs_bits, *refs),
        out_shape=(jax.ShapeDtypeStruct((length, feat), F32), gz, gz, jax.ShapeDtypeStruct((pieces, tall, LANE), F32)),
        compiler_params=params(8),
        name="early",
    )(x, nth, ntl, gh, gl, woh, wol, vfh, vfl, gate, zgrad, d_skip, xc, y)


def put_pieces(rs_bits, pieces_o, arrays, few=None):
    pieces = 1 << rs_bits
    mine = reverse_bits(lax.axis_index("seq"), rs_bits)
    for p in range(pieces):
        slot = mine ^ reverse_bits(p, rs_bits)
        at = 0
        for value, more in arrays:
            tall = value.shape[0] // pieces
            for lt in range(value.shape[1] // LANE):
                where = (slice(p * tall, (p + 1) * tall), slice(lt * LANE, (lt + 1) * LANE))
                block = value[where] if more is None else value[where] + more[where]
                pieces_o[slot, at : at + tall, :] = block
                at += tall
        if few is not None:
            tiles = few.shape[1] // LANE
            top = pieces // tiles * CH
            rest = (few.shape[0] - top) * tiles // pieces
            rb, lt = p // tiles, p % tiles
            pieces_o[slot, at : at + CH, :] = few[rb * CH : (rb + 1) * CH, lt * LANE : (lt + 1) * LANE]
            rows = []
            for v in range(rest * p, rest * (p + 1)):
                rb, lt = top + v // tiles, v % tiles
                rows.append(few[rb : rb + 1, lt * LANE : (lt + 1) * LANE])
            zeros = jnp.zeros((4, LANE), F32)
            rows = [zeros] + rows + [zeros[: 4 - rest]]
            pieces_o[slot, at + CH : at + 2 * CH, :] = jnp.concatenate(rows, axis=0)
            pieces_o[slot, at + 2 * CH : at + 3 * CH, :] = jnp.zeros((CH, LANE), F32)


def row_vectors(rows):
    return jnp.concatenate(
        [rows[b : b + 1, lt * LANE : (lt + 1) * LANE] for b in range(3) for lt in range(rows.shape[1] // LANE)],
        axis=0,
    )


def backward_kernel(
    dirn, mx, car, h_s, de_s, dx_s, bc_s, a2_s, decay, gy,
    sb_s, sa_s, accb, accc, ga_s,
    after_s,
):
    rows2, inner = de_s.shape
    length = rows2 // 2
    steps = length // CH
    tiles = inner // LANE
    state = a2_s.shape[0]
    order = list(range(steps)) if dirn == 0 else list(range(steps - 1, -1, -1))
    base = dirn * length
    m_row = 3 if dirn == 0 else 1
    group = 2
    cols_of = [slice(t * LANE, (t + 1) * LANE) for t in range(tiles)]
    sb_s[...] = jnp.zeros(sb_s.shape, F32)
    sa_s[...] = jnp.zeros(sa_s.shape, F32)
    for cols in cols_of:
        total = jnp.zeros((CH, LANE), F32)
        for j in range(steps):
            total = total + de_s[base + j * CH : base + (j + 1) * CH, cols]
        after_s[:, cols] = outside_sum(total, dirn != 0)

    def some(g, carry):
        n0 = g * group
        at_b, at_c = lanes_of(n0, group), lanes_of(state + n0, group)
        a2, q, ga = {}, {}, {}
        for n in range(group):
            for t, cols in enumerate(cols_of):
                a2[n, t] = a2_s[n0 + n, :, cols]
                into = jnp.exp2(after_s[:, cols] * a2[n, t]) * car[m_row * state + n0 + n, :, cols]
                q[n, t] = mx[dirn, n0 + n, :, cols] + into
                ga[n, t] = jnp.zeros((CH, LANE), F32)
        for at in range(steps - 1, -1, -1):
            j = order[at]
            rows = slice(base + j * CH, base + (j + 1) * CH)
            here = slice(j * CH, (j + 1) * CH)
            de = [de_s[rows, c] for c in cols_of]
            dx = [dx_s[rows, c] for c in cols_of]
            gyj = [gy[rows, c] for c in cols_of]
            sb, sa = [None] * tiles, [None] * tiles
            for n in range(group):
                b_n, c_n = bc_s[rows, at_b[n]], bc_s[rows, at_c[n]]
                to_b = to_c = None
                for t, cols in enumerate(cols_of):
                    gh = gyj[t] * c_n + q[n, t]
                    term_c = gyj[t] * h_s[dirn, at + 1, n0 + n, :, cols]
                    term_b = gh * dx[t]
                    to_b = term_b if t == 0 else to_b + term_b
                    to_c = term_c if t == 0 else to_c + term_c
                    q[n, t] = decay[dirn, at, n0 + n, :, cols] * gh
                    r = q[n, t] * h_s[dirn, at, n0 + n, :, cols]
                    ga[n, t] = ga[n, t] + de[t] * r
                    sb[t] = gh * b_n if n == 0 else sb[t] + gh * b_n
                    sa[t] = a2[n, t] * r if n == 0 else sa[t] + a2[n, t] * r
                accb[here, at_b[n]] = to_b
                accc[here, at_b[n]] = to_c
            for t, cols in enumerate(cols_of):
                sb_s[here, cols] += sb[t]
                sa_s[here, cols] += sa[t]
        for n in range(group):
            for t, cols in enumerate(cols_of):
                ga_s[n0 + n, :, cols] = ga[n, t]
        return carry

    lax.fori_loop(0, state // group, some, 0)


def backward(dirn, mx, car, h, de, dx, bc, a2, decay, gy):
    rows2, inner = de.shape
    state = a2.shape[0]
    length = rows2 // 2
    half = jax.ShapeDtypeStruct((length, inner), F32)
    acc = jax.ShapeDtypeStruct((length, state * LANE), F32)
    return pl.pallas_call(
        lambda *refs: backward_kernel(dirn, *refs),
        out_shape=(half, half, acc, acc, jax.ShapeDtypeStruct((state, CH, inner), F32)),
        scratch_shapes=[pltpu.VMEM((CH, inner), F32)],
        compiler_params=params(4),
        name="backward",
    )(mx, car, h, de, dx, bc, a2, decay, gy)


def inner_kernel(
    pad, conv_w, w_x, w_dt, d_skip, a2_s,
    xb, gy, xc, dt, sig, cgrad, mask, dbl, xbh, xch, xcl, skip_sum, pick_b, pick_c,
    sb_f, sa_f, accb_f, accc_f, ga_f, sb_r, sa_r, accb_r, accc_r, ga_r,
    gxh_o, gxl_o, halo_o, few_o,
    gp_s, gpre_s, xcg_s,
):
    inner, rank = w_x.shape[1], w_dt.shape[0]
    state = a2_s.shape[0]
    rows2 = xb.shape[0]
    length = rows2 // 2
    steps = length // CH
    tiles = inner // LANE
    sub = sub_iota()

    bias_rows = []
    for lt in range(tiles):
        cols = slice(lt * LANE, (lt + 1) * LANE)
        bias = jnp.zeros((1, LANE), F32)
        for dirn, sb, sa in ((0, sb_f, sa_f), (1, sb_r, sa_r)):
            rows = slice(dirn * length, (dirn + 1) * length)
            g_pre = (xc[rows, cols] * sb[:, cols] + LN2 * sa[:, cols]) * sig[rows, cols]
            gpre_s[rows, cols] = g_pre
            xcg_s[rows, cols] = d_skip[:, cols] * gy[rows, cols] + dt[rows, cols] * sb[:, cols]
            bias = bias + jnp.sum(g_pre, axis=0, keepdims=True)
        bias_rows.append(bias)

    b_parts = split(jnp.concatenate([accb_f[...], accb_r[...]], axis=0))
    c_parts = split(jnp.concatenate([accc_f[...], accc_r[...]], axis=0))
    g_bc = (nn(b_parts[0], pick_b[...]) + nn(b_parts[1], pick_b[...])) + (
        nn(c_parts[0], pick_c[...]) + nn(c_parts[1], pick_c[...])
    )
    gpre_parts = split(gpre_s[...])
    w_dt_parts = split(w_dt[...])
    g_rank = mm(nt, gpre_parts, w_dt_parts)
    width = rank + 2 * state
    g_dbl = jnp.concatenate([g_rank, g_bc[:, rank:width]], axis=1)
    g_dbl_parts = split(g_dbl)
    few_o[width + state : width + state + rank, :] = mm(tn, split(dbl[:, :rank]), gpre_parts)
    few_o[:width, :] = mm(tn, g_dbl_parts, (xch[...], xcl[...]))
    xcg_s[...] += mm(nn, g_dbl_parts, split(w_x[...]))

    cw_rows = [[] for _ in range(4)]
    cb_rows = []
    halo_f, halo_r = [], []
    for lt in range(tiles):
        cols = slice(lt * LANE, (lt + 1) * LANE)
        taps = [conv_w[k : k + 1, cols] for k in range(4)]
        xbh_t = xbh[:, cols]
        xf = [xb[j * CH : (j + 1) * CH, cols] for j in range(steps)]
        xf = [
            jnp.where(sub == 0, xbh_t[b : b + 1], pltpu.roll(xf[steps - 3 + b], 1, 0))
            for b in range(3)
        ] + xf
        gcw = [jnp.zeros((CH, LANE), F32) for _ in range(4)]
        gcb = jnp.zeros((CH, LANE), F32)
        grads = [None] * (steps + 3)
        for j in range(steps):
            rows = slice(j * CH, (j + 1) * CH)
            u = xcg_s[rows, cols] * cgrad[rows, cols]
            gcb = gcb + u
            for k in range(4):
                uk = u if k == 0 else u * mask[(k - 1) * length + j * CH : (k - 1) * length + (j + 1) * CH, :]
                gcw[k] = gcw[k] + uk * xf[j + 3 - k]
                add = taps[k] * uk
                at = j + 3 - k
                grads[at] = add if grads[at] is None else grads[at] + add
        for b in range(3):
            halo_f.append(grads[b][0:1])
            at = steps + b
            grads[at] = grads[at] + jnp.where(sub == CH - 1, 0.0, pltpu.roll(grads[b], CH - 1, 0))
        for j in range(steps):
            gp_s[j * CH : (j + 1) * CH, cols] = grads[j + 3]
        xr = [xb[length + j * CH : length + (j + 1) * CH, cols] for j in range(steps)]
        xr = xr + [
            jnp.where(sub == CH - 1, xbh_t[8 + b : 9 + b], pltpu.roll(xr[b], CH - 1, 0))
            for b in range(3)
        ]
        grads = [None] * (steps + 3)
        for j in range(steps):
            rows = slice(length + j * CH, length + (j + 1) * CH)
            u = xcg_s[rows, cols] * cgrad[rows, cols]
            gcb = gcb + u
            for k in range(4):
                uk = u if k == 0 else u * mask[(k + 2) * length + j * CH : (k + 2) * length + (j + 1) * CH, :]
                gcw[k] = gcw[k] + uk * xr[j + k]
                add = taps[k] * uk
                grads[j + k] = add if grads[j + k] is None else grads[j + k] + add
        for b in range(3):
            halo_r.append(grads[steps + b][CH - 1 : CH])
            grads[b] = grads[b] + jnp.where(sub == 0, 0.0, pltpu.roll(grads[steps + b], 1, 0))
        for j in range(steps):
            gp_s[length + j * CH : length + (j + 1) * CH, cols] = grads[j]
        for k in range(4):
            cw_rows[k].append(jnp.sum(gcw[k], axis=0, keepdims=True))
        cb_rows.append(jnp.sum(gcb, axis=0, keepdims=True))
    pad_col = spread(pad[...].astype(F32))
    pad_all = jnp.concatenate([pad_col, pad_col], axis=0)
    for lt in range(tiles):
        cols = slice(lt * LANE, (lt + 1) * LANE)
        gxh_o[:, cols], gxl_o[:, cols] = split(gp_s[:, cols] * pad_all)

    blank = jnp.zeros((5, inner), F32)

    def gather(found):
        return jnp.concatenate(
            [jnp.concatenate([found[lt * 3 + b] for lt in range(tiles)], axis=1) for b in range(3)]
            + [blank],
            axis=0,
        )

    halo_o[...] = jnp.concatenate([gather(halo_f), gather(halo_r)], axis=0)
    ga = jnp.concatenate(
        [jnp.sum(ga_f[n] + ga_r[n], axis=0, keepdims=True) * (a2_s[n, 0:1, :] * LN2) for n in range(state)], axis=0
    )
    few_o[width : width + state, :] = ga
    few_o[width + state + rank :, :] = jnp.concatenate(
        [jnp.concatenate(cw_rows[k], axis=1) for k in range(4)]
        + [
            jnp.concatenate(cb_rows, axis=1),
            jnp.concatenate(bias_rows, axis=1),
            skip_sum[...],
            jnp.zeros((1, inner), F32),
        ],
        axis=0,
    )


def inner_back(*arrays):
    w_x, w_dt, a2, xb = arrays[2], arrays[3], arrays[5], arrays[6]
    rows2, inner = xb.shape
    few = w_x.shape[0] + a2.shape[0] + w_dt.shape[0] + CH
    big = pltpu.VMEM((rows2, inner), F32)
    part = jax.ShapeDtypeStruct((rows2, inner), BF16)
    return pl.pallas_call(
        inner_kernel,
        out_shape=(
            part, part,
            jax.ShapeDtypeStruct((2 * CH, inner), F32),
            jax.ShapeDtypeStruct((few, inner), F32),
        ),
        scratch_shapes=[big, big, big],
        compiler_params=params(8),
        name="inner",
    )(*arrays)


def tail_kernel(
    rs_bits, sib, oth, gain, x_s, g_s, nth, ntl, wih, wil, wfh, wfl, gzh, gzl, gxh, gxl, halo, few,
    gtok_o, to_left_o, to_right_o, pieces_o,
):
    feat = gain.shape[1]
    rows2, inner = gxh.shape
    length = rows2 // 2
    left, right = pick_sides(sib[...], oth[...])
    factor_l, hn_l = normalize(left, gain[...])
    factor_r, hn_r = normalize(right, gain[...])
    flip = flip_matrix(feat)
    lh, ll = split(hn_l)
    rh, rl = split(hn_r)
    edge = (
        jnp.concatenate([lh, nn(rh, flip).astype(BF16)], axis=0),
        jnp.concatenate([ll, nn(rl, flip).astype(BF16)], axis=0),
    )
    x, g = x_s[...], g_s[...]
    factor = normalize(x, gain[...])[0]
    gh_parts = split(halo[...])
    gw_in = mm(nn, (nth[...], ntl[...]), (gxh[...], gxl[...]))
    gw_in_halo = mm(tn, edge, gh_parts)
    w_xb = (wih[:, :inner], wil[:, :inner])
    g_normed = (
        mm(nt, (gxh[:length], gxl[:length]), w_xb)
        + mm(nt, (gzh[:length], gzl[:length]), (wih[:, inner:], wil[:, inner:]))
    ) + (
        mm(nt, (gxh[length:], gxl[length:]), (wfh[:, :inner], wfl[:, :inner]))
        + mm(nt, (gzh[length:], gzl[length:]), (wfh[:, inner:], wfl[:, inner:]))
    )
    back_h = mm(nt, gh_parts, w_xb)
    gn_l = back_h[:CH]
    gn_r = flipped(back_h[CH:])

    def norm_back(x, factor, gn):
        scaled = gn * gain[...]
        return factor * scaled - x * (factor * factor * factor * jnp.mean(scaled * x, axis=1, keepdims=True))

    store_ordered(gtok_o, g + norm_back(x, factor, g_normed))
    to_left = norm_back(left, factor_l, gn_l)
    to_right = norm_back(right, factor_r, gn_r)
    to_left_o[...] = to_left
    to_right_o[...] = to_right
    three = lax.broadcasted_iota(jnp.int32, (CH, feat), 0) < 3
    g_gain = (
        jnp.sum(g_normed * (x * factor), axis=0, keepdims=True)
        + jnp.sum(jnp.where(three, gn_l * (left * factor_l) + gn_r * (right * factor_r), 0.0), axis=0, keepdims=True)
    )
    few_all = jnp.concatenate(
        [few[: few.shape[0] - CH, :], few[few.shape[0] - CH : few.shape[0] - 1, :]]
        + [jnp.concatenate([g_gain, jnp.zeros((1, inner - feat), F32)], axis=1)],
        axis=0,
    )
    put_pieces(rs_bits, pieces_o, [(gw_in, gw_in_halo)], few_all)
    pieces = 1 << rs_bits
    me = lax.axis_index("seq") & (pieces - 1)
    mine = reverse_bits(me, rs_bits)
    at = pieces_o.shape[1] - 2 * CH

    @pl.when(me < pieces - 1)
    def _():
        slot = mine ^ reverse_bits(me + 1, rs_bits)
        vectors = row_vectors(to_right)
        pieces_o[slot, at : at + 4, :] = vectors[:4]
        pieces_o[slot, at + CH : at + CH + 2, :] = vectors[4:]

    @pl.when(me > 0)
    def _():
        slot = mine ^ reverse_bits(me - 1, rs_bits)
        pieces_o[slot, at + CH + 2 : at + 2 * CH, :] = row_vectors(to_left)


def reverse_bits(value, bits):
    found = 0
    for i in range(bits):
        found = found | (((value >> i) & 1) << (bits - 1 - i))
    return found


def tail(rs_bits, *arrays):
    x, gxh = arrays[3], arrays[13]
    length, feat = x.shape
    inner = gxh.shape[1]
    pieces = 1 << rs_bits
    tall = feat * inner // LANE // pieces + 3 * CH
    return pl.pallas_call(
        lambda *refs: tail_kernel(rs_bits, *refs),
        out_shape=(
            jax.ShapeDtypeStruct((length, feat), F32),
            jax.ShapeDtypeStruct((CH, feat), F32),
            jax.ShapeDtypeStruct((CH, feat), F32),
            jax.ShapeDtypeStruct((pieces, tall, LANE), F32),
        ),
        compiler_params=params(8),
        name="tail",
    )(*arrays)


def unpack_kernel(
    rs_bits, near, far, gtok, halo, pad,
    gtok_o, gain_o, w_in_o, conv_w_o, conv_b_o, w_x_o, w_dt_o, dt_bias_o, a_log_o, d_skip_o, w_out_o, few_s, rest_s,
):
    feat = w_in_o.shape[0]
    inner = w_out_o.shape[0]
    tiles = inner // LANE
    pieces = 1 << rs_bits
    mine = reverse_bits(lax.axis_index("seq"), rs_bits)
    in_rows, out_rows = feat // pieces, inner // pieces
    for slot in range(pieces):
        source = near if slot < pieces // 2 else far
        i = slot % (pieces // 2)
        p = reverse_bits(mine ^ slot, rs_bits)
        at = 0
        in_at = pl.ds(pl.multiple_of(p * in_rows, in_rows), in_rows)
        out_at = pl.ds(pl.multiple_of(p * out_rows, out_rows), out_rows)
        for lt in range(tiles):
            w_in_o[in_at, inner + lt * LANE : inner + (lt + 1) * LANE] = source[i, at : at + in_rows, :]
            at += in_rows
        for lt in range(feat // LANE):
            w_out_o[out_at, lt * LANE : (lt + 1) * LANE] = source[i, at : at + out_rows, :]
            at += out_rows
        for lt in range(tiles):
            w_in_o[in_at, lt * LANE : (lt + 1) * LANE] = source[i, at : at + in_rows, :]
            at += in_rows
        few_s[p] = source[i, at : at + CH, :]
        rest_s[p] = source[i, at + CH : at + 2 * CH, :]

    top = pieces // tiles * CH
    total = w_x_o.shape[0] + a_log_o.shape[0] + w_dt_o.shape[0] + CH
    rest = (total - top) * tiles // pieces

    def few_rows(first, count):
        found = []
        for lt in range(tiles):
            if first < top:
                found.append(few_s[first // CH * tiles + lt])
                continue
            rows = []
            for row in range(first, first + count):
                v = (row - top) * tiles + lt
                rows.append(rest_s[v // rest, 4 + v % rest : 5 + v % rest, :])
            found.append(jnp.concatenate(rows, axis=0) if count > 1 else rows[0])
        return jnp.concatenate(found, axis=1)

    width, state = w_x_o.shape[0], a_log_o.shape[0]
    rank = w_dt_o.shape[0]
    w_x_o[...] = jnp.concatenate([few_rows(r, CH) for r in range(0, width, CH)], axis=0)
    at = width
    a_log_o[...] = jnp.concatenate([few_rows(r, CH) for r in range(at, at + state, CH)], axis=0)
    at += state
    w_dt_o[...] = jnp.concatenate([few_rows(r, CH) for r in range(at, at + rank, CH)], axis=0)
    at += rank
    conv_w_o[...] = few_rows(at, 4)
    conv_b_o[...] = few_rows(at + 4, 1)
    dt_bias_o[...] = few_rows(at + 5, 1)
    d_skip_o[...] = few_rows(at + 6, 1)
    gain_o[...] = few_rows(at + 7, 1)[:, :feat]

    length = gtok.shape[0]
    per = feat // LANE
    padded = spread_plain(pad[...].astype(F32), feat)

    def three(first):
        rows = [
            jnp.concatenate([halo[first + b * per + lt : first + b * per + lt + 1, :] for lt in range(per)], axis=1)
            for b in range(3)
        ]
        return rows, jnp.zeros((CH - 3, feat), F32)

    rows, blank = three(0)
    first = jnp.concatenate(rows + [blank], axis=0)
    rows, blank = three(3 * per)
    last = jnp.concatenate([blank] + rows, axis=0)
    gtok_o[...] = gtok[...]
    gtok_o[:CH] = gtok[:CH] + padded[:CH] * first
    gtok_o[length - CH :] = gtok[length - CH :] + padded[length - CH :] * last


def spread_plain(row, width):
    length = row.shape[1]
    rows = lax.broadcasted_iota(jnp.int32, (length, length), 0)
    cols = lax.broadcasted_iota(jnp.int32, (length, length), 1)
    picked = (jnp.where(rows == cols, 1.0, 0.0) * row).astype(BF16)
    return nn(picked, jnp.ones((length, width), BF16))


def unpack(rs_bits, near, far, gtok, halo, pad, state, rank):
    length, feat = gtok.shape
    pieces = 1 << rs_bits
    inner = state[1]
    width = rank + 2 * state[0]
    shape = lambda *dims: jax.ShapeDtypeStruct(dims, F32)
    return pl.pallas_call(
        lambda *refs: unpack_kernel(rs_bits, *refs),
        out_shape=(
            shape(length, feat),
            shape(1, feat),
            shape(feat, 2 * inner),
            shape(4, inner),
            shape(1, inner),
            shape(width, inner),
            shape(rank, inner),
            shape(1, inner),
            shape(state[0], inner),
            shape(1, inner),
            shape(inner, feat),
        ),
        scratch_shapes=[pltpu.VMEM((pieces, CH, LANE), F32)] * 2,
        compiler_params=params(6),
        name="unpack",
    )(near, far, gtok, halo, pad)


def body(tokens, resets, pad_mask, norm_gain, w_in, conv_w, conv_b, w_x, w_dt, dt_bias, a_log, d_skip, w_out, grad_out):
    count = lax.axis_size("seq")
    bits = count.bit_length() - 1
    rs_bits = min(5, bits)
    length = tokens.shape[0]
    keep_row, pad_row = resets.reshape(1, length), pad_mask.reshape(1, length)

    def exchange(value, apart):
        return lax.ppermute(value, "seq", [(i, i ^ apart) for i in range(count)])

    def swap(value, bit):
        return exchange(value, 1 << bit)

    across = [(i, i + 1) for i in range(1, count - 1, 2)] + [(i + 1, i) for i in range(1, count - 1, 2)]

    def swap_across(value):
        return lax.ppermute(value, "seq", across)

    to_sib, to_oth = edges(tokens, keep_row, pad_row)
    oth = swap_across(to_oth)
    sib = swap(to_sib, 0)
    (xb, z, go, gy), kept = project(
        tokens, pad_row, norm_gain, w_in[0], grad_out, w_out[0],
        keep_row, conv_w[0], conv_b, w_x[0].T, w_dt[0], dt_bias, a_log[0].T, d_skip,
    )
    (tok, pad, gain, w_in_0, gout, w_out_0, keep, conv_w_0, conv_b_0, w_x_t, w_dt_0, dt_bias_0, a_log_t, skip) = kept
    xc, dt, sig, conv, mask, dbl, xbh, sx, mx, total, de, dx, bc, a2, decay = prepare(
        sib, oth, keep, gain, w_in_0, conv_w_0, conv_b_0, w_x_t, w_dt_0, dt_bias_0, a_log_t, xb, gy
    )

    sibling = swap(total, 0)
    group = pair(a2, total, sibling)
    group, gate_in = lax.optimization_barrier((group, (z, go, conv, xc, gy)))
    at_hand = ready(w_dt.shape[1], a_log.shape[2], tok, gout, gain, w_in_0, w_out_0, skip, *gate_in)
    stages = []
    steps = [range(first, min(first + 2, bits)) for first in range(1, bits, 2)]
    step = steps[-1]
    distances = [i << step[0] for i in range(1, 1 << len(step))]
    for first_step in steps[:-1]:
        members = [group] + [exchange(group, i << first_step[0]) for i in range(1, 1 << len(first_step))]
        halves = distances if first_step is steps[-2] else ()
        entering, *group = stage(first_step[0], halves, a2, members)
        stages.append(entering)
        if not halves:
            (group,) = group
    group, at_hand = lax.optimization_barrier((group, at_hand))
    theirs = [exchange(value, apart) for value, apart in zip(group, distances)]
    stages.append(last_stage(step[0], a2, theirs))
    mine_half = enter(a2, stages)
    other_half = swap(mine_half, 0)

    y, h, car = forward(mine_half, other_half, sibling, sx, de, dx, bc, a2, decay)
    def reduced(part, step):
        size = part.shape[0] >> len(step)
        total = part[:size]
        for i in range(1, 1 << len(step)):
            slot = reverse_bits(i, len(step))
            total = total + exchange(part[slot * size : (slot + 1) * size], i << step[0])
        return total

    (x, g, nth, ntl, gh, gl, wih, wil, wfh, wfl, woh, wol, vfh, vfl, gate, zgrad, cgrad, xch, xcl, skip_sum,
     pick_b, pick_c) = at_hand
    rs_steps = [range(0, 1)] + [range(first, min(first + 2, rs_bits)) for first in range(1, rs_bits, 2)]
    mixed, gzh, gzl, part_a = early(rs_bits, x, nth, ntl, gh, gl, woh, wol, vfh, vfl, gate, zgrad, skip, xc, y)
    part_a, h = lax.optimization_barrier((part_a, h))
    part_a = reduced(part_a, range(0, 1))
    back_f = backward(0, mx, car, h, de, dx, bc, a2, decay, gy)
    part_a, back_f, h = lax.optimization_barrier((part_a, back_f, h))
    part_a = reduced(part_a, rs_steps[1])
    back_r = backward(1, mx, car, h, de, dx, bc, a2, decay, gy)
    gxh, gxl, halo_g, few = inner_back(
        pad, conv_w_0, w_x_t, w_dt_0, skip, a2,
        xb, gy, xc, dt, sig, cgrad, mask, dbl, xbh, xch, xcl, skip_sum, pick_b, pick_c, *back_f, *back_r,
    )
    part_a, gxh = lax.optimization_barrier((part_a, gxh))
    gtok, to_left, to_right, part_b = tail(
        rs_bits, sib, oth, gain, x, g, nth, ntl, wih, wil, wfh, wfl, gzh, gzl, gxh, gxl, halo_g, few
    )
    part_b = reduced(part_b, rs_steps[0])
    part_b = reduced(part_b, rs_steps[1])
    own = jnp.concatenate([part_a, part_b], axis=1)
    for step in rs_steps[2:]:
        own = reduced(own, step)
    for bit in range(rs_bits, bits):
        own = own + swap(own, bit)
    tall = own.shape[1]
    halo = jnp.concatenate([own[0, tall - 16 : tall - 12], own[0, tall - 8 :]], axis=0)
    if bits > rs_bits:
        pairs = [(i, i + 1) for i in range(count - 1)]
        from_left = lax.ppermute(to_right, "seq", pairs)[:3]
        from_right = lax.ppermute(to_left, "seq", [(j, i) for i, j in pairs])[:3]
        halo = jnp.concatenate([from_left.reshape(-1, LANE), from_right.reshape(-1, LANE)], axis=0)
    own = own[:, : tall - 8]
    for step in reversed(rs_steps[1:]):
        parts = [own] + [exchange(own, reverse_bits(i, len(step)) << step[0]) for i in range(1, 1 << len(step))]
        own = jnp.concatenate(parts, axis=0)
    far = swap(own, 0)
    outs = unpack(rs_bits, own, far, gtok, halo, pad, a_log_t.shape, w_dt.shape[1])
    gtok, g_gain, g_w_in, g_conv_w, g_conv_b, g_w_x, g_w_dt, g_dt_bias, g_a_log, g_d_skip, g_w_out = outs
    return (
        mixed, gtok, g_gain, g_w_in[None], g_conv_w[None], g_conv_b, g_w_x.T[None], g_w_dt[None],
        g_dt_bias, g_a_log.T[None], g_d_skip, g_w_out[None],
    )


def solution(mesh):
    rows, whole = P("seq", None), P()
    return jax.shard_map(
        body,
        mesh=mesh,
        in_specs=(rows, P("seq"), P("seq")) + (whole,) * 10 + (rows,),
        out_specs=(rows, rows) + (whole,) * 10,
        check_vma=False,
    )
```

time: 162 us -> 99.6 us (0.61)
  the two profiles are of different devices: /device:TPU:8 before, /device:TPU:0 now
where the time goes in v2:
time: 99.6 us; the launch traced here: 99.4 us
  waiting for transfers between devices  35.5 us (36%)
  starting transfers between devices  33.1 us (33%)
  Pallas kernels  29.5 us (30%)
    ppermute x27, waiting for transfers between devices, exchange(): return lax.ppermute(value, 'seq', [(i, i ^ apart) for i in range(count)])  35.5 us
    ppermute x27, starting transfers between devices, exchange(): return lax.ppermute(value, 'seq', [(i, i ^ apart) for i in range(count)])  32.4 us
    pallas_call x1, Pallas kernels, prepare(): pl.pallas_call(prepare_kernel, out_shape=(big, big, big, big, pltpu.VMEM(...  5.94 us
    pallas_call x2, Pallas kernels, backward(): pl.pallas_call(lambda *refs: backward_kernel(dirn, *refs), out_shape=(hal...  5.9 us
    pallas_call x1, Pallas kernels, project(): pl.pallas_call(project_kernel, out_shape=(big, big, big, big) + tuple((ja...  3.25 us
    pallas_call x1, Pallas kernels, tail(): pl.pallas_call(lambda *refs: tail_kernel(rs_bits, *refs), out_shape=(jax....  2.91 us
    pallas_call x1, Pallas kernels, inner_back(): pl.pallas_call(inner_kernel, out_shape=(part, part, jax.ShapeDtypeStruct(...  2.76 us
    pallas_call x1, Pallas kernels, forward(): pl.pallas_call(forward_kernel, out_shape=(jax.ShapeDtypeStruct((rows2, in...  2.17 us
  transfers between devices with their start and end apart: 28, of which 18 were waited for; matrix products, arithmetic and copies ran while one was open for 0% of the time, Pallas kernels for 14%

profile of v2, /device:TPU:0, one launch (start us, length us, event | category | flops | bytes accessed | tf_op | source)
XLA Modules:
  0.0 99.4 jit_solution(4654454347627923937)
XLA Ops:
  0.6 0.8 edges.1
  1.9 0.6 collective-permute-start.1
  2.6 3.3 %project.1 = (f32[256,512]{1,0:T(8,128)S(1)}, f32[256,512]{1,0:T(8,128)S(1)}, f32[256,512]{1,0:T(8,128)S(1)}, f32[256,512]{1,0:T(8,128)S(1)}, f32[128,256]{1,0:T...) custom-call(f32[128,256]{1,0:T(8,128)} %tok.1, ...), custom_call_target="tpu_custom_call" | custom-call | tf_op jit(solution)/shard_map/project/pallas_call | solution.py:182
  5.8 5.9 %prepare.1 = (f32[256,512]{1,0:T(8,128)S(1)}, f32[256,512]{1,0:T(8,128)S(1)}, f32[256,512]{1,0:T(8,128)S(1)}, f32[256,512]{1,0:T(8,128)S(1)}, f32[768,128]{1,0:T...) custom-call(f32[8,256]{1,0:T(8,128)S(1)} %collective-permute-done.si, ...), custom_call_target="tpu_custom_call" | custom-call | tf_op jit(solution)/shard_map/prepare/pallas_call | solution.py:418
  11.8 3.9 %collective-permute-start.2 = (f32[72,512]{1,0:T(8,128)S(1)}, f32[72,512]{1,0:T(8,128)S(1)}, u32[]{:S(2)}, u32[]{:S(2)}) collective-permute-start(f32[72,512]{1,0:T(8,128)S(1)} %get-tuple-element.163.mine), channel_id=1, source_target_pairs={{0,1},{1,0},{2,3},{3,2},{4,5},{5,4},{6,7},{7,6},{8,9},{9,8},{10,11... | collective-permute-start | bytes 442376 | tf_op jit(solution)/shard_map/ppermute | solution.py:1263
  15.7 1.0 %collective-permute-done.2.theirs.sibling = f32[72,512]{1,0:T(8,128)S(1)} collective-permute-done((f32[72,512]{1,0:T(8,128)S(1)}, f32[72,512]{1,0:T(8,128)S(1)}, u32[]{:S(2)}, u32[]{:S(2)}) %collective-permute-start.2) | collective-permute-done | bytes 147488 | tf_op jit(solution)/shard_map/ppermute | solution.py:1263
  16.8 1.6 %collective-permute-start.3 = (f32[72,256]{1,0:T(8,128)S(1)}, f32[72,256]{1,0:T(8,128)S(1)}, u32[]{:S(2)}, u32[]{:S(2)}) collective-permute-start(f32[72,256]{1,0:T(8,128)S(1)} %pair.1.refs_1_), channel_id=1, source_target_pairs={{0,2},{1,3},{2,0},{3,1},{4,6},{5,7},{6,4},{7,5},{8,10},{9,11},{10,... | collective-permute-start | bytes 221192 | tf_op jit(solution)/shard_map/ppermute | solution.py:1263
  18.4 2.0 %collective-permute-start.4 = (f32[72,256]{1,0:T(8,128)S(1)}, f32[72,256]{1,0:T(8,128)S(1)}, u32[]{:S(2)}, u32[]{:S(2)}) collective-permute-start(f32[72,256]{1,0:T(8,128)S(1)} %pair.1.refs_1_), channel_id=1, source_target_pairs={{0,4},{1,5},{2,6},{3,7},{4,0},{5,1},{6,2},{7,3},{8,12},{9,13},{10,... | collective-permute-start | bytes 221192 | tf_op jit(solution)/shard_map/ppermute | solution.py:1263
  20.3 2.1 %ready.1 = (f32[128,256]{1,0:T(8,128)S(1)}, f32[128,256]{1,0:T(8,128)S(1)}, bf16[256,256]{1,0:T(8,128)(2,1)S(1)}, bf16[256,256]{1,0:T(8,128)(2,1)S(1)}, bf16[256...) custom-call(f32[128,256]{1,0:T(8,128)S(1)} %get-tuple-element.172.re, ...), custom_call_target="tpu_custom_call" | custom-call | tf_op jit(solution)/shard_map/ready/pallas_call | solution.py:732
  22.4 1.3 %collective-permute-done.4.refs_3_ = f32[72,256]{1,0:T(8,128)S(1)} collective-permute-done((f32[72,256]{1,0:T(8,128)S(1)}, f32[72,256]{1,0:T(8,128)S(1)}, u32[]{:S(2)}, u32[]{:S(2)}) %collective-permute-start.4) | collective-permute-done | bytes 73760 | tf_op jit(solution)/shard_map/ppermute | solution.py:1263
  23.8 1.8 %collective-permute-done.5.refs_4_ = f32[72,256]{1,0:T(8,128)S(1)} collective-permute-done((f32[72,256]{1,0:T(8,128)S(1)}, f32[72,256]{1,0:T(8,128)S(1)}, u32[]{:S(2)}, u32[]{:S(2)}) %collective-permute-start.5) | collective-permute-done | bytes 73760 | tf_op jit(solution)/shard_map/ppermute | solution.py:1263
  25.6 1.6 %collective-permute-start.6 = (f32[40,256]{1,0:T(8,128)S(1)}, f32[40,256]{1,0:T(8,128)S(1)}, u32[]{:S(2)}, u32[]{:S(2)}) collective-permute-start(f32[40,256]{1,0:T(8,128)S(1)} %get-tuple-element.215), channel_id=1, source_target_pairs={{0,8},{1,9},{2,10},{3,11},{4,12},{5,13},{6,14},{7,15},{8,0},{9,1},... | collective-permute-start | bytes 122888 | tf_op jit(solution)/shard_map/ppermute | solution.py:1263
  27.3 1.5 %collective-permute-start.7 = (f32[40,256]{1,0:T(8,128)S(1)}, f32[40,256]{1,0:T(8,128)S(1)}, u32[]{:S(2)}, u32[]{:S(2)}) collective-permute-start(f32[40,256]{1,0:T(8,128)S(1)} %get-tuple-element.216), channel_id=1, source_target_pairs={{0,16},{1,17},{2,18},{3,19},{4,20},{5,21},{6,22},{7,23},{8,24},{9,... | collective-permute-start | bytes 122888 | tf_op jit(solution)/shard_map/ppermute | solution.py:1263
  28.8 1.3 %collective-permute-start.8 = (f32[40,256]{1,0:T(8,128)S(1)}, f32[40,256]{1,0:T(8,128)S(1)}, u32[]{:S(2)}, u32[]{:S(2)}) collective-permute-start(f32[40,256]{1,0:T(8,128)S(1)} %get-tuple-element.217), channel_id=1, source_target_pairs={{0,24},{1,25},{2,26},{3,27},{4,28},{5,29},{6,30},{7,31},{8,16},{9,... | collective-permute-start | bytes 122888 | tf_op jit(solution)/shard_map/ppermute | solution.py:1263
  30.1 2.7 %collective-permute-done.7.refs_2_ = f32[40,256]{1,0:T(8,128)S(1)} collective-permute-done((f32[40,256]{1,0:T(8,128)S(1)}, f32[40,256]{1,0:T(8,128)S(1)}, u32[]{:S(2)}, u32[]{:S(2)}) %collective-permute-start.7) | collective-permute-done | bytes 40992 | tf_op jit(solution)/shard_map/ppermute | solution.py:1263
  32.8 1.8 %collective-permute-done.8.refs_3_ = f32[40,256]{1,0:T(8,128)S(1)} collective-permute-done((f32[40,256]{1,0:T(8,128)S(1)}, f32[40,256]{1,0:T(8,128)S(1)}, u32[]{:S(2)}, u32[]{:S(2)}) %collective-permute-start.8) | collective-permute-done | bytes 40992 | tf_op jit(solution)/shard_map/ppermute | solution.py:1263
  34.8 1.2 %collective-permute-done.9.other_half = f32[64,256]{1,0:T(8,128)S(1)} collective-permute-done((f32[64,256]{1,0:T(8,128)S(1)}, f32[64,256]{1,0:T(8,128)S(1)}, u32[]{:S(2)}, u32[]{:S(2)}) %collective-permute-start.9) | collective-permute-done | bytes 65568 | tf_op jit(solution)/shard_map/ppermute | solution.py:1263
  36.0 2.2 %forward.1 = (f32[256,512]{1,0:T(8,128)S(1)}, f32[2,17,16,8,512]{4,3,2,1,0:T(8,128)S(1)}, f32[64,8,512]{2,1,0:T(8,128)S(1)}) custom-call(f32[64,256]{1,0:T(8,128)S(1)} %enter.1.mine_half, f32[64,256]{1,0:T(8,128)S(1)} %collective-permute-done.9.other_half, f32[72,512]{1,0:T(8,128)S(1)} %collective-permute-done.2.theirs.sibling, ...), custom_call_target="tpu_custom_call" | custom-call | tf_op jit(solution)/shard_map/forward/pallas_call | solution.py:676
  38.2 1.9 %early.1 = (f32[128,256]{1,0:T(8,128)}, bf16[256,512]{1,0:T(8,128)(2,1)S(1)}, bf16[256,512]{1,0:T(8,128)(2,1)S(1)}, f32[32,64,128]{2,1,0:T(8,128)S(1)}) custom-call(f32[128,256]{1,0:T(8,128)S(1)} %get-tuple-element.203.refs_0_.refs_3_, bf16[256,256]{1,0:T(8,128)(2,1)S(1)} %get-tuple-element.204.refs_1_.refs_5_, ...), custom_call_target="tpu_custom_call" | custom-call | tf_op jit(solution)/shard_map/early/pallas_call | solution.py:768
  40.4 2.9 %backward.2 = (f32[128,512]{1,0:T(8,128)S(1)}, f32[128,512]{1,0:T(8,128)S(1)}, f32[128,2048]{1,0:T(8,128)S(1)}, f32[128,2048]{1,0:T(8,128)S(1)}, f32[16,8,512]{2,1,0:T(8,128)S(1)}) custom-call(f32[2,16,8,512]{3,2,1,0:T(8,128)S(1)} %get-tuple-element.228.refs_0_, f32[64,8,512]{2,1,0:T(8,128)S(1)} %get-tuple-element.229.refs_1_, ...), custom_call_target="tpu_custom_call" | custom-call | tf_op jit(solution)/shard_map/backward/pallas_call | solution.py:886
  43.4 2.3 %collective-permute-start.13 = (f32[4,64,128]{2,1,0:T(8,128)S(1)}, f32[4,64,128]{2,1,0:T(8,128)S(1)}, u32[]{:S(2)}, u32[]{:S(2)}) collective-permute-start(f32[4,64,128]{2,1,0:T(8,128)S(1)} %get-tuple-element.287), channel_id=1, source_target_pairs={{0,6},{1,7},{2,4},{3,5},{4,2},{5,3},{6,0},{7,1},{8,14},{9,15},{10,... | collective-permute-start | bytes 393224 | tf_op jit(solution)/shard_map/ppermute | solution.py:1263
  45.7 0.7 collective-permute-start.12
  46.9 3.0 %backward.3 = (f32[128,512]{1,0:T(8,128)S(1)}, f32[128,512]{1,0:T(8,128)S(1)}, f32[128,2048]{1,0:T(8,128)S(1)}, f32[128,2048]{1,0:T(8,128)S(1)}, f32[16,8,512]{2,1,0:T(8,128)S(1)}) custom-call(f32[2,16,8,512]{3,2,1,0:T(8,128)S(1)} %get-tuple-element.228.refs_0_, f32[64,8,512]{2,1,0:T(8,128)S(1)} %get-tuple-element.229.refs_1_, ...), custom_call_target="tpu_custom_call" | custom-call | tf_op jit(solution)/shard_map/backward/pallas_call | solution.py:886
  50.0 2.8 %inner.1 = (bf16[256,512]{1,0:T(8,128)(2,1)S(1)}, bf16[256,512]{1,0:T(8,128)(2,1)S(1)}, f32[16,512]{1,0:T(8,128)S(1)}, f32[88,512]{1,0:T(8,128)S(1)}) custom-call(s32[1,128]{1,0:T(1,128)S(1)} %get-tuple-element.237.pad.refs_4_, f32[4,512]{1,0:T(4,128)S(1)} %get-tuple-element.154.conv_w, f32[48,512]{1,0:T(8,128)S(1)} %get-tuple-element.156.w_x, ...), custom_call_target="tpu_custom_call" | custom-call | tf_op jit(solution)/shard_map/inner/pallas_call | solution.py:1029
  52.9 2.9 %tail.1 = (f32[128,256]{1,0:T(8,128)S(1)}, f32[8,256]{1,0:T(8,128)}, f32[8,256]{1,0:T(8,128)}, f32[32,56,128]{2,1,0:T(8,128)S(1)}) custom-call(f32[8,256]{1,0:T(8,128)S(1)} %collective-permute-done.sib.refs_0_, f32[8,256]{1,0:T(8,128)S(1)} %collective-permute-done.1.oth.refs_1_, f32[1,256]{1,0:T(1,128)S(1)} %get-tuple-element.152.gain.refs_2_, ...), custom_call_target="tpu_custom_call" | custom-call | tf_op jit(solution)/shard_map/tail/pallas_call | solution.py:1127
  56.0 1.8 %collective-permute-done.14 = f32[16,56,128]{2,1,0:T(8,128)S(1)} collective-permute-done((f32[16,56,128]{2,1,0:T(8,128)S(1)}, f32[16,56,128]{2,1,0:T(8,128)S(1)}, u32[]{:S(2)}, u32[]{:S(2)}) %collective-permute-start.14) | collective-permute-done | bytes 458784 | tf_op jit(solution)/shard_map/ppermute | solution.py:1263
  57.9 2.2 %collective-permute-start.17 = (f32[4,56,128]{2,1,0:T(8,128)S(1)}, f32[4,56,128]{2,1,0:T(8,128)S(1)}, u32[]{:S(2)}, u32[]{:S(2)}) collective-permute-start(f32[4,56,128]{2,1,0:T(8,128)S(1)} %get-tuple-element.290), channel_id=1, source_target_pairs={{0,6},{1,7},{2,4},{3,5},{4,2},{5,3},{6,0},{7,1},{8,14},{9,15},{10,... | collective-permute-start | bytes 344072 | tf_op jit(solution)/shard_map/ppermute | solution.py:1263
  60.1 0.7 collective-permute-start.16
  60.8 0.6 collective-permute-start.15
  61.4 2.9 %collective-permute-done.17 = f32[4,56,128]{2,1,0:T(8,128)S(1)} collective-permute-done((f32[4,56,128]{2,1,0:T(8,128)S(1)}, f32[4,56,128]{2,1,0:T(8,128)S(1)}, u32[]{:S(2)}, u32[]{:S(2)}) %collective-permute-start.17) | collective-permute-done | bytes 114720 | tf_op jit(solution)/shard_map/ppermute | solution.py:1263
  64.3 2.2 %collective-permute-done.16 = f32[4,56,128]{2,1,0:T(8,128)S(1)} collective-permute-done((f32[4,56,128]{2,1,0:T(8,128)S(1)}, f32[4,56,128]{2,1,0:T(8,128)S(1)}, u32[]{:S(2)}, u32[]{:S(2)}) %collective-permute-start.16) | collective-permute-done | bytes 114720 | tf_op jit(solution)/shard_map/ppermute | solution.py:1263
  66.5 1.4 %collective-permute-start.20 = (f32[1,120,128]{2,1,0:T(8,128)S(1)}, f32[1,120,128]{2,1,0:T(8,128)S(1)}, u32[]{:S(2)}, u32[]{:S(2)}) collective-permute-start(f32[1,120,128]{2,1,0:T(8,128)S(1)} %get-tuple-element.293), channel_id=1, source_target_pairs={{0,24},{1,25},{2,26},{3,27},{4,28},{5,29},{6,30},{7,31},{8,16},{9,... | collective-permute-start | bytes 184328 | tf_op jit(solution)/shard_map/ppermute | solution.py:1263
  67.9 3.1 %collective-permute-start.18 = (f32[1,120,128]{2,1,0:T(8,128)S(1)}, f32[1,120,128]{2,1,0:T(8,128)S(1)}, u32[]{:S(2)}, u32[]{:S(2)}) collective-permute-start(f32[1,120,128]{2,1,0:T(8,128)S(1)} %get-tuple-element.292), channel_id=1, source_target_pairs={{0,8},{1,9},{2,10},{3,11},{4,12},{5,13},{6,14},{7,15},{8,0},{9,1},... | collective-permute-start | bytes 184328 | tf_op jit(solution)/shard_map/ppermute | solution.py:1263
  71.0 2.3 %collective-permute-done.20 = f32[1,120,128]{2,1,0:T(8,128)S(1)} collective-permute-done((f32[1,120,128]{2,1,0:T(8,128)S(1)}, f32[1,120,128]{2,1,0:T(8,128)S(1)}, u32[]{:S(2)}, u32[]{:S(2)}) %collective-permute-start.20) | collective-permute-done | bytes 61472 | tf_op jit(solution)/shard_map/ppermute | solution.py:1263
  73.3 1.6 %collective-permute-done.19 = f32[1,120,128]{2,1,0:T(8,128)S(1)} collective-permute-done((f32[1,120,128]{2,1,0:T(8,128)S(1)}, f32[1,120,128]{2,1,0:T(8,128)S(1)}, u32[]{:S(2)}, u32[]{:S(2)}) %collective-permute-start.19) | collective-permute-done | bytes 61472 | tf_op jit(solution)/shard_map/ppermute | solution.py:1263
  75.0 0.6 collective-permute-start.21
  75.6 1.3 %collective-permute-start.22 = (f32[1,112,128]{2,1,0:T(8,128)S(1)}, f32[1,112,128]{2,1,0:T(8,128)S(1)}, u32[]{:S(2)}, u32[]{:S(2)}) collective-permute-start(f32[1,112,128]{2,1,0:T(8,128)S(1)} %get-tuple-element.295), channel_id=1, source_target_pairs={{0,8},{1,9},{2,10},{3,11},{4,12},{5,13},{6,14},{7,15},{8,0},{9,1},... | collective-permute-start | bytes 172040 | tf_op jit(solution)/shard_map/ppermute | solution.py:1263
  76.9 2.5 %collective-permute-start.23 = (f32[1,112,128]{2,1,0:T(8,128)S(1)}, f32[1,112,128]{2,1,0:T(8,128)S(1)}, u32[]{:S(2)}, u32[]{:S(2)}) collective-permute-start(f32[1,112,128]{2,1,0:T(8,128)S(1)} %get-tuple-element.295), channel_id=1, source_target_pairs={{0,24},{1,25},{2,26},{3,27},{4,28},{5,29},{6,30},{7,31},{8,16},{9,... | collective-permute-start | bytes 172040 | tf_op jit(solution)/shard_map/ppermute | solution.py:1263
  79.4 2.0 %collective-permute-done.21 = f32[1,112,128]{2,1,0:T(8,128)S(1)} collective-permute-done((f32[1,112,128]{2,1,0:T(8,128)S(1)}, f32[1,112,128]{2,1,0:T(8,128)S(1)}, u32[]{:S(2)}, u32[]{:S(2)}) %collective-permute-start.21) | collective-permute-done | bytes 57376 | tf_op jit(solution)/shard_map/ppermute | solution.py:1263
  81.4 1.5 %collective-permute-done.23 = f32[1,112,128]{2,1,0:T(8,128)S(1)} collective-permute-done((f32[1,112,128]{2,1,0:T(8,128)S(1)}, f32[1,112,128]{2,1,0:T(8,128)S(1)}, u32[]{:S(2)}, u32[]{:S(2)}) %collective-permute-start.23) | collective-permute-done | bytes 57376 | tf_op jit(solution)/shard_map/ppermute | solution.py:1263
  82.9 1.0 collective-permute-start.24
  83.9 1.1 %collective-permute-start.25 = (f32[4,112,128]{2,1,0:T(8,128)S(1)}, f32[4,112,128]{2,1,0:T(8,128)S(1)}, u32[]{:S(2)}, u32[]{:S(2)}) collective-permute-start(f32[4,112,128]{2,1,0:T(8,128)S(1)} %pad_maximum_fusion), channel_id=1, source_target_pairs={{0,2},{1,3},{2,0},{3,1},{4,6},{5,7},{6,4},{7,5},{8,10},{9,11},{10,... | collective-permute-start | bytes 688136 | tf_op jit(solution)/shard_map/ppermute | solution.py:1263
  85.0 1.5 %collective-permute-start.26 = (f32[4,112,128]{2,1,0:T(8,128)S(1)}, f32[4,112,128]{2,1,0:T(8,128)S(1)}, u32[]{:S(2)}, u32[]{:S(2)}) collective-permute-start(f32[4,112,128]{2,1,0:T(8,128)S(1)} %pad_maximum_fusion), channel_id=1, source_target_pairs={{0,6},{1,7},{2,4},{3,5},{4,2},{5,3},{6,0},{7,1},{8,14},{9,15},{10,... | collective-permute-start | bytes 688136 | tf_op jit(solution)/shard_map/ppermute | solution.py:1263
  86.5 4.1 %collective-permute-done.24 = f32[4,112,128]{2,1,0:T(8,128)S(1)} collective-permute-done((f32[4,112,128]{2,1,0:T(8,128)S(1)}, f32[4,112,128]{2,1,0:T(8,128)S(1)}, u32[]{:S(2)}, u32[]{:S(2)}) %collective-permute-start.24) | collective-permute-done | bytes 229408 | tf_op jit(solution)/shard_map/ppermute | solution.py:1263
  90.7 1.1 %collective-permute-done.25 = f32[4,112,128]{2,1,0:T(8,128)S(1)} collective-permute-done((f32[4,112,128]{2,1,0:T(8,128)S(1)}, f32[4,112,128]{2,1,0:T(8,128)S(1)}, u32[]{:S(2)}, u32[]{:S(2)}) %collective-permute-start.25) | collective-permute-done | bytes 229408 | tf_op jit(solution)/shard_map/ppermute | solution.py:1263
  91.8 3.5 %collective-permute-done.26 = f32[4,112,128]{2,1,0:T(8,128)S(1)} collective-permute-done((f32[4,112,128]{2,1,0:T(8,128)S(1)}, f32[4,112,128]{2,1,0:T(8,128)S(1)}, u32[]{:S(2)}, u32[]{:S(2)}) %collective-permute-start.26) | collective-permute-done | bytes 229408 | tf_op jit(solution)/shard_map/ppermute | solution.py:1263
  95.5 2.4 %collective-permute-done.27.refs_1_ = f32[16,112,128]{2,1,0:T(8,128)S(1)} collective-permute-done((f32[16,112,128]{2,1,0:T(8,128)S(1)}, f32[16,112,128]{2,1,0:T(8,128)S(1)}, u32[]{:S(2)}, u32[]{:S(2)}) %collective-permute-start.27) | collective-permute-done | bytes 917536 | tf_op jit(solution)/shard_map/ppermute | solution.py:1263
  97.9 1.5 %unpack.1 = (f32[128,256]{1,0:T(8,128)}, f32[1,256]{1,0:T(1,128)}, f32[256,1024]{1,0:T(8,128)}, f32[4,512]{1,0:T(4,128)}, f32[1,512]{1,0:T(1,128)}, /*index=5*/f...) custom-call(f32[16,112,128]{2,1,0:T(8,128)S(1)} %constant_dynamic-up, ...), custom_call_target="tpu_custom_call" | custom-call | tf_op jit(solution)/shard_map/unpack/pallas_call | solution.py:1234
  (44 shorter events, 2.3 us)
Async XLA Ops:
  1.5 4.4 %collective-permute-start = (f32[8,256]{1,0:T(8,128)S(1)}, f32[8,256]{1,0:T(8,128)S(1)}, u32[]{:S(2)}, u32[]{:S(2)}) collective-permute-start(f32[8,256]{1,0:T(8,128)S(1)} %get-tuple-element.149), channel_id=1, source_target_pairs={{0,1},{1,0},{2,3},{3,2},{4,5},{5,4},{6,7},{7,6},{8,9},{9,8},{10,11... | collective-permute-start | bytes 24584 | tf_op jit(solution)/shard_map/ppermute | solution.py:1263
  1.9 3.9 %collective-permute-start.1 = (f32[8,256]{1,0:T(8,128)S(1)}, f32[8,256]{1,0:T(8,128)S(1)}, u32[]{:S(2)}, u32[]{:S(2)}) collective-permute-start(f32[8,256]{1,0:T(8,128)S(1)} %get-tuple-element.150), channel_id=1, source_target_pairs={{1,2},{3,4},{5,6},{7,8},{9,10},{11,12},{13,14},{15,16},{17,18},{19... | collective-permute-start | bytes 24584 | tf_op jit(solution)/shard_map/ppermute | solution.py:1271
  11.8 4.9 %collective-permute-start.2 = (f32[72,512]{1,0:T(8,128)S(1)}, f32[72,512]{1,0:T(8,128)S(1)}, u32[]{:S(2)}, u32[]{:S(2)}) collective-permute-start(f32[72,512]{1,0:T(8,128)S(1)} %get-tuple-element.163.mine), channel_id=1, source_target_pairs={{0,1},{1,0},{2,3},{3,2},{4,5},{5,4},{6,7},{7,6},{8,9},{9,8},{10,11... | collective-permute-start | bytes 442376 | tf_op jit(solution)/shard_map/ppermute | solution.py:1263
  16.8 5.7 %collective-permute-start.3 = (f32[72,256]{1,0:T(8,128)S(1)}, f32[72,256]{1,0:T(8,128)S(1)}, u32[]{:S(2)}, u32[]{:S(2)}) collective-permute-start(f32[72,256]{1,0:T(8,128)S(1)} %pair.1.refs_1_), channel_id=1, source_target_pairs={{0,2},{1,3},{2,0},{3,1},{4,6},{5,7},{6,4},{7,5},{8,10},{9,11},{10,... | collective-permute-start | bytes 221192 | tf_op jit(solution)/shard_map/ppermute | solution.py:1263
  18.4 5.4 %collective-permute-start.4 = (f32[72,256]{1,0:T(8,128)S(1)}, f32[72,256]{1,0:T(8,128)S(1)}, u32[]{:S(2)}, u32[]{:S(2)}) collective-permute-start(f32[72,256]{1,0:T(8,128)S(1)} %pair.1.refs_1_), channel_id=1, source_target_pairs={{0,4},{1,5},{2,6},{3,7},{4,0},{5,1},{6,2},{7,3},{8,12},{9,13},{10,... | collective-permute-start | bytes 221192 | tf_op jit(solution)/shard_map/ppermute | solution.py:1263
  20.3 5.3 %collective-permute-start.5 = (f32[72,256]{1,0:T(8,128)S(1)}, f32[72,256]{1,0:T(8,128)S(1)}, u32[]{:S(2)}, u32[]{:S(2)}) collective-permute-start(f32[72,256]{1,0:T(8,128)S(1)} %pair.1.refs_1_), channel_id=1, source_target_pairs={{0,6},{1,7},{2,4},{3,5},{4,2},{5,3},{6,0},{7,1},{8,14},{9,15},{10,... | collective-permute-start | bytes 221192 | tf_op jit(solution)/shard_map/ppermute | solution.py:1263
  25.6 4.5 %collective-permute-start.6 = (f32[40,256]{1,0:T(8,128)S(1)}, f32[40,256]{1,0:T(8,128)S(1)}, u32[]{:S(2)}, u32[]{:S(2)}) collective-permute-start(f32[40,256]{1,0:T(8,128)S(1)} %get-tuple-element.215), channel_id=1, source_target_pairs={{0,8},{1,9},{2,10},{3,11},{4,12},{5,13},{6,14},{7,15},{8,0},{9,1},... | collective-permute-start | bytes 122888 | tf_op jit(solution)/shard_map/ppermute | solution.py:1263
  27.3 5.5 %collective-permute-start.7 = (f32[40,256]{1,0:T(8,128)S(1)}, f32[40,256]{1,0:T(8,128)S(1)}, u32[]{:S(2)}, u32[]{:S(2)}) collective-permute-start(f32[40,256]{1,0:T(8,128)S(1)} %get-tuple-element.216), channel_id=1, source_target_pairs={{0,16},{1,17},{2,18},{3,19},{4,20},{5,21},{6,22},{7,23},{8,24},{9,... | collective-permute-start | bytes 122888 | tf_op jit(solution)/shard_map/ppermute | solution.py:1263
  28.8 5.8 %collective-permute-start.8 = (f32[40,256]{1,0:T(8,128)S(1)}, f32[40,256]{1,0:T(8,128)S(1)}, u32[]{:S(2)}, u32[]{:S(2)}) collective-permute-start(f32[40,256]{1,0:T(8,128)S(1)} %get-tuple-element.217), channel_id=1, source_target_pairs={{0,24},{1,25},{2,26},{3,27},{4,28},{5,29},{6,30},{7,31},{8,16},{9,... | collective-permute-start | bytes 122888 | tf_op jit(solution)/shard_map/ppermute | solution.py:1263
  34.7 1.3 %collective-permute-start.9 = (f32[64,256]{1,0:T(8,128)S(1)}, f32[64,256]{1,0:T(8,128)S(1)}, u32[]{:S(2)}, u32[]{:S(2)}) collective-permute-start(f32[64,256]{1,0:T(8,128)S(1)} %enter.1.mine_half), channel_id=1, source_target_pairs={{0,1},{1,0},{2,3},{3,2},{4,5},{5,4},{6,7},{7,6},{8,9},{9,8},{10,11... | collective-permute-start | bytes 196616 | tf_op jit(solution)/shard_map/ppermute | solution.py:1263
  40.2 3.1 %collective-permute-start.10 = (f32[16,64,128]{2,1,0:T(8,128)S(1)}, f32[16,64,128]{2,1,0:T(8,128)S(1)}, u32[]{:S(2)}, u32[]{:S(2)}) collective-permute-start(f32[16,64,128]{2,1,0:T(8,128)S(1)} %slice.58), channel_id=1, source_target_pairs={{0,1},{1,0},{2,3},{3,2},{4,5},{5,4},{6,7},{7,6},{8,9},{9,8},{10,11... | collective-permute-start | bytes 1572872 | tf_op jit(solution)/shard_map/ppermute | solution.py:1263
  43.4 9.4 %collective-permute-start.13 = (f32[4,64,128]{2,1,0:T(8,128)S(1)}, f32[4,64,128]{2,1,0:T(8,128)S(1)}, u32[]{:S(2)}, u32[]{:S(2)}) collective-permute-start(f32[4,64,128]{2,1,0:T(8,128)S(1)} %get-tuple-element.287), channel_id=1, source_target_pairs={{0,6},{1,7},{2,4},{3,5},{4,2},{5,3},{6,0},{7,1},{8,14},{9,15},{10,... | collective-permute-start | bytes 393224 | tf_op jit(solution)/shard_map/ppermute | solution.py:1263
  45.7 7.2 %collective-permute-start.12 = (f32[4,64,128]{2,1,0:T(8,128)S(1)}, f32[4,64,128]{2,1,0:T(8,128)S(1)}, u32[]{:S(2)}, u32[]{:S(2)}) collective-permute-start(f32[4,64,128]{2,1,0:T(8,128)S(1)} %get-tuple-element.288), channel_id=1, source_target_pairs={{0,4},{1,5},{2,6},{3,7},{4,0},{5,1},{6,2},{7,3},{8,12},{9,13},{10,... | collective-permute-start | bytes 393224 | tf_op jit(solution)/shard_map/ppermute | solution.py:1263
  46.4 6.5 %collective-permute-start.11 = (f32[4,64,128]{2,1,0:T(8,128)S(1)}, f32[4,64,128]{2,1,0:T(8,128)S(1)}, u32[]{:S(2)}, u32[]{:S(2)}) collective-permute-start(f32[4,64,128]{2,1,0:T(8,128)S(1)} %get-tuple-element.286), channel_id=1, source_target_pairs={{0,2},{1,3},{2,0},{3,1},{4,6},{5,7},{6,4},{7,5},{8,10},{9,11},{10,... | collective-permute-start | bytes 393224 | tf_op jit(solution)/shard_map/ppermute | solution.py:1263
  55.9 1.9 %collective-permute-start.14 = (f32[16,56,128]{2,1,0:T(8,128)S(1)}, f32[16,56,128]{2,1,0:T(8,128)S(1)}, u32[]{:S(2)}, u32[]{:S(2)}) collective-permute-start(f32[16,56,128]{2,1,0:T(8,128)S(1)} %slice.64), channel_id=1, source_target_pairs={{0,1},{1,0},{2,3},{3,2},{4,5},{5,4},{6,7},{7,6},{8,9},{9,8},{10,11... | collective-permute-start | bytes 1376264 | tf_op jit(solution)/shard_map/ppermute | solution.py:1263
  57.9 6.4 %collective-permute-start.17 = (f32[4,56,128]{2,1,0:T(8,128)S(1)}, f32[4,56,128]{2,1,0:T(8,128)S(1)}, u32[]{:S(2)}, u32[]{:S(2)}) collective-permute-start(f32[4,56,128]{2,1,0:T(8,128)S(1)} %get-tuple-element.290), channel_id=1, source_target_pairs={{0,6},{1,7},{2,4},{3,5},{4,2},{5,3},{6,0},{7,1},{8,14},{9,15},{10,... | collective-permute-start | bytes 344072 | tf_op jit(solution)/shard_map/ppermute | solution.py:1263
  60.1 6.4 %collective-permute-start.16 = (f32[4,56,128]{2,1,0:T(8,128)S(1)}, f32[4,56,128]{2,1,0:T(8,128)S(1)}, u32[]{:S(2)}, u32[]{:S(2)}) collective-permute-start(f32[4,56,128]{2,1,0:T(8,128)S(1)} %get-tuple-element.291), channel_id=1, source_target_pairs={{0,4},{1,5},{2,6},{3,7},{4,0},{5,1},{6,2},{7,3},{8,12},{9,13},{10,... | collective-permute-start | bytes 344072 | tf_op jit(solution)/shard_map/ppermute | solution.py:1263
  60.8 5.7 %collective-permute-start.15 = (f32[4,56,128]{2,1,0:T(8,128)S(1)}, f32[4,56,128]{2,1,0:T(8,128)S(1)}, u32[]{:S(2)}, u32[]{:S(2)}) collective-permute-start(f32[4,56,128]{2,1,0:T(8,128)S(1)} %get-tuple-element.289), channel_id=1, source_target_pairs={{0,2},{1,3},{2,0},{3,1},{4,6},{5,7},{6,4},{7,5},{8,10},{9,11},{10,... | collective-permute-start | bytes 344072 | tf_op jit(solution)/shard_map/ppermute | solution.py:1263
  66.5 6.8 %collective-permute-start.20 = (f32[1,120,128]{2,1,0:T(8,128)S(1)}, f32[1,120,128]{2,1,0:T(8,128)S(1)}, u32[]{:S(2)}, u32[]{:S(2)}) collective-permute-start(f32[1,120,128]{2,1,0:T(8,128)S(1)} %get-tuple-element.293), channel_id=1, source_target_pairs={{0,24},{1,25},{2,26},{3,27},{4,28},{5,29},{6,30},{7,31},{8,16},{9,... | collective-permute-start | bytes 184328 | tf_op jit(solution)/shard_map/ppermute | solution.py:1263
  67.9 7.0 %collective-permute-start.19 = (f32[1,120,128]{2,1,0:T(8,128)S(1)}, f32[1,120,128]{2,1,0:T(8,128)S(1)}, u32[]{:S(2)}, u32[]{:S(2)}) collective-permute-start(f32[1,120,128]{2,1,0:T(8,128)S(1)} %get-tuple-element.294), channel_id=1, source_target_pairs={{0,16},{1,17},{2,18},{3,19},{4,20},{5,21},{6,22},{7,23},{8,24},{9,... | collective-permute-start | bytes 184328 | tf_op jit(solution)/shard_map/ppermute | solution.py:1263
  67.9 7.0 %collective-permute-start.18 = (f32[1,120,128]{2,1,0:T(8,128)S(1)}, f32[1,120,128]{2,1,0:T(8,128)S(1)}, u32[]{:S(2)}, u32[]{:S(2)}) collective-permute-start(f32[1,120,128]{2,1,0:T(8,128)S(1)} %get-tuple-element.292), channel_id=1, source_target_pairs={{0,8},{1,9},{2,10},{3,11},{4,12},{5,13},{6,14},{7,15},{8,0},{9,1},... | collective-permute-start | bytes 184328 | tf_op jit(solution)/shard_map/ppermute | solution.py:1263
  75.0 6.4 %collective-permute-start.21 = (f32[1,112,128]{2,1,0:T(8,128)S(1)}, f32[1,112,128]{2,1,0:T(8,128)S(1)}, u32[]{:S(2)}, u32[]{:S(2)}) collective-permute-start(f32[1,112,128]{2,1,0:T(8,128)S(1)} %get-tuple-element.295), channel_id=1, source_target_pairs={{0,16},{1,17},{2,18},{3,19},{4,20},{5,21},{6,22},{7,23},{8,24},{9,... | collective-permute-start | bytes 172040 | tf_op jit(solution)/shard_map/ppermute | solution.py:1263
  75.6 5.8 %collective-permute-start.22 = (f32[1,112,128]{2,1,0:T(8,128)S(1)}, f32[1,112,128]{2,1,0:T(8,128)S(1)}, u32[]{:S(2)}, u32[]{:S(2)}) collective-permute-start(f32[1,112,128]{2,1,0:T(8,128)S(1)} %get-tuple-element.295), channel_id=1, source_target_pairs={{0,8},{1,9},{2,10},{3,11},{4,12},{5,13},{6,14},{7,15},{8,0},{9,1},... | collective-permute-start | bytes 172040 | tf_op jit(solution)/shard_map/ppermute | solution.py:1263
  76.9 6.0 %collective-permute-start.23 = (f32[1,112,128]{2,1,0:T(8,128)S(1)}, f32[1,112,128]{2,1,0:T(8,128)S(1)}, u32[]{:S(2)}, u32[]{:S(2)}) collective-permute-start(f32[1,112,128]{2,1,0:T(8,128)S(1)} %get-tuple-element.295), channel_id=1, source_target_pairs={{0,24},{1,25},{2,26},{3,27},{4,28},{5,29},{6,30},{7,31},{8,16},{9,... | collective-permute-start | bytes 172040 | tf_op jit(solution)/shard_map/ppermute | solution.py:1263
  82.9 7.7 %collective-permute-start.24 = (f32[4,112,128]{2,1,0:T(8,128)S(1)}, f32[4,112,128]{2,1,0:T(8,128)S(1)}, u32[]{:S(2)}, u32[]{:S(2)}) collective-permute-start(f32[4,112,128]{2,1,0:T(8,128)S(1)} %pad_maximum_fusion), channel_id=1, source_target_pairs={{0,4},{1,5},{2,6},{3,7},{4,0},{5,1},{6,2},{7,3},{8,12},{9,13},{10,... | collective-permute-start | bytes 688136 | tf_op jit(solution)/shard_map/ppermute | solution.py:1263
  83.9 7.9 %collective-permute-start.25 = (f32[4,112,128]{2,1,0:T(8,128)S(1)}, f32[4,112,128]{2,1,0:T(8,128)S(1)}, u32[]{:S(2)}, u32[]{:S(2)}) collective-permute-start(f32[4,112,128]{2,1,0:T(8,128)S(1)} %pad_maximum_fusion), channel_id=1, source_target_pairs={{0,2},{1,3},{2,0},{3,1},{4,6},{5,7},{6,4},{7,5},{8,10},{9,11},{10,... | collective-permute-start | bytes 688136 | tf_op jit(solution)/shard_map/ppermute | solution.py:1263
  85.0 10.4 %collective-permute-start.26 = (f32[4,112,128]{2,1,0:T(8,128)S(1)}, f32[4,112,128]{2,1,0:T(8,128)S(1)}, u32[]{:S(2)}, u32[]{:S(2)}) collective-permute-start(f32[4,112,128]{2,1,0:T(8,128)S(1)} %pad_maximum_fusion), channel_id=1, source_target_pairs={{0,6},{1,7},{2,4},{3,5},{4,2},{5,3},{6,0},{7,1},{8,14},{9,15},{10,... | collective-permute-start | bytes 688136 | tf_op jit(solution)/shard_map/ppermute | solution.py:1263
  95.4 2.5 %collective-permute-start.27 = (f32[16,112,128]{2,1,0:T(8,128)S(1)}, f32[16,112,128]{2,1,0:T(8,128)S(1)}, u32[]{:S(2)}, u32[]{:S(2)}) collective-permute-start(f32[16,112,128]{2,1,0:T(8,128)S(1)} %constant_dynamic-update-slice_fusion.refs_0_), channel_id=1, source_target_pairs={{0,1},{1,0},{2,3},{3,2},{4,5},{5,4},{6,7},{7,6},{8,9},{9,8},{10,11... | collective-permute-start | bytes 2752520 | tf_op jit(solution)/shard_map/ppermute | solution.py:1263

commit v3 on v2

--- a/solution.py
+++ b/solution.py
@@ -112,51 +112,42 @@
     return tuple(pltpu.with_memory_space_constraint(x, pltpu.HBM) for x in arrays)
 
 
-def edges_kernel(first_rows, last_rows, resets, pad, to_sib, to_oth):
-    length = resets.shape[1]
+def edges_kernel(tok, resets, pad, *refs):
+    more = (len(refs) - 5) // 2
+    to_sib, to_oth, *kept = refs[more:]
+    for ref, kept_o in zip((tok, resets, pad) + refs[:more], kept):
+        kept_o[...] = ref[...]
+    length, feat = tok.shape
     sub = lax.broadcasted_iota(jnp.int32, (CH, length), 0)
     lane = lax.broadcasted_iota(jnp.int32, (CH, length), 1)
     real = pad[...].astype(F32)
-    row = lax.broadcasted_iota(jnp.int32, first_rows.shape, 0)
-    kept = 1.0 - resets[...].astype(F32)
-    kept = jnp.concatenate([kept, jnp.zeros((1, first_rows.shape[1] - length), F32)], axis=1)
+    row = lax.broadcasted_iota(jnp.int32, (CH, feat), 0)
+    flags = 1.0 - resets[...].astype(F32)
+    flags = jnp.concatenate([flags, jnp.zeros((1, feat - length), F32)], axis=1)
 
     def message(rows, start):
         col = jnp.sum(jnp.where(lane == sub + start, real, 0.0), axis=1, keepdims=True)
-        return jnp.where(row < 3, rows * col, jnp.where(row == 3, kept, 0.0))
-
-    first = message(first_rows[...], 0)
-    last = message(pltpu.roll(last_rows[...], 3, 0), length - 3)
+        return jnp.where(row < 3, rows * col, jnp.where(row == 3, flags, 0.0))
+
+    first = message(tok[:CH, :], 0)
+    last = message(pltpu.roll(tok[length - CH :, :], 3, 0), length - 3)
     odd = (lax.axis_index("seq") & 1) == 1
     to_sib[...] = jnp.where(odd, first, last)
     to_oth[...] = jnp.where(odd, last, first)
 
 
-def edges(tok, resets, pad):
-    length, feat = tok.shape
-    shape = jax.ShapeDtypeStruct((CH, feat), F32)
-    whole = lambda *dims: pl.BlockSpec(dims, lambda i: (0, 0))
-    return pl.pallas_call(
+def edges(*arrays):
+    shape = jax.ShapeDtypeStruct((CH, arrays[0].shape[1]), F32)
+    found = pl.pallas_call(
         edges_kernel,
-        grid=(1,),
-        in_specs=[
-            whole(CH, feat),
-            pl.BlockSpec((CH, feat), lambda i: (length // CH - 1, 0)),
-            whole(1, length),
-            whole(1, length),
-        ],
-        out_specs=(whole(CH, feat), whole(CH, feat)),
-        out_shape=(shape, shape),
-        compiler_params=params(2),
+        out_shape=(shape, shape) + tuple(jax.ShapeDtypeStruct(x.shape, x.dtype) for x in arrays),
+        compiler_params=params(8),
         name="edges",
-    )(*in_hbm(tok, tok, resets, pad))
-
-
-def project_kernel(tok, pad, gain, w_in, gout, w_out, *refs):
-    more = (len(refs) - 10) // 2
-    xb_o, z_o, go_o, gy_o, *kept = refs[more:]
-    for ref, kept_o in zip((tok, pad, gain, w_in, gout, w_out) + refs[:more], kept):
-        kept_o[...] = ref[...]
+    )(*in_hbm(*arrays))
+    return found[0], found[1], found[2:]
+
+
+def project_kernel(tok, pad, gain, w_in, gout, w_out, xb_o, z_o, go_o, gy_o):
     inner = w_out.shape[0]
     x = ordered(tok)
     normed = normalize(x, gain[...])[1]
@@ -175,17 +166,14 @@
         gy_o[:, cols] = go[:, cols] * (z * sigmoid(z))
 
 
-def project(*arrays):
-    tok, w_out = arrays[0], arrays[5]
-    length, inner = tok.shape[0], w_out.shape[0]
-    big = jax.ShapeDtypeStruct((2 * length, inner), F32)
-    found = pl.pallas_call(
+def project(tok, pad, gain, w_in, gout, w_out):
+    big = jax.ShapeDtypeStruct((2 * tok.shape[0], w_out.shape[0]), F32)
+    return pl.pallas_call(
         project_kernel,
-        out_shape=(big, big, big, big) + tuple(jax.ShapeDtypeStruct(x.shape, x.dtype) for x in arrays),
+        out_shape=(big, big, big, big),
         compiler_params=params(8),
         name="project",
-    )(*in_hbm(*arrays))
-    return found[:4], found[4:]
+    )(tok, pad, gain, w_in, gout, w_out)
 
 
 def pick_sides(from_sibling, from_other):
@@ -1137,10 +1125,10 @@
     )(*arrays)
 
 
-def unpack_kernel(
-    rs_bits, near, far, gtok, halo, pad,
-    gtok_o, gain_o, w_in_o, conv_w_o, conv_b_o, w_x_o, w_dt_o, dt_bias_o, a_log_o, d_skip_o, w_out_o, few_s, rest_s,
-):
+def unpack_kernel(rs_bits, parts, *refs):
+    sources, refs = refs[:parts], refs[parts:]
+    (gtok, halo, pad, gtok_o, gain_o, w_in_o, conv_w_o, conv_b_o, w_x_o, w_dt_o, dt_bias_o, a_log_o, d_skip_o, w_out_o,
+     few_s, rest_s) = refs
     feat = w_in_o.shape[0]
     inner = w_out_o.shape[0]
     tiles = inner // LANE
@@ -1148,8 +1136,8 @@
     mine = reverse_bits(lax.axis_index("seq"), rs_bits)
     in_rows, out_rows = feat // pieces, inner // pieces
     for slot in range(pieces):
-        source = near if slot < pieces // 2 else far
-        i = slot % (pieces // 2)
+        source = sources[slot * parts // pieces]
+        i = slot % (pieces // parts)
         p = reverse_bits(mine ^ slot, rs_bits)
         at = 0
         in_at = pl.ds(pl.multiple_of(p * in_rows, in_rows), in_rows)
@@ -1225,14 +1213,14 @@
     return nn(picked, jnp.ones((length, width), BF16))
 
 
-def unpack(rs_bits, near, far, gtok, halo, pad, state, rank):
+def unpack(rs_bits, parts, gtok, halo, pad, state, rank):
     length, feat = gtok.shape
     pieces = 1 << rs_bits
     inner = state[1]
     width = rank + 2 * state[0]
     shape = lambda *dims: jax.ShapeDtypeStruct(dims, F32)
     return pl.pallas_call(
-        lambda *refs: unpack_kernel(rs_bits, *refs),
+        lambda *refs: unpack_kernel(rs_bits, len(parts), *refs),
         out_shape=(
             shape(length, feat),
             shape(1, feat),
@@ -1249,7 +1237,7 @@
         scratch_shapes=[pltpu.VMEM((pieces, CH, LANE), F32)] * 2,
         compiler_params=params(6),
         name="unpack",
-    )(near, far, gtok, halo, pad)
+    )(*parts, gtok, halo, pad)
 
 
 def body(tokens, resets, pad_mask, norm_gain, w_in, conv_w, conv_b, w_x, w_dt, dt_bias, a_log, d_skip, w_out, grad_out):
@@ -1270,14 +1258,14 @@
     def swap_across(value):
         return lax.ppermute(value, "seq", across)
 
-    to_sib, to_oth = edges(tokens, keep_row, pad_row)
+    to_sib, to_oth, kept = edges(
+        tokens, keep_row, pad_row, norm_gain, w_in[0], grad_out, w_out[0],
+        conv_w[0], conv_b, w_x[0].T, w_dt[0], dt_bias, a_log[0].T, d_skip,
+    )
+    (tok, keep, pad, gain, w_in_0, gout, w_out_0, conv_w_0, conv_b_0, w_x_t, w_dt_0, dt_bias_0, a_log_t, skip) = kept
     oth = swap_across(to_oth)
     sib = swap(to_sib, 0)
-    (xb, z, go, gy), kept = project(
-        tokens, pad_row, norm_gain, w_in[0], grad_out, w_out[0],
-        keep_row, conv_w[0], conv_b, w_x[0].T, w_dt[0], dt_bias, a_log[0].T, d_skip,
-    )
-    (tok, pad, gain, w_in_0, gout, w_out_0, keep, conv_w_0, conv_b_0, w_x_t, w_dt_0, dt_bias_0, a_log_t, skip) = kept
+    xb, z, go, gy = project(tok, pad, gain, w_in_0, gout, w_out_0)
     xc, dt, sig, conv, mask, dbl, xbh, sx, mx, total, de, dx, bc, a2, decay = prepare(
         sib, oth, keep, gain, w_in_0, conv_w_0, conv_b_0, w_x_t, w_dt_0, dt_bias_0, a_log_t, xb, gy
     )
@@ -1307,7 +1295,7 @@
     def reduced(part, step):
         size = part.shape[0] >> len(step)
         total = part[:size]
-        for i in range(1, 1 << len(step)):
+        for i in ((3, 1, 2) if len(step) == 2 else (1,)):
             slot = reverse_bits(i, len(step))
             total = total + exchange(part[slot * size : (slot + 1) * size], i << step[0])
         return total
@@ -1320,17 +1308,17 @@
     part_a = reduced(part_a, range(0, 1))
     back_f = backward(0, mx, car, h, de, dx, bc, a2, decay, gy)
     part_a, back_f, h = lax.optimization_barrier((part_a, back_f, h))
-    part_a = reduced(part_a, rs_steps[1])
+    part_a = reduced(part_a, range(1, 2))
     back_r = backward(1, mx, car, h, de, dx, bc, a2, decay, gy)
     gxh, gxl, halo_g, few = inner_back(
         pad, conv_w_0, w_x_t, w_dt_0, skip, a2,
         xb, gy, xc, dt, sig, cgrad, mask, dbl, xbh, xch, xcl, skip_sum, pick_b, pick_c, *back_f, *back_r,
     )
-    part_a, gxh = lax.optimization_barrier((part_a, gxh))
     gtok, to_left, to_right, part_b = tail(
         rs_bits, sib, oth, gain, x, g, nth, ntl, wih, wil, wfh, wfl, gzh, gzl, gxh, gxl, halo_g, few
     )
-    part_b = reduced(part_b, rs_steps[0])
+    part_a, part_b = lax.optimization_barrier((part_a, part_b))
+    part_a, part_b = reduced(part_a, range(2, 3)), reduced(part_b, rs_steps[0])
     part_b = reduced(part_b, rs_steps[1])
     own = jnp.concatenate([part_a, part_b], axis=1)
     for step in rs_steps[2:]:
@@ -1346,10 +1334,12 @@
         halo = jnp.concatenate([from_left.reshape(-1, LANE), from_right.reshape(-1, LANE)], axis=0)
     own = own[:, : tall - 8]
     for step in reversed(rs_steps[1:]):
-        parts = [own] + [exchange(own, reverse_bits(i, len(step)) << step[0]) for i in range(1, 1 << len(step))]
-        own = jnp.concatenate(parts, axis=0)
-    far = swap(own, 0)
-    outs = unpack(rs_bits, own, far, gtok, halo, pad, a_log_t.shape, w_dt.shape[1])
+        near = [exchange(own, reverse_bits(i, len(step)) << step[0]) for i in range((1 << len(step)) - 1, 0, -1)]
+        near = [own] + near[::-1]
+        if step is not rs_steps[1]:
+            own = jnp.concatenate(near, axis=0)
+    far = [swap(part, 0) for part in near]
+    outs = unpack(rs_bits, near + far, gtok, halo, pad, a_log_t.shape, w_dt.shape[1])
     gtok, g_gain, g_w_in, g_conv_w, g_conv_b, g_w_x, g_w_dt, g_dt_bias, g_a_log, g_d_skip, g_w_out = outs
     return (
         mixed, gtok, g_gain, g_w_in[None], g_conv_w[None], g_conv_b, g_w_x.T[None], g_w_dt[None],

time: 99.6 us -> 93.7 us (0.941)
  waiting for transfers between devices: 35.5 us -> 29.4 us
  starting transfers between devices: 33.1 us -> 34.3 us
    ppermute x27 -> x29, waiting for transfers between devices: 35.5 us -> 29.4 us  [exchange(): return lax.ppermute(value, 'seq', [(i, i ^ apart) for i in range(count)])]
    ppermute x27 -> x29, starting transfers between devices: 32.4 us -> 33.6 us  [exchange(): return lax.ppermute(value, 'seq', [(i, i ^ apart) for i in range(count)])]
  transfers between devices with their start and end apart: 28 -> 30, of which waited for: 18 -> 17; matrix products, arithmetic and copies ran while one was open for 0% -> 0% of each run, Pallas kernels for 14% -> 16%
where the time goes in v3:
time: 93.7 us; the launch traced here: 93.5 us
  starting transfers between devices  34.3 us (37%)
  waiting for transfers between devices  29.4 us (31%)
  Pallas kernels  28.6 us (31%)
    ppermute x29, starting transfers between devices, exchange(): return lax.ppermute(value, 'seq', [(i, i ^ apart) for i in range(count)])  33.6 us
    ppermute x29, waiting for transfers between devices, exchange(): return lax.ppermute(value, 'seq', [(i, i ^ apart) for i in range(count)])  29.4 us
    pallas_call x1, Pallas kernels, prepare(): pl.pallas_call(prepare_kernel, out_shape=(big, big, big, big, pltpu.VMEM(...  5.94 us
    pallas_call x2, Pallas kernels, backward(): pl.pallas_call(lambda *refs: backward_kernel(dirn, *refs), out_shape=(hal...  5.73 us
    pallas_call x1, Pallas kernels, tail(): pl.pallas_call(lambda *refs: tail_kernel(rs_bits, *refs), out_shape=(jax....  2.91 us
    pallas_call x1, Pallas kernels, inner_back(): pl.pallas_call(inner_kernel, out_shape=(part, part, jax.ShapeDtypeStruct(...  2.79 us
    pallas_call x1, Pallas kernels, forward(): pl.pallas_call(forward_kernel, out_shape=(jax.ShapeDtypeStruct((rows2, in...  2.14 us
    pallas_call x1, Pallas kernels, ready(): pl.pallas_call(lambda *refs: ready_kernel(rank, *refs), out_shape=(f32(le...  2.1 us
  transfers between devices with their start and end apart: 30, of which 17 were waited for; matrix products, arithmetic and copies ran while one was open for 0% of the time, Pallas kernels for 16%

profile of v3, /device:TPU:0, one launch (start us, length us, event | category | flops | bytes accessed | tf_op | source)
XLA Modules:
  0.0 93.5 jit_solution(8970277129591646309)
XLA Ops:
  0.6 1.8 %edges.1 = (f32[8,256]{1,0:T(8,128)S(1)}, f32[8,256]{1,0:T(8,128)S(1)}, f32[128,256]{1,0:T(8,128)S(1)}, s32[1,128]{1,0:T(1,128)S(1)}, s32[1,128]{1,0:T(1,128)S(1...) custom-call(f32[128,256]{1,0:T(8,128)} %tok.1, ...), custom_call_target="tpu_custom_call" | custom-call | tf_op jit(solution)/shard_map/edges/pallas_call | solution.py:141
  2.5 0.5 collective-permute-start
  3.0 0.6 collective-permute-start.1
  3.6 1.6 %project.1 = (f32[256,512]{1,0:T(8,128)S(1)}, f32[256,512]{1,0:T(8,128)S(1)}, f32[256,512]{1,0:T(8,128)S(1)}, f32[256,512]{1,0:T(8,128)S(1)}) custom-call(f32[128,256]{1,0:T(8,128)S(1)} %get-tuple-element.160.tok.refs_0_, s32[1,128]{1,0:T(1,128)S(1)} %get-tuple-element.161.pad.refs_10_, f32[1,256]{1,0:T(1,128)S(1)} %get-tuple-element.152.gain.refs_2_, ...), custom_call_target="tpu_custom_call" | custom-call | tf_op jit(solution)/shard_map/project/pallas_call | solution.py:171
  5.2 5.9 %prepare.1 = (f32[256,512]{1,0:T(8,128)S(1)}, f32[256,512]{1,0:T(8,128)S(1)}, f32[256,512]{1,0:T(8,128)S(1)}, f32[256,512]{1,0:T(8,128)S(1)}, f32[768,128]{1,0:T...) custom-call(f32[8,256]{1,0:T(8,128)S(1)} %collective-permute-done.si, ...), custom_call_target="tpu_custom_call" | custom-call | tf_op jit(solution)/shard_map/prepare/pallas_call | solution.py:406
  11.2 3.9 %collective-permute-start.2 = (f32[72,512]{1,0:T(8,128)S(1)}, f32[72,512]{1,0:T(8,128)S(1)}, u32[]{:S(2)}, u32[]{:S(2)}) collective-permute-start(f32[72,512]{1,0:T(8,128)S(1)} %get-tuple-element.167.mine), channel_id=1, source_target_pairs={{0,1},{1,0},{2,3},{3,2},{4,5},{5,4},{6,7},{7,6},{8,9},{9,8},{10,11... | collective-permute-start | bytes 442376 | tf_op jit(solution)/shard_map/ppermute | solution.py:1251
  15.1 1.0 %collective-permute-done.2.theirs.sibling = f32[72,512]{1,0:T(8,128)S(1)} collective-permute-done((f32[72,512]{1,0:T(8,128)S(1)}, f32[72,512]{1,0:T(8,128)S(1)}, u32[]{:S(2)}, u32[]{:S(2)}) %collective-permute-start.2) | collective-permute-done | bytes 147488 | tf_op jit(solution)/shard_map/ppermute | solution.py:1251
  16.1 2.8 %collective-permute-start.3 = (f32[72,256]{1,0:T(8,128)S(1)}, f32[72,256]{1,0:T(8,128)S(1)}, u32[]{:S(2)}, u32[]{:S(2)}) collective-permute-start(f32[72,256]{1,0:T(8,128)S(1)} %pair.1.refs_1_), channel_id=1, source_target_pairs={{0,2},{1,3},{2,0},{3,1},{4,6},{5,7},{6,4},{7,5},{8,10},{9,11},{10,... | collective-permute-start | bytes 221192 | tf_op jit(solution)/shard_map/ppermute | solution.py:1251
  19.0 2.4 %collective-permute-start.4 = (f32[72,256]{1,0:T(8,128)S(1)}, f32[72,256]{1,0:T(8,128)S(1)}, u32[]{:S(2)}, u32[]{:S(2)}) collective-permute-start(f32[72,256]{1,0:T(8,128)S(1)} %pair.1.refs_1_), channel_id=1, source_target_pairs={{0,4},{1,5},{2,6},{3,7},{4,0},{5,1},{6,2},{7,3},{8,12},{9,13},{10,... | collective-permute-start | bytes 221192 | tf_op jit(solution)/shard_map/ppermute | solution.py:1251
  21.4 2.1 %ready.1 = (f32[128,256]{1,0:T(8,128)S(1)}, f32[128,256]{1,0:T(8,128)S(1)}, bf16[256,256]{1,0:T(8,128)(2,1)S(1)}, bf16[256,256]{1,0:T(8,128)(2,1)S(1)}, bf16[256...) custom-call(f32[128,256]{1,0:T(8,128)S(1)} %get-tuple-element.160.to, ...), custom_call_target="tpu_custom_call" | custom-call | tf_op jit(solution)/shard_map/ready/pallas_call | solution.py:720
  23.5 1.3 %collective-permute-done.4.refs_3_ = f32[72,256]{1,0:T(8,128)S(1)} collective-permute-done((f32[72,256]{1,0:T(8,128)S(1)}, f32[72,256]{1,0:T(8,128)S(1)}, u32[]{:S(2)}, u32[]{:S(2)}) %collective-permute-start.4) | collective-permute-done | bytes 73760 | tf_op jit(solution)/shard_map/ppermute | solution.py:1251
  24.8 1.8 %collective-permute-done.5.refs_4_ = f32[72,256]{1,0:T(8,128)S(1)} collective-permute-done((f32[72,256]{1,0:T(8,128)S(1)}, f32[72,256]{1,0:T(8,128)S(1)}, u32[]{:S(2)}, u32[]{:S(2)}) %collective-permute-start.5) | collective-permute-done | bytes 73760 | tf_op jit(solution)/shard_map/ppermute | solution.py:1251
  26.7 1.6 %collective-permute-start.6 = (f32[40,256]{1,0:T(8,128)S(1)}, f32[40,256]{1,0:T(8,128)S(1)}, u32[]{:S(2)}, u32[]{:S(2)}) collective-permute-start(f32[40,256]{1,0:T(8,128)S(1)} %get-tuple-element.216), channel_id=1, source_target_pairs={{0,8},{1,9},{2,10},{3,11},{4,12},{5,13},{6,14},{7,15},{8,0},{9,1},... | collective-permute-start | bytes 122888 | tf_op jit(solution)/shard_map/ppermute | solution.py:1251
  28.4 1.1 %collective-permute-start.7 = (f32[40,256]{1,0:T(8,128)S(1)}, f32[40,256]{1,0:T(8,128)S(1)}, u32[]{:S(2)}, u32[]{:S(2)}) collective-permute-start(f32[40,256]{1,0:T(8,128)S(1)} %get-tuple-element.217), channel_id=1, source_target_pairs={{0,16},{1,17},{2,18},{3,19},{4,20},{5,21},{6,22},{7,23},{8,24},{9,... | collective-permute-start | bytes 122888 | tf_op jit(solution)/shard_map/ppermute | solution.py:1251
  29.5 1.7 %collective-permute-start.8 = (f32[40,256]{1,0:T(8,128)S(1)}, f32[40,256]{1,0:T(8,128)S(1)}, u32[]{:S(2)}, u32[]{:S(2)}) collective-permute-start(f32[40,256]{1,0:T(8,128)S(1)} %get-tuple-element.218), channel_id=1, source_target_pairs={{0,24},{1,25},{2,26},{3,27},{4,28},{5,29},{6,30},{7,31},{8,16},{9,... | collective-permute-start | bytes 122888 | tf_op jit(solution)/shard_map/ppermute | solution.py:1251
  31.2 2.6 %collective-permute-done.7.refs_2_ = f32[40,256]{1,0:T(8,128)S(1)} collective-permute-done((f32[40,256]{1,0:T(8,128)S(1)}, f32[40,256]{1,0:T(8,128)S(1)}, u32[]{:S(2)}, u32[]{:S(2)}) %collective-permute-start.7) | collective-permute-done | bytes 40992 | tf_op jit(solution)/shard_map/ppermute | solution.py:1251
  33.7 1.5 %collective-permute-done.8.refs_3_ = f32[40,256]{1,0:T(8,128)S(1)} collective-permute-done((f32[40,256]{1,0:T(8,128)S(1)}, f32[40,256]{1,0:T(8,128)S(1)}, u32[]{:S(2)}, u32[]{:S(2)}) %collective-permute-start.8) | collective-permute-done | bytes 40992 | tf_op jit(solution)/shard_map/ppermute | solution.py:1251
  35.5 1.2 %collective-permute-done.9.other_half = f32[64,256]{1,0:T(8,128)S(1)} collective-permute-done((f32[64,256]{1,0:T(8,128)S(1)}, f32[64,256]{1,0:T(8,128)S(1)}, u32[]{:S(2)}, u32[]{:S(2)}) %collective-permute-start.9) | collective-permute-done | bytes 65568 | tf_op jit(solution)/shard_map/ppermute | solution.py:1251
  36.7 2.1 %forward.1 = (f32[256,512]{1,0:T(8,128)S(1)}, f32[2,17,16,8,512]{4,3,2,1,0:T(8,128)S(1)}, f32[64,8,512]{2,1,0:T(8,128)S(1)}) custom-call(f32[64,256]{1,0:T(8,128)S(1)} %enter.1.mine_half, f32[64,256]{1,0:T(8,128)S(1)} %collective-permute-done.9.other_half, f32[72,512]{1,0:T(8,128)S(1)} %collective-permute-done.2.theirs.sibling, ...), custom_call_target="tpu_custom_call" | custom-call | tf_op jit(solution)/shard_map/forward/pallas_call | solution.py:664
  38.8 1.9 %early.1 = (f32[128,256]{1,0:T(8,128)}, bf16[256,512]{1,0:T(8,128)(2,1)S(1)}, bf16[256,512]{1,0:T(8,128)(2,1)S(1)}, f32[32,64,128]{2,1,0:T(8,128)S(1)}) custom-call(f32[128,256]{1,0:T(8,128)S(1)} %get-tuple-element.204.refs_0_.refs_3_, bf16[256,256]{1,0:T(8,128)(2,1)S(1)} %get-tuple-element.205.refs_1_.refs_5_, ...), custom_call_target="tpu_custom_call" | custom-call | tf_op jit(solution)/shard_map/early/pallas_call | solution.py:756
  41.0 2.9 %backward.2 = (f32[128,512]{1,0:T(8,128)S(1)}, f32[128,512]{1,0:T(8,128)S(1)}, f32[128,2048]{1,0:T(8,128)S(1)}, f32[128,2048]{1,0:T(8,128)S(1)}, f32[16,8,512]{2,1,0:T(8,128)S(1)}) custom-call(f32[2,16,8,512]{3,2,1,0:T(8,128)S(1)} %get-tuple-element.229.refs_0_, f32[64,8,512]{2,1,0:T(8,128)S(1)} %get-tuple-element.230.refs_1_, ...), custom_call_target="tpu_custom_call" | custom-call | tf_op jit(solution)/shard_map/backward/pallas_call | solution.py:874
  44.0 1.1 %collective-permute-start.11 = (f32[8,64,128]{2,1,0:T(8,128)S(1)}, f32[8,64,128]{2,1,0:T(8,128)S(1)}, u32[]{:S(2)}, u32[]{:S(2)}) collective-permute-start(f32[8,64,128]{2,1,0:T(8,128)S(1)} %slice.60), channel_id=1, source_target_pairs={{0,2},{1,3},{2,0},{3,1},{4,6},{5,7},{6,4},{7,5},{8,10},{9,11},{10,... | collective-permute-start | bytes 786440 | tf_op jit(solution)/shard_map/ppermute | solution.py:1251
  45.1 2.9 %backward.3 = (f32[128,512]{1,0:T(8,128)S(1)}, f32[128,512]{1,0:T(8,128)S(1)}, f32[128,2048]{1,0:T(8,128)S(1)}, f32[128,2048]{1,0:T(8,128)S(1)}, f32[16,8,512]{2,1,0:T(8,128)S(1)}) custom-call(f32[2,16,8,512]{3,2,1,0:T(8,128)S(1)} %get-tuple-element.229.refs_0_, f32[64,8,512]{2,1,0:T(8,128)S(1)} %get-tuple-element.230.refs_1_, ...), custom_call_target="tpu_custom_call" | custom-call | tf_op jit(solution)/shard_map/backward/pallas_call | solution.py:874
  48.0 2.8 %inner.1 = (bf16[256,512]{1,0:T(8,128)(2,1)S(1)}, bf16[256,512]{1,0:T(8,128)(2,1)S(1)}, f32[16,512]{1,0:T(8,128)S(1)}, f32[88,512]{1,0:T(8,128)S(1)}) custom-call(s32[1,128]{1,0:T(1,128)S(1)} %get-tuple-element.161.pad.refs_10_, f32[4,512]{1,0:T(4,128)S(1)} %get-tuple-element.154.conv_w, f32[48,512]{1,0:T(8,128)S(1)} %get-tuple-element.156.w_x, ...), custom_call_target="tpu_custom_call" | custom-call | tf_op jit(solution)/shard_map/inner/pallas_call | solution.py:1017
  50.8 2.9 %tail.1 = (f32[128,256]{1,0:T(8,128)S(1)}, f32[8,256]{1,0:T(8,128)}, f32[8,256]{1,0:T(8,128)}, f32[32,56,128]{2,1,0:T(8,128)S(1)}) custom-call(f32[8,256]{1,0:T(8,128)S(1)} %collective-permute-done.sib.refs_0_, f32[8,256]{1,0:T(8,128)S(1)} %collective-permute-done.1.oth.refs_1_, f32[1,256]{1,0:T(1,128)S(1)} %get-tuple-element.152.gain.refs_2_, ...), custom_call_target="tpu_custom_call" | custom-call | tf_op jit(solution)/shard_map/tail/pallas_call | solution.py:1115
  53.9 1.4 %collective-permute-start.12 = (f32[4,64,128]{2,1,0:T(8,128)S(1)}, f32[4,64,128]{2,1,0:T(8,128)S(1)}, u32[]{:S(2)}, u32[]{:S(2)}) collective-permute-start(f32[4,64,128]{2,1,0:T(8,128)S(1)} %slice.62), channel_id=1, source_target_pairs={{0,4},{1,5},{2,6},{3,7},{4,0},{5,1},{6,2},{7,3},{8,12},{9,13},{10,... | collective-permute-start | bytes 393224 | tf_op jit(solution)/shard_map/ppermute | solution.py:1251
  55.7 1.4 %collective-permute-start.16 = (f32[4,56,128]{2,1,0:T(8,128)S(1)}, f32[4,56,128]{2,1,0:T(8,128)S(1)}, u32[]{:S(2)}, u32[]{:S(2)}) collective-permute-start(f32[4,56,128]{2,1,0:T(8,128)S(1)} %get-tuple-element.287), channel_id=1, source_target_pairs={{0,4},{1,5},{2,6},{3,7},{4,0},{5,1},{6,2},{7,3},{8,12},{9,13},{10,... | collective-permute-start | bytes 344072 | tf_op jit(solution)/shard_map/ppermute | solution.py:1251
  57.2 0.7 collective-permute-start.15
  57.9 1.4 %collective-permute-start.14 = (f32[4,56,128]{2,1,0:T(8,128)S(1)}, f32[4,56,128]{2,1,0:T(8,128)S(1)}, u32[]{:S(2)}, u32[]{:S(2)}) collective-permute-start(f32[4,56,128]{2,1,0:T(8,128)S(1)} %get-tuple-element.286), channel_id=1, source_target_pairs={{0,6},{1,7},{2,4},{3,5},{4,2},{5,3},{6,0},{7,1},{8,14},{9,15},{10,... | collective-permute-start | bytes 344072 | tf_op jit(solution)/shard_map/ppermute | solution.py:1251
  59.3 1.0 %collective-permute-done.12 = f32[4,64,128]{2,1,0:T(8,128)S(1)} collective-permute-done((f32[4,64,128]{2,1,0:T(8,128)S(1)}, f32[4,64,128]{2,1,0:T(8,128)S(1)}, u32[]{:S(2)}, u32[]{:S(2)}) %collective-permute-start.12) | collective-permute-done | bytes 131104 | tf_op jit(solution)/shard_map/ppermute | solution.py:1251
  60.3 4.4 %collective-permute-done.16 = f32[4,56,128]{2,1,0:T(8,128)S(1)} collective-permute-done((f32[4,56,128]{2,1,0:T(8,128)S(1)}, f32[4,56,128]{2,1,0:T(8,128)S(1)}, u32[]{:S(2)}, u32[]{:S(2)}) %collective-permute-start.16) | collective-permute-done | bytes 114720 | tf_op jit(solution)/shard_map/ppermute | solution.py:1251
  65.0 1.4 %collective-permute-start.18 = (f32[1,120,128]{2,1,0:T(8,128)S(1)}, f32[1,120,128]{2,1,0:T(8,128)S(1)}, u32[]{:S(2)}, u32[]{:S(2)}) collective-permute-start(f32[1,120,128]{2,1,0:T(8,128)S(1)} %get-tuple-element.291), channel_id=1, source_target_pairs={{0,8},{1,9},{2,10},{3,11},{4,12},{5,13},{6,14},{7,15},{8,0},{9,1},... | collective-permute-start | bytes 184328 | tf_op jit(solution)/shard_map/ppermute | solution.py:1251
  66.4 2.8 %collective-permute-start.17 = (f32[1,120,128]{2,1,0:T(8,128)S(1)}, f32[1,120,128]{2,1,0:T(8,128)S(1)}, u32[]{:S(2)}, u32[]{:S(2)}) collective-permute-start(f32[1,120,128]{2,1,0:T(8,128)S(1)} %get-tuple-element.289), channel_id=1, source_target_pairs={{0,24},{1,25},{2,26},{3,27},{4,28},{5,29},{6,30},{7,31},{8,16},{9,... | collective-permute-start | bytes 184328 | tf_op jit(solution)/shard_map/ppermute | solution.py:1251
  69.3 1.4 %collective-permute-done.19 = f32[1,120,128]{2,1,0:T(8,128)S(1)} collective-permute-done((f32[1,120,128]{2,1,0:T(8,128)S(1)}, f32[1,120,128]{2,1,0:T(8,128)S(1)}, u32[]{:S(2)}, u32[]{:S(2)}) %collective-permute-start.19) | collective-permute-done | bytes 61472 | tf_op jit(solution)/shard_map/ppermute | solution.py:1251
  70.7 1.8 %collective-permute-done.17 = f32[1,120,128]{2,1,0:T(8,128)S(1)} collective-permute-done((f32[1,120,128]{2,1,0:T(8,128)S(1)}, f32[1,120,128]{2,1,0:T(8,128)S(1)}, u32[]{:S(2)}, u32[]{:S(2)}) %collective-permute-start.17) | collective-permute-done | bytes 61472 | tf_op jit(solution)/shard_map/ppermute | solution.py:1251
  72.5 2.9 %collective-permute-start.22 = (f32[1,112,128]{2,1,0:T(8,128)S(1)}, f32[1,112,128]{2,1,0:T(8,128)S(1)}, u32[]{:S(2)}, u32[]{:S(2)}) collective-permute-start(f32[1,112,128]{2,1,0:T(8,128)S(1)} %slice.86), channel_id=1, source_target_pairs={{0,24},{1,25},{2,26},{3,27},{4,28},{5,29},{6,30},{7,31},{8,16},{9,... | collective-permute-start | bytes 172040 | tf_op jit(solution)/shard_map/ppermute | solution.py:1251
  75.4 1.6 %collective-permute-start.20 = (f32[1,112,128]{2,1,0:T(8,128)S(1)}, f32[1,112,128]{2,1,0:T(8,128)S(1)}, u32[]{:S(2)}, u32[]{:S(2)}) collective-permute-start(f32[1,112,128]{2,1,0:T(8,128)S(1)} %slice.86), channel_id=1, source_target_pairs={{0,16},{1,17},{2,18},{3,19},{4,20},{5,21},{6,22},{7,23},{8,24},{9,... | collective-permute-start | bytes 172040 | tf_op jit(solution)/shard_map/ppermute | solution.py:1251
  77.0 1.8 %collective-permute-done.22 = f32[1,112,128]{2,1,0:T(8,128)S(1)} collective-permute-done((f32[1,112,128]{2,1,0:T(8,128)S(1)}, f32[1,112,128]{2,1,0:T(8,128)S(1)}, u32[]{:S(2)}, u32[]{:S(2)}) %collective-permute-start.22) | collective-permute-done | bytes 57376 | tf_op jit(solution)/shard_map/ppermute | solution.py:1251
  78.8 0.8 collective-permute-done.21
  79.6 0.9 collective-permute-done.20
  80.5 1.5 %collective-permute-start.23 = (f32[4,112,128]{2,1,0:T(8,128)S(1)}, f32[4,112,128]{2,1,0:T(8,128)S(1)}, u32[]{:S(2)}, u32[]{:S(2)}) collective-permute-start(f32[4,112,128]{2,1,0:T(8,128)S(1)} %pad_maximum_fusion.refs_0_), channel_id=1, source_target_pairs={{0,4},{1,5},{2,6},{3,7},{4,0},{5,1},{6,2},{7,3},{8,12},{9,13},{10,... | collective-permute-start | bytes 688136 | tf_op jit(solution)/shard_map/ppermute | solution.py:1251
  82.0 0.6 collective-permute-start.24
  82.6 1.4 %collective-permute-start.25 = (f32[4,112,128]{2,1,0:T(8,128)S(1)}, f32[4,112,128]{2,1,0:T(8,128)S(1)}, u32[]{:S(2)}, u32[]{:S(2)}) collective-permute-start(f32[4,112,128]{2,1,0:T(8,128)S(1)} %pad_maximum_fusion.refs_0_), channel_id=1, source_target_pairs={{0,6},{1,7},{2,4},{3,5},{4,2},{5,3},{6,0},{7,1},{8,14},{9,15},{10,... | collective-permute-start | bytes 688136 | tf_op jit(solution)/shard_map/ppermute | solution.py:1251
  84.0 4.0 %collective-permute-done.23.refs_1_ = f32[4,112,128]{2,1,0:T(8,128)S(1)} collective-permute-done((f32[4,112,128]{2,1,0:T(8,128)S(1)}, f32[4,112,128]{2,1,0:T(8,128)S(1)}, u32[]{:S(2)}, u32[]{:S(2)}) %collective-permute-start.23) | collective-permute-done | bytes 229408 | tf_op jit(solution)/shard_map/ppermute | solution.py:1251
  88.0 0.5 collective-permute-start.28
  88.5 2.0 %collective-permute-done.25.refs_3_ = f32[4,112,128]{2,1,0:T(8,128)S(1)} collective-permute-done((f32[4,112,128]{2,1,0:T(8,128)S(1)}, f32[4,112,128]{2,1,0:T(8,128)S(1)}, u32[]{:S(2)}, u32[]{:S(2)}) %collective-permute-start.25) | collective-permute-done | bytes 229408 | tf_op jit(solution)/shard_map/ppermute | solution.py:1251
  90.5 1.4 %collective-permute-done.29.refs_7_ = f32[4,112,128]{2,1,0:T(8,128)S(1)} collective-permute-done((f32[4,112,128]{2,1,0:T(8,128)S(1)}, f32[4,112,128]{2,1,0:T(8,128)S(1)}, u32[]{:S(2)}, u32[]{:S(2)}) %collective-permute-start.29) | collective-permute-done | bytes 229408 | tf_op jit(solution)/shard_map/ppermute | solution.py:1251
  92.0 1.5 %unpack.1 = (f32[128,256]{1,0:T(8,128)}, f32[1,256]{1,0:T(1,128)}, f32[256,1024]{1,0:T(8,128)}, f32[4,512]{1,0:T(4,128)}, f32[1,512]{1,0:T(1,128)}, /*index=5*/f...) custom-call(f32[4,112,128]{2,1,0:T(8,128)S(1)} %pad_maximum_fusion.r, ...), custom_call_target="tpu_custom_call" | custom-call | tf_op jit(solution)/shard_map/unpack/pallas_call | solution.py:1222
  (44 shorter events, 1.6 us)
Async XLA Ops:
  2.5 2.7 %collective-permute-start = (f32[8,256]{1,0:T(8,128)S(1)}, f32[8,256]{1,0:T(8,128)S(1)}, u32[]{:S(2)}, u32[]{:S(2)}) collective-permute-start(f32[8,256]{1,0:T(8,128)S(1)} %get-tuple-element.149), channel_id=1, source_target_pairs={{0,1},{1,0},{2,3},{3,2},{4,5},{5,4},{6,7},{7,6},{8,9},{9,8},{10,11... | collective-permute-start | bytes 24584 | tf_op jit(solution)/shard_map/ppermute | solution.py:1251
  3.0 2.2 %collective-permute-start.1 = (f32[8,256]{1,0:T(8,128)S(1)}, f32[8,256]{1,0:T(8,128)S(1)}, u32[]{:S(2)}, u32[]{:S(2)}) collective-permute-start(f32[8,256]{1,0:T(8,128)S(1)} %get-tuple-element.150), channel_id=1, source_target_pairs={{1,2},{3,4},{5,6},{7,8},{9,10},{11,12},{13,14},{15,16},{17,18},{19... | collective-permute-start | bytes 24584 | tf_op jit(solution)/shard_map/ppermute | solution.py:1259
  11.2 4.9 %collective-permute-start.2 = (f32[72,512]{1,0:T(8,128)S(1)}, f32[72,512]{1,0:T(8,128)S(1)}, u32[]{:S(2)}, u32[]{:S(2)}) collective-permute-start(f32[72,512]{1,0:T(8,128)S(1)} %get-tuple-element.167.mine), channel_id=1, source_target_pairs={{0,1},{1,0},{2,3},{3,2},{4,5},{5,4},{6,7},{7,6},{8,9},{9,8},{10,11... | collective-permute-start | bytes 442376 | tf_op jit(solution)/shard_map/ppermute | solution.py:1251
  16.1 7.3 %collective-permute-start.3 = (f32[72,256]{1,0:T(8,128)S(1)}, f32[72,256]{1,0:T(8,128)S(1)}, u32[]{:S(2)}, u32[]{:S(2)}) collective-permute-start(f32[72,256]{1,0:T(8,128)S(1)} %pair.1.refs_1_), channel_id=1, source_target_pairs={{0,2},{1,3},{2,0},{3,1},{4,6},{5,7},{6,4},{7,5},{8,10},{9,11},{10,... | collective-permute-start | bytes 221192 | tf_op jit(solution)/shard_map/ppermute | solution.py:1251
  19.0 5.9 %collective-permute-start.4 = (f32[72,256]{1,0:T(8,128)S(1)}, f32[72,256]{1,0:T(8,128)S(1)}, u32[]{:S(2)}, u32[]{:S(2)}) collective-permute-start(f32[72,256]{1,0:T(8,128)S(1)} %pair.1.refs_1_), channel_id=1, source_target_pairs={{0,4},{1,5},{2,6},{3,7},{4,0},{5,1},{6,2},{7,3},{8,12},{9,13},{10,... | collective-permute-start | bytes 221192 | tf_op jit(solution)/shard_map/ppermute | solution.py:1251
  21.4 5.3 %collective-permute-start.5 = (f32[72,256]{1,0:T(8,128)S(1)}, f32[72,256]{1,0:T(8,128)S(1)}, u32[]{:S(2)}, u32[]{:S(2)}) collective-permute-start(f32[72,256]{1,0:T(8,128)S(1)} %pair.1.refs_1_), channel_id=1, source_target_pairs={{0,6},{1,7},{2,4},{3,5},{4,2},{5,3},{6,0},{7,1},{8,14},{9,15},{10,... | collective-permute-start | bytes 221192 | tf_op jit(solution)/shard_map/ppermute | solution.py:1251
  26.7 4.5 %collective-permute-start.6 = (f32[40,256]{1,0:T(8,128)S(1)}, f32[40,256]{1,0:T(8,128)S(1)}, u32[]{:S(2)}, u32[]{:S(2)}) collective-permute-start(f32[40,256]{1,0:T(8,128)S(1)} %get-tuple-element.216), channel_id=1, source_target_pairs={{0,8},{1,9},{2,10},{3,11},{4,12},{5,13},{6,14},{7,15},{8,0},{9,1},... | collective-permute-start | bytes 122888 | tf_op jit(solution)/shard_map/ppermute | solution.py:1251
  28.4 5.4 %collective-permute-start.7 = (f32[40,256]{1,0:T(8,128)S(1)}, f32[40,256]{1,0:T(8,128)S(1)}, u32[]{:S(2)}, u32[]{:S(2)}) collective-permute-start(f32[40,256]{1,0:T(8,128)S(1)} %get-tuple-element.217), channel_id=1, source_target_pairs={{0,16},{1,17},{2,18},{3,19},{4,20},{5,21},{6,22},{7,23},{8,24},{9,... | collective-permute-start | bytes 122888 | tf_op jit(solution)/shard_map/ppermute | solution.py:1251
  29.5 5.8 %collective-permute-start.8 = (f32[40,256]{1,0:T(8,128)S(1)}, f32[40,256]{1,0:T(8,128)S(1)}, u32[]{:S(2)}, u32[]{:S(2)}) collective-permute-start(f32[40,256]{1,0:T(8,128)S(1)} %get-tuple-element.218), channel_id=1, source_target_pairs={{0,24},{1,25},{2,26},{3,27},{4,28},{5,29},{6,30},{7,31},{8,16},{9,... | collective-permute-start | bytes 122888 | tf_op jit(solution)/shard_map/ppermute | solution.py:1251
  35.4 1.3 %collective-permute-start.9 = (f32[64,256]{1,0:T(8,128)S(1)}, f32[64,256]{1,0:T(8,128)S(1)}, u32[]{:S(2)}, u32[]{:S(2)}) collective-permute-start(f32[64,256]{1,0:T(8,128)S(1)} %enter.1.mine_half), channel_id=1, source_target_pairs={{0,1},{1,0},{2,3},{3,2},{4,5},{5,4},{6,7},{7,6},{8,9},{9,8},{10,11... | collective-permute-start | bytes 196616 | tf_op jit(solution)/shard_map/ppermute | solution.py:1251
  40.8 3.1 %collective-permute-start.10 = (f32[16,64,128]{2,1,0:T(8,128)S(1)}, f32[16,64,128]{2,1,0:T(8,128)S(1)}, u32[]{:S(2)}, u32[]{:S(2)}) collective-permute-start(f32[16,64,128]{2,1,0:T(8,128)S(1)} %slice.58), channel_id=1, source_target_pairs={{0,1},{1,0},{2,3},{3,2},{4,5},{5,4},{6,7},{7,6},{8,9},{9,8},{10,11... | collective-permute-start | bytes 1572872 | tf_op jit(solution)/shard_map/ppermute | solution.py:1251
  44.0 9.7 %collective-permute-start.11 = (f32[8,64,128]{2,1,0:T(8,128)S(1)}, f32[8,64,128]{2,1,0:T(8,128)S(1)}, u32[]{:S(2)}, u32[]{:S(2)}) collective-permute-start(f32[8,64,128]{2,1,0:T(8,128)S(1)} %slice.60), channel_id=1, source_target_pairs={{0,2},{1,3},{2,0},{3,1},{4,6},{5,7},{6,4},{7,5},{8,10},{9,11},{10,... | collective-permute-start | bytes 786440 | tf_op jit(solution)/shard_map/ppermute | solution.py:1251
  53.8 1.9 %collective-permute-start.13 = (f32[16,56,128]{2,1,0:T(8,128)S(1)}, f32[16,56,128]{2,1,0:T(8,128)S(1)}, u32[]{:S(2)}, u32[]{:S(2)}) collective-permute-start(f32[16,56,128]{2,1,0:T(8,128)S(1)} %slice.64), channel_id=1, source_target_pairs={{0,1},{1,0},{2,3},{3,2},{4,5},{5,4},{6,7},{7,6},{8,9},{9,8},{10,11... | collective-permute-start | bytes 1376264 | tf_op jit(solution)/shard_map/ppermute | solution.py:1251
  53.9 6.4 %collective-permute-start.12 = (f32[4,64,128]{2,1,0:T(8,128)S(1)}, f32[4,64,128]{2,1,0:T(8,128)S(1)}, u32[]{:S(2)}, u32[]{:S(2)}) collective-permute-start(f32[4,64,128]{2,1,0:T(8,128)S(1)} %slice.62), channel_id=1, source_target_pairs={{0,4},{1,5},{2,6},{3,7},{4,0},{5,1},{6,2},{7,3},{8,12},{9,13},{10,... | collective-permute-start | bytes 393224 | tf_op jit(solution)/shard_map/ppermute | solution.py:1251
  55.7 9.0 %collective-permute-start.16 = (f32[4,56,128]{2,1,0:T(8,128)S(1)}, f32[4,56,128]{2,1,0:T(8,128)S(1)}, u32[]{:S(2)}, u32[]{:S(2)}) collective-permute-start(f32[4,56,128]{2,1,0:T(8,128)S(1)} %get-tuple-element.287), channel_id=1, source_target_pairs={{0,4},{1,5},{2,6},{3,7},{4,0},{5,1},{6,2},{7,3},{8,12},{9,13},{10,... | collective-permute-start | bytes 344072 | tf_op jit(solution)/shard_map/ppermute | solution.py:1251
  57.2 7.6 %collective-permute-start.15 = (f32[4,56,128]{2,1,0:T(8,128)S(1)}, f32[4,56,128]{2,1,0:T(8,128)S(1)}, u32[]{:S(2)}, u32[]{:S(2)}) collective-permute-start(f32[4,56,128]{2,1,0:T(8,128)S(1)} %get-tuple-element.288), channel_id=1, source_target_pairs={{0,2},{1,3},{2,0},{3,1},{4,6},{5,7},{6,4},{7,5},{8,10},{9,11},{10,... | collective-permute-start | bytes 344072 | tf_op jit(solution)/shard_map/ppermute | solution.py:1251
  57.9 6.9 %collective-permute-start.14 = (f32[4,56,128]{2,1,0:T(8,128)S(1)}, f32[4,56,128]{2,1,0:T(8,128)S(1)}, u32[]{:S(2)}, u32[]{:S(2)}) collective-permute-start(f32[4,56,128]{2,1,0:T(8,128)S(1)} %get-tuple-element.286), channel_id=1, source_target_pairs={{0,6},{1,7},{2,4},{3,5},{4,2},{5,3},{6,0},{7,1},{8,14},{9,15},{10,... | collective-permute-start | bytes 344072 | tf_op jit(solution)/shard_map/ppermute | solution.py:1251
  64.8 5.8 %collective-permute-start.19 = (f32[1,120,128]{2,1,0:T(8,128)S(1)}, f32[1,120,128]{2,1,0:T(8,128)S(1)}, u32[]{:S(2)}, u32[]{:S(2)}) collective-permute-start(f32[1,120,128]{2,1,0:T(8,128)S(1)} %get-tuple-element.290), channel_id=1, source_target_pairs={{0,16},{1,17},{2,18},{3,19},{4,20},{5,21},{6,22},{7,23},{8,24},{9,... | collective-permute-start | bytes 184328 | tf_op jit(solution)/shard_map/ppermute | solution.py:1251
  65.0 5.6 %collective-permute-start.18 = (f32[1,120,128]{2,1,0:T(8,128)S(1)}, f32[1,120,128]{2,1,0:T(8,128)S(1)}, u32[]{:S(2)}, u32[]{:S(2)}) collective-permute-start(f32[1,120,128]{2,1,0:T(8,128)S(1)} %get-tuple-element.291), channel_id=1, source_target_pairs={{0,8},{1,9},{2,10},{3,11},{4,12},{5,13},{6,14},{7,15},{8,0},{9,1},... | collective-permute-start | bytes 184328 | tf_op jit(solution)/shard_map/ppermute | solution.py:1251
  66.4 6.1 %collective-permute-start.17 = (f32[1,120,128]{2,1,0:T(8,128)S(1)}, f32[1,120,128]{2,1,0:T(8,128)S(1)}, u32[]{:S(2)}, u32[]{:S(2)}) collective-permute-start(f32[1,120,128]{2,1,0:T(8,128)S(1)} %get-tuple-element.289), channel_id=1, source_target_pairs={{0,24},{1,25},{2,26},{3,27},{4,28},{5,29},{6,30},{7,31},{8,16},{9,... | collective-permute-start | bytes 184328 | tf_op jit(solution)/shard_map/ppermute | solution.py:1251
  72.5 6.2 %collective-permute-start.22 = (f32[1,112,128]{2,1,0:T(8,128)S(1)}, f32[1,112,128]{2,1,0:T(8,128)S(1)}, u32[]{:S(2)}, u32[]{:S(2)}) collective-permute-start(f32[1,112,128]{2,1,0:T(8,128)S(1)} %slice.86), channel_id=1, source_target_pairs={{0,24},{1,25},{2,26},{3,27},{4,28},{5,29},{6,30},{7,31},{8,16},{9,... | collective-permute-start | bytes 172040 | tf_op jit(solution)/shard_map/ppermute | solution.py:1251
  75.4 4.2 %collective-permute-start.21 = (f32[1,112,128]{2,1,0:T(8,128)S(1)}, f32[1,112,128]{2,1,0:T(8,128)S(1)}, u32[]{:S(2)}, u32[]{:S(2)}) collective-permute-start(f32[1,112,128]{2,1,0:T(8,128)S(1)} %slice.86), channel_id=1, source_target_pairs={{0,8},{1,9},{2,10},{3,11},{4,12},{5,13},{6,14},{7,15},{8,0},{9,1},... | collective-permute-start | bytes 172040 | tf_op jit(solution)/shard_map/ppermute | solution.py:1251
  75.4 5.1 %collective-permute-start.20 = (f32[1,112,128]{2,1,0:T(8,128)S(1)}, f32[1,112,128]{2,1,0:T(8,128)S(1)}, u32[]{:S(2)}, u32[]{:S(2)}) collective-permute-start(f32[1,112,128]{2,1,0:T(8,128)S(1)} %slice.86), channel_id=1, source_target_pairs={{0,16},{1,17},{2,18},{3,19},{4,20},{5,21},{6,22},{7,23},{8,24},{9,... | collective-permute-start | bytes 172040 | tf_op jit(solution)/shard_map/ppermute | solution.py:1251
  80.5 7.5 %collective-permute-start.23 = (f32[4,112,128]{2,1,0:T(8,128)S(1)}, f32[4,112,128]{2,1,0:T(8,128)S(1)}, u32[]{:S(2)}, u32[]{:S(2)}) collective-permute-start(f32[4,112,128]{2,1,0:T(8,128)S(1)} %pad_maximum_fusion.refs_0_), channel_id=1, source_target_pairs={{0,4},{1,5},{2,6},{3,7},{4,0},{5,1},{6,2},{7,3},{8,12},{9,13},{10,... | collective-permute-start | bytes 688136 | tf_op jit(solution)/shard_map/ppermute | solution.py:1251
  82.0 6.0 %collective-permute-start.24 = (f32[4,112,128]{2,1,0:T(8,128)S(1)}, f32[4,112,128]{2,1,0:T(8,128)S(1)}, u32[]{:S(2)}, u32[]{:S(2)}) collective-permute-start(f32[4,112,128]{2,1,0:T(8,128)S(1)} %pad_maximum_fusion.refs_0_), channel_id=1, source_target_pairs={{0,2},{1,3},{2,0},{3,1},{4,6},{5,7},{6,4},{7,5},{8,10},{9,11},{10,... | collective-permute-start | bytes 688136 | tf_op jit(solution)/shard_map/ppermute | solution.py:1251
  82.6 7.9 %collective-permute-start.25 = (f32[4,112,128]{2,1,0:T(8,128)S(1)}, f32[4,112,128]{2,1,0:T(8,128)S(1)}, u32[]{:S(2)}, u32[]{:S(2)}) collective-permute-start(f32[4,112,128]{2,1,0:T(8,128)S(1)} %pad_maximum_fusion.refs_0_), channel_id=1, source_target_pairs={{0,6},{1,7},{2,4},{3,5},{4,2},{5,3},{6,0},{7,1},{8,14},{9,15},{10,... | collective-permute-start | bytes 688136 | tf_op jit(solution)/shard_map/ppermute | solution.py:1251
  84.0 6.5 %collective-permute-start.26 = (f32[4,112,128]{2,1,0:T(8,128)S(1)}, f32[4,112,128]{2,1,0:T(8,128)S(1)}, u32[]{:S(2)}, u32[]{:S(2)}) collective-permute-start(f32[4,112,128]{2,1,0:T(8,128)S(1)} %pad_maximum_fusion.refs_0_), channel_id=1, source_target_pairs={{0,1},{1,0},{2,3},{3,2},{4,5},{5,4},{6,7},{7,6},{8,9},{9,8},{10,11... | collective-permute-start | bytes 688136 | tf_op jit(solution)/shard_map/ppermute | solution.py:1251
  88.0 2.5 %collective-permute-start.27 = (f32[4,112,128]{2,1,0:T(8,128)S(1)}, f32[4,112,128]{2,1,0:T(8,128)S(1)}, u32[]{:S(2)}, u32[]{:S(2)}) collective-permute-start(f32[4,112,128]{2,1,0:T(8,128)S(1)} %collective-permute-done.23.refs_1_), channel_id=1, source_target_pairs={{0,1},{1,0},{2,3},{3,2},{4,5},{5,4},{6,7},{7,6},{8,9},{9,8},{10,11... | collective-permute-start | bytes 688136 | tf_op jit(solution)/shard_map/ppermute | solution.py:1251
  88.0 2.5 %collective-permute-start.28 = (f32[4,112,128]{2,1,0:T(8,128)S(1)}, f32[4,112,128]{2,1,0:T(8,128)S(1)}, u32[]{:S(2)}, u32[]{:S(2)}) collective-permute-start(f32[4,112,128]{2,1,0:T(8,128)S(1)} %collective-permute-done.24.refs_2_), channel_id=1, source_target_pairs={{0,1},{1,0},{2,3},{3,2},{4,5},{5,4},{6,7},{7,6},{8,9},{9,8},{10,11... | collective-permute-start | bytes 688136 | tf_op jit(solution)/shard_map/ppermute | solution.py:1251
  90.5 1.5 %collective-permute-start.29 = (f32[4,112,128]{2,1,0:T(8,128)S(1)}, f32[4,112,128]{2,1,0:T(8,128)S(1)}, u32[]{:S(2)}, u32[]{:S(2)}) collective-permute-start(f32[4,112,128]{2,1,0:T(8,128)S(1)} %collective-permute-done.25.refs_3_), channel_id=1, source_target_pairs={{0,1},{1,0},{2,3},{3,2},{4,5},{5,4},{6,7},{7,6},{8,9},{9,8},{10,11... | collective-permute-start | bytes 688136 | tf_op jit(solution)/shard_map/ppermute | solution.py:1251

commit v4 on v3

--- a/solution.py
+++ b/solution.py
@@ -80,9 +80,9 @@
     ref[...] = exact(tn, order_matrix(ref.shape[0]), value)
 
 
-def spread(row):
+def spread(row, order=None):
     length = row.shape[1]
-    picked = (order_matrix(length) * row).astype(BF16)
+    picked = ((order_matrix(length) if order is None else order) * row).astype(BF16)
     return nn(picked, jnp.ones((length, LANE), BF16))
 
 
@@ -147,11 +147,13 @@
     return found[0], found[1], found[2:]
 
 
-def project_kernel(tok, pad, gain, w_in, gout, w_out, xb_o, z_o, go_o, gy_o):
+def project_kernel(tok, pad, gain, w_in, gout, w_out, a_log, xb_o, z_o, go_o, gy_o, wih_o, wil_o, spread_o, a2_o):
     inner = w_out.shape[0]
     x = ordered(tok)
     normed = normalize(x, gain[...])[1]
-    proj = mm(nn, both_orders(normed), split(w_in[...]))
+    w_parts = split(w_in[...])
+    wih_o[...], wil_o[...] = w_parts
+    proj = mm(nn, both_orders(normed), w_parts)
     pad_col = spread(pad[...].astype(F32))
     pad_all = jnp.concatenate([pad_col, pad_col], axis=0)
     g = ordered(gout)
@@ -164,16 +166,30 @@
         z_o[:, cols] = z
         go_o[:, cols] = go[:, cols]
         gy_o[:, cols] = go[:, cols] * (z * sigmoid(z))
-
-
-def project(tok, pad, gain, w_in, gout, w_out):
+    width = spread_o.shape[0] // 3
+    row = lax.broadcasted_iota(jnp.int32, spread_o.shape, 0)
+    entry = lax.broadcasted_iota(jnp.int32, spread_o.shape, 1) >> 7
+    row = jnp.where(row >= 2 * width, row - 2 * width, jnp.where(row >= width, row - width, row))
+    spread_o[...] = jnp.where(row == entry, 1.0, 0.0).astype(BF16)
+    a2 = jnp.exp(a_log[...]) * (-LOG2E)
+    for n in range(a2.shape[0]):
+        a2_o[n] = jnp.broadcast_to(a2[n : n + 1], (CH, inner))
+
+
+def project(tok, pad, gain, w_in, gout, w_out, a_log):
     big = jax.ShapeDtypeStruct((2 * tok.shape[0], w_out.shape[0]), F32)
+    part = jax.ShapeDtypeStruct(w_in.shape, BF16)
+    state, inner = a_log.shape
     return pl.pallas_call(
         project_kernel,
-        out_shape=(big, big, big, big),
+        out_shape=(
+            big, big, big, big, part, part,
+            jax.ShapeDtypeStruct((6 * state, 2 * state * LANE), BF16),
+            jax.ShapeDtypeStruct((state, CH, inner), F32),
+        ),
         compiler_params=params(8),
         name="project",
-    )(tok, pad, gain, w_in, gout, w_out)
+    )(tok, pad, gain, w_in, gout, w_out, a_log)
 
 
 def pick_sides(from_sibling, from_other):
@@ -226,12 +242,12 @@
 
 
 def prepare_kernel(
-    sib, oth, keep, gain, w_in, conv_w, conv_b, w_x, w_dt, dt_bias, a_log, xb, gy,
-    xc_o, dt_o, sig_o, conv_o, mask_o, dbl_o, xbh_o, sx_o, mx_o, sum_o, de_s, dx_s, bc_s, a2_s, decay_o,
+    sib, oth, keep, gain, wih, wil, conv_w, conv_b, w_x, w_dt, dt_bias, spread_s, a2_s, xb, gy,
+    xc_o, dt_o, pre_o, conv_o, mask_o, dbl_o, xbh_o, sx_o, mx_o, sum_o, de_s, dx_s, bc_s, decay_o, drive_o,
     leave_s,
 ):
     inner, rank = w_x.shape[1], w_dt.shape[0]
-    state = a_log.shape[0]
+    state = a2_s.shape[0]
     length = xb.shape[0] // 2
     steps = length // CH
     tiles = inner // LANE
@@ -245,7 +261,7 @@
         jnp.concatenate([lh, nn(rh, flip).astype(BF16)], axis=0),
         jnp.concatenate([ll, nn(rl, flip).astype(BF16)], axis=0),
     )
-    xbh = mm(nn, halo, split(w_in[:, :inner]))
+    xbh = mm(nn, halo, (wih[:, :inner], wil[:, :inner]))
     xbh_o[...] = xbh
     lane = lax.broadcasted_iota(jnp.int32, (1, length), 1)
     here = 1.0 - keep[...].astype(F32)
@@ -267,8 +283,9 @@
     r1 = ahead(1)
     r2 = r1 * ahead(2)
     r3 = r2 * ahead(3)
+    token_order = order_matrix(length)
     for i, row in enumerate((f1, f2, f3, r1, r2, r3)):
-        mask_o[i * length : (i + 1) * length, :] = spread(row)
+        mask_o[i * length : (i + 1) * length, :] = spread(row, token_order)
 
     sub = sub_iota()
 
@@ -308,10 +325,7 @@
     dbl = mm(nt, xc_o[...], w_x[...])
     dbl_o[...] = dbl
     pre_all = mm(nn, dbl[:, :rank], w_dt[...])
-    expand_bc(dbl, rank, state, bc_s)
-    a2 = jnp.exp(a_log[...]) * (-LOG2E)
-    for n in range(state):
-        a2_s[n] = jnp.broadcast_to(a2[n : n + 1], (CH, inner))
+    bc_s[...] = nn(jnp.concatenate(split3(dbl[:, rank:]), axis=1), spread_s[...])
     for lt in range(tiles):
         cols = slice(lt * LANE, (lt + 1) * LANE)
         pre = pre_all[:, cols] + dt_bias[:, cols]
@@ -320,12 +334,12 @@
         log1p = jnp.where(u == 1.0, e, jnp.log(u) * (e / (u - 1.0)))
         dt = jnp.maximum(pre, 0.0) + log1p
         dt_o[:, cols] = dt
-        sig_o[:, cols] = jnp.where(pre >= 0.0, 1.0, e) / u
+        pre_o[:, cols] = pre
         dx_s[:, cols] = dt * xc_o[:, cols]
         cut = jnp.concatenate([mask_o[:length], mask_o[3 * length : 4 * length]], axis=0)
         de_s[:, cols] = dt + BIG * (1.0 - cut)
 
-    group = 4
+    group = 8
     cols_of = [slice(t * LANE, (t + 1) * LANE) for t in range(tiles)]
     for dirn in range(2):
         order = list(range(steps)) if dirn == 0 else list(range(steps - 1, -1, -1))
@@ -355,7 +369,9 @@
                     for t, cols in enumerate(cols_of):
                         d = jnp.exp2(de[t] * a2[n, t])
                         decay_o[dirn, at, n0 + n, :, cols] = d
-                        h[n, t] = dx[t] * b_n if at == 0 else d * h[n, t] + dx[t] * b_n
+                        drive = dx[t] * b_n
+                        drive_o[dirn, at, n0 + n, :, cols] = drive
+                        h[n, t] = drive if at == 0 else d * h[n, t] + drive
             for at in range(steps - 1, -1, -1):
                 rows = slice(base + order[at] * CH, base + (order[at] + 1) * CH)
                 gyj = [gy[rows, c] for c in cols_of]
@@ -387,20 +403,9 @@
     return [pl.ds(pl.multiple_of((first + n) * LANE, LANE), LANE) for n in range(count)]
 
 
-def expand_bc(dbl, rank, state, bc_s):
-    pieces = split3(dbl[:, rank:])
-    width = dbl.shape[1] - rank
-    lhs = jnp.concatenate(pieces, axis=1)
-    rows = lax.broadcasted_iota(jnp.int32, (3 * width, width * LANE), 0)
-    cols = lax.broadcasted_iota(jnp.int32, (3 * width, width * LANE), 1)
-    entry = cols >> 7
-    hit = (rows == entry) | (rows == entry + width) | (rows == entry + 2 * width)
-    bc_s[...] = nn(lhs, jnp.where(hit, 1.0, 0.0).astype(BF16))
-
-
-def prepare(sib, oth, keep, gain, w_in, conv_w, conv_b, w_x, w_dt, dt_bias, a_log, xb, gy):
+def prepare(sib, oth, keep, gain, wih, wil, conv_w, conv_b, w_x, w_dt, dt_bias, spread_s, a2, xb, gy):
     rows, inner = xb.shape
-    state, width = a_log.shape[0], w_x.shape[0]
+    state, width = a2.shape[0], w_x.shape[0]
     big = pltpu.VMEM((rows, inner), F32)
     edge = pltpu.VMEM((2, state, CH, inner), F32)
     return pl.pallas_call(
@@ -414,13 +419,13 @@
             pltpu.VMEM((4 * state + 8, inner), F32),
             big, big,
             pltpu.VMEM((rows, 2 * state * LANE), F32),
-            pltpu.VMEM((state, CH, inner), F32),
+            pltpu.VMEM((2, rows // 2 // CH, state, CH, inner), F32),
             pltpu.VMEM((2, rows // 2 // CH, state, CH, inner), F32),
         ),
         scratch_shapes=[pltpu.VMEM((4 * state, CH, inner), F32)],
         compiler_params=params(8),
         name="prepare",
-    )(sib, oth, keep, gain, w_in, conv_w, conv_b, w_x, w_dt, dt_bias, a_log, xb, gy)
+    )(sib, oth, keep, gain, wih, wil, conv_w, conv_b, w_x, w_dt, dt_bias, spread_s, a2, xb, gy)
 
 
 def summary_parts(ref_value, state):
@@ -607,7 +612,7 @@
 
 
 def forward_kernel(
-    mine_half, other_half, sibling, sx, de_s, dx_s, bc_s, a2_s, decay,
+    mine_half, other_half, sibling, sx, de_s, dx_s, bc_s, a2_s, decay, drive,
     y_s, h_s, car_o,
     before_s,
 ):
@@ -644,9 +649,9 @@
                 dx = [dx_s[rows, c] for c in cols_of]
                 y = [None] * tiles
                 for n in range(group):
-                    b_n, c_n = bc_s[rows, at_b[n]], bc_s[rows, at_c[n]]
+                    c_n = bc_s[rows, at_c[n]]
                     for t, cols in enumerate(cols_of):
-                        h[n, t] = decay[dirn, at, n0 + n, :, cols] * h[n, t] + dx[t] * b_n
+                        h[n, t] = decay[dirn, at, n0 + n, :, cols] * h[n, t] + drive[dirn, at, n0 + n, :, cols]
                         h_s[dirn, at + 1, n0 + n, :, cols] = h[n, t]
                         term = h[n, t] * c_n
                         y[t] = term if n == 0 else y[t] + term
@@ -657,7 +662,7 @@
         lax.fori_loop(0, state // group, some, 0)
 
 
-def forward(mine_half, other_half, sibling, sx, de, dx, bc, a2, decay):
+def forward(mine_half, other_half, sibling, sx, de, dx, bc, a2, decay, drive):
     rows2, inner = de.shape
     state = a2.shape[0]
     steps = rows2 // 2 // CH
@@ -671,13 +676,13 @@
         scratch_shapes=[pltpu.VMEM((CH, inner), F32)],
         compiler_params=params(4),
         name="forward",
-    )(mine_half, other_half, sibling, sx, de, dx, bc, a2, decay)
+    )(mine_half, other_half, sibling, sx, de, dx, bc, a2, decay, drive)
 
 
 def ready_kernel(
-    rank, tok, gout, gain, w_in, w_out, d_skip, z, go, conv, xc, gy,
-    x_o, g_o, nth_o, ntl_o, gh_o, gl_o, wih_o, wil_o, wfh_o, wfl_o, woh_o, wol_o, vfh_o, vfl_o,
-    gate_o, zgrad_o, cgrad_o, xch_o, xcl_o, skip_o, pickb_o, pickc_o,
+    rank, tok, gout, gain, wih, wil, w_out, d_skip, z, go, conv, pre, xc, gy,
+    x_o, g_o, nth_o, ntl_o, gh_o, gl_o, wfh_o, wfl_o, woh_o, wol_o, vfh_o, vfl_o,
+    gate_o, zgrad_o, cgrad_o, sig_o, xch_o, xcl_o, skip_o, pickb_o, pickc_o,
 ):
     feat, inner = gain.shape[1], w_out.shape[0]
     x = ordered(tok)
@@ -689,9 +694,7 @@
     ntl_o[...] = low.astype(F32).T.astype(BF16)
     gh_o[...], gl_o[...] = both_orders(g)
     flip = flip_matrix(feat)
-    high, low = split(w_in[...])
-    wih_o[...], wil_o[...] = high, low
-    wfh_o[...], wfl_o[...] = nn(flip, high).astype(BF16), nn(flip, low).astype(BF16)
+    wfh_o[...], wfl_o[...] = nn(flip, wih[...]).astype(BF16), nn(flip, wil[...]).astype(BF16)
     high, low = split(w_out[...])
     woh_o[...], wol_o[...] = high, low
     vfh_o[...], vfl_o[...] = nn(high, flip).astype(BF16), nn(low, flip).astype(BF16)
@@ -704,14 +707,15 @@
         zgrad_o[:, cols] = go[:, cols] * (s * (1.0 + zt * (1.0 - s)))
         s = sigmoid(v)
         cgrad_o[:, cols] = s * (1.0 + v * (1.0 - s))
+        sig_o[:, cols] = sigmoid(pre[:, cols])
         skip_o[:, cols] = jnp.sum(gy[:, cols] * xc[:, cols], axis=0, keepdims=True)
-    row = lax.broadcasted_iota(jnp.int32, pickb_o.shape, 0) >> 7
+    row = lax.broadcasted_iota(jnp.int32, pickb_o.shape, 0) >> 6
     col = lax.broadcasted_iota(jnp.int32, pickb_o.shape, 1)
     pickb_o[...] = jnp.where(col == row + rank, 1.0, 0.0).astype(BF16)
-    pickc_o[...] = jnp.where(col == row + (rank + pickb_o.shape[0] // LANE), 1.0, 0.0).astype(BF16)
-
-
-def ready(rank, state, tok, gout, gain, w_in, w_out, d_skip, z, go, conv, xc, gy):
+    pickc_o[...] = jnp.where(col == row + (rank + pickb_o.shape[0] // (LANE // 2)), 1.0, 0.0).astype(BF16)
+
+
+def ready(rank, state, tok, gout, gain, wih, wil, w_out, d_skip, z, go, conv, pre, xc, gy):
     length, feat = tok.shape
     rows2, inner = z.shape
     f32 = lambda *dims: jax.ShapeDtypeStruct(dims, F32)
@@ -720,45 +724,40 @@
     return pl.pallas_call(
         lambda *refs: ready_kernel(rank, *refs),
         out_shape=(f32(length, feat), f32(length, feat))
-        + both(feat, rows2) + both(rows2, feat) + both(feat, 2 * inner) + both(feat, 2 * inner)
+        + both(feat, rows2) + both(rows2, feat) + both(feat, 2 * inner)
         + both(inner, feat) + both(inner, feat)
-        + (f32(rows2, inner), f32(rows2, inner), f32(rows2, inner))
-        + both(rows2, inner) + (f32(1, inner),) + both(state * LANE, LANE),
+        + (f32(rows2, inner),) * 4
+        + both(rows2, inner) + (f32(1, inner),) + both(state * LANE // 2, LANE),
         compiler_params=params(8),
         name="ready",
-    )(tok, gout, gain, w_in, w_out, d_skip, z, go, conv, xc, gy)
+    )(tok, gout, gain, wih, wil, w_out, d_skip, z, go, conv, pre, xc, gy)
 
 
 def early_kernel(
-    rs_bits, x, nth, ntl, gh, gl, woh, wol, vfh, vfl, gate, zgrad, d_skip, xc, y_s,
-    mixed_o, gzh_o, gzl_o, pieces_o,
+    rs_bits, nth, ntl, gh, gl, gate, zgrad, d_skip, xc, y_s, gzh_o, gzl_o, outh_o, outl_o, pieces_o,
 ):
-    rows2, inner = xc.shape
-    length = rows2 // 2
     y = y_s[...] + d_skip[...] * xc[...]
     gz = split(zgrad[...] * y)
     gzh_o[...], gzl_o[...] = gz
     out = split(y * gate[...])
     gw_out = mm(tn, out, (gh[...], gl[...]))
     gw_in = mm(nn, (nth[...], ntl[...]), gz)
+    outh_o[...], outl_o[...] = out
     put_pieces(rs_bits, pieces_o, [(gw_in, None), (gw_out, None)])
-    fwd = mm(nn, (out[0][:length], out[1][:length]), (woh[...], wol[...]))
-    rev = mm(nn, (out[0][length:], out[1][length:]), (vfh[...], vfl[...]))
-    store_ordered(mixed_o, x[...] + (fwd + rev))
-
-
-def early(rs_bits, x, nth, ntl, gh, gl, woh, wol, vfh, vfl, gate, zgrad, d_skip, xc, y):
-    length, feat = x.shape
+
+
+def early(rs_bits, nth, ntl, gh, gl, gate, zgrad, d_skip, xc, y):
+    feat = nth.shape[0]
     rows2, inner = xc.shape
     pieces = 1 << rs_bits
     tall = 2 * feat * inner // LANE // pieces
     gz = jax.ShapeDtypeStruct((rows2, inner), BF16)
     return pl.pallas_call(
         lambda *refs: early_kernel(rs_bits, *refs),
-        out_shape=(jax.ShapeDtypeStruct((length, feat), F32), gz, gz, jax.ShapeDtypeStruct((pieces, tall, LANE), F32)),
+        out_shape=(gz, gz, gz, gz, jax.ShapeDtypeStruct((pieces, tall, LANE), F32)),
         compiler_params=params(8),
         name="early",
-    )(x, nth, ntl, gh, gl, woh, wol, vfh, vfl, gate, zgrad, d_skip, xc, y)
+    )(nth, ntl, gh, gl, gate, zgrad, d_skip, xc, y)
 
 
 def put_pieces(rs_bits, pieces_o, arrays, few=None):
@@ -811,6 +810,7 @@
     base = dirn * length
     m_row = 3 if dirn == 0 else 1
     group = 2
+    low = lax.broadcasted_iota(jnp.int32, (CH, LANE), 1) < LANE // 2
     cols_of = [slice(t * LANE, (t + 1) * LANE) for t in range(tiles)]
     sb_s[...] = jnp.zeros(sb_s.shape, F32)
     sa_s[...] = jnp.zeros(sa_s.shape, F32)
@@ -830,30 +830,33 @@
                 into = jnp.exp2(after_s[:, cols] * a2[n, t]) * car[m_row * state + n0 + n, :, cols]
                 q[n, t] = mx[dirn, n0 + n, :, cols] + into
                 ga[n, t] = jnp.zeros((CH, LANE), F32)
-        for at in range(steps - 1, -1, -1):
-            j = order[at]
+        for time in range(steps - 1, -1, -1):
+            j = order[time]
             rows = slice(base + j * CH, base + (j + 1) * CH)
             here = slice(j * CH, (j + 1) * CH)
             de = [de_s[rows, c] for c in cols_of]
             dx = [dx_s[rows, c] for c in cols_of]
             gyj = [gy[rows, c] for c in cols_of]
             sb, sa = [None] * tiles, [None] * tiles
+            sums = []
             for n in range(group):
                 b_n, c_n = bc_s[rows, at_b[n]], bc_s[rows, at_c[n]]
                 to_b = to_c = None
                 for t, cols in enumerate(cols_of):
                     gh = gyj[t] * c_n + q[n, t]
-                    term_c = gyj[t] * h_s[dirn, at + 1, n0 + n, :, cols]
+                    term_c = gyj[t] * h_s[dirn, time + 1, n0 + n, :, cols]
                     term_b = gh * dx[t]
                     to_b = term_b if t == 0 else to_b + term_b
                     to_c = term_c if t == 0 else to_c + term_c
-                    q[n, t] = decay[dirn, at, n0 + n, :, cols] * gh
-                    r = q[n, t] * h_s[dirn, at, n0 + n, :, cols]
+                    q[n, t] = decay[dirn, time, n0 + n, :, cols] * gh
+                    r = q[n, t] * h_s[dirn, time, n0 + n, :, cols]
                     ga[n, t] = ga[n, t] + de[t] * r
                     sb[t] = gh * b_n if n == 0 else sb[t] + gh * b_n
                     sa[t] = a2[n, t] * r if n == 0 else sa[t] + a2[n, t] * r
-                accb[here, at_b[n]] = to_b
-                accc[here, at_b[n]] = to_c
+                sums.append((to_b, to_c))
+            at = pl.ds(pl.multiple_of(g * LANE, LANE), LANE)
+            for acc, one, two in ((accb, sums[0][0], sums[1][0]), (accc, sums[0][1], sums[1][1])):
+                acc[here, at] = jnp.where(low, one, two) + pltpu.roll(jnp.where(low, two, one), LANE // 2, 1)
             for t, cols in enumerate(cols_of):
                 sb_s[here, cols] += sb[t]
                 sa_s[here, cols] += sa[t]
@@ -870,7 +873,7 @@
     state = a2.shape[0]
     length = rows2 // 2
     half = jax.ShapeDtypeStruct((length, inner), F32)
-    acc = jax.ShapeDtypeStruct((length, state * LANE), F32)
+    acc = jax.ShapeDtypeStruct((length, state * LANE // 2), F32)
     return pl.pallas_call(
         lambda *refs: backward_kernel(dirn, *refs),
         out_shape=(half, half, acc, acc, jax.ShapeDtypeStruct((state, CH, inner), F32)),
@@ -1028,8 +1031,8 @@
 
 
 def tail_kernel(
-    rs_bits, sib, oth, gain, x_s, g_s, nth, ntl, wih, wil, wfh, wfl, gzh, gzl, gxh, gxl, halo, few,
-    gtok_o, to_left_o, to_right_o, pieces_o,
+    rs_bits, sib, oth, gain, x_s, nth, ntl, wih, wil, wfh, wfl, gzh, gzl, gxh, gxl, halo, few,
+    normed_o, pieces_o, *edges_o,
 ):
     feat = gain.shape[1]
     rows2, inner = gxh.shape
@@ -1044,7 +1047,7 @@
         jnp.concatenate([lh, nn(rh, flip).astype(BF16)], axis=0),
         jnp.concatenate([ll, nn(rl, flip).astype(BF16)], axis=0),
     )
-    x, g = x_s[...], g_s[...]
+    x = x_s[...]
     factor = normalize(x, gain[...])[0]
     gh_parts = split(halo[...])
     gw_in = mm(nn, (nth[...], ntl[...]), (gxh[...], gxl[...]))
@@ -1061,15 +1064,11 @@
     gn_l = back_h[:CH]
     gn_r = flipped(back_h[CH:])
 
-    def norm_back(x, factor, gn):
-        scaled = gn * gain[...]
-        return factor * scaled - x * (factor * factor * factor * jnp.mean(scaled * x, axis=1, keepdims=True))
-
-    store_ordered(gtok_o, g + norm_back(x, factor, g_normed))
-    to_left = norm_back(left, factor_l, gn_l)
-    to_right = norm_back(right, factor_r, gn_r)
-    to_left_o[...] = to_left
-    to_right_o[...] = to_right
+    normed_o[...] = g_normed
+    to_left = norm_back(left, factor_l, gn_l, gain[...])
+    to_right = norm_back(right, factor_r, gn_r, gain[...])
+    for ref, value in zip(edges_o, (to_left, to_right)):
+        ref[...] = value
     three = lax.broadcasted_iota(jnp.int32, (CH, feat), 0) < 3
     g_gain = (
         jnp.sum(g_normed * (x * factor), axis=0, keepdims=True)
@@ -1106,8 +1105,33 @@
     return found
 
 
-def tail(rs_bits, *arrays):
-    x, gxh = arrays[3], arrays[13]
+def norm_back(x, factor, gn, gain):
+    scaled = gn * gain
+    return factor * scaled - x * (factor * factor * factor * jnp.mean(scaled * x, axis=1, keepdims=True))
+
+
+def finish_kernel(x_s, g, gain, g_normed, outh, outl, woh, wol, vfh, vfl, mixed_o, gtok_o):
+    length = x_s.shape[0]
+    x = x_s[...]
+    fwd = mm(nn, (outh[:length], outl[:length]), (woh[...], wol[...]))
+    rev = mm(nn, (outh[length:], outl[length:]), (vfh[...], vfl[...]))
+    store_ordered(mixed_o, x + (fwd + rev))
+    factor = normalize(x, gain[...])[0]
+    store_ordered(gtok_o, g[...] + norm_back(x, factor, g_normed[...], gain[...]))
+
+
+def finish(*arrays):
+    shape = jax.ShapeDtypeStruct(arrays[0].shape, F32)
+    return pl.pallas_call(
+        finish_kernel,
+        out_shape=(shape, shape),
+        compiler_params=params(6),
+        name="finish",
+    )(*arrays)
+
+
+def tail(rs_bits, alone, *arrays):
+    x, gxh = arrays[3], arrays[12]
     length, feat = x.shape
     inner = gxh.shape[1]
     pieces = 1 << rs_bits
@@ -1116,10 +1140,9 @@
         lambda *refs: tail_kernel(rs_bits, *refs),
         out_shape=(
             jax.ShapeDtypeStruct((length, feat), F32),
-            jax.ShapeDtypeStruct((CH, feat), F32),
-            jax.ShapeDtypeStruct((CH, feat), F32),
             jax.ShapeDtypeStruct((pieces, tall, LANE), F32),
-        ),
+        )
+        + (jax.ShapeDtypeStruct((CH, feat), F32),) * (2 if alone else 0),
         compiler_params=params(8),
         name="tail",
     )(*arrays)
@@ -1265,15 +1288,15 @@
     (tok, keep, pad, gain, w_in_0, gout, w_out_0, conv_w_0, conv_b_0, w_x_t, w_dt_0, dt_bias_0, a_log_t, skip) = kept
     oth = swap_across(to_oth)
     sib = swap(to_sib, 0)
-    xb, z, go, gy = project(tok, pad, gain, w_in_0, gout, w_out_0)
-    xc, dt, sig, conv, mask, dbl, xbh, sx, mx, total, de, dx, bc, a2, decay = prepare(
-        sib, oth, keep, gain, w_in_0, conv_w_0, conv_b_0, w_x_t, w_dt_0, dt_bias_0, a_log_t, xb, gy
+    xb, z, go, gy, wih, wil, spread_s, a2 = project(tok, pad, gain, w_in_0, gout, w_out_0, a_log_t)
+    xc, dt, pre, conv, mask, dbl, xbh, sx, mx, total, de, dx, bc, decay, drive = prepare(
+        sib, oth, keep, gain, wih, wil, conv_w_0, conv_b_0, w_x_t, w_dt_0, dt_bias_0, spread_s, a2, xb, gy
     )
 
     sibling = swap(total, 0)
     group = pair(a2, total, sibling)
-    group, gate_in = lax.optimization_barrier((group, (z, go, conv, xc, gy)))
-    at_hand = ready(w_dt.shape[1], a_log.shape[2], tok, gout, gain, w_in_0, w_out_0, skip, *gate_in)
+    group, gate_in = lax.optimization_barrier((group, (z, go, conv, pre, xc, gy)))
+    at_hand = ready(w_dt.shape[1], a_log.shape[2], tok, gout, gain, wih, wil, w_out_0, skip, *gate_in)
     stages = []
     steps = [range(first, min(first + 2, bits)) for first in range(1, bits, 2)]
     step = steps[-1]
@@ -1291,19 +1314,19 @@
     mine_half = enter(a2, stages)
     other_half = swap(mine_half, 0)
 
-    y, h, car = forward(mine_half, other_half, sibling, sx, de, dx, bc, a2, decay)
+    y, h, car = forward(mine_half, other_half, sibling, sx, de, dx, bc, a2, decay, drive)
     def reduced(part, step):
         size = part.shape[0] >> len(step)
         total = part[:size]
-        for i in ((3, 1, 2) if len(step) == 2 else (1,)):
+        for i in ((2, 3, 1) if len(step) == 2 else (1,)):
             slot = reverse_bits(i, len(step))
             total = total + exchange(part[slot * size : (slot + 1) * size], i << step[0])
         return total
 
-    (x, g, nth, ntl, gh, gl, wih, wil, wfh, wfl, woh, wol, vfh, vfl, gate, zgrad, cgrad, xch, xcl, skip_sum,
+    (x, g, nth, ntl, gh, gl, wfh, wfl, woh, wol, vfh, vfl, gate, zgrad, cgrad, sig, xch, xcl, skip_sum,
      pick_b, pick_c) = at_hand
     rs_steps = [range(0, 1)] + [range(first, min(first + 2, rs_bits)) for first in range(1, rs_bits, 2)]
-    mixed, gzh, gzl, part_a = early(rs_bits, x, nth, ntl, gh, gl, woh, wol, vfh, vfl, gate, zgrad, skip, xc, y)
+    gzh, gzl, outh, outl, part_a = early(rs_bits, nth, ntl, gh, gl, gate, zgrad, skip, xc, y)
     part_a, h = lax.optimization_barrier((part_a, h))
     part_a = reduced(part_a, range(0, 1))
     back_f = backward(0, mx, car, h, de, dx, bc, a2, decay, gy)
@@ -1314,12 +1337,15 @@
         pad, conv_w_0, w_x_t, w_dt_0, skip, a2,
         xb, gy, xc, dt, sig, cgrad, mask, dbl, xbh, xch, xcl, skip_sum, pick_b, pick_c, *back_f, *back_r,
     )
-    gtok, to_left, to_right, part_b = tail(
-        rs_bits, sib, oth, gain, x, g, nth, ntl, wih, wil, wfh, wfl, gzh, gzl, gxh, gxl, halo_g, few
+    g_normed, part_b, *to_sides = tail(
+        rs_bits, bits > rs_bits, sib, oth, gain, x, nth, ntl, wih, wil, wfh, wfl, gzh, gzl, gxh, gxl, halo_g, few
     )
     part_a, part_b = lax.optimization_barrier((part_a, part_b))
     part_a, part_b = reduced(part_a, range(2, 3)), reduced(part_b, rs_steps[0])
+    part_b, g_normed = lax.optimization_barrier((part_b, g_normed))
     part_b = reduced(part_b, rs_steps[1])
+    mixed, gtok = finish(x, g, gain, g_normed, outh, outl, woh, wol, vfh, vfl)
+    part_b, mixed, gtok = lax.optimization_barrier((part_b, mixed, gtok))
     own = jnp.concatenate([part_a, part_b], axis=1)
     for step in rs_steps[2:]:
         own = reduced(own, step)
@@ -1329,8 +1355,8 @@
     halo = jnp.concatenate([own[0, tall - 16 : tall - 12], own[0, tall - 8 :]], axis=0)
     if bits > rs_bits:
         pairs = [(i, i + 1) for i in range(count - 1)]
-        from_left = lax.ppermute(to_right, "seq", pairs)[:3]
-        from_right = lax.ppermute(to_left, "seq", [(j, i) for i, j in pairs])[:3]
+        from_left = lax.ppermute(to_sides[1], "seq", pairs)[:3]
+        from_right = lax.ppermute(to_sides[0], "seq", [(j, i) for i, j in pairs])[:3]
         halo = jnp.concatenate([from_left.reshape(-1, LANE), from_right.reshape(-1, LANE)], axis=0)
     own = own[:, : tall - 8]
     for step in reversed(rs_steps[1:]):

time: 93.7 us -> 90.1 us (0.962)
  Pallas kernels: 28.6 us -> 26.8 us
    pallas_call x2 -> x3, Pallas kernels: 3.49 us -> 3.81 us  [the longest x1 1.72 us: project(): pl.pallas_call(project_kernel, out_shape=(big, big, big, big, part, part,...]
  transfers between devices with their start and end apart: 30 -> 30, of which waited for: 17 -> 19; matrix products, arithmetic and copies ran while one was open for 0% -> 0% of each run, Pallas kernels for 16% -> 17%
where the time goes in v4:
time: 90.1 us; the launch traced here: 90 us
  starting transfers between devices  33.4 us (37%)
  waiting for transfers between devices  28.5 us (32%)
  Pallas kernels  26.8 us (30%)
    ppermute x29, starting transfers between devices, exchange(): return lax.ppermute(value, 'seq', [(i, i ^ apart) for i in range(count)])  32.8 us
    ppermute x29, waiting for transfers between devices, exchange(): return lax.ppermute(value, 'seq', [(i, i ^ apart) for i in range(count)])  28.5 us
    pallas_call x1, Pallas kernels, prepare(): pl.pallas_call(prepare_kernel, out_shape=(big, big, big, big, pltpu.VMEM(...  5.83 us
    pallas_call x2, Pallas kernels, backward(): pl.pallas_call(lambda *refs: backward_kernel(dirn, *refs), out_shape=(hal...  5.58 us
    pallas_call x1, Pallas kernels, inner_back(): pl.pallas_call(inner_kernel, out_shape=(part, part, jax.ShapeDtypeStruct(...  2.24 us
    pallas_call x1, Pallas kernels, tail(): pl.pallas_call(lambda *refs: tail_kernel(rs_bits, *refs), out_shape=(jax....  2.18 us
    pallas_call x1, Pallas kernels, ready(): pl.pallas_call(lambda *refs: ready_kernel(rank, *refs), out_shape=(f32(le...  1.92 us
    pallas_call x1, Pallas kernels, edges(): pl.pallas_call(edges_kernel, out_shape=(shape, shape) + tuple((jax.ShapeD...  1.8 us
  transfers between devices with their start and end apart: 30, of which 19 were waited for; matrix products, arithmetic and copies ran while one was open for 0% of the time, Pallas kernels for 17%

profile of v4, /device:TPU:0, one launch (start us, length us, event | category | flops | bytes accessed | tf_op | source)
XLA Modules:
  0.0 90.0 jit_solution(4967423818300310283)
XLA Ops:
  0.6 1.8 %edges.1 = (f32[8,256]{1,0:T(8,128)S(1)}, f32[8,256]{1,0:T(8,128)S(1)}, f32[128,256]{1,0:T(8,128)S(1)}, s32[1,128]{1,0:T(1,128)S(1)}, s32[1,128]{1,0:T(1,128)S(1...) custom-call(f32[128,256]{1,0:T(8,128)} %tok.1, ...), custom_call_target="tpu_custom_call" | custom-call | tf_op jit(solution)/shard_map/edges/pallas_call | solution.py:141
  3.0 0.6 collective-permute-start.1
  3.6 1.7 %project.1 = (f32[256,512]{1,0:T(8,128)S(1)}, f32[256,512]{1,0:T(8,128)S(1)}, f32[256,512]{1,0:T(8,128)S(1)}, f32[256,512]{1,0:T(8,128)S(1)}, bf16[256,1024]{1,0...) custom-call(f32[128,256]{1,0:T(8,128)S(1)} %get-tuple-element.160.tok.ref, ...), custom_call_target="tpu_custom_call" | custom-call | tf_op jit(solution)/shard_map/project/pallas_call | solution.py:183
  5.4 5.8 %prepare.1 = (f32[256,512]{1,0:T(8,128)S(1)}, f32[256,512]{1,0:T(8,128)S(1)}, f32[256,512]{1,0:T(8,128)S(1)}, f32[256,512]{1,0:T(8,128)S(1)}, f32[768,128]{1,0:T...) custom-call(f32[8,256]{1,0:T(8,128)S(1)} %collective-permute-done.si, ...), custom_call_target="tpu_custom_call" | custom-call | tf_op jit(solution)/shard_map/prepare/pallas_call | solution.py:411
  11.2 3.9 %collective-permute-start.2 = (f32[72,512]{1,0:T(8,128)S(1)}, f32[72,512]{1,0:T(8,128)S(1)}, u32[]{:S(2)}, u32[]{:S(2)}) collective-permute-start(f32[72,512]{1,0:T(8,128)S(1)} %get-tuple-element.181.mine), channel_id=1, source_target_pairs={{0,1},{1,0},{2,3},{3,2},{4,5},{5,4},{6,7},{7,6},{8,9},{9,8},{10,11... | collective-permute-start | bytes 442376 | tf_op jit(solution)/shard_map/ppermute | solution.py:1274
  15.2 1.0 %collective-permute-done.2.theirs.sibling = f32[72,512]{1,0:T(8,128)S(1)} collective-permute-done((f32[72,512]{1,0:T(8,128)S(1)}, f32[72,512]{1,0:T(8,128)S(1)}, u32[]{:S(2)}, u32[]{:S(2)}) %collective-permute-start.2) | collective-permute-done | bytes 147488 | tf_op jit(solution)/shard_map/ppermute | solution.py:1274
  16.2 4.5 %collective-permute-start.5 = (f32[72,256]{1,0:T(8,128)S(1)}, f32[72,256]{1,0:T(8,128)S(1)}, u32[]{:S(2)}, u32[]{:S(2)}) collective-permute-start(f32[72,256]{1,0:T(8,128)S(1)} %pair.1.refs_1_), channel_id=1, source_target_pairs={{0,6},{1,7},{2,4},{3,5},{4,2},{5,3},{6,0},{7,1},{8,14},{9,15},{10,... | collective-permute-start | bytes 221192 | tf_op jit(solution)/shard_map/ppermute | solution.py:1274
  20.7 0.6 collective-permute-start.3
  21.3 1.9 %ready.1 = (f32[128,256]{1,0:T(8,128)S(1)}, f32[128,256]{1,0:T(8,128)S(1)}, bf16[256,256]{1,0:T(8,128)(2,1)S(1)}, bf16[256,256]{1,0:T(8,128)(2,1)S(1)}, bf16[256...) custom-call(f32[128,256]{1,0:T(8,128)S(1)} %get-tuple-element.160.to, ...), custom_call_target="tpu_custom_call" | custom-call | tf_op jit(solution)/shard_map/ready/pallas_call | solution.py:724
  23.5 1.6 %collective-permute-done.4.refs_3_ = f32[72,256]{1,0:T(8,128)S(1)} collective-permute-done((f32[72,256]{1,0:T(8,128)S(1)}, f32[72,256]{1,0:T(8,128)S(1)}, u32[]{:S(2)}, u32[]{:S(2)}) %collective-permute-start.4) | collective-permute-done | bytes 73760 | tf_op jit(solution)/shard_map/ppermute | solution.py:1274
  25.1 1.6 %collective-permute-start.6 = (f32[40,256]{1,0:T(8,128)S(1)}, f32[40,256]{1,0:T(8,128)S(1)}, u32[]{:S(2)}, u32[]{:S(2)}) collective-permute-start(f32[40,256]{1,0:T(8,128)S(1)} %get-tuple-element.226), channel_id=1, source_target_pairs={{0,8},{1,9},{2,10},{3,11},{4,12},{5,13},{6,14},{7,15},{8,0},{9,1},... | collective-permute-start | bytes 122888 | tf_op jit(solution)/shard_map/ppermute | solution.py:1274
  26.8 2.2 %collective-permute-start.7 = (f32[40,256]{1,0:T(8,128)S(1)}, f32[40,256]{1,0:T(8,128)S(1)}, u32[]{:S(2)}, u32[]{:S(2)}) collective-permute-start(f32[40,256]{1,0:T(8,128)S(1)} %get-tuple-element.227), channel_id=1, source_target_pairs={{0,16},{1,17},{2,18},{3,19},{4,20},{5,21},{6,22},{7,23},{8,24},{9,... | collective-permute-start | bytes 122888 | tf_op jit(solution)/shard_map/ppermute | solution.py:1274
  29.0 0.6 collective-permute-start.8
  29.6 3.0 %collective-permute-done.7.refs_2_ = f32[40,256]{1,0:T(8,128)S(1)} collective-permute-done((f32[40,256]{1,0:T(8,128)S(1)}, f32[40,256]{1,0:T(8,128)S(1)}, u32[]{:S(2)}, u32[]{:S(2)}) %collective-permute-start.7) | collective-permute-done | bytes 40992 | tf_op jit(solution)/shard_map/ppermute | solution.py:1274
  32.6 2.2 %collective-permute-done.8.refs_3_ = f32[40,256]{1,0:T(8,128)S(1)} collective-permute-done((f32[40,256]{1,0:T(8,128)S(1)}, f32[40,256]{1,0:T(8,128)S(1)}, u32[]{:S(2)}, u32[]{:S(2)}) %collective-permute-start.8) | collective-permute-done | bytes 40992 | tf_op jit(solution)/shard_map/ppermute | solution.py:1274
  34.9 1.2 %collective-permute-done.9.other_half = f32[64,256]{1,0:T(8,128)S(1)} collective-permute-done((f32[64,256]{1,0:T(8,128)S(1)}, f32[64,256]{1,0:T(8,128)S(1)}, u32[]{:S(2)}, u32[]{:S(2)}) %collective-permute-start.9) | collective-permute-done | bytes 65568 | tf_op jit(solution)/shard_map/ppermute | solution.py:1274
  36.2 1.7 %forward.1 = (f32[256,512]{1,0:T(8,128)S(1)}, f32[2,17,16,8,512]{4,3,2,1,0:T(8,128)S(1)}, f32[64,8,512]{2,1,0:T(8,128)S(1)}) custom-call(f32[64,256]{1,0:T(8,128)S(1)} %enter.1.mine_half, f32[64,256]{1,0:T(8,128)S(1)} %collective-permute-done.9.other_half, f32[72,512]{1,0:T(8,128)S(1)} %collective-permute-done.2.theirs.sibling, ...), custom_call_target="tpu_custom_call" | custom-call | tf_op jit(solution)/shard_map/forward/pallas_call | solution.py:669
  37.9 0.7 early.1
  38.9 2.8 %backward.2 = (f32[128,512]{1,0:T(8,128)S(1)}, f32[128,512]{1,0:T(8,128)S(1)}, f32[128,1024]{1,0:T(8,128)S(1)}, f32[128,1024]{1,0:T(8,128)S(1)}, f32[16,8,512]{2,1,0:T(8,128)S(1)}) custom-call(f32[2,16,8,512]{3,2,1,0:T(8,128)S(1)} %get-tuple-element.239.refs_0_, f32[64,8,512]{2,1,0:T(8,128)S(1)} %get-tuple-element.240.refs_1_, ...), custom_call_target="tpu_custom_call" | custom-call | tf_op jit(solution)/shard_map/backward/pallas_call | solution.py:877
  41.7 1.4 %collective-permute-start.11 = (f32[8,64,128]{2,1,0:T(8,128)S(1)}, f32[8,64,128]{2,1,0:T(8,128)S(1)}, u32[]{:S(2)}, u32[]{:S(2)}) collective-permute-start(f32[8,64,128]{2,1,0:T(8,128)S(1)} %slice.60), channel_id=1, source_target_pairs={{0,2},{1,3},{2,0},{3,1},{4,6},{5,7},{6,4},{7,5},{8,10},{9,11},{10,... | collective-permute-start | bytes 786440 | tf_op jit(solution)/shard_map/ppermute | solution.py:1274
  43.1 2.8 %backward.3 = (f32[128,512]{1,0:T(8,128)S(1)}, f32[128,512]{1,0:T(8,128)S(1)}, f32[128,1024]{1,0:T(8,128)S(1)}, f32[128,1024]{1,0:T(8,128)S(1)}, f32[16,8,512]{2,1,0:T(8,128)S(1)}) custom-call(f32[2,16,8,512]{3,2,1,0:T(8,128)S(1)} %get-tuple-element.239.refs_0_, f32[64,8,512]{2,1,0:T(8,128)S(1)} %get-tuple-element.240.refs_1_, ...), custom_call_target="tpu_custom_call" | custom-call | tf_op jit(solution)/shard_map/backward/pallas_call | solution.py:877
  45.9 2.2 %inner.1 = (bf16[256,512]{1,0:T(8,128)(2,1)S(1)}, bf16[256,512]{1,0:T(8,128)(2,1)S(1)}, f32[16,512]{1,0:T(8,128)S(1)}, f32[88,512]{1,0:T(8,128)S(1)}) custom-call(s32[1,128]{1,0:T(1,128)S(1)} %get-tuple-element.161.pad.refs_10_, f32[4,512]{1,0:T(4,128)S(1)} %get-tuple-element.173.conv_w, f32[48,512]{1,0:T(8,128)S(1)} %get-tuple-element.175.w_x, ...), custom_call_target="tpu_custom_call" | custom-call | tf_op jit(solution)/shard_map/inner/pallas_call | solution.py:1020
  48.2 2.2 %tail.1 = (f32[128,256]{1,0:T(8,128)S(1)}, f32[32,56,128]{2,1,0:T(8,128)S(1)}) custom-call(f32[8,256]{1,0:T(8,128)S(1)} %collective-permute-done.sib.refs_0_, f32[8,256]{1,0:T(8,128)S(1)} %collective-permute-done.1.oth.refs_1_, f32[1,256]{1,0:T(1,128)S(1)} %get-tuple-element.162.gain.refs_2_, f32[128,256]{1,0:T(8,128)S(1)} %get-tuple-element.248.refs_3_.x_s, ...), custom_call_target="tpu_custom_call" | custom-call | tf_op jit(solution)/shard_map/tail/pallas_call | solution.py:1139
  50.6 0.9 %collective-permute-start.16 = (f32[4,64,128]{2,1,0:T(8,128)S(1)}, f32[4,64,128]{2,1,0:T(8,128)S(1)}, u32[]{:S(2)}, u32[]{:S(2)}) collective-permute-start(f32[4,64,128]{2,1,0:T(8,128)S(1)} %slice.68), channel_id=1, source_target_pairs={{0,4},{1,5},{2,6},{3,7},{4,0},{5,1},{6,2},{7,3},{8,12},{9,13},{10,... | collective-permute-start | bytes 393224 | tf_op jit(solution)/shard_map/ppermute | solution.py:1274
  51.6 0.8 collective-permute-done.12
  52.4 1.0 %collective-permute-start.13 = (f32[4,56,128]{2,1,0:T(8,128)S(1)}, f32[4,56,128]{2,1,0:T(8,128)S(1)}, u32[]{:S(2)}, u32[]{:S(2)}) collective-permute-start(f32[4,56,128]{2,1,0:T(8,128)S(1)} %get-tuple-element.308), channel_id=1, source_target_pairs={{0,4},{1,5},{2,6},{3,7},{4,0},{5,1},{6,2},{7,3},{8,12},{9,13},{10,... | collective-permute-start | bytes 344072 | tf_op jit(solution)/shard_map/ppermute | solution.py:1274
  53.4 1.0 %collective-permute-start.15 = (f32[4,56,128]{2,1,0:T(8,128)S(1)}, f32[4,56,128]{2,1,0:T(8,128)S(1)}, u32[]{:S(2)}, u32[]{:S(2)}) collective-permute-start(f32[4,56,128]{2,1,0:T(8,128)S(1)} %get-tuple-element.309), channel_id=1, source_target_pairs={{0,2},{1,3},{2,0},{3,1},{4,6},{5,7},{6,4},{7,5},{8,10},{9,11},{10,... | collective-permute-start | bytes 344072 | tf_op jit(solution)/shard_map/ppermute | solution.py:1274
  54.4 1.6 %collective-permute-start.14 = (f32[4,56,128]{2,1,0:T(8,128)S(1)}, f32[4,56,128]{2,1,0:T(8,128)S(1)}, u32[]{:S(2)}, u32[]{:S(2)}) collective-permute-start(f32[4,56,128]{2,1,0:T(8,128)S(1)} %get-tuple-element.310), channel_id=1, source_target_pairs={{0,6},{1,7},{2,4},{3,5},{4,2},{5,3},{6,0},{7,1},{8,14},{9,15},{10,... | collective-permute-start | bytes 344072 | tf_op jit(solution)/shard_map/ppermute | solution.py:1274
  56.0 1.0 %collective-permute-done.16 = f32[4,64,128]{2,1,0:T(8,128)S(1)} collective-permute-done((f32[4,64,128]{2,1,0:T(8,128)S(1)}, f32[4,64,128]{2,1,0:T(8,128)S(1)}, u32[]{:S(2)}, u32[]{:S(2)}) %collective-permute-start.16) | collective-permute-done | bytes 131104 | tf_op jit(solution)/shard_map/ppermute | solution.py:1274
  57.0 1.3 %finish.1 = (f32[128,256]{1,0:T(8,128)}, f32[128,256]{1,0:T(8,128)S(1)}) custom-call(f32[128,256]{1,0:T(8,128)S(1)} %get-tuple-element.248.refs_3_.x_s, f32[128,256]{1,0:T(8,128)S(1)} %get-tuple-element.283.g, f32[1,256]{1,0:T(1,128)S(1)} %get-tuple-element.162.gain.refs_2_, f32[128,256]{1,0:T(8,128)S(1)} %get-tuple-element.284.g_normed, ...), custom_call_target="tpu_custom_call" | custom-call | tf_op jit(solution)/shard_map/finish/pallas_call | solution.py:1125
  58.4 3.1 %collective-permute-done.13 = f32[4,56,128]{2,1,0:T(8,128)S(1)} collective-permute-done((f32[4,56,128]{2,1,0:T(8,128)S(1)}, f32[4,56,128]{2,1,0:T(8,128)S(1)}, u32[]{:S(2)}, u32[]{:S(2)}) %collective-permute-start.13) | collective-permute-done | bytes 114720 | tf_op jit(solution)/shard_map/ppermute | solution.py:1274
  61.6 1.7 %collective-permute-start.19 = (f32[1,120,128]{2,1,0:T(8,128)S(1)}, f32[1,120,128]{2,1,0:T(8,128)S(1)}, u32[]{:S(2)}, u32[]{:S(2)}) collective-permute-start(f32[1,120,128]{2,1,0:T(8,128)S(1)} %get-tuple-element.312), channel_id=1, source_target_pairs={{0,8},{1,9},{2,10},{3,11},{4,12},{5,13},{6,14},{7,15},{8,0},{9,1},... | collective-permute-start | bytes 184328 | tf_op jit(solution)/shard_map/ppermute | solution.py:1274
  63.3 2.6 %collective-permute-start.18 = (f32[1,120,128]{2,1,0:T(8,128)S(1)}, f32[1,120,128]{2,1,0:T(8,128)S(1)}, u32[]{:S(2)}, u32[]{:S(2)}) collective-permute-start(f32[1,120,128]{2,1,0:T(8,128)S(1)} %get-tuple-element.313), channel_id=1, source_target_pairs={{0,24},{1,25},{2,26},{3,27},{4,28},{5,29},{6,30},{7,31},{8,16},{9,... | collective-permute-start | bytes 184328 | tf_op jit(solution)/shard_map/ppermute | solution.py:1274
  66.0 1.4 %collective-permute-done.17 = f32[1,120,128]{2,1,0:T(8,128)S(1)} collective-permute-done((f32[1,120,128]{2,1,0:T(8,128)S(1)}, f32[1,120,128]{2,1,0:T(8,128)S(1)}, u32[]{:S(2)}, u32[]{:S(2)}) %collective-permute-start.17) | collective-permute-done | bytes 61472 | tf_op jit(solution)/shard_map/ppermute | solution.py:1274
  67.4 2.0 %collective-permute-done.18 = f32[1,120,128]{2,1,0:T(8,128)S(1)} collective-permute-done((f32[1,120,128]{2,1,0:T(8,128)S(1)}, f32[1,120,128]{2,1,0:T(8,128)S(1)}, u32[]{:S(2)}, u32[]{:S(2)}) %collective-permute-start.18) | collective-permute-done | bytes 61472 | tf_op jit(solution)/shard_map/ppermute | solution.py:1274
  69.5 2.6 %collective-permute-start.22 = (f32[1,112,128]{2,1,0:T(8,128)S(1)}, f32[1,112,128]{2,1,0:T(8,128)S(1)}, u32[]{:S(2)}, u32[]{:S(2)}) collective-permute-start(f32[1,112,128]{2,1,0:T(8,128)S(1)} %slice.82), channel_id=1, source_target_pairs={{0,24},{1,25},{2,26},{3,27},{4,28},{5,29},{6,30},{7,31},{8,16},{9,... | collective-permute-start | bytes 172040 | tf_op jit(solution)/shard_map/ppermute | solution.py:1274
  72.1 1.8 %collective-permute-start.20 = (f32[1,112,128]{2,1,0:T(8,128)S(1)}, f32[1,112,128]{2,1,0:T(8,128)S(1)}, u32[]{:S(2)}, u32[]{:S(2)}) collective-permute-start(f32[1,112,128]{2,1,0:T(8,128)S(1)} %slice.82), channel_id=1, source_target_pairs={{0,16},{1,17},{2,18},{3,19},{4,20},{5,21},{6,22},{7,23},{8,24},{9,... | collective-permute-start | bytes 172040 | tf_op jit(solution)/shard_map/ppermute | solution.py:1274
  73.9 1.6 %collective-permute-done.22 = f32[1,112,128]{2,1,0:T(8,128)S(1)} collective-permute-done((f32[1,112,128]{2,1,0:T(8,128)S(1)}, f32[1,112,128]{2,1,0:T(8,128)S(1)}, u32[]{:S(2)}, u32[]{:S(2)}) %collective-permute-start.22) | collective-permute-done | bytes 57376 | tf_op jit(solution)/shard_map/ppermute | solution.py:1274
  75.5 0.7 collective-permute-done.21
  76.3 0.9 %collective-permute-done.20 = f32[1,112,128]{2,1,0:T(8,128)S(1)} collective-permute-done((f32[1,112,128]{2,1,0:T(8,128)S(1)}, f32[1,112,128]{2,1,0:T(8,128)S(1)}, u32[]{:S(2)}, u32[]{:S(2)}) %collective-permute-start.20) | collective-permute-done | bytes 57376 | tf_op jit(solution)/shard_map/ppermute | solution.py:1274
  77.2 1.4 %collective-permute-start.25 = (f32[4,112,128]{2,1,0:T(8,128)S(1)}, f32[4,112,128]{2,1,0:T(8,128)S(1)}, u32[]{:S(2)}, u32[]{:S(2)}) collective-permute-start(f32[4,112,128]{2,1,0:T(8,128)S(1)} %pad_maximum_fusion.refs_0_), channel_id=1, source_target_pairs={{0,6},{1,7},{2,4},{3,5},{4,2},{5,3},{6,0},{7,1},{8,14},{9,15},{10,... | collective-permute-start | bytes 688136 | tf_op jit(solution)/shard_map/ppermute | solution.py:1274
  78.6 1.2 %collective-permute-start.24 = (f32[4,112,128]{2,1,0:T(8,128)S(1)}, f32[4,112,128]{2,1,0:T(8,128)S(1)}, u32[]{:S(2)}, u32[]{:S(2)}) collective-permute-start(f32[4,112,128]{2,1,0:T(8,128)S(1)} %pad_maximum_fusion.refs_0_), channel_id=1, source_target_pairs={{0,2},{1,3},{2,0},{3,1},{4,6},{5,7},{6,4},{7,5},{8,10},{9,11},{10,... | collective-permute-start | bytes 688136 | tf_op jit(solution)/shard_map/ppermute | solution.py:1274
  79.7 1.0 %collective-permute-start.23 = (f32[4,112,128]{2,1,0:T(8,128)S(1)}, f32[4,112,128]{2,1,0:T(8,128)S(1)}, u32[]{:S(2)}, u32[]{:S(2)}) collective-permute-start(f32[4,112,128]{2,1,0:T(8,128)S(1)} %pad_maximum_fusion.refs_0_), channel_id=1, source_target_pairs={{0,4},{1,5},{2,6},{3,7},{4,0},{5,1},{6,2},{7,3},{8,12},{9,13},{10,... | collective-permute-start | bytes 688136 | tf_op jit(solution)/shard_map/ppermute | solution.py:1274
  80.7 3.8 %collective-permute-done.25.refs_3_ = f32[4,112,128]{2,1,0:T(8,128)S(1)} collective-permute-done((f32[4,112,128]{2,1,0:T(8,128)S(1)}, f32[4,112,128]{2,1,0:T(8,128)S(1)}, u32[]{:S(2)}, u32[]{:S(2)}) %collective-permute-start.25) | collective-permute-done | bytes 229408 | tf_op jit(solution)/shard_map/ppermute | solution.py:1274
  84.6 1.7 %collective-permute-done.24.refs_2_ = f32[4,112,128]{2,1,0:T(8,128)S(1)} collective-permute-done((f32[4,112,128]{2,1,0:T(8,128)S(1)}, f32[4,112,128]{2,1,0:T(8,128)S(1)}, u32[]{:S(2)}, u32[]{:S(2)}) %collective-permute-start.24) | collective-permute-done | bytes 229408 | tf_op jit(solution)/shard_map/ppermute | solution.py:1274
  87.0 0.8 collective-permute-done.28.refs_6_
  87.8 0.6 collective-permute-done.27.refs_5_
  88.4 1.5 %unpack.1 = (f32[128,256]{1,0:T(8,128)}, f32[1,256]{1,0:T(1,128)}, f32[256,1024]{1,0:T(8,128)}, f32[4,512]{1,0:T(4,128)}, f32[1,512]{1,0:T(1,128)}, /*index=5*/f...) custom-call(f32[4,112,128]{2,1,0:T(8,128)S(1)} %pad_maximum_fusion.r, ...), custom_call_target="tpu_custom_call" | custom-call | tf_op jit(solution)/shard_map/unpack/pallas_call | solution.py:1245
  (45 shorter events, 2.5 us)
Async XLA Ops:
  2.5 2.9 %collective-permute-start = (f32[8,256]{1,0:T(8,128)S(1)}, f32[8,256]{1,0:T(8,128)S(1)}, u32[]{:S(2)}, u32[]{:S(2)}) collective-permute-start(f32[8,256]{1,0:T(8,128)S(1)} %get-tuple-element.168), channel_id=1, source_target_pairs={{0,1},{1,0},{2,3},{3,2},{4,5},{5,4},{6,7},{7,6},{8,9},{9,8},{10,11... | collective-permute-start | bytes 24584 | tf_op jit(solution)/shard_map/ppermute | solution.py:1274
  3.0 2.4 %collective-permute-start.1 = (f32[8,256]{1,0:T(8,128)S(1)}, f32[8,256]{1,0:T(8,128)S(1)}, u32[]{:S(2)}, u32[]{:S(2)}) collective-permute-start(f32[8,256]{1,0:T(8,128)S(1)} %get-tuple-element.169), channel_id=1, source_target_pairs={{1,2},{3,4},{5,6},{7,8},{9,10},{11,12},{13,14},{15,16},{17,18},{19... | collective-permute-start | bytes 24584 | tf_op jit(solution)/shard_map/ppermute | solution.py:1282
  11.2 5.0 %collective-permute-start.2 = (f32[72,512]{1,0:T(8,128)S(1)}, f32[72,512]{1,0:T(8,128)S(1)}, u32[]{:S(2)}, u32[]{:S(2)}) collective-permute-start(f32[72,512]{1,0:T(8,128)S(1)} %get-tuple-element.181.mine), channel_id=1, source_target_pairs={{0,1},{1,0},{2,3},{3,2},{4,5},{5,4},{6,7},{7,6},{8,9},{9,8},{10,11... | collective-permute-start | bytes 442376 | tf_op jit(solution)/shard_map/ppermute | solution.py:1274
  16.2 7.3 %collective-permute-start.5 = (f32[72,256]{1,0:T(8,128)S(1)}, f32[72,256]{1,0:T(8,128)S(1)}, u32[]{:S(2)}, u32[]{:S(2)}) collective-permute-start(f32[72,256]{1,0:T(8,128)S(1)} %pair.1.refs_1_), channel_id=1, source_target_pairs={{0,6},{1,7},{2,4},{3,5},{4,2},{5,3},{6,0},{7,1},{8,14},{9,15},{10,... | collective-permute-start | bytes 221192 | tf_op jit(solution)/shard_map/ppermute | solution.py:1274
  20.7 4.4 %collective-permute-start.4 = (f32[72,256]{1,0:T(8,128)S(1)}, f32[72,256]{1,0:T(8,128)S(1)}, u32[]{:S(2)}, u32[]{:S(2)}) collective-permute-start(f32[72,256]{1,0:T(8,128)S(1)} %pair.1.refs_1_), channel_id=1, source_target_pairs={{0,4},{1,5},{2,6},{3,7},{4,0},{5,1},{6,2},{7,3},{8,12},{9,13},{10,... | collective-permute-start | bytes 221192 | tf_op jit(solution)/shard_map/ppermute | solution.py:1274
  20.7 4.4 %collective-permute-start.3 = (f32[72,256]{1,0:T(8,128)S(1)}, f32[72,256]{1,0:T(8,128)S(1)}, u32[]{:S(2)}, u32[]{:S(2)}) collective-permute-start(f32[72,256]{1,0:T(8,128)S(1)} %pair.1.refs_1_), channel_id=1, source_target_pairs={{0,2},{1,3},{2,0},{3,1},{4,6},{5,7},{6,4},{7,5},{8,10},{9,11},{10,... | collective-permute-start | bytes 221192 | tf_op jit(solution)/shard_map/ppermute | solution.py:1274
  25.1 4.5 %collective-permute-start.6 = (f32[40,256]{1,0:T(8,128)S(1)}, f32[40,256]{1,0:T(8,128)S(1)}, u32[]{:S(2)}, u32[]{:S(2)}) collective-permute-start(f32[40,256]{1,0:T(8,128)S(1)} %get-tuple-element.226), channel_id=1, source_target_pairs={{0,8},{1,9},{2,10},{3,11},{4,12},{5,13},{6,14},{7,15},{8,0},{9,1},... | collective-permute-start | bytes 122888 | tf_op jit(solution)/shard_map/ppermute | solution.py:1274
  26.8 5.8 %collective-permute-start.7 = (f32[40,256]{1,0:T(8,128)S(1)}, f32[40,256]{1,0:T(8,128)S(1)}, u32[]{:S(2)}, u32[]{:S(2)}) collective-permute-start(f32[40,256]{1,0:T(8,128)S(1)} %get-tuple-element.227), channel_id=1, source_target_pairs={{0,16},{1,17},{2,18},{3,19},{4,20},{5,21},{6,22},{7,23},{8,24},{9,... | collective-permute-start | bytes 122888 | tf_op jit(solution)/shard_map/ppermute | solution.py:1274
  29.0 5.8 %collective-permute-start.8 = (f32[40,256]{1,0:T(8,128)S(1)}, f32[40,256]{1,0:T(8,128)S(1)}, u32[]{:S(2)}, u32[]{:S(2)}) collective-permute-start(f32[40,256]{1,0:T(8,128)S(1)} %get-tuple-element.228), channel_id=1, source_target_pairs={{0,24},{1,25},{2,26},{3,27},{4,28},{5,29},{6,30},{7,31},{8,16},{9,... | collective-permute-start | bytes 122888 | tf_op jit(solution)/shard_map/ppermute | solution.py:1274
  34.9 1.3 %collective-permute-start.9 = (f32[64,256]{1,0:T(8,128)S(1)}, f32[64,256]{1,0:T(8,128)S(1)}, u32[]{:S(2)}, u32[]{:S(2)}) collective-permute-start(f32[64,256]{1,0:T(8,128)S(1)} %enter.1.mine_half), channel_id=1, source_target_pairs={{0,1},{1,0},{2,3},{3,2},{4,5},{5,4},{6,7},{7,6},{8,9},{9,8},{10,11... | collective-permute-start | bytes 196616 | tf_op jit(solution)/shard_map/ppermute | solution.py:1274
  38.6 3.0 %collective-permute-start.10 = (f32[16,64,128]{2,1,0:T(8,128)S(1)}, f32[16,64,128]{2,1,0:T(8,128)S(1)}, u32[]{:S(2)}, u32[]{:S(2)}) collective-permute-start(f32[16,64,128]{2,1,0:T(8,128)S(1)} %slice.58), channel_id=1, source_target_pairs={{0,1},{1,0},{2,3},{3,2},{4,5},{5,4},{6,7},{7,6},{8,9},{9,8},{10,11... | collective-permute-start | bytes 1572872 | tf_op jit(solution)/shard_map/ppermute | solution.py:1274
  41.7 8.6 %collective-permute-start.11 = (f32[8,64,128]{2,1,0:T(8,128)S(1)}, f32[8,64,128]{2,1,0:T(8,128)S(1)}, u32[]{:S(2)}, u32[]{:S(2)}) collective-permute-start(f32[8,64,128]{2,1,0:T(8,128)S(1)} %slice.60), channel_id=1, source_target_pairs={{0,2},{1,3},{2,0},{3,1},{4,6},{5,7},{6,4},{7,5},{8,10},{9,11},{10,... | collective-permute-start | bytes 786440 | tf_op jit(solution)/shard_map/ppermute | solution.py:1274
  50.5 1.9 %collective-permute-start.12 = (f32[16,56,128]{2,1,0:T(8,128)S(1)}, f32[16,56,128]{2,1,0:T(8,128)S(1)}, u32[]{:S(2)}, u32[]{:S(2)}) collective-permute-start(f32[16,56,128]{2,1,0:T(8,128)S(1)} %slice.62), channel_id=1, source_target_pairs={{0,1},{1,0},{2,3},{3,2},{4,5},{5,4},{6,7},{7,6},{8,9},{9,8},{10,11... | collective-permute-start | bytes 1376264 | tf_op jit(solution)/shard_map/ppermute | solution.py:1274
  50.6 6.4 %collective-permute-start.16 = (f32[4,64,128]{2,1,0:T(8,128)S(1)}, f32[4,64,128]{2,1,0:T(8,128)S(1)}, u32[]{:S(2)}, u32[]{:S(2)}) collective-permute-start(f32[4,64,128]{2,1,0:T(8,128)S(1)} %slice.68), channel_id=1, source_target_pairs={{0,4},{1,5},{2,6},{3,7},{4,0},{5,1},{6,2},{7,3},{8,12},{9,13},{10,... | collective-permute-start | bytes 393224 | tf_op jit(solution)/shard_map/ppermute | solution.py:1274
  52.4 9.0 %collective-permute-start.13 = (f32[4,56,128]{2,1,0:T(8,128)S(1)}, f32[4,56,128]{2,1,0:T(8,128)S(1)}, u32[]{:S(2)}, u32[]{:S(2)}) collective-permute-start(f32[4,56,128]{2,1,0:T(8,128)S(1)} %get-tuple-element.308), channel_id=1, source_target_pairs={{0,4},{1,5},{2,6},{3,7},{4,0},{5,1},{6,2},{7,3},{8,12},{9,13},{10,... | collective-permute-start | bytes 344072 | tf_op jit(solution)/shard_map/ppermute | solution.py:1274
  53.4 8.0 %collective-permute-start.15 = (f32[4,56,128]{2,1,0:T(8,128)S(1)}, f32[4,56,128]{2,1,0:T(8,128)S(1)}, u32[]{:S(2)}, u32[]{:S(2)}) collective-permute-start(f32[4,56,128]{2,1,0:T(8,128)S(1)} %get-tuple-element.309), channel_id=1, source_target_pairs={{0,2},{1,3},{2,0},{3,1},{4,6},{5,7},{6,4},{7,5},{8,10},{9,11},{10,... | collective-permute-start | bytes 344072 | tf_op jit(solution)/shard_map/ppermute | solution.py:1274
  54.4 7.0 %collective-permute-start.14 = (f32[4,56,128]{2,1,0:T(8,128)S(1)}, f32[4,56,128]{2,1,0:T(8,128)S(1)}, u32[]{:S(2)}, u32[]{:S(2)}) collective-permute-start(f32[4,56,128]{2,1,0:T(8,128)S(1)} %get-tuple-element.310), channel_id=1, source_target_pairs={{0,6},{1,7},{2,4},{3,5},{4,2},{5,3},{6,0},{7,1},{8,14},{9,15},{10,... | collective-permute-start | bytes 344072 | tf_op jit(solution)/shard_map/ppermute | solution.py:1274
  61.5 5.9 %collective-permute-start.17 = (f32[1,120,128]{2,1,0:T(8,128)S(1)}, f32[1,120,128]{2,1,0:T(8,128)S(1)}, u32[]{:S(2)}, u32[]{:S(2)}) collective-permute-start(f32[1,120,128]{2,1,0:T(8,128)S(1)} %get-tuple-element.311), channel_id=1, source_target_pairs={{0,16},{1,17},{2,18},{3,19},{4,20},{5,21},{6,22},{7,23},{8,24},{9,... | collective-permute-start | bytes 184328 | tf_op jit(solution)/shard_map/ppermute | solution.py:1274
  61.6 5.8 %collective-permute-start.19 = (f32[1,120,128]{2,1,0:T(8,128)S(1)}, f32[1,120,128]{2,1,0:T(8,128)S(1)}, u32[]{:S(2)}, u32[]{:S(2)}) collective-permute-start(f32[1,120,128]{2,1,0:T(8,128)S(1)} %get-tuple-element.312), channel_id=1, source_target_pairs={{0,8},{1,9},{2,10},{3,11},{4,12},{5,13},{6,14},{7,15},{8,0},{9,1},... | collective-permute-start | bytes 184328 | tf_op jit(solution)/shard_map/ppermute | solution.py:1274
  63.3 6.1 %collective-permute-start.18 = (f32[1,120,128]{2,1,0:T(8,128)S(1)}, f32[1,120,128]{2,1,0:T(8,128)S(1)}, u32[]{:S(2)}, u32[]{:S(2)}) collective-permute-start(f32[1,120,128]{2,1,0:T(8,128)S(1)} %get-tuple-element.313), channel_id=1, source_target_pairs={{0,24},{1,25},{2,26},{3,27},{4,28},{5,29},{6,30},{7,31},{8,16},{9,... | collective-permute-start | bytes 184328 | tf_op jit(solution)/shard_map/ppermute | solution.py:1274
  69.5 6.0 %collective-permute-start.22 = (f32[1,112,128]{2,1,0:T(8,128)S(1)}, f32[1,112,128]{2,1,0:T(8,128)S(1)}, u32[]{:S(2)}, u32[]{:S(2)}) collective-permute-start(f32[1,112,128]{2,1,0:T(8,128)S(1)} %slice.82), channel_id=1, source_target_pairs={{0,24},{1,25},{2,26},{3,27},{4,28},{5,29},{6,30},{7,31},{8,16},{9,... | collective-permute-start | bytes 172040 | tf_op jit(solution)/shard_map/ppermute | solution.py:1274
  72.1 4.2 %collective-permute-start.21 = (f32[1,112,128]{2,1,0:T(8,128)S(1)}, f32[1,112,128]{2,1,0:T(8,128)S(1)}, u32[]{:S(2)}, u32[]{:S(2)}) collective-permute-start(f32[1,112,128]{2,1,0:T(8,128)S(1)} %slice.82), channel_id=1, source_target_pairs={{0,8},{1,9},{2,10},{3,11},{4,12},{5,13},{6,14},{7,15},{8,0},{9,1},... | collective-permute-start | bytes 172040 | tf_op jit(solution)/shard_map/ppermute | solution.py:1274
  72.1 5.1 %collective-permute-start.20 = (f32[1,112,128]{2,1,0:T(8,128)S(1)}, f32[1,112,128]{2,1,0:T(8,128)S(1)}, u32[]{:S(2)}, u32[]{:S(2)}) collective-permute-start(f32[1,112,128]{2,1,0:T(8,128)S(1)} %slice.82), channel_id=1, source_target_pairs={{0,16},{1,17},{2,18},{3,19},{4,20},{5,21},{6,22},{7,23},{8,24},{9,... | collective-permute-start | bytes 172040 | tf_op jit(solution)/shard_map/ppermute | solution.py:1274
  77.2 7.4 %collective-permute-start.25 = (f32[4,112,128]{2,1,0:T(8,128)S(1)}, f32[4,112,128]{2,1,0:T(8,128)S(1)}, u32[]{:S(2)}, u32[]{:S(2)}) collective-permute-start(f32[4,112,128]{2,1,0:T(8,128)S(1)} %pad_maximum_fusion.refs_0_), channel_id=1, source_target_pairs={{0,6},{1,7},{2,4},{3,5},{4,2},{5,3},{6,0},{7,1},{8,14},{9,15},{10,... | collective-permute-start | bytes 688136 | tf_op jit(solution)/shard_map/ppermute | solution.py:1274
  78.6 7.8 %collective-permute-start.24 = (f32[4,112,128]{2,1,0:T(8,128)S(1)}, f32[4,112,128]{2,1,0:T(8,128)S(1)}, u32[]{:S(2)}, u32[]{:S(2)}) collective-permute-start(f32[4,112,128]{2,1,0:T(8,128)S(1)} %pad_maximum_fusion.refs_0_), channel_id=1, source_target_pairs={{0,2},{1,3},{2,0},{3,1},{4,6},{5,7},{6,4},{7,5},{8,10},{9,11},{10,... | collective-permute-start | bytes 688136 | tf_op jit(solution)/shard_map/ppermute | solution.py:1274
  79.7 7.2 %collective-permute-start.23 = (f32[4,112,128]{2,1,0:T(8,128)S(1)}, f32[4,112,128]{2,1,0:T(8,128)S(1)}, u32[]{:S(2)}, u32[]{:S(2)}) collective-permute-start(f32[4,112,128]{2,1,0:T(8,128)S(1)} %pad_maximum_fusion.refs_0_), channel_id=1, source_target_pairs={{0,4},{1,5},{2,6},{3,7},{4,0},{5,1},{6,2},{7,3},{8,12},{9,13},{10,... | collective-permute-start | bytes 688136 | tf_op jit(solution)/shard_map/ppermute | solution.py:1274
  80.7 6.2 %collective-permute-start.26 = (f32[4,112,128]{2,1,0:T(8,128)S(1)}, f32[4,112,128]{2,1,0:T(8,128)S(1)}, u32[]{:S(2)}, u32[]{:S(2)}) collective-permute-start(f32[4,112,128]{2,1,0:T(8,128)S(1)} %pad_maximum_fusion.refs_0_), channel_id=1, source_target_pairs={{0,1},{1,0},{2,3},{3,2},{4,5},{5,4},{6,7},{7,6},{8,9},{9,8},{10,11... | collective-permute-start | bytes 688136 | tf_op jit(solution)/shard_map/ppermute | solution.py:1274
  84.6 2.4 %collective-permute-start.29 = (f32[4,112,128]{2,1,0:T(8,128)S(1)}, f32[4,112,128]{2,1,0:T(8,128)S(1)}, u32[]{:S(2)}, u32[]{:S(2)}) collective-permute-start(f32[4,112,128]{2,1,0:T(8,128)S(1)} %collective-permute-done.25.refs_3_), channel_id=1, source_target_pairs={{0,1},{1,0},{2,3},{3,2},{4,5},{5,4},{6,7},{7,6},{8,9},{9,8},{10,11... | collective-permute-start | bytes 688136 | tf_op jit(solution)/shard_map/ppermute | solution.py:1274
  86.3 1.5 %collective-permute-start.28 = (f32[4,112,128]{2,1,0:T(8,128)S(1)}, f32[4,112,128]{2,1,0:T(8,128)S(1)}, u32[]{:S(2)}, u32[]{:S(2)}) collective-permute-start(f32[4,112,128]{2,1,0:T(8,128)S(1)} %collective-permute-done.24.refs_2_), channel_id=1, source_target_pairs={{0,1},{1,0},{2,3},{3,2},{4,5},{5,4},{6,7},{7,6},{8,9},{9,8},{10,11... | collective-permute-start | bytes 688136 | tf_op jit(solution)/shard_map/ppermute | solution.py:1274
  87.0 1.5 %collective-permute-start.27 = (f32[4,112,128]{2,1,0:T(8,128)S(1)}, f32[4,112,128]{2,1,0:T(8,128)S(1)}, u32[]{:S(2)}, u32[]{:S(2)}) collective-permute-start(f32[4,112,128]{2,1,0:T(8,128)S(1)} %collective-permute-done.23.refs_1_), channel_id=1, source_target_pairs={{0,1},{1,0},{2,3},{3,2},{4,5},{5,4},{6,7},{7,6},{8,9},{9,8},{10,11... | collective-permute-start | bytes 688136 | tf_op jit(solution)/shard_map/ppermute | solution.py:1274

commit v5 on v4

--- a/solution.py
+++ b/solution.py
@@ -112,11 +112,15 @@
     return tuple(pltpu.with_memory_space_constraint(x, pltpu.HBM) for x in arrays)
 
 
-def edges_kernel(tok, resets, pad, *refs):
-    more = (len(refs) - 5) // 2
-    to_sib, to_oth, *kept = refs[more:]
-    for ref, kept_o in zip((tok, resets, pad) + refs[:more], kept):
-        kept_o[...] = ref[...]
+def edges_kernel(*refs):
+    count = (len(refs) - 3) // 2
+    far, to_sib, to_oth, near, arrived = refs[:count], refs[count], refs[count + 1], refs[count + 2 : -1], refs[-1]
+    copies = [pltpu.make_async_copy(one, two, arrived.at[i]) for i, (one, two) in enumerate(zip(far, near))]
+    for copy in copies:
+        copy.start()
+    for copy in copies[:3]:
+        copy.wait()
+    tok, resets, pad = near[:3]
     length, feat = tok.shape
     sub = lax.broadcasted_iota(jnp.int32, (CH, length), 0)
     lane = lax.broadcasted_iota(jnp.int32, (CH, length), 1)
@@ -134,13 +138,18 @@
     odd = (lax.axis_index("seq") & 1) == 1
     to_sib[...] = jnp.where(odd, first, last)
     to_oth[...] = jnp.where(odd, last, first)
+    for copy in copies[3:]:
+        copy.wait()
 
 
 def edges(*arrays):
     shape = jax.ShapeDtypeStruct((CH, arrays[0].shape[1]), F32)
     found = pl.pallas_call(
         edges_kernel,
+        in_specs=[pl.BlockSpec(memory_space=pl.ANY)] * len(arrays),
+        out_specs=(pl.BlockSpec(memory_space=pltpu.VMEM),) * (2 + len(arrays)),
         out_shape=(shape, shape) + tuple(jax.ShapeDtypeStruct(x.shape, x.dtype) for x in arrays),
+        scratch_shapes=[pltpu.SemaphoreType.DMA((len(arrays),))],
         compiler_params=params(8),
         name="edges",
     )(*in_hbm(*arrays))
@@ -623,7 +632,7 @@
     state = a2_s.shape[0]
     carry_in(car_o, a2_s, mine_half, other_half, sibling)
     y_s[...] = jnp.zeros(y_s.shape, F32)
-    group = 4
+    group = 8
     cols_of = [slice(t * LANE, (t + 1) * LANE) for t in range(tiles)]
     for dirn in range(2):
         order = list(range(steps)) if dirn == 0 else list(range(steps - 1, -1, -1))
@@ -809,7 +818,7 @@
     order = list(range(steps)) if dirn == 0 else list(range(steps - 1, -1, -1))
     base = dirn * length
     m_row = 3 if dirn == 0 else 1
-    group = 2
+    group = 8
     low = lax.broadcasted_iota(jnp.int32, (CH, LANE), 1) < LANE // 2
     cols_of = [slice(t * LANE, (t + 1) * LANE) for t in range(tiles)]
     sb_s[...] = jnp.zeros(sb_s.shape, F32)
@@ -823,13 +832,14 @@
     def some(g, carry):
         n0 = g * group
         at_b, at_c = lanes_of(n0, group), lanes_of(state + n0, group)
-        a2, q, ga = {}, {}, {}
+        a2, q, ga, now = {}, {}, {}, {}
         for n in range(group):
             for t, cols in enumerate(cols_of):
                 a2[n, t] = a2_s[n0 + n, :, cols]
                 into = jnp.exp2(after_s[:, cols] * a2[n, t]) * car[m_row * state + n0 + n, :, cols]
                 q[n, t] = mx[dirn, n0 + n, :, cols] + into
                 ga[n, t] = jnp.zeros((CH, LANE), F32)
+                now[n, t] = h_s[dirn, steps, n0 + n, :, cols]
         for time in range(steps - 1, -1, -1):
             j = order[time]
             rows = slice(base + j * CH, base + (j + 1) * CH)
@@ -844,19 +854,20 @@
                 to_b = to_c = None
                 for t, cols in enumerate(cols_of):
                     gh = gyj[t] * c_n + q[n, t]
-                    term_c = gyj[t] * h_s[dirn, time + 1, n0 + n, :, cols]
+                    term_c = gyj[t] * now[n, t]
                     term_b = gh * dx[t]
                     to_b = term_b if t == 0 else to_b + term_b
                     to_c = term_c if t == 0 else to_c + term_c
                     q[n, t] = decay[dirn, time, n0 + n, :, cols] * gh
-                    r = q[n, t] * h_s[dirn, time, n0 + n, :, cols]
+                    now[n, t] = h_s[dirn, time, n0 + n, :, cols]
+                    r = q[n, t] * now[n, t]
                     ga[n, t] = ga[n, t] + de[t] * r
                     sb[t] = gh * b_n if n == 0 else sb[t] + gh * b_n
                     sa[t] = a2[n, t] * r if n == 0 else sa[t] + a2[n, t] * r
                 sums.append((to_b, to_c))
-            at = pl.ds(pl.multiple_of(g * LANE, LANE), LANE)
-            for acc, one, two in ((accb, sums[0][0], sums[1][0]), (accc, sums[0][1], sums[1][1])):
-                acc[here, at] = jnp.where(low, one, two) + pltpu.roll(jnp.where(low, two, one), LANE // 2, 1)
+            for i, at in enumerate(lanes_of(g * (group // 2), group // 2)):
+                for acc, one, two in zip((accb, accc), sums[2 * i], sums[2 * i + 1]):
+                    acc[here, at] = jnp.where(low, one, two) + pltpu.roll(jnp.where(low, two, one), LANE // 2, 1)
             for t, cols in enumerate(cols_of):
                 sb_s[here, cols] += sb[t]
                 sa_s[here, cols] += sa[t]

time: 90.1 us -> 89.3 us (level)
  Pallas kernels: 26.8 us -> 25.6 us
  transfers between devices with their start and end apart: 30 -> 30, of which waited for: 19 -> 21; matrix products, arithmetic and copies ran while one was open for 0% -> 0% of each run, Pallas kernels for 17% -> 16%
where the time goes in v5:
time: 89.3 us; the launch traced here: 89.1 us
  starting transfers between devices  33.5 us (38%)
  waiting for transfers between devices  28.8 us (32%)
  Pallas kernels  25.6 us (29%)
    ppermute x29, starting transfers between devices, exchange(): return lax.ppermute(value, 'seq', [(i, i ^ apart) for i in range(count)])  32.9 us
    ppermute x29, waiting for transfers between devices, exchange(): return lax.ppermute(value, 'seq', [(i, i ^ apart) for i in range(count)])  28.8 us
    pallas_call x1, Pallas kernels, prepare(): pl.pallas_call(prepare_kernel, out_shape=(big, big, big, big, pltpu.VMEM(...  5.83 us
    pallas_call x2, Pallas kernels, backward(): pl.pallas_call(lambda *refs: backward_kernel(dirn, *refs), out_shape=(hal...  4.77 us
    pallas_call x1, Pallas kernels, inner_back(): pl.pallas_call(inner_kernel, out_shape=(part, part, jax.ShapeDtypeStruct(...  2.25 us
    pallas_call x1, Pallas kernels, tail(): pl.pallas_call(lambda *refs: tail_kernel(rs_bits, *refs), out_shape=(jax....  2 us
    pallas_call x1, Pallas kernels, ready(): pl.pallas_call(lambda *refs: ready_kernel(rank, *refs), out_shape=(f32(le...  1.92 us
  transfers between devices with their start and end apart: 30, of which 21 were waited for; matrix products, arithmetic and copies ran while one was open for 0% of the time, Pallas kernels for 16%

profile of v5, /device:TPU:0, one launch (start us, length us, event | category | flops | bytes accessed | tf_op | source)
XLA Modules:
  0.0 89.1 jit_solution(892603347868866914)
XLA Ops:
  0.6 1.7 %edges.1 = (f32[8,256]{1,0:T(8,128)S(1)}, f32[8,256]{1,0:T(8,128)S(1)}, f32[128,256]{1,0:T(8,128)S(1)}, s32[1,128]{1,0:T(1,128)S(1)}, s32[1,128]{1,0:T(1,128)S(1...) custom-call(f32[128,256]{1,0:T(8,128)} %refs_0_.1, ...), custom_call_target="tpu_custom_call" | custom-call | tf_op jit(solution)/shard_map/edges/pallas_call | solution.py:147
  2.9 0.6 collective-permute-start.1
  3.5 1.7 %project.1 = (f32[256,512]{1,0:T(8,128)S(1)}, f32[256,512]{1,0:T(8,128)S(1)}, f32[256,512]{1,0:T(8,128)S(1)}, f32[256,512]{1,0:T(8,128)S(1)}, bf16[256,1024]{1,0...) custom-call(f32[128,256]{1,0:T(8,128)S(1)} %get-tuple-element.160.tok.ref, ...), custom_call_target="tpu_custom_call" | custom-call | tf_op jit(solution)/shard_map/project/pallas_call | solution.py:192
  5.3 5.8 %prepare.1 = (f32[256,512]{1,0:T(8,128)S(1)}, f32[256,512]{1,0:T(8,128)S(1)}, f32[256,512]{1,0:T(8,128)S(1)}, f32[256,512]{1,0:T(8,128)S(1)}, f32[768,128]{1,0:T...) custom-call(f32[8,256]{1,0:T(8,128)S(1)} %collective-permute-done.si, ...), custom_call_target="tpu_custom_call" | custom-call | tf_op jit(solution)/shard_map/prepare/pallas_call | solution.py:420
  11.1 3.9 %collective-permute-start.2 = (f32[72,512]{1,0:T(8,128)S(1)}, f32[72,512]{1,0:T(8,128)S(1)}, u32[]{:S(2)}, u32[]{:S(2)}) collective-permute-start(f32[72,512]{1,0:T(8,128)S(1)} %get-tuple-element.181.mine), channel_id=1, source_target_pairs={{0,1},{1,0},{2,3},{3,2},{4,5},{5,4},{6,7},{7,6},{8,9},{9,8},{10,11... | collective-permute-start | bytes 442376 | tf_op jit(solution)/shard_map/ppermute | solution.py:1285
  15.1 1.0 %collective-permute-done.2.theirs.sibling = f32[72,512]{1,0:T(8,128)S(1)} collective-permute-done((f32[72,512]{1,0:T(8,128)S(1)}, f32[72,512]{1,0:T(8,128)S(1)}, u32[]{:S(2)}, u32[]{:S(2)}) %collective-permute-start.2) | collective-permute-done | bytes 147488 | tf_op jit(solution)/shard_map/ppermute | solution.py:1285
  16.1 4.5 %collective-permute-start.5 = (f32[72,256]{1,0:T(8,128)S(1)}, f32[72,256]{1,0:T(8,128)S(1)}, u32[]{:S(2)}, u32[]{:S(2)}) collective-permute-start(f32[72,256]{1,0:T(8,128)S(1)} %pair.1.refs_1_), channel_id=1, source_target_pairs={{0,6},{1,7},{2,4},{3,5},{4,2},{5,3},{6,0},{7,1},{8,14},{9,15},{10,... | collective-permute-start | bytes 221192 | tf_op jit(solution)/shard_map/ppermute | solution.py:1285
  20.6 0.6 collective-permute-start.3
  21.2 1.9 %ready.1 = (f32[128,256]{1,0:T(8,128)S(1)}, f32[128,256]{1,0:T(8,128)S(1)}, bf16[256,256]{1,0:T(8,128)(2,1)S(1)}, bf16[256,256]{1,0:T(8,128)(2,1)S(1)}, bf16[256...) custom-call(f32[128,256]{1,0:T(8,128)S(1)} %get-tuple-element.160.to, ...), custom_call_target="tpu_custom_call" | custom-call | tf_op jit(solution)/shard_map/ready/pallas_call | solution.py:733
  23.4 1.6 %collective-permute-done.4.refs_3_ = f32[72,256]{1,0:T(8,128)S(1)} collective-permute-done((f32[72,256]{1,0:T(8,128)S(1)}, f32[72,256]{1,0:T(8,128)S(1)}, u32[]{:S(2)}, u32[]{:S(2)}) %collective-permute-start.4) | collective-permute-done | bytes 73760 | tf_op jit(solution)/shard_map/ppermute | solution.py:1285
  25.0 1.6 %collective-permute-start.6 = (f32[40,256]{1,0:T(8,128)S(1)}, f32[40,256]{1,0:T(8,128)S(1)}, u32[]{:S(2)}, u32[]{:S(2)}) collective-permute-start(f32[40,256]{1,0:T(8,128)S(1)} %get-tuple-element.226), channel_id=1, source_target_pairs={{0,8},{1,9},{2,10},{3,11},{4,12},{5,13},{6,14},{7,15},{8,0},{9,1},... | collective-permute-start | bytes 122888 | tf_op jit(solution)/shard_map/ppermute | solution.py:1285
  26.7 2.2 %collective-permute-start.7 = (f32[40,256]{1,0:T(8,128)S(1)}, f32[40,256]{1,0:T(8,128)S(1)}, u32[]{:S(2)}, u32[]{:S(2)}) collective-permute-start(f32[40,256]{1,0:T(8,128)S(1)} %get-tuple-element.227), channel_id=1, source_target_pairs={{0,16},{1,17},{2,18},{3,19},{4,20},{5,21},{6,22},{7,23},{8,24},{9,... | collective-permute-start | bytes 122888 | tf_op jit(solution)/shard_map/ppermute | solution.py:1285
  28.9 0.6 collective-permute-start.8
  29.5 3.0 %collective-permute-done.7.refs_2_ = f32[40,256]{1,0:T(8,128)S(1)} collective-permute-done((f32[40,256]{1,0:T(8,128)S(1)}, f32[40,256]{1,0:T(8,128)S(1)}, u32[]{:S(2)}, u32[]{:S(2)}) %collective-permute-start.7) | collective-permute-done | bytes 40992 | tf_op jit(solution)/shard_map/ppermute | solution.py:1285
  32.5 2.2 %collective-permute-done.8.refs_3_ = f32[40,256]{1,0:T(8,128)S(1)} collective-permute-done((f32[40,256]{1,0:T(8,128)S(1)}, f32[40,256]{1,0:T(8,128)S(1)}, u32[]{:S(2)}, u32[]{:S(2)}) %collective-permute-start.8) | collective-permute-done | bytes 40992 | tf_op jit(solution)/shard_map/ppermute | solution.py:1285
  34.8 1.2 %collective-permute-done.9.other_half = f32[64,256]{1,0:T(8,128)S(1)} collective-permute-done((f32[64,256]{1,0:T(8,128)S(1)}, f32[64,256]{1,0:T(8,128)S(1)}, u32[]{:S(2)}, u32[]{:S(2)}) %collective-permute-start.9) | collective-permute-done | bytes 65568 | tf_op jit(solution)/shard_map/ppermute | solution.py:1285
  36.1 1.5 %forward.1 = (f32[256,512]{1,0:T(8,128)S(1)}, f32[2,17,16,8,512]{4,3,2,1,0:T(8,128)S(1)}, f32[64,8,512]{2,1,0:T(8,128)S(1)}) custom-call(f32[64,256]{1,0:T(8,128)S(1)} %enter.1.mine_half, f32[64,256]{1,0:T(8,128)S(1)} %collective-permute-done.9.other_half, f32[72,512]{1,0:T(8,128)S(1)} %collective-permute-done.2.theirs.sibling, ...), custom_call_target="tpu_custom_call" | custom-call | tf_op jit(solution)/shard_map/forward/pallas_call | solution.py:678
  37.6 0.7 early.1
  38.6 2.3 %backward.2 = (f32[128,512]{1,0:T(8,128)S(1)}, f32[128,512]{1,0:T(8,128)S(1)}, f32[128,1024]{1,0:T(8,128)S(1)}, f32[128,1024]{1,0:T(8,128)S(1)}, f32[16,8,512]{2,1,0:T(8,128)S(1)}) custom-call(f32[2,16,8,512]{3,2,1,0:T(8,128)S(1)} %get-tuple-element.239.refs_0_, f32[64,8,512]{2,1,0:T(8,128)S(1)} %get-tuple-element.240.refs_1_, ...), custom_call_target="tpu_custom_call" | custom-call | tf_op jit(solution)/shard_map/backward/pallas_call | solution.py:888
  41.1 1.4 %collective-permute-start.11 = (f32[8,64,128]{2,1,0:T(8,128)S(1)}, f32[8,64,128]{2,1,0:T(8,128)S(1)}, u32[]{:S(2)}, u32[]{:S(2)}) collective-permute-start(f32[8,64,128]{2,1,0:T(8,128)S(1)} %slice.60), channel_id=1, source_target_pairs={{0,2},{1,3},{2,0},{3,1},{4,6},{5,7},{6,4},{7,5},{8,10},{9,11},{10,... | collective-permute-start | bytes 786440 | tf_op jit(solution)/shard_map/ppermute | solution.py:1285
  42.4 2.5 %backward.3 = (f32[128,512]{1,0:T(8,128)S(1)}, f32[128,512]{1,0:T(8,128)S(1)}, f32[128,1024]{1,0:T(8,128)S(1)}, f32[128,1024]{1,0:T(8,128)S(1)}, f32[16,8,512]{2,1,0:T(8,128)S(1)}) custom-call(f32[2,16,8,512]{3,2,1,0:T(8,128)S(1)} %get-tuple-element.239.refs_0_, f32[64,8,512]{2,1,0:T(8,128)S(1)} %get-tuple-element.240.refs_1_, ...), custom_call_target="tpu_custom_call" | custom-call | tf_op jit(solution)/shard_map/backward/pallas_call | solution.py:888
  44.9 2.3 %inner.1 = (bf16[256,512]{1,0:T(8,128)(2,1)S(1)}, bf16[256,512]{1,0:T(8,128)(2,1)S(1)}, f32[16,512]{1,0:T(8,128)S(1)}, f32[88,512]{1,0:T(8,128)S(1)}) custom-call(s32[1,128]{1,0:T(1,128)S(1)} %get-tuple-element.161.pad.refs_10_, f32[4,512]{1,0:T(4,128)S(1)} %get-tuple-element.173.conv_w, f32[48,512]{1,0:T(8,128)S(1)} %get-tuple-element.175.w_x, ...), custom_call_target="tpu_custom_call" | custom-call | tf_op jit(solution)/shard_map/inner/pallas_call | solution.py:1031
  47.2 2.0 %tail.1 = (f32[128,256]{1,0:T(8,128)S(1)}, f32[32,56,128]{2,1,0:T(8,128)S(1)}) custom-call(f32[8,256]{1,0:T(8,128)S(1)} %collective-permute-done.sib.refs_0_, f32[8,256]{1,0:T(8,128)S(1)} %collective-permute-done.1.oth.refs_1_, f32[1,256]{1,0:T(1,128)S(1)} %get-tuple-element.162.gain.refs_2_, f32[128,256]{1,0:T(8,128)S(1)} %get-tuple-element.248.refs_3_.x_s, ...), custom_call_target="tpu_custom_call" | custom-call | tf_op jit(solution)/shard_map/tail/pallas_call | solution.py:1150
  49.9 1.0 %collective-permute-start.16 = (f32[4,64,128]{2,1,0:T(8,128)S(1)}, f32[4,64,128]{2,1,0:T(8,128)S(1)}, u32[]{:S(2)}, u32[]{:S(2)}) collective-permute-start(f32[4,64,128]{2,1,0:T(8,128)S(1)} %slice.68), channel_id=1, source_target_pairs={{0,4},{1,5},{2,6},{3,7},{4,0},{5,1},{6,2},{7,3},{8,12},{9,13},{10,... | collective-permute-start | bytes 393224 | tf_op jit(solution)/shard_map/ppermute | solution.py:1285
  50.9 0.8 collective-permute-done.12
  51.8 1.0 %collective-permute-start.13 = (f32[4,56,128]{2,1,0:T(8,128)S(1)}, f32[4,56,128]{2,1,0:T(8,128)S(1)}, u32[]{:S(2)}, u32[]{:S(2)}) collective-permute-start(f32[4,56,128]{2,1,0:T(8,128)S(1)} %get-tuple-element.308), channel_id=1, source_target_pairs={{0,4},{1,5},{2,6},{3,7},{4,0},{5,1},{6,2},{7,3},{8,12},{9,13},{10,... | collective-permute-start | bytes 344072 | tf_op jit(solution)/shard_map/ppermute | solution.py:1285
  52.8 1.0 %collective-permute-start.15 = (f32[4,56,128]{2,1,0:T(8,128)S(1)}, f32[4,56,128]{2,1,0:T(8,128)S(1)}, u32[]{:S(2)}, u32[]{:S(2)}) collective-permute-start(f32[4,56,128]{2,1,0:T(8,128)S(1)} %get-tuple-element.309), channel_id=1, source_target_pairs={{0,2},{1,3},{2,0},{3,1},{4,6},{5,7},{6,4},{7,5},{8,10},{9,11},{10,... | collective-permute-start | bytes 344072 | tf_op jit(solution)/shard_map/ppermute | solution.py:1285
  53.7 1.6 %collective-permute-start.14 = (f32[4,56,128]{2,1,0:T(8,128)S(1)}, f32[4,56,128]{2,1,0:T(8,128)S(1)}, u32[]{:S(2)}, u32[]{:S(2)}) collective-permute-start(f32[4,56,128]{2,1,0:T(8,128)S(1)} %get-tuple-element.310), channel_id=1, source_target_pairs={{0,6},{1,7},{2,4},{3,5},{4,2},{5,3},{6,0},{7,1},{8,14},{9,15},{10,... | collective-permute-start | bytes 344072 | tf_op jit(solution)/shard_map/ppermute | solution.py:1285
  55.3 0.9 %collective-permute-done.16 = f32[4,64,128]{2,1,0:T(8,128)S(1)} collective-permute-done((f32[4,64,128]{2,1,0:T(8,128)S(1)}, f32[4,64,128]{2,1,0:T(8,128)S(1)}, u32[]{:S(2)}, u32[]{:S(2)}) %collective-permute-start.16) | collective-permute-done | bytes 131104 | tf_op jit(solution)/shard_map/ppermute | solution.py:1285
  56.2 1.3 %finish.1 = (f32[128,256]{1,0:T(8,128)}, f32[128,256]{1,0:T(8,128)S(1)}) custom-call(f32[128,256]{1,0:T(8,128)S(1)} %get-tuple-element.248.refs_3_.x_s, f32[128,256]{1,0:T(8,128)S(1)} %get-tuple-element.283.g, f32[1,256]{1,0:T(1,128)S(1)} %get-tuple-element.162.gain.refs_2_, f32[128,256]{1,0:T(8,128)S(1)} %get-tuple-element.284.g_normed, ...), custom_call_target="tpu_custom_call" | custom-call | tf_op jit(solution)/shard_map/finish/pallas_call | solution.py:1136
  57.6 1.8 %collective-permute-done.13 = f32[4,56,128]{2,1,0:T(8,128)S(1)} collective-permute-done((f32[4,56,128]{2,1,0:T(8,128)S(1)}, f32[4,56,128]{2,1,0:T(8,128)S(1)}, u32[]{:S(2)}, u32[]{:S(2)}) %collective-permute-start.13) | collective-permute-done | bytes 114720 | tf_op jit(solution)/shard_map/ppermute | solution.py:1285
  59.4 1.3 %collective-permute-done.14 = f32[4,56,128]{2,1,0:T(8,128)S(1)} collective-permute-done((f32[4,56,128]{2,1,0:T(8,128)S(1)}, f32[4,56,128]{2,1,0:T(8,128)S(1)}, u32[]{:S(2)}, u32[]{:S(2)}) %collective-permute-start.14) | collective-permute-done | bytes 114720 | tf_op jit(solution)/shard_map/ppermute | solution.py:1285
  60.9 1.5 %collective-permute-start.19 = (f32[1,120,128]{2,1,0:T(8,128)S(1)}, f32[1,120,128]{2,1,0:T(8,128)S(1)}, u32[]{:S(2)}, u32[]{:S(2)}) collective-permute-start(f32[1,120,128]{2,1,0:T(8,128)S(1)} %get-tuple-element.312), channel_id=1, source_target_pairs={{0,8},{1,9},{2,10},{3,11},{4,12},{5,13},{6,14},{7,15},{8,0},{9,1},... | collective-permute-start | bytes 184328 | tf_op jit(solution)/shard_map/ppermute | solution.py:1285
  62.3 2.9 %collective-permute-start.18 = (f32[1,120,128]{2,1,0:T(8,128)S(1)}, f32[1,120,128]{2,1,0:T(8,128)S(1)}, u32[]{:S(2)}, u32[]{:S(2)}) collective-permute-start(f32[1,120,128]{2,1,0:T(8,128)S(1)} %get-tuple-element.313), channel_id=1, source_target_pairs={{0,24},{1,25},{2,26},{3,27},{4,28},{5,29},{6,30},{7,31},{8,16},{9,... | collective-permute-start | bytes 184328 | tf_op jit(solution)/shard_map/ppermute | solution.py:1285
  65.3 1.4 %collective-permute-done.17 = f32[1,120,128]{2,1,0:T(8,128)S(1)} collective-permute-done((f32[1,120,128]{2,1,0:T(8,128)S(1)}, f32[1,120,128]{2,1,0:T(8,128)S(1)}, u32[]{:S(2)}, u32[]{:S(2)}) %collective-permute-start.17) | collective-permute-done | bytes 61472 | tf_op jit(solution)/shard_map/ppermute | solution.py:1285
  66.6 1.8 %collective-permute-done.18 = f32[1,120,128]{2,1,0:T(8,128)S(1)} collective-permute-done((f32[1,120,128]{2,1,0:T(8,128)S(1)}, f32[1,120,128]{2,1,0:T(8,128)S(1)}, u32[]{:S(2)}, u32[]{:S(2)}) %collective-permute-start.18) | collective-permute-done | bytes 61472 | tf_op jit(solution)/shard_map/ppermute | solution.py:1285
  68.4 3.0 %collective-permute-start.22 = (f32[1,112,128]{2,1,0:T(8,128)S(1)}, f32[1,112,128]{2,1,0:T(8,128)S(1)}, u32[]{:S(2)}, u32[]{:S(2)}) collective-permute-start(f32[1,112,128]{2,1,0:T(8,128)S(1)} %slice.82), channel_id=1, source_target_pairs={{0,24},{1,25},{2,26},{3,27},{4,28},{5,29},{6,30},{7,31},{8,16},{9,... | collective-permute-start | bytes 172040 | tf_op jit(solution)/shard_map/ppermute | solution.py:1285
  71.4 1.5 %collective-permute-start.20 = (f32[1,112,128]{2,1,0:T(8,128)S(1)}, f32[1,112,128]{2,1,0:T(8,128)S(1)}, u32[]{:S(2)}, u32[]{:S(2)}) collective-permute-start(f32[1,112,128]{2,1,0:T(8,128)S(1)} %slice.82), channel_id=1, source_target_pairs={{0,16},{1,17},{2,18},{3,19},{4,20},{5,21},{6,22},{7,23},{8,24},{9,... | collective-permute-start | bytes 172040 | tf_op jit(solution)/shard_map/ppermute | solution.py:1285
  72.9 1.8 %collective-permute-done.22 = f32[1,112,128]{2,1,0:T(8,128)S(1)} collective-permute-done((f32[1,112,128]{2,1,0:T(8,128)S(1)}, f32[1,112,128]{2,1,0:T(8,128)S(1)}, u32[]{:S(2)}, u32[]{:S(2)}) %collective-permute-start.22) | collective-permute-done | bytes 57376 | tf_op jit(solution)/shard_map/ppermute | solution.py:1285
  74.7 0.9 %collective-permute-done.21 = f32[1,112,128]{2,1,0:T(8,128)S(1)} collective-permute-done((f32[1,112,128]{2,1,0:T(8,128)S(1)}, f32[1,112,128]{2,1,0:T(8,128)S(1)}, u32[]{:S(2)}, u32[]{:S(2)}) %collective-permute-start.21) | collective-permute-done | bytes 57376 | tf_op jit(solution)/shard_map/ppermute | solution.py:1285
  75.6 0.9 %collective-permute-done.20 = f32[1,112,128]{2,1,0:T(8,128)S(1)} collective-permute-done((f32[1,112,128]{2,1,0:T(8,128)S(1)}, f32[1,112,128]{2,1,0:T(8,128)S(1)}, u32[]{:S(2)}, u32[]{:S(2)}) %collective-permute-start.20) | collective-permute-done | bytes 57376 | tf_op jit(solution)/shard_map/ppermute | solution.py:1285
  76.5 1.4 %collective-permute-start.25 = (f32[4,112,128]{2,1,0:T(8,128)S(1)}, f32[4,112,128]{2,1,0:T(8,128)S(1)}, u32[]{:S(2)}, u32[]{:S(2)}) collective-permute-start(f32[4,112,128]{2,1,0:T(8,128)S(1)} %pad_maximum_fusion.refs_0_), channel_id=1, source_target_pairs={{0,6},{1,7},{2,4},{3,5},{4,2},{5,3},{6,0},{7,1},{8,14},{9,15},{10,... | collective-permute-start | bytes 688136 | tf_op jit(solution)/shard_map/ppermute | solution.py:1285
  77.9 1.2 %collective-permute-start.24 = (f32[4,112,128]{2,1,0:T(8,128)S(1)}, f32[4,112,128]{2,1,0:T(8,128)S(1)}, u32[]{:S(2)}, u32[]{:S(2)}) collective-permute-start(f32[4,112,128]{2,1,0:T(8,128)S(1)} %pad_maximum_fusion.refs_0_), channel_id=1, source_target_pairs={{0,2},{1,3},{2,0},{3,1},{4,6},{5,7},{6,4},{7,5},{8,10},{9,11},{10,... | collective-permute-start | bytes 688136 | tf_op jit(solution)/shard_map/ppermute | solution.py:1285
  79.1 1.0 %collective-permute-start.23 = (f32[4,112,128]{2,1,0:T(8,128)S(1)}, f32[4,112,128]{2,1,0:T(8,128)S(1)}, u32[]{:S(2)}, u32[]{:S(2)}) collective-permute-start(f32[4,112,128]{2,1,0:T(8,128)S(1)} %pad_maximum_fusion.refs_0_), channel_id=1, source_target_pairs={{0,4},{1,5},{2,6},{3,7},{4,0},{5,1},{6,2},{7,3},{8,12},{9,13},{10,... | collective-permute-start | bytes 688136 | tf_op jit(solution)/shard_map/ppermute | solution.py:1285
  80.1 3.7 %collective-permute-done.25.refs_3_ = f32[4,112,128]{2,1,0:T(8,128)S(1)} collective-permute-done((f32[4,112,128]{2,1,0:T(8,128)S(1)}, f32[4,112,128]{2,1,0:T(8,128)S(1)}, u32[]{:S(2)}, u32[]{:S(2)}) %collective-permute-start.25) | collective-permute-done | bytes 229408 | tf_op jit(solution)/shard_map/ppermute | solution.py:1285
  83.7 1.9 %collective-permute-done.24.refs_2_ = f32[4,112,128]{2,1,0:T(8,128)S(1)} collective-permute-done((f32[4,112,128]{2,1,0:T(8,128)S(1)}, f32[4,112,128]{2,1,0:T(8,128)S(1)}, u32[]{:S(2)}, u32[]{:S(2)}) %collective-permute-start.24) | collective-permute-done | bytes 229408 | tf_op jit(solution)/shard_map/ppermute | solution.py:1285
  86.2 1.0 %collective-permute-done.28.refs_6_ = f32[4,112,128]{2,1,0:T(8,128)S(1)} collective-permute-done((f32[4,112,128]{2,1,0:T(8,128)S(1)}, f32[4,112,128]{2,1,0:T(8,128)S(1)}, u32[]{:S(2)}, u32[]{:S(2)}) %collective-permute-start.28) | collective-permute-done | bytes 229408 | tf_op jit(solution)/shard_map/ppermute | solution.py:1285
  87.6 1.5 %unpack.1 = (f32[128,256]{1,0:T(8,128)}, f32[1,256]{1,0:T(1,128)}, f32[256,1024]{1,0:T(8,128)}, f32[4,512]{1,0:T(4,128)}, f32[1,512]{1,0:T(1,128)}, /*index=5*/f...) custom-call(f32[4,112,128]{2,1,0:T(8,128)S(1)} %pad_maximum_fusion.r, ...), custom_call_target="tpu_custom_call" | custom-call | tf_op jit(solution)/shard_map/unpack/pallas_call | solution.py:1256
  (45 shorter events, 3.3 us)
Async XLA Ops:
  2.4 2.9 %collective-permute-start = (f32[8,256]{1,0:T(8,128)S(1)}, f32[8,256]{1,0:T(8,128)S(1)}, u32[]{:S(2)}, u32[]{:S(2)}) collective-permute-start(f32[8,256]{1,0:T(8,128)S(1)} %get-tuple-element.168), channel_id=1, source_target_pairs={{0,1},{1,0},{2,3},{3,2},{4,5},{5,4},{6,7},{7,6},{8,9},{9,8},{10,11... | collective-permute-start | bytes 24584 | tf_op jit(solution)/shard_map/ppermute | solution.py:1285
  2.9 2.4 %collective-permute-start.1 = (f32[8,256]{1,0:T(8,128)S(1)}, f32[8,256]{1,0:T(8,128)S(1)}, u32[]{:S(2)}, u32[]{:S(2)}) collective-permute-start(f32[8,256]{1,0:T(8,128)S(1)} %get-tuple-element.169), channel_id=1, source_target_pairs={{1,2},{3,4},{5,6},{7,8},{9,10},{11,12},{13,14},{15,16},{17,18},{19... | collective-permute-start | bytes 24584 | tf_op jit(solution)/shard_map/ppermute | solution.py:1293
  11.1 4.9 %collective-permute-start.2 = (f32[72,512]{1,0:T(8,128)S(1)}, f32[72,512]{1,0:T(8,128)S(1)}, u32[]{:S(2)}, u32[]{:S(2)}) collective-permute-start(f32[72,512]{1,0:T(8,128)S(1)} %get-tuple-element.181.mine), channel_id=1, source_target_pairs={{0,1},{1,0},{2,3},{3,2},{4,5},{5,4},{6,7},{7,6},{8,9},{9,8},{10,11... | collective-permute-start | bytes 442376 | tf_op jit(solution)/shard_map/ppermute | solution.py:1285
  16.1 7.3 %collective-permute-start.5 = (f32[72,256]{1,0:T(8,128)S(1)}, f32[72,256]{1,0:T(8,128)S(1)}, u32[]{:S(2)}, u32[]{:S(2)}) collective-permute-start(f32[72,256]{1,0:T(8,128)S(1)} %pair.1.refs_1_), channel_id=1, source_target_pairs={{0,6},{1,7},{2,4},{3,5},{4,2},{5,3},{6,0},{7,1},{8,14},{9,15},{10,... | collective-permute-start | bytes 221192 | tf_op jit(solution)/shard_map/ppermute | solution.py:1285
  20.6 4.4 %collective-permute-start.4 = (f32[72,256]{1,0:T(8,128)S(1)}, f32[72,256]{1,0:T(8,128)S(1)}, u32[]{:S(2)}, u32[]{:S(2)}) collective-permute-start(f32[72,256]{1,0:T(8,128)S(1)} %pair.1.refs_1_), channel_id=1, source_target_pairs={{0,4},{1,5},{2,6},{3,7},{4,0},{5,1},{6,2},{7,3},{8,12},{9,13},{10,... | collective-permute-start | bytes 221192 | tf_op jit(solution)/shard_map/ppermute | solution.py:1285
  20.6 4.4 %collective-permute-start.3 = (f32[72,256]{1,0:T(8,128)S(1)}, f32[72,256]{1,0:T(8,128)S(1)}, u32[]{:S(2)}, u32[]{:S(2)}) collective-permute-start(f32[72,256]{1,0:T(8,128)S(1)} %pair.1.refs_1_), channel_id=1, source_target_pairs={{0,2},{1,3},{2,0},{3,1},{4,6},{5,7},{6,4},{7,5},{8,10},{9,11},{10,... | collective-permute-start | bytes 221192 | tf_op jit(solution)/shard_map/ppermute | solution.py:1285
  25.0 4.5 %collective-permute-start.6 = (f32[40,256]{1,0:T(8,128)S(1)}, f32[40,256]{1,0:T(8,128)S(1)}, u32[]{:S(2)}, u32[]{:S(2)}) collective-permute-start(f32[40,256]{1,0:T(8,128)S(1)} %get-tuple-element.226), channel_id=1, source_target_pairs={{0,8},{1,9},{2,10},{3,11},{4,12},{5,13},{6,14},{7,15},{8,0},{9,1},... | collective-permute-start | bytes 122888 | tf_op jit(solution)/shard_map/ppermute | solution.py:1285
  26.7 5.8 %collective-permute-start.7 = (f32[40,256]{1,0:T(8,128)S(1)}, f32[40,256]{1,0:T(8,128)S(1)}, u32[]{:S(2)}, u32[]{:S(2)}) collective-permute-start(f32[40,256]{1,0:T(8,128)S(1)} %get-tuple-element.227), channel_id=1, source_target_pairs={{0,16},{1,17},{2,18},{3,19},{4,20},{5,21},{6,22},{7,23},{8,24},{9,... | collective-permute-start | bytes 122888 | tf_op jit(solution)/shard_map/ppermute | solution.py:1285
  28.9 5.8 %collective-permute-start.8 = (f32[40,256]{1,0:T(8,128)S(1)}, f32[40,256]{1,0:T(8,128)S(1)}, u32[]{:S(2)}, u32[]{:S(2)}) collective-permute-start(f32[40,256]{1,0:T(8,128)S(1)} %get-tuple-element.228), channel_id=1, source_target_pairs={{0,24},{1,25},{2,26},{3,27},{4,28},{5,29},{6,30},{7,31},{8,16},{9,... | collective-permute-start | bytes 122888 | tf_op jit(solution)/shard_map/ppermute | solution.py:1285
  34.8 1.3 %collective-permute-start.9 = (f32[64,256]{1,0:T(8,128)S(1)}, f32[64,256]{1,0:T(8,128)S(1)}, u32[]{:S(2)}, u32[]{:S(2)}) collective-permute-start(f32[64,256]{1,0:T(8,128)S(1)} %enter.1.mine_half), channel_id=1, source_target_pairs={{0,1},{1,0},{2,3},{3,2},{4,5},{5,4},{6,7},{7,6},{8,9},{9,8},{10,11... | collective-permute-start | bytes 196616 | tf_op jit(solution)/shard_map/ppermute | solution.py:1285
  38.4 2.5 %collective-permute-start.10 = (f32[16,64,128]{2,1,0:T(8,128)S(1)}, f32[16,64,128]{2,1,0:T(8,128)S(1)}, u32[]{:S(2)}, u32[]{:S(2)}) collective-permute-start(f32[16,64,128]{2,1,0:T(8,128)S(1)} %slice.58), channel_id=1, source_target_pairs={{0,1},{1,0},{2,3},{3,2},{4,5},{5,4},{6,7},{7,6},{8,9},{9,8},{10,11... | collective-permute-start | bytes 1572872 | tf_op jit(solution)/shard_map/ppermute | solution.py:1285
  41.1 8.6 %collective-permute-start.11 = (f32[8,64,128]{2,1,0:T(8,128)S(1)}, f32[8,64,128]{2,1,0:T(8,128)S(1)}, u32[]{:S(2)}, u32[]{:S(2)}) collective-permute-start(f32[8,64,128]{2,1,0:T(8,128)S(1)} %slice.60), channel_id=1, source_target_pairs={{0,2},{1,3},{2,0},{3,1},{4,6},{5,7},{6,4},{7,5},{8,10},{9,11},{10,... | collective-permute-start | bytes 786440 | tf_op jit(solution)/shard_map/ppermute | solution.py:1285
  49.8 1.9 %collective-permute-start.12 = (f32[16,56,128]{2,1,0:T(8,128)S(1)}, f32[16,56,128]{2,1,0:T(8,128)S(1)}, u32[]{:S(2)}, u32[]{:S(2)}) collective-permute-start(f32[16,56,128]{2,1,0:T(8,128)S(1)} %slice.62), channel_id=1, source_target_pairs={{0,1},{1,0},{2,3},{3,2},{4,5},{5,4},{6,7},{7,6},{8,9},{9,8},{10,11... | collective-permute-start | bytes 1376264 | tf_op jit(solution)/shard_map/ppermute | solution.py:1285
  49.9 6.4 %collective-permute-start.16 = (f32[4,64,128]{2,1,0:T(8,128)S(1)}, f32[4,64,128]{2,1,0:T(8,128)S(1)}, u32[]{:S(2)}, u32[]{:S(2)}) collective-permute-start(f32[4,64,128]{2,1,0:T(8,128)S(1)} %slice.68), channel_id=1, source_target_pairs={{0,4},{1,5},{2,6},{3,7},{4,0},{5,1},{6,2},{7,3},{8,12},{9,13},{10,... | collective-permute-start | bytes 393224 | tf_op jit(solution)/shard_map/ppermute | solution.py:1285
  51.8 7.7 %collective-permute-start.13 = (f32[4,56,128]{2,1,0:T(8,128)S(1)}, f32[4,56,128]{2,1,0:T(8,128)S(1)}, u32[]{:S(2)}, u32[]{:S(2)}) collective-permute-start(f32[4,56,128]{2,1,0:T(8,128)S(1)} %get-tuple-element.308), channel_id=1, source_target_pairs={{0,4},{1,5},{2,6},{3,7},{4,0},{5,1},{6,2},{7,3},{8,12},{9,13},{10,... | collective-permute-start | bytes 344072 | tf_op jit(solution)/shard_map/ppermute | solution.py:1285
  52.8 6.7 %collective-permute-start.15 = (f32[4,56,128]{2,1,0:T(8,128)S(1)}, f32[4,56,128]{2,1,0:T(8,128)S(1)}, u32[]{:S(2)}, u32[]{:S(2)}) collective-permute-start(f32[4,56,128]{2,1,0:T(8,128)S(1)} %get-tuple-element.309), channel_id=1, source_target_pairs={{0,2},{1,3},{2,0},{3,1},{4,6},{5,7},{6,4},{7,5},{8,10},{9,11},{10,... | collective-permute-start | bytes 344072 | tf_op jit(solution)/shard_map/ppermute | solution.py:1285
  53.7 7.0 %collective-permute-start.14 = (f32[4,56,128]{2,1,0:T(8,128)S(1)}, f32[4,56,128]{2,1,0:T(8,128)S(1)}, u32[]{:S(2)}, u32[]{:S(2)}) collective-permute-start(f32[4,56,128]{2,1,0:T(8,128)S(1)} %get-tuple-element.310), channel_id=1, source_target_pairs={{0,6},{1,7},{2,4},{3,5},{4,2},{5,3},{6,0},{7,1},{8,14},{9,15},{10,... | collective-permute-start | bytes 344072 | tf_op jit(solution)/shard_map/ppermute | solution.py:1285
  60.8 5.8 %collective-permute-start.17 = (f32[1,120,128]{2,1,0:T(8,128)S(1)}, f32[1,120,128]{2,1,0:T(8,128)S(1)}, u32[]{:S(2)}, u32[]{:S(2)}) collective-permute-start(f32[1,120,128]{2,1,0:T(8,128)S(1)} %get-tuple-element.311), channel_id=1, source_target_pairs={{0,16},{1,17},{2,18},{3,19},{4,20},{5,21},{6,22},{7,23},{8,24},{9,... | collective-permute-start | bytes 184328 | tf_op jit(solution)/shard_map/ppermute | solution.py:1285
  60.9 5.8 %collective-permute-start.19 = (f32[1,120,128]{2,1,0:T(8,128)S(1)}, f32[1,120,128]{2,1,0:T(8,128)S(1)}, u32[]{:S(2)}, u32[]{:S(2)}) collective-permute-start(f32[1,120,128]{2,1,0:T(8,128)S(1)} %get-tuple-element.312), channel_id=1, source_target_pairs={{0,8},{1,9},{2,10},{3,11},{4,12},{5,13},{6,14},{7,15},{8,0},{9,1},... | collective-permute-start | bytes 184328 | tf_op jit(solution)/shard_map/ppermute | solution.py:1285
  62.3 6.1 %collective-permute-start.18 = (f32[1,120,128]{2,1,0:T(8,128)S(1)}, f32[1,120,128]{2,1,0:T(8,128)S(1)}, u32[]{:S(2)}, u32[]{:S(2)}) collective-permute-start(f32[1,120,128]{2,1,0:T(8,128)S(1)} %get-tuple-element.313), channel_id=1, source_target_pairs={{0,24},{1,25},{2,26},{3,27},{4,28},{5,29},{6,30},{7,31},{8,16},{9,... | collective-permute-start | bytes 184328 | tf_op jit(solution)/shard_map/ppermute | solution.py:1285
  68.4 6.2 %collective-permute-start.22 = (f32[1,112,128]{2,1,0:T(8,128)S(1)}, f32[1,112,128]{2,1,0:T(8,128)S(1)}, u32[]{:S(2)}, u32[]{:S(2)}) collective-permute-start(f32[1,112,128]{2,1,0:T(8,128)S(1)} %slice.82), channel_id=1, source_target_pairs={{0,24},{1,25},{2,26},{3,27},{4,28},{5,29},{6,30},{7,31},{8,16},{9,... | collective-permute-start | bytes 172040 | tf_op jit(solution)/shard_map/ppermute | solution.py:1285
  71.4 4.2 %collective-permute-start.21 = (f32[1,112,128]{2,1,0:T(8,128)S(1)}, f32[1,112,128]{2,1,0:T(8,128)S(1)}, u32[]{:S(2)}, u32[]{:S(2)}) collective-permute-start(f32[1,112,128]{2,1,0:T(8,128)S(1)} %slice.82), channel_id=1, source_target_pairs={{0,8},{1,9},{2,10},{3,11},{4,12},{5,13},{6,14},{7,15},{8,0},{9,1},... | collective-permute-start | bytes 172040 | tf_op jit(solution)/shard_map/ppermute | solution.py:1285
  71.4 5.1 %collective-permute-start.20 = (f32[1,112,128]{2,1,0:T(8,128)S(1)}, f32[1,112,128]{2,1,0:T(8,128)S(1)}, u32[]{:S(2)}, u32[]{:S(2)}) collective-permute-start(f32[1,112,128]{2,1,0:T(8,128)S(1)} %slice.82), channel_id=1, source_target_pairs={{0,16},{1,17},{2,18},{3,19},{4,20},{5,21},{6,22},{7,23},{8,24},{9,... | collective-permute-start | bytes 172040 | tf_op jit(solution)/shard_map/ppermute | solution.py:1285
  76.5 7.2 %collective-permute-start.25 = (f32[4,112,128]{2,1,0:T(8,128)S(1)}, f32[4,112,128]{2,1,0:T(8,128)S(1)}, u32[]{:S(2)}, u32[]{:S(2)}) collective-permute-start(f32[4,112,128]{2,1,0:T(8,128)S(1)} %pad_maximum_fusion.refs_0_), channel_id=1, source_target_pairs={{0,6},{1,7},{2,4},{3,5},{4,2},{5,3},{6,0},{7,1},{8,14},{9,15},{10,... | collective-permute-start | bytes 688136 | tf_op jit(solution)/shard_map/ppermute | solution.py:1285
  77.9 7.8 %collective-permute-start.24 = (f32[4,112,128]{2,1,0:T(8,128)S(1)}, f32[4,112,128]{2,1,0:T(8,128)S(1)}, u32[]{:S(2)}, u32[]{:S(2)}) collective-permute-start(f32[4,112,128]{2,1,0:T(8,128)S(1)} %pad_maximum_fusion.refs_0_), channel_id=1, source_target_pairs={{0,2},{1,3},{2,0},{3,1},{4,6},{5,7},{6,4},{7,5},{8,10},{9,11},{10,... | collective-permute-start | bytes 688136 | tf_op jit(solution)/shard_map/ppermute | solution.py:1285
  79.1 7.0 %collective-permute-start.23 = (f32[4,112,128]{2,1,0:T(8,128)S(1)}, f32[4,112,128]{2,1,0:T(8,128)S(1)}, u32[]{:S(2)}, u32[]{:S(2)}) collective-permute-start(f32[4,112,128]{2,1,0:T(8,128)S(1)} %pad_maximum_fusion.refs_0_), channel_id=1, source_target_pairs={{0,4},{1,5},{2,6},{3,7},{4,0},{5,1},{6,2},{7,3},{8,12},{9,13},{10,... | collective-permute-start | bytes 688136 | tf_op jit(solution)/shard_map/ppermute | solution.py:1285
  80.1 6.1 %collective-permute-start.26 = (f32[4,112,128]{2,1,0:T(8,128)S(1)}, f32[4,112,128]{2,1,0:T(8,128)S(1)}, u32[]{:S(2)}, u32[]{:S(2)}) collective-permute-start(f32[4,112,128]{2,1,0:T(8,128)S(1)} %pad_maximum_fusion.refs_0_), channel_id=1, source_target_pairs={{0,1},{1,0},{2,3},{3,2},{4,5},{5,4},{6,7},{7,6},{8,9},{9,8},{10,11... | collective-permute-start | bytes 688136 | tf_op jit(solution)/shard_map/ppermute | solution.py:1285
  83.7 2.4 %collective-permute-start.29 = (f32[4,112,128]{2,1,0:T(8,128)S(1)}, f32[4,112,128]{2,1,0:T(8,128)S(1)}, u32[]{:S(2)}, u32[]{:S(2)}) collective-permute-start(f32[4,112,128]{2,1,0:T(8,128)S(1)} %collective-permute-done.25.refs_3_), channel_id=1, source_target_pairs={{0,1},{1,0},{2,3},{3,2},{4,5},{5,4},{6,7},{7,6},{8,9},{9,8},{10,11... | collective-permute-start | bytes 688136 | tf_op jit(solution)/shard_map/ppermute | solution.py:1285
  85.6 1.5 %collective-permute-start.28 = (f32[4,112,128]{2,1,0:T(8,128)S(1)}, f32[4,112,128]{2,1,0:T(8,128)S(1)}, u32[]{:S(2)}, u32[]{:S(2)}) collective-permute-start(f32[4,112,128]{2,1,0:T(8,128)S(1)} %collective-permute-done.24.refs_2_), channel_id=1, source_target_pairs={{0,1},{1,0},{2,3},{3,2},{4,5},{5,4},{6,7},{7,6},{8,9},{9,8},{10,11... | collective-permute-start | bytes 688136 | tf_op jit(solution)/shard_map/ppermute | solution.py:1285
  86.1 1.5 %collective-permute-start.27 = (f32[4,112,128]{2,1,0:T(8,128)S(1)}, f32[4,112,128]{2,1,0:T(8,128)S(1)}, u32[]{:S(2)}, u32[]{:S(2)}) collective-permute-start(f32[4,112,128]{2,1,0:T(8,128)S(1)} %collective-permute-done.23.refs_1_), channel_id=1, source_target_pairs={{0,1},{1,0},{2,3},{3,2},{4,5},{5,4},{6,7},{7,6},{8,9},{9,8},{10,11... | collective-permute-start | bytes 688136 | tf_op jit(solution)/shard_map/ppermute | solution.py:1285

commit v6 on v5

--- a/solution.py
+++ b/solution.py
@@ -1161,7 +1161,7 @@
 
 def unpack_kernel(rs_bits, parts, *refs):
     sources, refs = refs[:parts], refs[parts:]
-    (gtok, halo, pad, gtok_o, gain_o, w_in_o, conv_w_o, conv_b_o, w_x_o, w_dt_o, dt_bias_o, a_log_o, d_skip_o, w_out_o,
+    (gain_o, w_in_o, conv_w_o, conv_b_o, w_x_o, w_dt_o, dt_bias_o, a_log_o, d_skip_o, w_out_o,
      few_s, rest_s) = refs
     feat = w_in_o.shape[0]
     inner = w_out_o.shape[0]
@@ -1219,6 +1219,9 @@
     d_skip_o[...] = few_rows(at + 6, 1)
     gain_o[...] = few_rows(at + 7, 1)[:, :feat]
 
+
+def close_kernel(gtok, halo, pad, gtok_o):
+    feat = gtok.shape[1]
     length = gtok.shape[0]
     per = feat // LANE
     padded = spread_plain(pad[...].astype(F32), feat)
@@ -1239,6 +1242,15 @@
     gtok_o[length - CH :] = gtok[length - CH :] + padded[length - CH :] * last
 
 
+def close(*arrays):
+    return pl.pallas_call(
+        close_kernel,
+        out_shape=jax.ShapeDtypeStruct(arrays[0].shape, F32),
+        compiler_params=params(4),
+        name="close",
+    )(*arrays)
+
+
 def spread_plain(row, width):
     length = row.shape[1]
     rows = lax.broadcasted_iota(jnp.int32, (length, length), 0)
@@ -1247,8 +1259,7 @@
     return nn(picked, jnp.ones((length, width), BF16))
 
 
-def unpack(rs_bits, parts, gtok, halo, pad, state, rank):
-    length, feat = gtok.shape
+def unpack(rs_bits, parts, feat, state, rank):
     pieces = 1 << rs_bits
     inner = state[1]
     width = rank + 2 * state[0]
@@ -1256,7 +1267,6 @@
     return pl.pallas_call(
         lambda *refs: unpack_kernel(rs_bits, len(parts), *refs),
         out_shape=(
-            shape(length, feat),
             shape(1, feat),
             shape(feat, 2 * inner),
             shape(4, inner),
@@ -1271,7 +1281,7 @@
         scratch_shapes=[pltpu.VMEM((pieces, CH, LANE), F32)] * 2,
         compiler_params=params(6),
         name="unpack",
-    )(*parts, gtok, halo, pad)
+    )(*parts)
 
 
 def body(tokens, resets, pad_mask, norm_gain, w_in, conv_w, conv_b, w_x, w_dt, dt_bias, a_log, d_skip, w_out, grad_out):
@@ -1370,14 +1380,15 @@
         from_right = lax.ppermute(to_sides[0], "seq", [(j, i) for i, j in pairs])[:3]
         halo = jnp.concatenate([from_left.reshape(-1, LANE), from_right.reshape(-1, LANE)], axis=0)
     own = own[:, : tall - 8]
+    gtok = close(gtok, halo, pad)
     for step in reversed(rs_steps[1:]):
         near = [exchange(own, reverse_bits(i, len(step)) << step[0]) for i in range((1 << len(step)) - 1, 0, -1)]
         near = [own] + near[::-1]
         if step is not rs_steps[1]:
-            own = jnp.concatenate(near, axis=0)
+            own, gtok = lax.optimization_barrier((jnp.concatenate(near, axis=0), gtok))
     far = [swap(part, 0) for part in near]
-    outs = unpack(rs_bits, near + far, gtok, halo, pad, a_log_t.shape, w_dt.shape[1])
-    gtok, g_gain, g_w_in, g_conv_w, g_conv_b, g_w_x, g_w_dt, g_dt_bias, g_a_log, g_d_skip, g_w_out = outs
+    outs = unpack(rs_bits, near + far, tokens.shape[1], a_log_t.shape, w_dt.shape[1])
+    g_gain, g_w_in, g_conv_w, g_conv_b, g_w_x, g_w_dt, g_dt_bias, g_a_log, g_d_skip, g_w_out = outs
     return (
         mixed, gtok, g_gain, g_w_in[None], g_conv_w[None], g_conv_b, g_w_x.T[None], g_w_dt[None],
         g_dt_bias, g_a_log.T[None], g_d_skip, g_w_out[None],

time: 89.3 us -> 89.2 us (level)
  transfers between devices with their start and end apart: 30 -> 30, of which waited for: 21 -> 21; matrix products, arithmetic and copies ran while one was open for 0% -> 0% of each run, Pallas kernels for 16% -> 17%
where the time goes in v6:
time: 89.2 us; the launch traced here: 89 us
  starting transfers between devices  33.5 us (38%)
  waiting for transfers between devices  28 us (31%)
  Pallas kernels  26.2 us (29%)
    ppermute x29, starting transfers between devices, exchange(): return lax.ppermute(value, 'seq', [(i, i ^ apart) for i in range(count)])  32.9 us
    ppermute x29, waiting for transfers between devices, exchange(): return lax.ppermute(value, 'seq', [(i, i ^ apart) for i in range(count)])  28 us
    pallas_call x1, Pallas kernels, prepare(): pl.pallas_call(prepare_kernel, out_shape=(big, big, big, big, pltpu.VMEM(...  5.83 us
    pallas_call x2, Pallas kernels, backward(): pl.pallas_call(lambda *refs: backward_kernel(dirn, *refs), out_shape=(hal...  4.77 us
    pallas_call x1, Pallas kernels, inner_back(): pl.pallas_call(inner_kernel, out_shape=(part, part, jax.ShapeDtypeStruct(...  2.25 us
    pallas_call x1, Pallas kernels, tail(): pl.pallas_call(lambda *refs: tail_kernel(rs_bits, *refs), out_shape=(jax....  2 us
    pallas_call x1, Pallas kernels, ready(): pl.pallas_call(lambda *refs: ready_kernel(rank, *refs), out_shape=(f32(le...  1.92 us
  transfers between devices with their start and end apart: 30, of which 21 were waited for; matrix products, arithmetic and copies ran while one was open for 0% of the time, Pallas kernels for 17%

profile of v6, /device:TPU:0, one launch (start us, length us, event | category | flops | bytes accessed | tf_op | source)
XLA Modules:
  0.0 89.0 jit_solution(6740544319419833126)
XLA Ops:
  0.6 1.7 %edges.1 = (f32[8,256]{1,0:T(8,128)S(1)}, f32[8,256]{1,0:T(8,128)S(1)}, f32[128,256]{1,0:T(8,128)S(1)}, s32[1,128]{1,0:T(1,128)S(1)}, s32[1,128]{1,0:T(1,128)S(1...) custom-call(f32[128,256]{1,0:T(8,128)} %refs_0_.1, ...), custom_call_target="tpu_custom_call" | custom-call | tf_op jit(solution)/shard_map/edges/pallas_call | solution.py:147
  2.9 0.6 collective-permute-start.1
  3.5 1.7 %project.1 = (f32[256,512]{1,0:T(8,128)S(1)}, f32[256,512]{1,0:T(8,128)S(1)}, f32[256,512]{1,0:T(8,128)S(1)}, f32[256,512]{1,0:T(8,128)S(1)}, bf16[256,1024]{1,0...) custom-call(f32[128,256]{1,0:T(8,128)S(1)} %get-tuple-element.161.tok.ref, ...), custom_call_target="tpu_custom_call" | custom-call | tf_op jit(solution)/shard_map/project/pallas_call | solution.py:192
  5.3 5.8 %prepare.1 = (f32[256,512]{1,0:T(8,128)S(1)}, f32[256,512]{1,0:T(8,128)S(1)}, f32[256,512]{1,0:T(8,128)S(1)}, f32[256,512]{1,0:T(8,128)S(1)}, f32[768,128]{1,0:T...) custom-call(f32[8,256]{1,0:T(8,128)S(1)} %collective-permute-done.si, ...), custom_call_target="tpu_custom_call" | custom-call | tf_op jit(solution)/shard_map/prepare/pallas_call | solution.py:420
  11.1 3.9 %collective-permute-start.2 = (f32[72,512]{1,0:T(8,128)S(1)}, f32[72,512]{1,0:T(8,128)S(1)}, u32[]{:S(2)}, u32[]{:S(2)}) collective-permute-start(f32[72,512]{1,0:T(8,128)S(1)} %get-tuple-element.182.mine), channel_id=1, source_target_pairs={{0,1},{1,0},{2,3},{3,2},{4,5},{5,4},{6,7},{7,6},{8,9},{9,8},{10,11... | collective-permute-start | bytes 442376 | tf_op jit(solution)/shard_map/ppermute | solution.py:1295
  15.1 1.0 %collective-permute-done.2.theirs.sibling = f32[72,512]{1,0:T(8,128)S(1)} collective-permute-done((f32[72,512]{1,0:T(8,128)S(1)}, f32[72,512]{1,0:T(8,128)S(1)}, u32[]{:S(2)}, u32[]{:S(2)}) %collective-permute-start.2) | collective-permute-done | bytes 147488 | tf_op jit(solution)/shard_map/ppermute | solution.py:1295
  16.1 4.5 %collective-permute-start.5 = (f32[72,256]{1,0:T(8,128)S(1)}, f32[72,256]{1,0:T(8,128)S(1)}, u32[]{:S(2)}, u32[]{:S(2)}) collective-permute-start(f32[72,256]{1,0:T(8,128)S(1)} %pair.1.refs_1_), channel_id=1, source_target_pairs={{0,6},{1,7},{2,4},{3,5},{4,2},{5,3},{6,0},{7,1},{8,14},{9,15},{10,... | collective-permute-start | bytes 221192 | tf_op jit(solution)/shard_map/ppermute | solution.py:1295
  20.6 0.6 collective-permute-start.3
  21.2 1.9 %ready.1 = (f32[128,256]{1,0:T(8,128)S(1)}, f32[128,256]{1,0:T(8,128)S(1)}, bf16[256,256]{1,0:T(8,128)(2,1)S(1)}, bf16[256,256]{1,0:T(8,128)(2,1)S(1)}, bf16[256...) custom-call(f32[128,256]{1,0:T(8,128)S(1)} %get-tuple-element.161.to, ...), custom_call_target="tpu_custom_call" | custom-call | tf_op jit(solution)/shard_map/ready/pallas_call | solution.py:733
  23.4 1.6 %collective-permute-done.4.refs_3_ = f32[72,256]{1,0:T(8,128)S(1)} collective-permute-done((f32[72,256]{1,0:T(8,128)S(1)}, f32[72,256]{1,0:T(8,128)S(1)}, u32[]{:S(2)}, u32[]{:S(2)}) %collective-permute-start.4) | collective-permute-done | bytes 73760 | tf_op jit(solution)/shard_map/ppermute | solution.py:1295
  25.0 1.6 %collective-permute-start.6 = (f32[40,256]{1,0:T(8,128)S(1)}, f32[40,256]{1,0:T(8,128)S(1)}, u32[]{:S(2)}, u32[]{:S(2)}) collective-permute-start(f32[40,256]{1,0:T(8,128)S(1)} %get-tuple-element.227), channel_id=1, source_target_pairs={{0,8},{1,9},{2,10},{3,11},{4,12},{5,13},{6,14},{7,15},{8,0},{9,1},... | collective-permute-start | bytes 122888 | tf_op jit(solution)/shard_map/ppermute | solution.py:1295
  26.7 2.2 %collective-permute-start.7 = (f32[40,256]{1,0:T(8,128)S(1)}, f32[40,256]{1,0:T(8,128)S(1)}, u32[]{:S(2)}, u32[]{:S(2)}) collective-permute-start(f32[40,256]{1,0:T(8,128)S(1)} %get-tuple-element.228), channel_id=1, source_target_pairs={{0,16},{1,17},{2,18},{3,19},{4,20},{5,21},{6,22},{7,23},{8,24},{9,... | collective-permute-start | bytes 122888 | tf_op jit(solution)/shard_map/ppermute | solution.py:1295
  29.5 3.0 %collective-permute-done.7.refs_2_ = f32[40,256]{1,0:T(8,128)S(1)} collective-permute-done((f32[40,256]{1,0:T(8,128)S(1)}, f32[40,256]{1,0:T(8,128)S(1)}, u32[]{:S(2)}, u32[]{:S(2)}) %collective-permute-start.7) | collective-permute-done | bytes 40992 | tf_op jit(solution)/shard_map/ppermute | solution.py:1295
  32.5 2.2 %collective-permute-done.8.refs_3_ = f32[40,256]{1,0:T(8,128)S(1)} collective-permute-done((f32[40,256]{1,0:T(8,128)S(1)}, f32[40,256]{1,0:T(8,128)S(1)}, u32[]{:S(2)}, u32[]{:S(2)}) %collective-permute-start.8) | collective-permute-done | bytes 40992 | tf_op jit(solution)/shard_map/ppermute | solution.py:1295
  34.8 1.2 %collective-permute-done.9.other_half = f32[64,256]{1,0:T(8,128)S(1)} collective-permute-done((f32[64,256]{1,0:T(8,128)S(1)}, f32[64,256]{1,0:T(8,128)S(1)}, u32[]{:S(2)}, u32[]{:S(2)}) %collective-permute-start.9) | collective-permute-done | bytes 65568 | tf_op jit(solution)/shard_map/ppermute | solution.py:1295
  36.1 1.5 %forward.1 = (f32[256,512]{1,0:T(8,128)S(1)}, f32[2,17,16,8,512]{4,3,2,1,0:T(8,128)S(1)}, f32[64,8,512]{2,1,0:T(8,128)S(1)}) custom-call(f32[64,256]{1,0:T(8,128)S(1)} %enter.1.mine_half, f32[64,256]{1,0:T(8,128)S(1)} %collective-permute-done.9.other_half, f32[72,512]{1,0:T(8,128)S(1)} %collective-permute-done.2.theirs.sibling, ...), custom_call_target="tpu_custom_call" | custom-call | tf_op jit(solution)/shard_map/forward/pallas_call | solution.py:678
  37.6 0.7 early.1
  38.6 2.3 %backward.2 = (f32[128,512]{1,0:T(8,128)S(1)}, f32[128,512]{1,0:T(8,128)S(1)}, f32[128,1024]{1,0:T(8,128)S(1)}, f32[128,1024]{1,0:T(8,128)S(1)}, f32[16,8,512]{2,1,0:T(8,128)S(1)}) custom-call(f32[2,16,8,512]{3,2,1,0:T(8,128)S(1)} %get-tuple-element.240.refs_0_, f32[64,8,512]{2,1,0:T(8,128)S(1)} %get-tuple-element.241.refs_1_, ...), custom_call_target="tpu_custom_call" | custom-call | tf_op jit(solution)/shard_map/backward/pallas_call | solution.py:888
  41.1 1.4 %collective-permute-start.11 = (f32[8,64,128]{2,1,0:T(8,128)S(1)}, f32[8,64,128]{2,1,0:T(8,128)S(1)}, u32[]{:S(2)}, u32[]{:S(2)}) collective-permute-start(f32[8,64,128]{2,1,0:T(8,128)S(1)} %slice.60), channel_id=1, source_target_pairs={{0,2},{1,3},{2,0},{3,1},{4,6},{5,7},{6,4},{7,5},{8,10},{9,11},{10,... | collective-permute-start | bytes 786440 | tf_op jit(solution)/shard_map/ppermute | solution.py:1295
  42.4 2.5 %backward.3 = (f32[128,512]{1,0:T(8,128)S(1)}, f32[128,512]{1,0:T(8,128)S(1)}, f32[128,1024]{1,0:T(8,128)S(1)}, f32[128,1024]{1,0:T(8,128)S(1)}, f32[16,8,512]{2,1,0:T(8,128)S(1)}) custom-call(f32[2,16,8,512]{3,2,1,0:T(8,128)S(1)} %get-tuple-element.240.refs_0_, f32[64,8,512]{2,1,0:T(8,128)S(1)} %get-tuple-element.241.refs_1_, ...), custom_call_target="tpu_custom_call" | custom-call | tf_op jit(solution)/shard_map/backward/pallas_call | solution.py:888
  44.9 2.3 %inner.1 = (bf16[256,512]{1,0:T(8,128)(2,1)S(1)}, bf16[256,512]{1,0:T(8,128)(2,1)S(1)}, f32[16,512]{1,0:T(8,128)S(1)}, f32[88,512]{1,0:T(8,128)S(1)}) custom-call(s32[1,128]{1,0:T(1,128)S(1)} %get-tuple-element.162.pad, f32[4,512]{1,0:T(4,128)S(1)} %get-tuple-element.174.conv_w, f32[48,512]{1,0:T(8,128)S(1)} %get-tuple-element.176.w_x, ...), custom_call_target="tpu_custom_call" | custom-call | tf_op jit(solution)/shard_map/inner/pallas_call | solution.py:1031
  47.2 2.0 %tail.1 = (f32[128,256]{1,0:T(8,128)S(1)}, f32[32,56,128]{2,1,0:T(8,128)S(1)}) custom-call(f32[8,256]{1,0:T(8,128)S(1)} %collective-permute-done.sib.refs_0_, f32[8,256]{1,0:T(8,128)S(1)} %collective-permute-done.1.oth.refs_1_, f32[1,256]{1,0:T(1,128)S(1)} %get-tuple-element.163.gain.refs_2_, f32[128,256]{1,0:T(8,128)S(1)} %get-tuple-element.249.refs_3_.x_s, ...), custom_call_target="tpu_custom_call" | custom-call | tf_op jit(solution)/shard_map/tail/pallas_call | solution.py:1150
  49.9 1.0 %collective-permute-start.16 = (f32[4,64,128]{2,1,0:T(8,128)S(1)}, f32[4,64,128]{2,1,0:T(8,128)S(1)}, u32[]{:S(2)}, u32[]{:S(2)}) collective-permute-start(f32[4,64,128]{2,1,0:T(8,128)S(1)} %slice.68), channel_id=1, source_target_pairs={{0,4},{1,5},{2,6},{3,7},{4,0},{5,1},{6,2},{7,3},{8,12},{9,13},{10,... | collective-permute-start | bytes 393224 | tf_op jit(solution)/shard_map/ppermute | solution.py:1295
  50.9 0.8 collective-permute-done.12
  51.8 1.0 %collective-permute-start.13 = (f32[4,56,128]{2,1,0:T(8,128)S(1)}, f32[4,56,128]{2,1,0:T(8,128)S(1)}, u32[]{:S(2)}, u32[]{:S(2)}) collective-permute-start(f32[4,56,128]{2,1,0:T(8,128)S(1)} %get-tuple-element.310), channel_id=1, source_target_pairs={{0,4},{1,5},{2,6},{3,7},{4,0},{5,1},{6,2},{7,3},{8,12},{9,13},{10,... | collective-permute-start | bytes 344072 | tf_op jit(solution)/shard_map/ppermute | solution.py:1295
  52.8 1.0 %collective-permute-start.15 = (f32[4,56,128]{2,1,0:T(8,128)S(1)}, f32[4,56,128]{2,1,0:T(8,128)S(1)}, u32[]{:S(2)}, u32[]{:S(2)}) collective-permute-start(f32[4,56,128]{2,1,0:T(8,128)S(1)} %get-tuple-element.311), channel_id=1, source_target_pairs={{0,2},{1,3},{2,0},{3,1},{4,6},{5,7},{6,4},{7,5},{8,10},{9,11},{10,... | collective-permute-start | bytes 344072 | tf_op jit(solution)/shard_map/ppermute | solution.py:1295
  53.7 1.6 %collective-permute-start.14 = (f32[4,56,128]{2,1,0:T(8,128)S(1)}, f32[4,56,128]{2,1,0:T(8,128)S(1)}, u32[]{:S(2)}, u32[]{:S(2)}) collective-permute-start(f32[4,56,128]{2,1,0:T(8,128)S(1)} %get-tuple-element.312), channel_id=1, source_target_pairs={{0,6},{1,7},{2,4},{3,5},{4,2},{5,3},{6,0},{7,1},{8,14},{9,15},{10,... | collective-permute-start | bytes 344072 | tf_op jit(solution)/shard_map/ppermute | solution.py:1295
  55.3 0.9 %collective-permute-done.16 = f32[4,64,128]{2,1,0:T(8,128)S(1)} collective-permute-done((f32[4,64,128]{2,1,0:T(8,128)S(1)}, f32[4,64,128]{2,1,0:T(8,128)S(1)}, u32[]{:S(2)}, u32[]{:S(2)}) %collective-permute-start.16) | collective-permute-done | bytes 131104 | tf_op jit(solution)/shard_map/ppermute | solution.py:1295
  56.2 1.3 %finish.1 = (f32[128,256]{1,0:T(8,128)}, f32[128,256]{1,0:T(8,128)S(1)}) custom-call(f32[128,256]{1,0:T(8,128)S(1)} %get-tuple-element.249.refs_3_.x_s, f32[128,256]{1,0:T(8,128)S(1)} %get-tuple-element.284.g, f32[1,256]{1,0:T(1,128)S(1)} %get-tuple-element.163.gain.refs_2_, f32[128,256]{1,0:T(8,128)S(1)} %get-tuple-element.285.g_normed, ...), custom_call_target="tpu_custom_call" | custom-call | tf_op jit(solution)/shard_map/finish/pallas_call | solution.py:1136
  57.6 1.8 %collective-permute-done.13 = f32[4,56,128]{2,1,0:T(8,128)S(1)} collective-permute-done((f32[4,56,128]{2,1,0:T(8,128)S(1)}, f32[4,56,128]{2,1,0:T(8,128)S(1)}, u32[]{:S(2)}, u32[]{:S(2)}) %collective-permute-start.13) | collective-permute-done | bytes 114720 | tf_op jit(solution)/shard_map/ppermute | solution.py:1295
  59.4 1.3 %collective-permute-done.14 = f32[4,56,128]{2,1,0:T(8,128)S(1)} collective-permute-done((f32[4,56,128]{2,1,0:T(8,128)S(1)}, f32[4,56,128]{2,1,0:T(8,128)S(1)}, u32[]{:S(2)}, u32[]{:S(2)}) %collective-permute-start.14) | collective-permute-done | bytes 114720 | tf_op jit(solution)/shard_map/ppermute | solution.py:1295
  60.9 1.5 %collective-permute-start.19 = (f32[1,120,128]{2,1,0:T(8,128)S(1)}, f32[1,120,128]{2,1,0:T(8,128)S(1)}, u32[]{:S(2)}, u32[]{:S(2)}) collective-permute-start(f32[1,120,128]{2,1,0:T(8,128)S(1)} %get-tuple-element.314), channel_id=1, source_target_pairs={{0,8},{1,9},{2,10},{3,11},{4,12},{5,13},{6,14},{7,15},{8,0},{9,1},... | collective-permute-start | bytes 184328 | tf_op jit(solution)/shard_map/ppermute | solution.py:1295
  62.3 2.9 %collective-permute-start.18 = (f32[1,120,128]{2,1,0:T(8,128)S(1)}, f32[1,120,128]{2,1,0:T(8,128)S(1)}, u32[]{:S(2)}, u32[]{:S(2)}) collective-permute-start(f32[1,120,128]{2,1,0:T(8,128)S(1)} %get-tuple-element.315), channel_id=1, source_target_pairs={{0,24},{1,25},{2,26},{3,27},{4,28},{5,29},{6,30},{7,31},{8,16},{9,... | collective-permute-start | bytes 184328 | tf_op jit(solution)/shard_map/ppermute | solution.py:1295
  65.3 1.4 %collective-permute-done.17 = f32[1,120,128]{2,1,0:T(8,128)S(1)} collective-permute-done((f32[1,120,128]{2,1,0:T(8,128)S(1)}, f32[1,120,128]{2,1,0:T(8,128)S(1)}, u32[]{:S(2)}, u32[]{:S(2)}) %collective-permute-start.17) | collective-permute-done | bytes 61472 | tf_op jit(solution)/shard_map/ppermute | solution.py:1295
  66.6 1.8 %collective-permute-done.18 = f32[1,120,128]{2,1,0:T(8,128)S(1)} collective-permute-done((f32[1,120,128]{2,1,0:T(8,128)S(1)}, f32[1,120,128]{2,1,0:T(8,128)S(1)}, u32[]{:S(2)}, u32[]{:S(2)}) %collective-permute-start.18) | collective-permute-done | bytes 61472 | tf_op jit(solution)/shard_map/ppermute | solution.py:1295
  68.5 3.0 %collective-permute-start.22 = (f32[1,112,128]{2,1,0:T(8,128)S(1)}, f32[1,112,128]{2,1,0:T(8,128)S(1)}, u32[]{:S(2)}, u32[]{:S(2)}) collective-permute-start(f32[1,112,128]{2,1,0:T(8,128)S(1)} %slice.82), channel_id=1, source_target_pairs={{0,24},{1,25},{2,26},{3,27},{4,28},{5,29},{6,30},{7,31},{8,16},{9,... | collective-permute-start | bytes 172040 | tf_op jit(solution)/shard_map/ppermute | solution.py:1295
  71.5 1.4 %collective-permute-start.20 = (f32[1,112,128]{2,1,0:T(8,128)S(1)}, f32[1,112,128]{2,1,0:T(8,128)S(1)}, u32[]{:S(2)}, u32[]{:S(2)}) collective-permute-start(f32[1,112,128]{2,1,0:T(8,128)S(1)} %slice.82), channel_id=1, source_target_pairs={{0,16},{1,17},{2,18},{3,19},{4,20},{5,21},{6,22},{7,23},{8,24},{9,... | collective-permute-start | bytes 172040 | tf_op jit(solution)/shard_map/ppermute | solution.py:1295
  72.9 0.8 close.1
  73.7 1.0 %collective-permute-done.22 = f32[1,112,128]{2,1,0:T(8,128)S(1)} collective-permute-done((f32[1,112,128]{2,1,0:T(8,128)S(1)}, f32[1,112,128]{2,1,0:T(8,128)S(1)}, u32[]{:S(2)}, u32[]{:S(2)}) %collective-permute-start.22) | collective-permute-done | bytes 57376 | tf_op jit(solution)/shard_map/ppermute | solution.py:1295
  74.7 1.0 %collective-permute-done.21 = f32[1,112,128]{2,1,0:T(8,128)S(1)} collective-permute-done((f32[1,112,128]{2,1,0:T(8,128)S(1)}, f32[1,112,128]{2,1,0:T(8,128)S(1)}, u32[]{:S(2)}, u32[]{:S(2)}) %collective-permute-start.21) | collective-permute-done | bytes 57376 | tf_op jit(solution)/shard_map/ppermute | solution.py:1295
  75.6 0.9 %collective-permute-done.20 = f32[1,112,128]{2,1,0:T(8,128)S(1)} collective-permute-done((f32[1,112,128]{2,1,0:T(8,128)S(1)}, f32[1,112,128]{2,1,0:T(8,128)S(1)}, u32[]{:S(2)}, u32[]{:S(2)}) %collective-permute-start.20) | collective-permute-done | bytes 57376 | tf_op jit(solution)/shard_map/ppermute | solution.py:1295
  76.6 1.4 %collective-permute-start.25 = (f32[4,112,128]{2,1,0:T(8,128)S(1)}, f32[4,112,128]{2,1,0:T(8,128)S(1)}, u32[]{:S(2)}, u32[]{:S(2)}) collective-permute-start(f32[4,112,128]{2,1,0:T(8,128)S(1)} %pad_maximum_fusion.refs_0_), channel_id=1, source_target_pairs={{0,6},{1,7},{2,4},{3,5},{4,2},{5,3},{6,0},{7,1},{8,14},{9,15},{10,... | collective-permute-start | bytes 688136 | tf_op jit(solution)/shard_map/ppermute | solution.py:1295
  77.9 1.2 %collective-permute-start.24 = (f32[4,112,128]{2,1,0:T(8,128)S(1)}, f32[4,112,128]{2,1,0:T(8,128)S(1)}, u32[]{:S(2)}, u32[]{:S(2)}) collective-permute-start(f32[4,112,128]{2,1,0:T(8,128)S(1)} %pad_maximum_fusion.refs_0_), channel_id=1, source_target_pairs={{0,2},{1,3},{2,0},{3,1},{4,6},{5,7},{6,4},{7,5},{8,10},{9,11},{10,... | collective-permute-start | bytes 688136 | tf_op jit(solution)/shard_map/ppermute | solution.py:1295
  79.1 1.0 %collective-permute-start.23 = (f32[4,112,128]{2,1,0:T(8,128)S(1)}, f32[4,112,128]{2,1,0:T(8,128)S(1)}, u32[]{:S(2)}, u32[]{:S(2)}) collective-permute-start(f32[4,112,128]{2,1,0:T(8,128)S(1)} %pad_maximum_fusion.refs_0_), channel_id=1, source_target_pairs={{0,4},{1,5},{2,6},{3,7},{4,0},{5,1},{6,2},{7,3},{8,12},{9,13},{10,... | collective-permute-start | bytes 688136 | tf_op jit(solution)/shard_map/ppermute | solution.py:1295
  80.1 3.6 %collective-permute-done.25.refs_3_ = f32[4,112,128]{2,1,0:T(8,128)S(1)} collective-permute-done((f32[4,112,128]{2,1,0:T(8,128)S(1)}, f32[4,112,128]{2,1,0:T(8,128)S(1)}, u32[]{:S(2)}, u32[]{:S(2)}) %collective-permute-start.25) | collective-permute-done | bytes 229408 | tf_op jit(solution)/shard_map/ppermute | solution.py:1295
  83.8 1.9 %collective-permute-done.24.refs_2_ = f32[4,112,128]{2,1,0:T(8,128)S(1)} collective-permute-done((f32[4,112,128]{2,1,0:T(8,128)S(1)}, f32[4,112,128]{2,1,0:T(8,128)S(1)}, u32[]{:S(2)}, u32[]{:S(2)}) %collective-permute-start.24) | collective-permute-done | bytes 229408 | tf_op jit(solution)/shard_map/ppermute | solution.py:1295
  86.2 1.0 %collective-permute-done.28.refs_6_ = f32[4,112,128]{2,1,0:T(8,128)S(1)} collective-permute-done((f32[4,112,128]{2,1,0:T(8,128)S(1)}, f32[4,112,128]{2,1,0:T(8,128)S(1)}, u32[]{:S(2)}, u32[]{:S(2)}) %collective-permute-start.28) | collective-permute-done | bytes 229408 | tf_op jit(solution)/shard_map/ppermute | solution.py:1295
  87.6 1.4 %unpack.1 = (f32[1,256]{1,0:T(1,128)}, f32[256,1024]{1,0:T(8,128)}, f32[4,512]{1,0:T(4,128)}, f32[1,512]{1,0:T(1,128)}, f32[48,512]{1,0:T(8,128)}, /*index=5*/f3...) custom-call(f32[4,112,128]{2,1,0:T(8,128)S(1)} %pad_maximum_fusion.refs_0_, ...), custom_call_target="tpu_custom_call" | custom-call | tf_op jit(solution)/shard_map/unpack/pallas_call | solution.py:1267
  (46 shorter events, 4.0 us)
Async XLA Ops:
  2.4 2.9 %collective-permute-start = (f32[8,256]{1,0:T(8,128)S(1)}, f32[8,256]{1,0:T(8,128)S(1)}, u32[]{:S(2)}, u32[]{:S(2)}) collective-permute-start(f32[8,256]{1,0:T(8,128)S(1)} %get-tuple-element.169), channel_id=1, source_target_pairs={{0,1},{1,0},{2,3},{3,2},{4,5},{5,4},{6,7},{7,6},{8,9},{9,8},{10,11... | collective-permute-start | bytes 24584 | tf_op jit(solution)/shard_map/ppermute | solution.py:1295
  2.9 2.4 %collective-permute-start.1 = (f32[8,256]{1,0:T(8,128)S(1)}, f32[8,256]{1,0:T(8,128)S(1)}, u32[]{:S(2)}, u32[]{:S(2)}) collective-permute-start(f32[8,256]{1,0:T(8,128)S(1)} %get-tuple-element.170), channel_id=1, source_target_pairs={{1,2},{3,4},{5,6},{7,8},{9,10},{11,12},{13,14},{15,16},{17,18},{19... | collective-permute-start | bytes 24584 | tf_op jit(solution)/shard_map/ppermute | solution.py:1303
  11.1 4.9 %collective-permute-start.2 = (f32[72,512]{1,0:T(8,128)S(1)}, f32[72,512]{1,0:T(8,128)S(1)}, u32[]{:S(2)}, u32[]{:S(2)}) collective-permute-start(f32[72,512]{1,0:T(8,128)S(1)} %get-tuple-element.182.mine), channel_id=1, source_target_pairs={{0,1},{1,0},{2,3},{3,2},{4,5},{5,4},{6,7},{7,6},{8,9},{9,8},{10,11... | collective-permute-start | bytes 442376 | tf_op jit(solution)/shard_map/ppermute | solution.py:1295
  16.1 7.3 %collective-permute-start.5 = (f32[72,256]{1,0:T(8,128)S(1)}, f32[72,256]{1,0:T(8,128)S(1)}, u32[]{:S(2)}, u32[]{:S(2)}) collective-permute-start(f32[72,256]{1,0:T(8,128)S(1)} %pair.1.refs_1_), channel_id=1, source_target_pairs={{0,6},{1,7},{2,4},{3,5},{4,2},{5,3},{6,0},{7,1},{8,14},{9,15},{10,... | collective-permute-start | bytes 221192 | tf_op jit(solution)/shard_map/ppermute | solution.py:1295
  20.6 4.4 %collective-permute-start.4 = (f32[72,256]{1,0:T(8,128)S(1)}, f32[72,256]{1,0:T(8,128)S(1)}, u32[]{:S(2)}, u32[]{:S(2)}) collective-permute-start(f32[72,256]{1,0:T(8,128)S(1)} %pair.1.refs_1_), channel_id=1, source_target_pairs={{0,4},{1,5},{2,6},{3,7},{4,0},{5,1},{6,2},{7,3},{8,12},{9,13},{10,... | collective-permute-start | bytes 221192 | tf_op jit(solution)/shard_map/ppermute | solution.py:1295
  20.6 4.4 %collective-permute-start.3 = (f32[72,256]{1,0:T(8,128)S(1)}, f32[72,256]{1,0:T(8,128)S(1)}, u32[]{:S(2)}, u32[]{:S(2)}) collective-permute-start(f32[72,256]{1,0:T(8,128)S(1)} %pair.1.refs_1_), channel_id=1, source_target_pairs={{0,2},{1,3},{2,0},{3,1},{4,6},{5,7},{6,4},{7,5},{8,10},{9,11},{10,... | collective-permute-start | bytes 221192 | tf_op jit(solution)/shard_map/ppermute | solution.py:1295
  25.0 4.5 %collective-permute-start.6 = (f32[40,256]{1,0:T(8,128)S(1)}, f32[40,256]{1,0:T(8,128)S(1)}, u32[]{:S(2)}, u32[]{:S(2)}) collective-permute-start(f32[40,256]{1,0:T(8,128)S(1)} %get-tuple-element.227), channel_id=1, source_target_pairs={{0,8},{1,9},{2,10},{3,11},{4,12},{5,13},{6,14},{7,15},{8,0},{9,1},... | collective-permute-start | bytes 122888 | tf_op jit(solution)/shard_map/ppermute | solution.py:1295
  26.7 5.8 %collective-permute-start.7 = (f32[40,256]{1,0:T(8,128)S(1)}, f32[40,256]{1,0:T(8,128)S(1)}, u32[]{:S(2)}, u32[]{:S(2)}) collective-permute-start(f32[40,256]{1,0:T(8,128)S(1)} %get-tuple-element.228), channel_id=1, source_target_pairs={{0,16},{1,17},{2,18},{3,19},{4,20},{5,21},{6,22},{7,23},{8,24},{9,... | collective-permute-start | bytes 122888 | tf_op jit(solution)/shard_map/ppermute | solution.py:1295
  28.9 5.8 %collective-permute-start.8 = (f32[40,256]{1,0:T(8,128)S(1)}, f32[40,256]{1,0:T(8,128)S(1)}, u32[]{:S(2)}, u32[]{:S(2)}) collective-permute-start(f32[40,256]{1,0:T(8,128)S(1)} %get-tuple-element.229), channel_id=1, source_target_pairs={{0,24},{1,25},{2,26},{3,27},{4,28},{5,29},{6,30},{7,31},{8,16},{9,... | collective-permute-start | bytes 122888 | tf_op jit(solution)/shard_map/ppermute | solution.py:1295
  34.8 1.3 %collective-permute-start.9 = (f32[64,256]{1,0:T(8,128)S(1)}, f32[64,256]{1,0:T(8,128)S(1)}, u32[]{:S(2)}, u32[]{:S(2)}) collective-permute-start(f32[64,256]{1,0:T(8,128)S(1)} %enter.1.mine_half), channel_id=1, source_target_pairs={{0,1},{1,0},{2,3},{3,2},{4,5},{5,4},{6,7},{7,6},{8,9},{9,8},{10,11... | collective-permute-start | bytes 196616 | tf_op jit(solution)/shard_map/ppermute | solution.py:1295
  38.4 2.5 %collective-permute-start.10 = (f32[16,64,128]{2,1,0:T(8,128)S(1)}, f32[16,64,128]{2,1,0:T(8,128)S(1)}, u32[]{:S(2)}, u32[]{:S(2)}) collective-permute-start(f32[16,64,128]{2,1,0:T(8,128)S(1)} %slice.58), channel_id=1, source_target_pairs={{0,1},{1,0},{2,3},{3,2},{4,5},{5,4},{6,7},{7,6},{8,9},{9,8},{10,11... | collective-permute-start | bytes 1572872 | tf_op jit(solution)/shard_map/ppermute | solution.py:1295
  41.1 8.6 %collective-permute-start.11 = (f32[8,64,128]{2,1,0:T(8,128)S(1)}, f32[8,64,128]{2,1,0:T(8,128)S(1)}, u32[]{:S(2)}, u32[]{:S(2)}) collective-permute-start(f32[8,64,128]{2,1,0:T(8,128)S(1)} %slice.60), channel_id=1, source_target_pairs={{0,2},{1,3},{2,0},{3,1},{4,6},{5,7},{6,4},{7,5},{8,10},{9,11},{10,... | collective-permute-start | bytes 786440 | tf_op jit(solution)/shard_map/ppermute | solution.py:1295
  49.8 1.9 %collective-permute-start.12 = (f32[16,56,128]{2,1,0:T(8,128)S(1)}, f32[16,56,128]{2,1,0:T(8,128)S(1)}, u32[]{:S(2)}, u32[]{:S(2)}) collective-permute-start(f32[16,56,128]{2,1,0:T(8,128)S(1)} %slice.62), channel_id=1, source_target_pairs={{0,1},{1,0},{2,3},{3,2},{4,5},{5,4},{6,7},{7,6},{8,9},{9,8},{10,11... | collective-permute-start | bytes 1376264 | tf_op jit(solution)/shard_map/ppermute | solution.py:1295
  49.9 6.4 %collective-permute-start.16 = (f32[4,64,128]{2,1,0:T(8,128)S(1)}, f32[4,64,128]{2,1,0:T(8,128)S(1)}, u32[]{:S(2)}, u32[]{:S(2)}) collective-permute-start(f32[4,64,128]{2,1,0:T(8,128)S(1)} %slice.68), channel_id=1, source_target_pairs={{0,4},{1,5},{2,6},{3,7},{4,0},{5,1},{6,2},{7,3},{8,12},{9,13},{10,... | collective-permute-start | bytes 393224 | tf_op jit(solution)/shard_map/ppermute | solution.py:1295
  51.8 7.7 %collective-permute-start.13 = (f32[4,56,128]{2,1,0:T(8,128)S(1)}, f32[4,56,128]{2,1,0:T(8,128)S(1)}, u32[]{:S(2)}, u32[]{:S(2)}) collective-permute-start(f32[4,56,128]{2,1,0:T(8,128)S(1)} %get-tuple-element.310), channel_id=1, source_target_pairs={{0,4},{1,5},{2,6},{3,7},{4,0},{5,1},{6,2},{7,3},{8,12},{9,13},{10,... | collective-permute-start | bytes 344072 | tf_op jit(solution)/shard_map/ppermute | solution.py:1295
  52.8 6.7 %collective-permute-start.15 = (f32[4,56,128]{2,1,0:T(8,128)S(1)}, f32[4,56,128]{2,1,0:T(8,128)S(1)}, u32[]{:S(2)}, u32[]{:S(2)}) collective-permute-start(f32[4,56,128]{2,1,0:T(8,128)S(1)} %get-tuple-element.311), channel_id=1, source_target_pairs={{0,2},{1,3},{2,0},{3,1},{4,6},{5,7},{6,4},{7,5},{8,10},{9,11},{10,... | collective-permute-start | bytes 344072 | tf_op jit(solution)/shard_map/ppermute | solution.py:1295
  53.7 7.0 %collective-permute-start.14 = (f32[4,56,128]{2,1,0:T(8,128)S(1)}, f32[4,56,128]{2,1,0:T(8,128)S(1)}, u32[]{:S(2)}, u32[]{:S(2)}) collective-permute-start(f32[4,56,128]{2,1,0:T(8,128)S(1)} %get-tuple-element.312), channel_id=1, source_target_pairs={{0,6},{1,7},{2,4},{3,5},{4,2},{5,3},{6,0},{7,1},{8,14},{9,15},{10,... | collective-permute-start | bytes 344072 | tf_op jit(solution)/shard_map/ppermute | solution.py:1295
  60.8 5.8 %collective-permute-start.17 = (f32[1,120,128]{2,1,0:T(8,128)S(1)}, f32[1,120,128]{2,1,0:T(8,128)S(1)}, u32[]{:S(2)}, u32[]{:S(2)}) collective-permute-start(f32[1,120,128]{2,1,0:T(8,128)S(1)} %get-tuple-element.313), channel_id=1, source_target_pairs={{0,16},{1,17},{2,18},{3,19},{4,20},{5,21},{6,22},{7,23},{8,24},{9,... | collective-permute-start | bytes 184328 | tf_op jit(solution)/shard_map/ppermute | solution.py:1295
  60.9 5.8 %collective-permute-start.19 = (f32[1,120,128]{2,1,0:T(8,128)S(1)}, f32[1,120,128]{2,1,0:T(8,128)S(1)}, u32[]{:S(2)}, u32[]{:S(2)}) collective-permute-start(f32[1,120,128]{2,1,0:T(8,128)S(1)} %get-tuple-element.314), channel_id=1, source_target_pairs={{0,8},{1,9},{2,10},{3,11},{4,12},{5,13},{6,14},{7,15},{8,0},{9,1},... | collective-permute-start | bytes 184328 | tf_op jit(solution)/shard_map/ppermute | solution.py:1295
  62.3 6.1 %collective-permute-start.18 = (f32[1,120,128]{2,1,0:T(8,128)S(1)}, f32[1,120,128]{2,1,0:T(8,128)S(1)}, u32[]{:S(2)}, u32[]{:S(2)}) collective-permute-start(f32[1,120,128]{2,1,0:T(8,128)S(1)} %get-tuple-element.315), channel_id=1, source_target_pairs={{0,24},{1,25},{2,26},{3,27},{4,28},{5,29},{6,30},{7,31},{8,16},{9,... | collective-permute-start | bytes 184328 | tf_op jit(solution)/shard_map/ppermute | solution.py:1295
  68.5 6.2 %collective-permute-start.22 = (f32[1,112,128]{2,1,0:T(8,128)S(1)}, f32[1,112,128]{2,1,0:T(8,128)S(1)}, u32[]{:S(2)}, u32[]{:S(2)}) collective-permute-start(f32[1,112,128]{2,1,0:T(8,128)S(1)} %slice.82), channel_id=1, source_target_pairs={{0,24},{1,25},{2,26},{3,27},{4,28},{5,29},{6,30},{7,31},{8,16},{9,... | collective-permute-start | bytes 172040 | tf_op jit(solution)/shard_map/ppermute | solution.py:1295
  71.5 4.2 %collective-permute-start.21 = (f32[1,112,128]{2,1,0:T(8,128)S(1)}, f32[1,112,128]{2,1,0:T(8,128)S(1)}, u32[]{:S(2)}, u32[]{:S(2)}) collective-permute-start(f32[1,112,128]{2,1,0:T(8,128)S(1)} %slice.82), channel_id=1, source_target_pairs={{0,8},{1,9},{2,10},{3,11},{4,12},{5,13},{6,14},{7,15},{8,0},{9,1},... | collective-permute-start | bytes 172040 | tf_op jit(solution)/shard_map/ppermute | solution.py:1295
  71.5 5.1 %collective-permute-start.20 = (f32[1,112,128]{2,1,0:T(8,128)S(1)}, f32[1,112,128]{2,1,0:T(8,128)S(1)}, u32[]{:S(2)}, u32[]{:S(2)}) collective-permute-start(f32[1,112,128]{2,1,0:T(8,128)S(1)} %slice.82), channel_id=1, source_target_pairs={{0,16},{1,17},{2,18},{3,19},{4,20},{5,21},{6,22},{7,23},{8,24},{9,... | collective-permute-start | bytes 172040 | tf_op jit(solution)/shard_map/ppermute | solution.py:1295
  76.6 7.2 %collective-permute-start.25 = (f32[4,112,128]{2,1,0:T(8,128)S(1)}, f32[4,112,128]{2,1,0:T(8,128)S(1)}, u32[]{:S(2)}, u32[]{:S(2)}) collective-permute-start(f32[4,112,128]{2,1,0:T(8,128)S(1)} %pad_maximum_fusion.refs_0_), channel_id=1, source_target_pairs={{0,6},{1,7},{2,4},{3,5},{4,2},{5,3},{6,0},{7,1},{8,14},{9,15},{10,... | collective-permute-start | bytes 688136 | tf_op jit(solution)/shard_map/ppermute | solution.py:1295
  77.9 7.8 %collective-permute-start.24 = (f32[4,112,128]{2,1,0:T(8,128)S(1)}, f32[4,112,128]{2,1,0:T(8,128)S(1)}, u32[]{:S(2)}, u32[]{:S(2)}) collective-permute-start(f32[4,112,128]{2,1,0:T(8,128)S(1)} %pad_maximum_fusion.refs_0_), channel_id=1, source_target_pairs={{0,2},{1,3},{2,0},{3,1},{4,6},{5,7},{6,4},{7,5},{8,10},{9,11},{10,... | collective-permute-start | bytes 688136 | tf_op jit(solution)/shard_map/ppermute | solution.py:1295
  79.1 7.0 %collective-permute-start.23 = (f32[4,112,128]{2,1,0:T(8,128)S(1)}, f32[4,112,128]{2,1,0:T(8,128)S(1)}, u32[]{:S(2)}, u32[]{:S(2)}) collective-permute-start(f32[4,112,128]{2,1,0:T(8,128)S(1)} %pad_maximum_fusion.refs_0_), channel_id=1, source_target_pairs={{0,4},{1,5},{2,6},{3,7},{4,0},{5,1},{6,2},{7,3},{8,12},{9,13},{10,... | collective-permute-start | bytes 688136 | tf_op jit(solution)/shard_map/ppermute | solution.py:1295
  80.1 6.1 %collective-permute-start.26 = (f32[4,112,128]{2,1,0:T(8,128)S(1)}, f32[4,112,128]{2,1,0:T(8,128)S(1)}, u32[]{:S(2)}, u32[]{:S(2)}) collective-permute-start(f32[4,112,128]{2,1,0:T(8,128)S(1)} %pad_maximum_fusion.refs_0_), channel_id=1, source_target_pairs={{0,1},{1,0},{2,3},{3,2},{4,5},{5,4},{6,7},{7,6},{8,9},{9,8},{10,11... | collective-permute-start | bytes 688136 | tf_op jit(solution)/shard_map/ppermute | solution.py:1295
  83.8 2.4 %collective-permute-start.29 = (f32[4,112,128]{2,1,0:T(8,128)S(1)}, f32[4,112,128]{2,1,0:T(8,128)S(1)}, u32[]{:S(2)}, u32[]{:S(2)}) collective-permute-start(f32[4,112,128]{2,1,0:T(8,128)S(1)} %collective-permute-done.25.refs_3_), channel_id=1, source_target_pairs={{0,1},{1,0},{2,3},{3,2},{4,5},{5,4},{6,7},{7,6},{8,9},{9,8},{10,11... | collective-permute-start | bytes 688136 | tf_op jit(solution)/shard_map/ppermute | solution.py:1295
  85.7 1.5 %collective-permute-start.28 = (f32[4,112,128]{2,1,0:T(8,128)S(1)}, f32[4,112,128]{2,1,0:T(8,128)S(1)}, u32[]{:S(2)}, u32[]{:S(2)}) collective-permute-start(f32[4,112,128]{2,1,0:T(8,128)S(1)} %collective-permute-done.24.refs_2_), channel_id=1, source_target_pairs={{0,1},{1,0},{2,3},{3,2},{4,5},{5,4},{6,7},{7,6},{8,9},{9,8},{10,11... | collective-permute-start | bytes 688136 | tf_op jit(solution)/shard_map/ppermute | solution.py:1295
  86.1 1.5 %collective-permute-start.27 = (f32[4,112,128]{2,1,0:T(8,128)S(1)}, f32[4,112,128]{2,1,0:T(8,128)S(1)}, u32[]{:S(2)}, u32[]{:S(2)}) collective-permute-start(f32[4,112,128]{2,1,0:T(8,128)S(1)} %collective-permute-done.23.refs_1_), channel_id=1, source_target_pairs={{0,1},{1,0},{2,3},{3,2},{4,5},{5,4},{6,7},{7,6},{8,9},{9,8},{10,11... | collective-permute-start | bytes 688136 | tf_op jit(solution)/shard_map/ppermute | solution.py:1295

commit v7 on v6

--- a/solution.py
+++ b/solution.py
@@ -293,8 +293,8 @@
     r2 = r1 * ahead(2)
     r3 = r2 * ahead(3)
     token_order = order_matrix(length)
-    for i, row in enumerate((f1, f2, f3, r1, r2, r3)):
-        mask_o[i * length : (i + 1) * length, :] = spread(row, token_order)
+    picked = [(token_order * row).astype(BF16) for row in (f1, f2, f3, r1, r2, r3)]
+    mask_o[...] = nn(jnp.concatenate(picked, axis=0), jnp.ones((length, LANE), BF16))
 
     sub = sub_iota()
 

time: 89.2 us -> 89.1 us (level)
  no operation moved by 1% of the time
where the time goes in v7:
time: 89.1 us; the launch traced here: 89 us
  starting transfers between devices  33.5 us (38%)
  waiting for transfers between devices  28 us (31%)
  Pallas kernels  26.2 us (29%)
    ppermute x29, starting transfers between devices, exchange(): return lax.ppermute(value, 'seq', [(i, i ^ apart) for i in range(count)])  32.9 us
    ppermute x29, waiting for transfers between devices, exchange(): return lax.ppermute(value, 'seq', [(i, i ^ apart) for i in range(count)])  28 us
    pallas_call x1, Pallas kernels, prepare(): pl.pallas_call(prepare_kernel, out_shape=(big, big, big, big, pltpu.VMEM(...  5.77 us
    pallas_call x2, Pallas kernels, backward(): pl.pallas_call(lambda *refs: backward_kernel(dirn, *refs), out_shape=(hal...  4.77 us
    pallas_call x1, Pallas kernels, inner_back(): pl.pallas_call(inner_kernel, out_shape=(part, part, jax.ShapeDtypeStruct(...  2.25 us
    pallas_call x1, Pallas kernels, tail(): pl.pallas_call(lambda *refs: tail_kernel(rs_bits, *refs), out_shape=(jax....  2 us
    pallas_call x1, Pallas kernels, ready(): pl.pallas_call(lambda *refs: ready_kernel(rank, *refs), out_shape=(f32(le...  1.92 us
  transfers between devices with their start and end apart: 30, of which 21 were waited for; matrix products, arithmetic and copies ran while one was open for 0% of the time, Pallas kernels for 17%

profile of v7, /device:TPU:0, one launch (start us, length us, event | category | flops | bytes accessed | tf_op | source)
XLA Modules:
  0.0 89.0 jit_solution(6486884552032240861)
XLA Ops:
  0.6 1.7 %edges.1 = (f32[8,256]{1,0:T(8,128)S(1)}, f32[8,256]{1,0:T(8,128)S(1)}, f32[128,256]{1,0:T(8,128)S(1)}, s32[1,128]{1,0:T(1,128)S(1)}, s32[1,128]{1,0:T(1,128)S(1...) custom-call(f32[128,256]{1,0:T(8,128)} %refs_0_.1, ...), custom_call_target="tpu_custom_call" | custom-call | tf_op jit(solution)/shard_map/edges/pallas_call | solution.py:147
  2.9 0.6 collective-permute-start.1
  3.5 1.7 %project.1 = (f32[256,512]{1,0:T(8,128)S(1)}, f32[256,512]{1,0:T(8,128)S(1)}, f32[256,512]{1,0:T(8,128)S(1)}, f32[256,512]{1,0:T(8,128)S(1)}, bf16[256,1024]{1,0...) custom-call(f32[128,256]{1,0:T(8,128)S(1)} %get-tuple-element.161.tok.ref, ...), custom_call_target="tpu_custom_call" | custom-call | tf_op jit(solution)/shard_map/project/pallas_call | solution.py:192
  5.3 5.8 %prepare.1 = (f32[256,512]{1,0:T(8,128)S(1)}, f32[256,512]{1,0:T(8,128)S(1)}, f32[256,512]{1,0:T(8,128)S(1)}, f32[256,512]{1,0:T(8,128)S(1)}, f32[768,128]{1,0:T...) custom-call(f32[8,256]{1,0:T(8,128)S(1)} %collective-permute-done.si, ...), custom_call_target="tpu_custom_call" | custom-call | tf_op jit(solution)/shard_map/prepare/pallas_call | solution.py:420
  11.1 3.9 %collective-permute-start.2 = (f32[72,512]{1,0:T(8,128)S(1)}, f32[72,512]{1,0:T(8,128)S(1)}, u32[]{:S(2)}, u32[]{:S(2)}) collective-permute-start(f32[72,512]{1,0:T(8,128)S(1)} %get-tuple-element.182.mine), channel_id=1, source_target_pairs={{0,1},{1,0},{2,3},{3,2},{4,5},{5,4},{6,7},{7,6},{8,9},{9,8},{10,11... | collective-permute-start | bytes 442376 | tf_op jit(solution)/shard_map/ppermute | solution.py:1295
  15.0 1.0 %collective-permute-done.2.theirs.sibling = f32[72,512]{1,0:T(8,128)S(1)} collective-permute-done((f32[72,512]{1,0:T(8,128)S(1)}, f32[72,512]{1,0:T(8,128)S(1)}, u32[]{:S(2)}, u32[]{:S(2)}) %collective-permute-start.2) | collective-permute-done | bytes 147488 | tf_op jit(solution)/shard_map/ppermute | solution.py:1295
  16.0 4.5 %collective-permute-start.5 = (f32[72,256]{1,0:T(8,128)S(1)}, f32[72,256]{1,0:T(8,128)S(1)}, u32[]{:S(2)}, u32[]{:S(2)}) collective-permute-start(f32[72,256]{1,0:T(8,128)S(1)} %pair.1.refs_1_), channel_id=1, source_target_pairs={{0,6},{1,7},{2,4},{3,5},{4,2},{5,3},{6,0},{7,1},{8,14},{9,15},{10,... | collective-permute-start | bytes 221192 | tf_op jit(solution)/shard_map/ppermute | solution.py:1295
  20.5 0.6 collective-permute-start.3
  21.2 1.9 %ready.1 = (f32[128,256]{1,0:T(8,128)S(1)}, f32[128,256]{1,0:T(8,128)S(1)}, bf16[256,256]{1,0:T(8,128)(2,1)S(1)}, bf16[256,256]{1,0:T(8,128)(2,1)S(1)}, bf16[256...) custom-call(f32[128,256]{1,0:T(8,128)S(1)} %get-tuple-element.161.to, ...), custom_call_target="tpu_custom_call" | custom-call | tf_op jit(solution)/shard_map/ready/pallas_call | solution.py:733
  23.3 1.6 %collective-permute-done.4.refs_3_ = f32[72,256]{1,0:T(8,128)S(1)} collective-permute-done((f32[72,256]{1,0:T(8,128)S(1)}, f32[72,256]{1,0:T(8,128)S(1)}, u32[]{:S(2)}, u32[]{:S(2)}) %collective-permute-start.4) | collective-permute-done | bytes 73760 | tf_op jit(solution)/shard_map/ppermute | solution.py:1295
  25.0 1.6 %collective-permute-start.6 = (f32[40,256]{1,0:T(8,128)S(1)}, f32[40,256]{1,0:T(8,128)S(1)}, u32[]{:S(2)}, u32[]{:S(2)}) collective-permute-start(f32[40,256]{1,0:T(8,128)S(1)} %get-tuple-element.227), channel_id=1, source_target_pairs={{0,8},{1,9},{2,10},{3,11},{4,12},{5,13},{6,14},{7,15},{8,0},{9,1},... | collective-permute-start | bytes 122888 | tf_op jit(solution)/shard_map/ppermute | solution.py:1295
  26.6 2.2 %collective-permute-start.7 = (f32[40,256]{1,0:T(8,128)S(1)}, f32[40,256]{1,0:T(8,128)S(1)}, u32[]{:S(2)}, u32[]{:S(2)}) collective-permute-start(f32[40,256]{1,0:T(8,128)S(1)} %get-tuple-element.228), channel_id=1, source_target_pairs={{0,16},{1,17},{2,18},{3,19},{4,20},{5,21},{6,22},{7,23},{8,24},{9,... | collective-permute-start | bytes 122888 | tf_op jit(solution)/shard_map/ppermute | solution.py:1295
  29.4 3.0 %collective-permute-done.7.refs_2_ = f32[40,256]{1,0:T(8,128)S(1)} collective-permute-done((f32[40,256]{1,0:T(8,128)S(1)}, f32[40,256]{1,0:T(8,128)S(1)}, u32[]{:S(2)}, u32[]{:S(2)}) %collective-permute-start.7) | collective-permute-done | bytes 40992 | tf_op jit(solution)/shard_map/ppermute | solution.py:1295
  32.4 2.2 %collective-permute-done.8.refs_3_ = f32[40,256]{1,0:T(8,128)S(1)} collective-permute-done((f32[40,256]{1,0:T(8,128)S(1)}, f32[40,256]{1,0:T(8,128)S(1)}, u32[]{:S(2)}, u32[]{:S(2)}) %collective-permute-start.8) | collective-permute-done | bytes 40992 | tf_op jit(solution)/shard_map/ppermute | solution.py:1295
  34.8 1.2 %collective-permute-done.9.other_half = f32[64,256]{1,0:T(8,128)S(1)} collective-permute-done((f32[64,256]{1,0:T(8,128)S(1)}, f32[64,256]{1,0:T(8,128)S(1)}, u32[]{:S(2)}, u32[]{:S(2)}) %collective-permute-start.9) | collective-permute-done | bytes 65568 | tf_op jit(solution)/shard_map/ppermute | solution.py:1295
  36.0 1.5 %forward.1 = (f32[256,512]{1,0:T(8,128)S(1)}, f32[2,17,16,8,512]{4,3,2,1,0:T(8,128)S(1)}, f32[64,8,512]{2,1,0:T(8,128)S(1)}) custom-call(f32[64,256]{1,0:T(8,128)S(1)} %enter.1.mine_half, f32[64,256]{1,0:T(8,128)S(1)} %collective-permute-done.9.other_half, f32[72,512]{1,0:T(8,128)S(1)} %collective-permute-done.2.theirs.sibling, ...), custom_call_target="tpu_custom_call" | custom-call | tf_op jit(solution)/shard_map/forward/pallas_call | solution.py:678
  37.6 0.7 early.1
  38.6 2.3 %backward.2 = (f32[128,512]{1,0:T(8,128)S(1)}, f32[128,512]{1,0:T(8,128)S(1)}, f32[128,1024]{1,0:T(8,128)S(1)}, f32[128,1024]{1,0:T(8,128)S(1)}, f32[16,8,512]{2,1,0:T(8,128)S(1)}) custom-call(f32[2,16,8,512]{3,2,1,0:T(8,128)S(1)} %get-tuple-element.240.refs_0_, f32[64,8,512]{2,1,0:T(8,128)S(1)} %get-tuple-element.241.refs_1_, ...), custom_call_target="tpu_custom_call" | custom-call | tf_op jit(solution)/shard_map/backward/pallas_call | solution.py:888
  41.0 1.4 %collective-permute-start.11 = (f32[8,64,128]{2,1,0:T(8,128)S(1)}, f32[8,64,128]{2,1,0:T(8,128)S(1)}, u32[]{:S(2)}, u32[]{:S(2)}) collective-permute-start(f32[8,64,128]{2,1,0:T(8,128)S(1)} %slice.60), channel_id=1, source_target_pairs={{0,2},{1,3},{2,0},{3,1},{4,6},{5,7},{6,4},{7,5},{8,10},{9,11},{10,... | collective-permute-start | bytes 786440 | tf_op jit(solution)/shard_map/ppermute | solution.py:1295
  42.4 2.5 %backward.3 = (f32[128,512]{1,0:T(8,128)S(1)}, f32[128,512]{1,0:T(8,128)S(1)}, f32[128,1024]{1,0:T(8,128)S(1)}, f32[128,1024]{1,0:T(8,128)S(1)}, f32[16,8,512]{2,1,0:T(8,128)S(1)}) custom-call(f32[2,16,8,512]{3,2,1,0:T(8,128)S(1)} %get-tuple-element.240.refs_0_, f32[64,8,512]{2,1,0:T(8,128)S(1)} %get-tuple-element.241.refs_1_, ...), custom_call_target="tpu_custom_call" | custom-call | tf_op jit(solution)/shard_map/backward/pallas_call | solution.py:888
  44.8 2.3 %inner.1 = (bf16[256,512]{1,0:T(8,128)(2,1)S(1)}, bf16[256,512]{1,0:T(8,128)(2,1)S(1)}, f32[16,512]{1,0:T(8,128)S(1)}, f32[88,512]{1,0:T(8,128)S(1)}) custom-call(s32[1,128]{1,0:T(1,128)S(1)} %get-tuple-element.162.pad, f32[4,512]{1,0:T(4,128)S(1)} %get-tuple-element.174.conv_w, f32[48,512]{1,0:T(8,128)S(1)} %get-tuple-element.176.w_x, ...), custom_call_target="tpu_custom_call" | custom-call | tf_op jit(solution)/shard_map/inner/pallas_call | solution.py:1031
  47.1 2.0 %tail.1 = (f32[128,256]{1,0:T(8,128)S(1)}, f32[32,56,128]{2,1,0:T(8,128)S(1)}) custom-call(f32[8,256]{1,0:T(8,128)S(1)} %collective-permute-done.sib.refs_0_, f32[8,256]{1,0:T(8,128)S(1)} %collective-permute-done.1.oth.refs_1_, f32[1,256]{1,0:T(1,128)S(1)} %get-tuple-element.163.gain.refs_2_, f32[128,256]{1,0:T(8,128)S(1)} %get-tuple-element.249.refs_3_.x_s, ...), custom_call_target="tpu_custom_call" | custom-call | tf_op jit(solution)/shard_map/tail/pallas_call | solution.py:1150
  49.8 1.0 %collective-permute-start.16 = (f32[4,64,128]{2,1,0:T(8,128)S(1)}, f32[4,64,128]{2,1,0:T(8,128)S(1)}, u32[]{:S(2)}, u32[]{:S(2)}) collective-permute-start(f32[4,64,128]{2,1,0:T(8,128)S(1)} %slice.68), channel_id=1, source_target_pairs={{0,4},{1,5},{2,6},{3,7},{4,0},{5,1},{6,2},{7,3},{8,12},{9,13},{10,... | collective-permute-start | bytes 393224 | tf_op jit(solution)/shard_map/ppermute | solution.py:1295
  50.8 0.8 collective-permute-done.12
  51.7 1.0 %collective-permute-start.13 = (f32[4,56,128]{2,1,0:T(8,128)S(1)}, f32[4,56,128]{2,1,0:T(8,128)S(1)}, u32[]{:S(2)}, u32[]{:S(2)}) collective-permute-start(f32[4,56,128]{2,1,0:T(8,128)S(1)} %get-tuple-element.310), channel_id=1, source_target_pairs={{0,4},{1,5},{2,6},{3,7},{4,0},{5,1},{6,2},{7,3},{8,12},{9,13},{10,... | collective-permute-start | bytes 344072 | tf_op jit(solution)/shard_map/ppermute | solution.py:1295
  52.7 1.0 %collective-permute-start.15 = (f32[4,56,128]{2,1,0:T(8,128)S(1)}, f32[4,56,128]{2,1,0:T(8,128)S(1)}, u32[]{:S(2)}, u32[]{:S(2)}) collective-permute-start(f32[4,56,128]{2,1,0:T(8,128)S(1)} %get-tuple-element.311), channel_id=1, source_target_pairs={{0,2},{1,3},{2,0},{3,1},{4,6},{5,7},{6,4},{7,5},{8,10},{9,11},{10,... | collective-permute-start | bytes 344072 | tf_op jit(solution)/shard_map/ppermute | solution.py:1295
  53.7 1.6 %collective-permute-start.14 = (f32[4,56,128]{2,1,0:T(8,128)S(1)}, f32[4,56,128]{2,1,0:T(8,128)S(1)}, u32[]{:S(2)}, u32[]{:S(2)}) collective-permute-start(f32[4,56,128]{2,1,0:T(8,128)S(1)} %get-tuple-element.312), channel_id=1, source_target_pairs={{0,6},{1,7},{2,4},{3,5},{4,2},{5,3},{6,0},{7,1},{8,14},{9,15},{10,... | collective-permute-start | bytes 344072 | tf_op jit(solution)/shard_map/ppermute | solution.py:1295
  55.2 0.9 %collective-permute-done.16 = f32[4,64,128]{2,1,0:T(8,128)S(1)} collective-permute-done((f32[4,64,128]{2,1,0:T(8,128)S(1)}, f32[4,64,128]{2,1,0:T(8,128)S(1)}, u32[]{:S(2)}, u32[]{:S(2)}) %collective-permute-start.16) | collective-permute-done | bytes 131104 | tf_op jit(solution)/shard_map/ppermute | solution.py:1295
  56.2 1.3 %finish.1 = (f32[128,256]{1,0:T(8,128)}, f32[128,256]{1,0:T(8,128)S(1)}) custom-call(f32[128,256]{1,0:T(8,128)S(1)} %get-tuple-element.249.refs_3_.x_s, f32[128,256]{1,0:T(8,128)S(1)} %get-tuple-element.284.g, f32[1,256]{1,0:T(1,128)S(1)} %get-tuple-element.163.gain.refs_2_, f32[128,256]{1,0:T(8,128)S(1)} %get-tuple-element.285.g_normed, ...), custom_call_target="tpu_custom_call" | custom-call | tf_op jit(solution)/shard_map/finish/pallas_call | solution.py:1136
  57.5 1.8 %collective-permute-done.13 = f32[4,56,128]{2,1,0:T(8,128)S(1)} collective-permute-done((f32[4,56,128]{2,1,0:T(8,128)S(1)}, f32[4,56,128]{2,1,0:T(8,128)S(1)}, u32[]{:S(2)}, u32[]{:S(2)}) %collective-permute-start.13) | collective-permute-done | bytes 114720 | tf_op jit(solution)/shard_map/ppermute | solution.py:1295
  59.4 1.3 %collective-permute-done.14 = f32[4,56,128]{2,1,0:T(8,128)S(1)} collective-permute-done((f32[4,56,128]{2,1,0:T(8,128)S(1)}, f32[4,56,128]{2,1,0:T(8,128)S(1)}, u32[]{:S(2)}, u32[]{:S(2)}) %collective-permute-start.14) | collective-permute-done | bytes 114720 | tf_op jit(solution)/shard_map/ppermute | solution.py:1295
  60.8 1.5 %collective-permute-start.19 = (f32[1,120,128]{2,1,0:T(8,128)S(1)}, f32[1,120,128]{2,1,0:T(8,128)S(1)}, u32[]{:S(2)}, u32[]{:S(2)}) collective-permute-start(f32[1,120,128]{2,1,0:T(8,128)S(1)} %get-tuple-element.314), channel_id=1, source_target_pairs={{0,8},{1,9},{2,10},{3,11},{4,12},{5,13},{6,14},{7,15},{8,0},{9,1},... | collective-permute-start | bytes 184328 | tf_op jit(solution)/shard_map/ppermute | solution.py:1295
  62.3 2.9 %collective-permute-start.18 = (f32[1,120,128]{2,1,0:T(8,128)S(1)}, f32[1,120,128]{2,1,0:T(8,128)S(1)}, u32[]{:S(2)}, u32[]{:S(2)}) collective-permute-start(f32[1,120,128]{2,1,0:T(8,128)S(1)} %get-tuple-element.315), channel_id=1, source_target_pairs={{0,24},{1,25},{2,26},{3,27},{4,28},{5,29},{6,30},{7,31},{8,16},{9,... | collective-permute-start | bytes 184328 | tf_op jit(solution)/shard_map/ppermute | solution.py:1295
  65.2 1.4 %collective-permute-done.17 = f32[1,120,128]{2,1,0:T(8,128)S(1)} collective-permute-done((f32[1,120,128]{2,1,0:T(8,128)S(1)}, f32[1,120,128]{2,1,0:T(8,128)S(1)}, u32[]{:S(2)}, u32[]{:S(2)}) %collective-permute-start.17) | collective-permute-done | bytes 61472 | tf_op jit(solution)/shard_map/ppermute | solution.py:1295
  66.6 1.8 %collective-permute-done.18 = f32[1,120,128]{2,1,0:T(8,128)S(1)} collective-permute-done((f32[1,120,128]{2,1,0:T(8,128)S(1)}, f32[1,120,128]{2,1,0:T(8,128)S(1)}, u32[]{:S(2)}, u32[]{:S(2)}) %collective-permute-start.18) | collective-permute-done | bytes 61472 | tf_op jit(solution)/shard_map/ppermute | solution.py:1295
  68.4 3.0 %collective-permute-start.22 = (f32[1,112,128]{2,1,0:T(8,128)S(1)}, f32[1,112,128]{2,1,0:T(8,128)S(1)}, u32[]{:S(2)}, u32[]{:S(2)}) collective-permute-start(f32[1,112,128]{2,1,0:T(8,128)S(1)} %slice.82), channel_id=1, source_target_pairs={{0,24},{1,25},{2,26},{3,27},{4,28},{5,29},{6,30},{7,31},{8,16},{9,... | collective-permute-start | bytes 172040 | tf_op jit(solution)/shard_map/ppermute | solution.py:1295
  71.4 1.4 %collective-permute-start.20 = (f32[1,112,128]{2,1,0:T(8,128)S(1)}, f32[1,112,128]{2,1,0:T(8,128)S(1)}, u32[]{:S(2)}, u32[]{:S(2)}) collective-permute-start(f32[1,112,128]{2,1,0:T(8,128)S(1)} %slice.82), channel_id=1, source_target_pairs={{0,16},{1,17},{2,18},{3,19},{4,20},{5,21},{6,22},{7,23},{8,24},{9,... | collective-permute-start | bytes 172040 | tf_op jit(solution)/shard_map/ppermute | solution.py:1295
  72.9 0.8 close.1
  73.7 1.0 %collective-permute-done.22 = f32[1,112,128]{2,1,0:T(8,128)S(1)} collective-permute-done((f32[1,112,128]{2,1,0:T(8,128)S(1)}, f32[1,112,128]{2,1,0:T(8,128)S(1)}, u32[]{:S(2)}, u32[]{:S(2)}) %collective-permute-start.22) | collective-permute-done | bytes 57376 | tf_op jit(solution)/shard_map/ppermute | solution.py:1295
  74.6 1.0 %collective-permute-done.21 = f32[1,112,128]{2,1,0:T(8,128)S(1)} collective-permute-done((f32[1,112,128]{2,1,0:T(8,128)S(1)}, f32[1,112,128]{2,1,0:T(8,128)S(1)}, u32[]{:S(2)}, u32[]{:S(2)}) %collective-permute-start.21) | collective-permute-done | bytes 57376 | tf_op jit(solution)/shard_map/ppermute | solution.py:1295
  75.6 0.9 %collective-permute-done.20 = f32[1,112,128]{2,1,0:T(8,128)S(1)} collective-permute-done((f32[1,112,128]{2,1,0:T(8,128)S(1)}, f32[1,112,128]{2,1,0:T(8,128)S(1)}, u32[]{:S(2)}, u32[]{:S(2)}) %collective-permute-start.20) | collective-permute-done | bytes 57376 | tf_op jit(solution)/shard_map/ppermute | solution.py:1295
  76.5 1.4 %collective-permute-start.25 = (f32[4,112,128]{2,1,0:T(8,128)S(1)}, f32[4,112,128]{2,1,0:T(8,128)S(1)}, u32[]{:S(2)}, u32[]{:S(2)}) collective-permute-start(f32[4,112,128]{2,1,0:T(8,128)S(1)} %pad_maximum_fusion.refs_0_), channel_id=1, source_target_pairs={{0,6},{1,7},{2,4},{3,5},{4,2},{5,3},{6,0},{7,1},{8,14},{9,15},{10,... | collective-permute-start | bytes 688136 | tf_op jit(solution)/shard_map/ppermute | solution.py:1295
  77.9 1.1 %collective-permute-start.24 = (f32[4,112,128]{2,1,0:T(8,128)S(1)}, f32[4,112,128]{2,1,0:T(8,128)S(1)}, u32[]{:S(2)}, u32[]{:S(2)}) collective-permute-start(f32[4,112,128]{2,1,0:T(8,128)S(1)} %pad_maximum_fusion.refs_0_), channel_id=1, source_target_pairs={{0,2},{1,3},{2,0},{3,1},{4,6},{5,7},{6,4},{7,5},{8,10},{9,11},{10,... | collective-permute-start | bytes 688136 | tf_op jit(solution)/shard_map/ppermute | solution.py:1295
  79.0 1.0 %collective-permute-start.23 = (f32[4,112,128]{2,1,0:T(8,128)S(1)}, f32[4,112,128]{2,1,0:T(8,128)S(1)}, u32[]{:S(2)}, u32[]{:S(2)}) collective-permute-start(f32[4,112,128]{2,1,0:T(8,128)S(1)} %pad_maximum_fusion.refs_0_), channel_id=1, source_target_pairs={{0,4},{1,5},{2,6},{3,7},{4,0},{5,1},{6,2},{7,3},{8,12},{9,13},{10,... | collective-permute-start | bytes 688136 | tf_op jit(solution)/shard_map/ppermute | solution.py:1295
  80.1 3.6 %collective-permute-done.25.refs_3_ = f32[4,112,128]{2,1,0:T(8,128)S(1)} collective-permute-done((f32[4,112,128]{2,1,0:T(8,128)S(1)}, f32[4,112,128]{2,1,0:T(8,128)S(1)}, u32[]{:S(2)}, u32[]{:S(2)}) %collective-permute-start.25) | collective-permute-done | bytes 229408 | tf_op jit(solution)/shard_map/ppermute | solution.py:1295
  83.7 1.9 %collective-permute-done.24.refs_2_ = f32[4,112,128]{2,1,0:T(8,128)S(1)} collective-permute-done((f32[4,112,128]{2,1,0:T(8,128)S(1)}, f32[4,112,128]{2,1,0:T(8,128)S(1)}, u32[]{:S(2)}, u32[]{:S(2)}) %collective-permute-start.24) | collective-permute-done | bytes 229408 | tf_op jit(solution)/shard_map/ppermute | solution.py:1295
  86.1 1.0 %collective-permute-done.28.refs_6_ = f32[4,112,128]{2,1,0:T(8,128)S(1)} collective-permute-done((f32[4,112,128]{2,1,0:T(8,128)S(1)}, f32[4,112,128]{2,1,0:T(8,128)S(1)}, u32[]{:S(2)}, u32[]{:S(2)}) %collective-permute-start.28) | collective-permute-done | bytes 229408 | tf_op jit(solution)/shard_map/ppermute | solution.py:1295
  87.5 1.4 %unpack.1 = (f32[1,256]{1,0:T(1,128)}, f32[256,1024]{1,0:T(8,128)}, f32[4,512]{1,0:T(4,128)}, f32[1,512]{1,0:T(1,128)}, f32[48,512]{1,0:T(8,128)}, /*index=5*/f3...) custom-call(f32[4,112,128]{2,1,0:T(8,128)S(1)} %pad_maximum_fusion.refs_0_, ...), custom_call_target="tpu_custom_call" | custom-call | tf_op jit(solution)/shard_map/unpack/pallas_call | solution.py:1267
  (46 shorter events, 4.0 us)
Async XLA Ops:
  2.4 2.9 %collective-permute-start = (f32[8,256]{1,0:T(8,128)S(1)}, f32[8,256]{1,0:T(8,128)S(1)}, u32[]{:S(2)}, u32[]{:S(2)}) collective-permute-start(f32[8,256]{1,0:T(8,128)S(1)} %get-tuple-element.169), channel_id=1, source_target_pairs={{0,1},{1,0},{2,3},{3,2},{4,5},{5,4},{6,7},{7,6},{8,9},{9,8},{10,11... | collective-permute-start | bytes 24584 | tf_op jit(solution)/shard_map/ppermute | solution.py:1295
  2.9 2.4 %collective-permute-start.1 = (f32[8,256]{1,0:T(8,128)S(1)}, f32[8,256]{1,0:T(8,128)S(1)}, u32[]{:S(2)}, u32[]{:S(2)}) collective-permute-start(f32[8,256]{1,0:T(8,128)S(1)} %get-tuple-element.170), channel_id=1, source_target_pairs={{1,2},{3,4},{5,6},{7,8},{9,10},{11,12},{13,14},{15,16},{17,18},{19... | collective-permute-start | bytes 24584 | tf_op jit(solution)/shard_map/ppermute | solution.py:1303
  11.1 4.9 %collective-permute-start.2 = (f32[72,512]{1,0:T(8,128)S(1)}, f32[72,512]{1,0:T(8,128)S(1)}, u32[]{:S(2)}, u32[]{:S(2)}) collective-permute-start(f32[72,512]{1,0:T(8,128)S(1)} %get-tuple-element.182.mine), channel_id=1, source_target_pairs={{0,1},{1,0},{2,3},{3,2},{4,5},{5,4},{6,7},{7,6},{8,9},{9,8},{10,11... | collective-permute-start | bytes 442376 | tf_op jit(solution)/shard_map/ppermute | solution.py:1295
  16.0 7.3 %collective-permute-start.5 = (f32[72,256]{1,0:T(8,128)S(1)}, f32[72,256]{1,0:T(8,128)S(1)}, u32[]{:S(2)}, u32[]{:S(2)}) collective-permute-start(f32[72,256]{1,0:T(8,128)S(1)} %pair.1.refs_1_), channel_id=1, source_target_pairs={{0,6},{1,7},{2,4},{3,5},{4,2},{5,3},{6,0},{7,1},{8,14},{9,15},{10,... | collective-permute-start | bytes 221192 | tf_op jit(solution)/shard_map/ppermute | solution.py:1295
  20.5 4.4 %collective-permute-start.4 = (f32[72,256]{1,0:T(8,128)S(1)}, f32[72,256]{1,0:T(8,128)S(1)}, u32[]{:S(2)}, u32[]{:S(2)}) collective-permute-start(f32[72,256]{1,0:T(8,128)S(1)} %pair.1.refs_1_), channel_id=1, source_target_pairs={{0,4},{1,5},{2,6},{3,7},{4,0},{5,1},{6,2},{7,3},{8,12},{9,13},{10,... | collective-permute-start | bytes 221192 | tf_op jit(solution)/shard_map/ppermute | solution.py:1295
  20.5 4.4 %collective-permute-start.3 = (f32[72,256]{1,0:T(8,128)S(1)}, f32[72,256]{1,0:T(8,128)S(1)}, u32[]{:S(2)}, u32[]{:S(2)}) collective-permute-start(f32[72,256]{1,0:T(8,128)S(1)} %pair.1.refs_1_), channel_id=1, source_target_pairs={{0,2},{1,3},{2,0},{3,1},{4,6},{5,7},{6,4},{7,5},{8,10},{9,11},{10,... | collective-permute-start | bytes 221192 | tf_op jit(solution)/shard_map/ppermute | solution.py:1295
  25.0 4.5 %collective-permute-start.6 = (f32[40,256]{1,0:T(8,128)S(1)}, f32[40,256]{1,0:T(8,128)S(1)}, u32[]{:S(2)}, u32[]{:S(2)}) collective-permute-start(f32[40,256]{1,0:T(8,128)S(1)} %get-tuple-element.227), channel_id=1, source_target_pairs={{0,8},{1,9},{2,10},{3,11},{4,12},{5,13},{6,14},{7,15},{8,0},{9,1},... | collective-permute-start | bytes 122888 | tf_op jit(solution)/shard_map/ppermute | solution.py:1295
  26.6 5.8 %collective-permute-start.7 = (f32[40,256]{1,0:T(8,128)S(1)}, f32[40,256]{1,0:T(8,128)S(1)}, u32[]{:S(2)}, u32[]{:S(2)}) collective-permute-start(f32[40,256]{1,0:T(8,128)S(1)} %get-tuple-element.228), channel_id=1, source_target_pairs={{0,16},{1,17},{2,18},{3,19},{4,20},{5,21},{6,22},{7,23},{8,24},{9,... | collective-permute-start | bytes 122888 | tf_op jit(solution)/shard_map/ppermute | solution.py:1295
  28.8 5.8 %collective-permute-start.8 = (f32[40,256]{1,0:T(8,128)S(1)}, f32[40,256]{1,0:T(8,128)S(1)}, u32[]{:S(2)}, u32[]{:S(2)}) collective-permute-start(f32[40,256]{1,0:T(8,128)S(1)} %get-tuple-element.229), channel_id=1, source_target_pairs={{0,24},{1,25},{2,26},{3,27},{4,28},{5,29},{6,30},{7,31},{8,16},{9,... | collective-permute-start | bytes 122888 | tf_op jit(solution)/shard_map/ppermute | solution.py:1295
  34.7 1.3 %collective-permute-start.9 = (f32[64,256]{1,0:T(8,128)S(1)}, f32[64,256]{1,0:T(8,128)S(1)}, u32[]{:S(2)}, u32[]{:S(2)}) collective-permute-start(f32[64,256]{1,0:T(8,128)S(1)} %enter.1.mine_half), channel_id=1, source_target_pairs={{0,1},{1,0},{2,3},{3,2},{4,5},{5,4},{6,7},{7,6},{8,9},{9,8},{10,11... | collective-permute-start | bytes 196616 | tf_op jit(solution)/shard_map/ppermute | solution.py:1295
  38.4 2.5 %collective-permute-start.10 = (f32[16,64,128]{2,1,0:T(8,128)S(1)}, f32[16,64,128]{2,1,0:T(8,128)S(1)}, u32[]{:S(2)}, u32[]{:S(2)}) collective-permute-start(f32[16,64,128]{2,1,0:T(8,128)S(1)} %slice.58), channel_id=1, source_target_pairs={{0,1},{1,0},{2,3},{3,2},{4,5},{5,4},{6,7},{7,6},{8,9},{9,8},{10,11... | collective-permute-start | bytes 1572872 | tf_op jit(solution)/shard_map/ppermute | solution.py:1295
  41.0 8.6 %collective-permute-start.11 = (f32[8,64,128]{2,1,0:T(8,128)S(1)}, f32[8,64,128]{2,1,0:T(8,128)S(1)}, u32[]{:S(2)}, u32[]{:S(2)}) collective-permute-start(f32[8,64,128]{2,1,0:T(8,128)S(1)} %slice.60), channel_id=1, source_target_pairs={{0,2},{1,3},{2,0},{3,1},{4,6},{5,7},{6,4},{7,5},{8,10},{9,11},{10,... | collective-permute-start | bytes 786440 | tf_op jit(solution)/shard_map/ppermute | solution.py:1295
  49.7 1.9 %collective-permute-start.12 = (f32[16,56,128]{2,1,0:T(8,128)S(1)}, f32[16,56,128]{2,1,0:T(8,128)S(1)}, u32[]{:S(2)}, u32[]{:S(2)}) collective-permute-start(f32[16,56,128]{2,1,0:T(8,128)S(1)} %slice.62), channel_id=1, source_target_pairs={{0,1},{1,0},{2,3},{3,2},{4,5},{5,4},{6,7},{7,6},{8,9},{9,8},{10,11... | collective-permute-start | bytes 1376264 | tf_op jit(solution)/shard_map/ppermute | solution.py:1295
  49.8 6.4 %collective-permute-start.16 = (f32[4,64,128]{2,1,0:T(8,128)S(1)}, f32[4,64,128]{2,1,0:T(8,128)S(1)}, u32[]{:S(2)}, u32[]{:S(2)}) collective-permute-start(f32[4,64,128]{2,1,0:T(8,128)S(1)} %slice.68), channel_id=1, source_target_pairs={{0,4},{1,5},{2,6},{3,7},{4,0},{5,1},{6,2},{7,3},{8,12},{9,13},{10,... | collective-permute-start | bytes 393224 | tf_op jit(solution)/shard_map/ppermute | solution.py:1295
  51.7 7.7 %collective-permute-start.13 = (f32[4,56,128]{2,1,0:T(8,128)S(1)}, f32[4,56,128]{2,1,0:T(8,128)S(1)}, u32[]{:S(2)}, u32[]{:S(2)}) collective-permute-start(f32[4,56,128]{2,1,0:T(8,128)S(1)} %get-tuple-element.310), channel_id=1, source_target_pairs={{0,4},{1,5},{2,6},{3,7},{4,0},{5,1},{6,2},{7,3},{8,12},{9,13},{10,... | collective-permute-start | bytes 344072 | tf_op jit(solution)/shard_map/ppermute | solution.py:1295
  52.7 6.7 %collective-permute-start.15 = (f32[4,56,128]{2,1,0:T(8,128)S(1)}, f32[4,56,128]{2,1,0:T(8,128)S(1)}, u32[]{:S(2)}, u32[]{:S(2)}) collective-permute-start(f32[4,56,128]{2,1,0:T(8,128)S(1)} %get-tuple-element.311), channel_id=1, source_target_pairs={{0,2},{1,3},{2,0},{3,1},{4,6},{5,7},{6,4},{7,5},{8,10},{9,11},{10,... | collective-permute-start | bytes 344072 | tf_op jit(solution)/shard_map/ppermute | solution.py:1295
  53.7 7.0 %collective-permute-start.14 = (f32[4,56,128]{2,1,0:T(8,128)S(1)}, f32[4,56,128]{2,1,0:T(8,128)S(1)}, u32[]{:S(2)}, u32[]{:S(2)}) collective-permute-start(f32[4,56,128]{2,1,0:T(8,128)S(1)} %get-tuple-element.312), channel_id=1, source_target_pairs={{0,6},{1,7},{2,4},{3,5},{4,2},{5,3},{6,0},{7,1},{8,14},{9,15},{10,... | collective-permute-start | bytes 344072 | tf_op jit(solution)/shard_map/ppermute | solution.py:1295
  60.7 5.8 %collective-permute-start.17 = (f32[1,120,128]{2,1,0:T(8,128)S(1)}, f32[1,120,128]{2,1,0:T(8,128)S(1)}, u32[]{:S(2)}, u32[]{:S(2)}) collective-permute-start(f32[1,120,128]{2,1,0:T(8,128)S(1)} %get-tuple-element.313), channel_id=1, source_target_pairs={{0,16},{1,17},{2,18},{3,19},{4,20},{5,21},{6,22},{7,23},{8,24},{9,... | collective-permute-start | bytes 184328 | tf_op jit(solution)/shard_map/ppermute | solution.py:1295
  60.8 5.8 %collective-permute-start.19 = (f32[1,120,128]{2,1,0:T(8,128)S(1)}, f32[1,120,128]{2,1,0:T(8,128)S(1)}, u32[]{:S(2)}, u32[]{:S(2)}) collective-permute-start(f32[1,120,128]{2,1,0:T(8,128)S(1)} %get-tuple-element.314), channel_id=1, source_target_pairs={{0,8},{1,9},{2,10},{3,11},{4,12},{5,13},{6,14},{7,15},{8,0},{9,1},... | collective-permute-start | bytes 184328 | tf_op jit(solution)/shard_map/ppermute | solution.py:1295
  62.3 6.1 %collective-permute-start.18 = (f32[1,120,128]{2,1,0:T(8,128)S(1)}, f32[1,120,128]{2,1,0:T(8,128)S(1)}, u32[]{:S(2)}, u32[]{:S(2)}) collective-permute-start(f32[1,120,128]{2,1,0:T(8,128)S(1)} %get-tuple-element.315), channel_id=1, source_target_pairs={{0,24},{1,25},{2,26},{3,27},{4,28},{5,29},{6,30},{7,31},{8,16},{9,... | collective-permute-start | bytes 184328 | tf_op jit(solution)/shard_map/ppermute | solution.py:1295
  68.4 6.2 %collective-permute-start.22 = (f32[1,112,128]{2,1,0:T(8,128)S(1)}, f32[1,112,128]{2,1,0:T(8,128)S(1)}, u32[]{:S(2)}, u32[]{:S(2)}) collective-permute-start(f32[1,112,128]{2,1,0:T(8,128)S(1)} %slice.82), channel_id=1, source_target_pairs={{0,24},{1,25},{2,26},{3,27},{4,28},{5,29},{6,30},{7,31},{8,16},{9,... | collective-permute-start | bytes 172040 | tf_op jit(solution)/shard_map/ppermute | solution.py:1295
  71.4 4.2 %collective-permute-start.21 = (f32[1,112,128]{2,1,0:T(8,128)S(1)}, f32[1,112,128]{2,1,0:T(8,128)S(1)}, u32[]{:S(2)}, u32[]{:S(2)}) collective-permute-start(f32[1,112,128]{2,1,0:T(8,128)S(1)} %slice.82), channel_id=1, source_target_pairs={{0,8},{1,9},{2,10},{3,11},{4,12},{5,13},{6,14},{7,15},{8,0},{9,1},... | collective-permute-start | bytes 172040 | tf_op jit(solution)/shard_map/ppermute | solution.py:1295
  71.4 5.1 %collective-permute-start.20 = (f32[1,112,128]{2,1,0:T(8,128)S(1)}, f32[1,112,128]{2,1,0:T(8,128)S(1)}, u32[]{:S(2)}, u32[]{:S(2)}) collective-permute-start(f32[1,112,128]{2,1,0:T(8,128)S(1)} %slice.82), channel_id=1, source_target_pairs={{0,16},{1,17},{2,18},{3,19},{4,20},{5,21},{6,22},{7,23},{8,24},{9,... | collective-permute-start | bytes 172040 | tf_op jit(solution)/shard_map/ppermute | solution.py:1295
  76.5 7.2 %collective-permute-start.25 = (f32[4,112,128]{2,1,0:T(8,128)S(1)}, f32[4,112,128]{2,1,0:T(8,128)S(1)}, u32[]{:S(2)}, u32[]{:S(2)}) collective-permute-start(f32[4,112,128]{2,1,0:T(8,128)S(1)} %pad_maximum_fusion.refs_0_), channel_id=1, source_target_pairs={{0,6},{1,7},{2,4},{3,5},{4,2},{5,3},{6,0},{7,1},{8,14},{9,15},{10,... | collective-permute-start | bytes 688136 | tf_op jit(solution)/shard_map/ppermute | solution.py:1295
  77.9 7.7 %collective-permute-start.24 = (f32[4,112,128]{2,1,0:T(8,128)S(1)}, f32[4,112,128]{2,1,0:T(8,128)S(1)}, u32[]{:S(2)}, u32[]{:S(2)}) collective-permute-start(f32[4,112,128]{2,1,0:T(8,128)S(1)} %pad_maximum_fusion.refs_0_), channel_id=1, source_target_pairs={{0,2},{1,3},{2,0},{3,1},{4,6},{5,7},{6,4},{7,5},{8,10},{9,11},{10,... | collective-permute-start | bytes 688136 | tf_op jit(solution)/shard_map/ppermute | solution.py:1295
  79.0 7.0 %collective-permute-start.23 = (f32[4,112,128]{2,1,0:T(8,128)S(1)}, f32[4,112,128]{2,1,0:T(8,128)S(1)}, u32[]{:S(2)}, u32[]{:S(2)}) collective-permute-start(f32[4,112,128]{2,1,0:T(8,128)S(1)} %pad_maximum_fusion.refs_0_), channel_id=1, source_target_pairs={{0,4},{1,5},{2,6},{3,7},{4,0},{5,1},{6,2},{7,3},{8,12},{9,13},{10,... | collective-permute-start | bytes 688136 | tf_op jit(solution)/shard_map/ppermute | solution.py:1295
  80.1 6.1 %collective-permute-start.26 = (f32[4,112,128]{2,1,0:T(8,128)S(1)}, f32[4,112,128]{2,1,0:T(8,128)S(1)}, u32[]{:S(2)}, u32[]{:S(2)}) collective-permute-start(f32[4,112,128]{2,1,0:T(8,128)S(1)} %pad_maximum_fusion.refs_0_), channel_id=1, source_target_pairs={{0,1},{1,0},{2,3},{3,2},{4,5},{5,4},{6,7},{7,6},{8,9},{9,8},{10,11... | collective-permute-start | bytes 688136 | tf_op jit(solution)/shard_map/ppermute | solution.py:1295
  83.7 2.4 %collective-permute-start.29 = (f32[4,112,128]{2,1,0:T(8,128)S(1)}, f32[4,112,128]{2,1,0:T(8,128)S(1)}, u32[]{:S(2)}, u32[]{:S(2)}) collective-permute-start(f32[4,112,128]{2,1,0:T(8,128)S(1)} %collective-permute-done.25.refs_3_), channel_id=1, source_target_pairs={{0,1},{1,0},{2,3},{3,2},{4,5},{5,4},{6,7},{7,6},{8,9},{9,8},{10,11... | collective-permute-start | bytes 688136 | tf_op jit(solution)/shard_map/ppermute | solution.py:1295
  85.6 1.5 %collective-permute-start.28 = (f32[4,112,128]{2,1,0:T(8,128)S(1)}, f32[4,112,128]{2,1,0:T(8,128)S(1)}, u32[]{:S(2)}, u32[]{:S(2)}) collective-permute-start(f32[4,112,128]{2,1,0:T(8,128)S(1)} %collective-permute-done.24.refs_2_), channel_id=1, source_target_pairs={{0,1},{1,0},{2,3},{3,2},{4,5},{5,4},{6,7},{7,6},{8,9},{9,8},{10,11... | collective-permute-start | bytes 688136 | tf_op jit(solution)/shard_map/ppermute | solution.py:1295
  86.1 1.5 %collective-permute-start.27 = (f32[4,112,128]{2,1,0:T(8,128)S(1)}, f32[4,112,128]{2,1,0:T(8,128)S(1)}, u32[]{:S(2)}, u32[]{:S(2)}) collective-permute-start(f32[4,112,128]{2,1,0:T(8,128)S(1)} %collective-permute-done.23.refs_1_), channel_id=1, source_target_pairs={{0,1},{1,0},{2,3},{3,2},{4,5},{5,4},{6,7},{7,6},{8,9},{9,8},{10,11... | collective-permute-start | bytes 688136 | tf_op jit(solution)/shard_map/ppermute | solution.py:1295
